TPU v7x, 128 devices: a whole 4x4x4 slice. The times are simulated.
128 devices in a mesh: ctx: 16 (over z, x_lo, core), fsdp: 8 (over y, x_hi).
Axes of the slice: x: 4 (x_hi: 2, x_lo: 2; x = x_hi * 2 + x_lo), y: 4, z: 4, core: 2. Of those that a mesh axis runs over, the one named last changes fastest.
Arguments:
- hidden: bfloat16 [8, 2048, 2048], P('fsdp', 'ctx'), may hold values from -6 to 6
- positions: int32 [8, 2048], P('fsdp', 'ctx'), may hold values from 0 to 2047, as said below
- gain_attn: bfloat16 [2048], replicated, may hold values from 0.5 to 1.5
- w_qkv: bfloat16 [2560, 2048], P('fsdp'), may hold values from -0.125 to 0.125
- w_out: bfloat16 [2048, 2048], P('fsdp'), may hold values from -3 to 3
- gain_mlp: bfloat16 [2048], replicated, may hold values from 0.5 to 1.5
- w_gate_up: bfloat16 [2, 5632, 2048], P(None, 'fsdp'), may hold values from -0.125 to 0.125
- w_down: bfloat16 [2048, 5632], P(None, 'fsdp'), may hold values from -0.078125 to 0.078125
- cotangent: bfloat16 [8, 2048, 2048], P('fsdp', 'ctx'), may hold values from -6 to 6
Outputs:
- output: bfloat16 [8, 2048, 2048], P('fsdp', 'ctx')
- grad_hidden: float32 [8, 2048, 2048], P('fsdp', 'ctx')
- grad_gain_attn: float32 [2048], P('fsdp')
- grad_w_qkv: float32 [2560, 2048], P('fsdp')
- grad_w_out: float32 [2048, 2048], P('fsdp')
- grad_gain_mlp: float32 [2048], P('fsdp')
- grad_w_gate_up: float32 [2, 5632, 2048], P(None, 'fsdp')
- grad_w_down: float32 [2048, 5632], P(None, 'fsdp')
Inputs may be any that keep to these rules, and one draw needn't show every extreme that they name: Each row lists the positions of one sequence's stored tokens: a permutation of 0 to 2047 made of runs of 64 consecutive rising values, each run starting at a multiple of 64.
All inputs are finite; a program needn't handle non-finite values.
Results may differ from a plain program's by a relative error of at most 0.03.
Values may be sent and summed in bfloat16 or wider, within the bound.
A program may use at most 384 MiB of HBM per device.

v0:
```python
import jax
import jax.numpy as jnp
from jax import lax
from jax.sharding import PartitionSpec as P

H = 32
KV = 4
HD = 64


EPSILON = 1e-05
FILLER = -1e30


def passed_along(block, axis, distance):
    devices = range(lax.axis_size(axis))
    route = [((i - distance) % len(devices), i) for i in devices]
    return lax.ppermute(block, axis, route)


def rotary(values_in, cosine, sine_part):
    half_width = values_in.shape[-1] // 2
    turned = jnp.concatenate([-values_in[..., half_width:], values_in[..., :half_width]], axis=-1)
    return values_in * cosine + turned * sine_part


def angles(places):
    steps_half = jnp.arange(HD // 2, dtype=jnp.float32)
    inverse = jnp.power(10000.0, steps_half * (-2.0 / HD))
    turning = places.astype(jnp.float32)[:, None] * inverse[None, :]
    turning = jnp.concatenate([turning, turning], axis=-1)
    return (jnp.cos(turning), jnp.sin(turning))


def norm_back(grad_norm, normal, inverse):
    return inverse * (grad_norm - normal * jnp.mean(grad_norm * normal, axis=-1, keepdims=True))


def contract_rows(left_side, right_side):
    return lax.dot_general(
        left_side, right_side, (((0,), (0,)), ((), ())), preferred_element_type=jnp.float32
    )


def contract_last(left_side, right_side):
    return lax.dot_general(
        left_side, right_side, (((1,), (1,)), ((), ())), preferred_element_type=jnp.float32
    )


def product(left_side, right_side):
    return jnp.dot(left_side, right_side, preferred_element_type=jnp.float32)


def feed_forward(inputs, back_rows, gate_up, down_part):
    gate_values = contract_last(inputs, gate_up[0])
    upward = contract_last(inputs, gate_up[1])
    sigmoid_gate = jax.nn.sigmoid(gate_values)
    swish_gate = gate_values * sigmoid_gate
    active = (swish_gate * upward).astype(jnp.bfloat16)
    branch = contract_last(active, down_part)
    grad_active = product(back_rows, down_part)
    grad_upward = (grad_active * swish_gate).astype(jnp.bfloat16)
    grad_gate = (
        grad_active * upward * sigmoid_gate * (1.0 + gate_values * (1.0 - sigmoid_gate))
    ).astype(jnp.bfloat16)
    grad_inputs = product(grad_gate, gate_up[0]) + product(grad_upward, gate_up[1])
    grad_gate_up = jnp.stack([contract_rows(grad_gate, inputs), contract_rows(grad_upward, inputs)])
    grad_down = contract_rows(back_rows, active)
    return (branch, grad_inputs, grad_gate_up, grad_down)


def body(hidden, positions, gain_attn, w_qkv, w_out, gain_mlp, w_gate_up, w_down, cotangent):
    tokens = hidden[0].astype(jnp.float32)
    places = positions[0]
    length = tokens.shape[0]
    group_size = H // KV
    width_q = H * HD
    width_kv = KV * HD
    rows_total = group_size * length
    factor = HD ** (-0.5)
    block_count = lax.axis_size("ctx")
    block_index = lax.axis_index("ctx")
    all_places = lax.all_gather(places, "ctx", axis=0, tiled=True)
    gain_one = gain_attn.astype(jnp.float32)
    gain_two = gain_mlp.astype(jnp.float32)
    inverse_one = lax.rsqrt(jnp.mean(tokens * tokens, axis=-1, keepdims=True) + EPSILON)
    normal_one = tokens * inverse_one
    input_one = (normal_one * gain_one).astype(jnp.bfloat16)
    qkv_full, out_full = (
        lax.all_gather(w_qkv, "fsdp", axis=0, tiled=True),
        lax.all_gather(w_out, "fsdp", axis=0, tiled=True),
    )
    projected = contract_last(input_one, qkv_full)
    cosine, sine_part = angles(places)
    cosine = cosine[:, None, :]
    sine_part = sine_part[:, None, :]
    query_heads = rotary(projected[:, :width_q].reshape(length, H, HD), cosine, sine_part).astype(
        jnp.bfloat16
    )
    key_heads = rotary(
        projected[:, width_q : width_q + width_kv].reshape(length, KV, HD), cosine, sine_part
    )
    key_flat = key_heads.reshape(length, width_kv).astype(jnp.bfloat16)
    value_flat = projected[:, width_q + width_kv :].astype(jnp.bfloat16)
    query_groups = (
        query_heads.reshape(length, KV, group_size, HD)
        .transpose(1, 2, 0, 3)
        .reshape(KV, rows_total, HD)
    )
    query_places = jnp.tile(places, group_size)

    def source_places(turn_index):
        source = (block_index - turn_index) % block_count
        return lax.dynamic_slice_in_dim(all_places, source * length, length)

    def visible(key_places):
        return (key_places[None, :] <= query_places[:, None])[None]

    def attend(running, key_part, value_part, key_places):
        highest, totals, gathered = running
        key_mat = key_part.reshape(-1, KV, HD)
        value_mat = value_part.reshape(-1, KV, HD)
        scores = (
            jnp.einsum("kqd,tkd->kqt", query_groups, key_mat, preferred_element_type=jnp.float32)
            * factor
        )
        allowed = visible(key_places)
        scores = jnp.where(allowed, scores, FILLER)
        new_high = jnp.maximum(highest, jnp.max(scores, axis=-1))
        weights = jnp.where(allowed, jnp.exp(scores - new_high[..., None]), 0.0)
        rescale = jnp.exp(highest - new_high)
        totals = totals * rescale + jnp.sum(weights, axis=-1)
        gathered = gathered * rescale[..., None] + jnp.einsum(
            "kqt,tkd->kqd",
            weights.astype(jnp.bfloat16),
            value_mat,
            preferred_element_type=jnp.float32,
        )
        return (new_high, totals, gathered)

    def forward_turn(turn_index, carried):
        running, key_part, value_part = carried
        running = attend(running, key_part, value_part, source_places(turn_index))
        key_part, value_part = passed_along((key_part, value_part), "ctx", 1)
        return (running, key_part, value_part)

    start_state = (
        jnp.full((KV, rows_total), FILLER, jnp.float32),
        jnp.zeros((KV, rows_total), jnp.float32),
        jnp.zeros((KV, rows_total, HD), jnp.float32),
    )
    running, key_last, value_last = lax.fori_loop(
        0, block_count - 1, forward_turn, (start_state, key_flat, value_flat)
    )
    highest, totals, gathered = attend(
        running, key_last, value_last, source_places(block_count - 1)
    )
    attended = gathered / totals[..., None]
    log_totals = highest + jnp.log(totals)
    attended_low = attended.astype(jnp.bfloat16)
    attended_rows = (
        attended_low.reshape(KV, group_size, length, HD)
        .transpose(2, 0, 1, 3)
        .reshape(length, width_q)
    )
    middle = tokens + contract_last(attended_rows, out_full)
    inverse_two = lax.rsqrt(jnp.mean(middle * middle, axis=-1, keepdims=True) + EPSILON)
    normal_two = middle * inverse_two
    input_two = (normal_two * gain_two).astype(jnp.bfloat16)
    gate_up_full, down_full = (
        lax.all_gather(w_gate_up, "fsdp", axis=1, tiled=True),
        lax.all_gather(w_down, "fsdp", axis=1, tiled=True),
    )
    branch, grad_input_two, gate_up_term, down_term = feed_forward(
        input_two, cotangent[0], gate_up_full, down_full
    )
    grad_gate_up, grad_down = (
        lax.psum_scatter(
            gate_up_term.astype(jnp.bfloat16), "fsdp", scatter_dimension=1, tiled=True
        ).astype(jnp.float32),
        lax.psum_scatter(
            down_term.astype(jnp.bfloat16), "fsdp", scatter_dimension=1, tiled=True
        ).astype(jnp.float32),
    )
    output = (middle + branch).astype(jnp.bfloat16)
    grad_output = cotangent[0].astype(jnp.float32)
    grad_gain_two = jnp.sum(normal_two * grad_input_two, axis=0)
    grad_middle = grad_output + norm_back(grad_input_two * gain_two, normal_two, inverse_two)
    grad_branch = grad_middle.astype(jnp.bfloat16)
    grad_out_term = contract_rows(grad_branch, attended_rows)
    grad_attended = product(grad_branch, out_full).astype(jnp.bfloat16)
    grad_groups = (
        grad_attended.reshape(length, KV, group_size, HD)
        .transpose(1, 2, 0, 3)
        .reshape(KV, rows_total, HD)
    )
    softmax_dot = jnp.sum(grad_groups.astype(jnp.float32) * attended, axis=-1)

    def attend_back(grad_query, key_part, value_part, key_places):
        key_mat = key_part.reshape(-1, KV, HD)
        value_mat = value_part.reshape(-1, KV, HD)
        scores = (
            jnp.einsum("kqd,tkd->kqt", query_groups, key_mat, preferred_element_type=jnp.float32)
            * factor
        )
        allowed = visible(key_places)
        scores = jnp.where(allowed, scores, FILLER)
        probabilities = jnp.where(allowed, jnp.exp(scores - log_totals[..., None]), 0.0)
        grad_probs = jnp.einsum(
            "kqd,tkd->kqt", grad_groups, value_mat, preferred_element_type=jnp.float32
        )
        grad_scores = (probabilities * (grad_probs - softmax_dot[..., None])).astype(jnp.bfloat16)
        grad_query = (
            grad_query
            + jnp.einsum("kqt,tkd->kqd", grad_scores, key_mat, preferred_element_type=jnp.float32)
            * factor
        )
        key_term = (
            jnp.einsum(
                "kqt,kqd->tkd", grad_scores, query_groups, preferred_element_type=jnp.float32
            )
            * factor
        ).reshape(-1, width_kv)
        value_term = jnp.einsum(
            "kqt,kqd->tkd",
            probabilities.astype(jnp.bfloat16),
            grad_groups,
            preferred_element_type=jnp.float32,
        ).reshape(-1, width_kv)
        return (grad_query, key_term, value_term)

    def pass_grads(grad_key, grad_value):
        return (
            passed_along(grad_key.astype(jnp.bfloat16), "ctx", 1).astype(grad_key.dtype),
            passed_along(grad_value.astype(jnp.bfloat16), "ctx", 1).astype(grad_value.dtype),
        )

    def backward_turn(turn_index, carried):
        grad_query, key_part, value_part, grad_key, grad_value = carried
        grad_query, key_term, value_term = attend_back(
            grad_query, key_part, value_part, source_places(turn_index)
        )
        grad_key, grad_value = pass_grads(grad_key + key_term, grad_value + value_term)
        key_part, value_part = passed_along((key_part, value_part), "ctx", 1)
        return (grad_query, key_part, value_part, grad_key, grad_value)

    zeros_kv = jnp.zeros((length, width_kv), jnp.float32)
    carried = lax.fori_loop(
        0,
        block_count - 1,
        backward_turn,
        (jnp.zeros((KV, rows_total, HD), jnp.float32), key_flat, value_flat, zeros_kv, zeros_kv),
    )
    grad_query, key_last, value_last, grad_key, grad_value = carried
    grad_query, key_term, value_term = attend_back(
        grad_query, key_last, value_last, source_places(block_count - 1)
    )
    grad_key, grad_value = pass_grads(grad_key + key_term, grad_value + value_term)
    grad_query = (
        grad_query.reshape(KV, group_size, length, HD).transpose(2, 0, 1, 3).reshape(length, H, HD)
    )
    grad_query = rotary(grad_query, cosine, -sine_part).reshape(length, width_q)
    grad_key = rotary(grad_key.reshape(length, KV, HD), cosine, -sine_part).reshape(
        length, width_kv
    )
    grad_projected = jnp.concatenate([grad_query, grad_key, grad_value], axis=1).astype(
        jnp.bfloat16
    )
    grad_qkv_term = contract_rows(grad_projected, input_one)
    grad_input_one = product(grad_projected, qkv_full)
    grad_gain_one = jnp.sum(normal_one * grad_input_one, axis=0)
    qkv_share, out_share, gain_one_share, gain_two_share = (
        lax.psum_scatter(
            grad_qkv_term.astype(jnp.bfloat16), "fsdp", scatter_dimension=0, tiled=True
        ).astype(jnp.float32),
        lax.psum_scatter(
            grad_out_term.astype(jnp.bfloat16), "fsdp", scatter_dimension=0, tiled=True
        ).astype(jnp.float32),
        lax.psum_scatter(
            grad_gain_one.astype(jnp.bfloat16), "fsdp", scatter_dimension=0, tiled=True
        ).astype(jnp.float32),
        lax.psum_scatter(
            grad_gain_two.astype(jnp.bfloat16), "fsdp", scatter_dimension=0, tiled=True
        ).astype(jnp.float32),
    )
    grad_tokens = grad_middle + norm_back(grad_input_one * gain_one, normal_one, inverse_one)
    summed = (
        lax.psum(gain_one_share.astype(jnp.bfloat16), "ctx").astype(jnp.float32),
        lax.psum(qkv_share.astype(jnp.bfloat16), "ctx").astype(jnp.float32),
        lax.psum(out_share.astype(jnp.bfloat16), "ctx").astype(jnp.float32),
        lax.psum(gain_two_share.astype(jnp.bfloat16), "ctx").astype(jnp.float32),
        lax.psum(grad_gate_up.astype(jnp.bfloat16), "ctx").astype(jnp.float32),
        lax.psum(grad_down.astype(jnp.bfloat16), "ctx").astype(jnp.float32),
    )
    return (
        output[None],
        grad_tokens[None],
        summed[0],
        summed[1],
        summed[2],
        summed[3],
        summed[4],
        summed[5],
    )


def solution(mesh):
    placed = (
        P("fsdp", "ctx", None),
        P("fsdp", "ctx"),
        P(),
        P("fsdp", None),
        P("fsdp", None),
        P(),
        P(None, "fsdp", None),
        P(None, "fsdp"),
        P("fsdp", "ctx", None),
    )
    return jax.shard_map(
        body,
        mesh=mesh,
        in_specs=placed,
        out_specs=(
            P("fsdp", "ctx", None),
            P("fsdp", "ctx", None),
            P("fsdp"),
            P("fsdp", None),
            P("fsdp", None),
            P("fsdp"),
            P(None, "fsdp", None),
            P(None, "fsdp"),
        ),
        check_vma=False,
    )
```

profile of v0, /device:TPU:9, one launch (start us, length us, event | category | flops | bytes accessed | tf_op | source)
XLA Modules:
  0.0 2386.3 jit_solution(10411532235979735490)
XLA Ops:
  11.7 21.2 all-gather
  34.6 102.3 %all-gather.6.cloned.1.call-done = bf16[2560,2048]{1,0:T(8,128)(2,1)} async-done(((bf16[320,2048]{1,0:T(8,128)(2,1)}), bf16[2560,2048]{1,0:T(8,128)(2,1)}) %all-gather.6.cloned.1.call-update) | async-done | bytes 10485776 | tf_op jit(solution)/shard_map/all_gather | solution.py:91
  136.9 7.6 fusion.68
  152.0 110.7 %while.48 = (s32[]{:T(128)}, f32[4,1024]{1,0:T(4,128)S(1)}, f32[4,1024]{1,0:T(4,128)S(1)}, f32[4,1024,64]{1,2,0:T(8,128)}, bf16[128,256]{0,1:T(8,128)(2,1)S(1)},...) while((s32[]{:T(128)}, f32[4,1024]{1,0:T(4,128)S(1)}, ...), condition=%wide.region_4.5_spmd.clone, body=%wide.region_1.4_spmd.clone.sunk | while | flops 141971472 | bytes 19016148 | solution.py:153
  158.6 2.5 collective-permute-start
  166.0 3.1 collective-permute-start
  179.4 2.8 collective-permute-start
  192.5 2.6 collective-permute-start
  200.0 3.1 collective-permute-start
  208.2 3.1 collective-permute-start
  232.3 3.6 collective-permute-done
  266.5 9.2 multiply_reduce_fusion.3
  275.8 427.2 %all-gather.10.cloned.1.call-done = bf16[2,5632,2048]{2,1,0:T(8,128)(2,1)} async-done(((bf16[2,704,2048]{2,1,0:T(8,128)(2,1)}), bf16[2,5632,2048]{2,1,0:T(8,128)(2,1)}) %all-gather.10.cloned.1.call-update) | async-done | bytes 46137360 | tf_op jit(solution)/shard_map/all_gather | solution.py:172
  703.0 13.2 fusion.23
  716.2 15.3 fusion.25
  731.5 211.0 %all-gather.12.cloned.1.call-done = bf16[2048,5632]{0,1:T(8,128)(2,1)} async-done(((bf16[2048,704]{0,1:T(8,128)(2,1)}), bf16[2048,5632]{0,1:T(8,128)(2,1)}) %all-gather.12.cloned.1.call-update) | async-done | bytes 23068688 | tf_op jit(solution)/shard_map/all_gather | solution.py:173
  942.5 15.3 multiply_convert_fusion.1
  957.8 9.8 fusion.22
  967.6 10.4 multiply_reduce_fusion
  979.7 5.7 convolution_convert_fusion.1
  985.4 4.6 convolution_convert_fusion.2
  994.6 266.0 %while.49 = (s32[]{:T(128)}, f32[4,1024,64]{1,2,0:T(8,128)S(1)}, bf16[128,256]{0,1:T(8,128)(2,1)}, bf16[128,256]{0,1:T(8,128)(2,1)}, f32[128,256]{0,1:T(8,128)S(...) while((s32[]{:T(128)}, f32[4,1024,64]{1,2,0:T(8,128)S(1)}, ...), condition=%wide.region_11.12_spmd.clone, body=%wide.region_10.11_spmd.clone.sunk | while | flops 340951040 | bytes 16755204 | solution.py:249
  1004.9 2.6 collective-permute-start.4
  1014.2 2.5 collective-permute-start.2
  1043.4 2.9 collective-permute-start.4
  1052.7 2.5 collective-permute-start.2
  1070.0 2.5 collective-permute-start.2
  1105.6 2.5 collective-permute-start.2
  1150.0 3.1 collective-permute-start.4
  1185.3 2.7 collective-permute-start.4
  1219.7 3.2 collective-permute-start.4
  1270.6 7.7 convolution_convert_fusion
  1279.8 11.4 convert_bitcast_fusion
  1292.2 12.4 convert_bitcast_fusion.1
  1304.6 11.5 convert_bitcast_fusion.2
  1316.1 31.9 %pad_maximum_fusion = bf16[2,5632,2048]{2,1,0:T(8,128)(2,1)} fusion(bf16[1,5632,2048]{2,1,0:T(8,128)(2,1)} %convert_bitcast_fusion.1, bf16[1,5632,2048]{2,1,0:T(8,128)(2,1)} %convert_bitcast_fusion.2), kind=kLoop, calls=%fused_computation.36 | loop fusion | flops 23068672 | bytes 92274688 | tf_op jit(solution)/shard_map/stack | solution.py:68
  1348.4 61.2 %reduce-scatter.5.cloned.1.call-done = bf16[320,2048]{1,0:T(8,128)(2,1)} async-done(((bf16[2560,2048]{1,0:T(8,128)(2,1)}), bf16[320,2048]{1,0:T(8,128)(2,1)}) %reduce-scatter.5.cloned.1.call-update) | async-done | bytes 1310736 | tf_op jit(solution)/shard_map/reduce_scatter | solution.py:274
  1409.5 245.7 %reduce-scatter.11.cloned.1.call-done = bf16[2048,704]{0,1:T(8,128)(2,1)} async-done(((bf16[2048,5632]{0,1:T(8,128)(2,1)}), bf16[2048,704]{0,1:T(8,128)(2,1)}) %reduce-scatter.11.cloned.1.call-update) | async-done | bytes 2883600 | tf_op jit(solution)/shard_map/reduce_scatter | solution.py:182
  1655.2 455.0 %reduce-scatter.9.cloned.1.call-done = bf16[2,704,2048]{2,1,0:T(8,128)(2,1)} async-done(((bf16[2,5632,2048]{2,1,0:T(8,128)(2,1)}), bf16[2,704,2048]{2,1,0:T(8,128)(2,1)}) %reduce-scatter.9.cloned.1.call-update) | async-done | bytes 5767184 | tf_op jit(solution)/shard_map/reduce_scatter | solution.py:179
  2112.2 12.3 fusion.29
  2124.5 2.6 fusion.47
  2127.1 20.1 all-reduce.4
  2147.4 34.0 %all-reduce.2 = (bf16[256]{0:T(256)(128)(2,1)S(1)}, bf16[256]{0:T(256)(128)(2,1)S(1)}) all-reduce(bf16[256]{0:T(256)(128)(2,1)S(1)} %dynamic-slice.2, bf16[256]{0:T(256)(128)(2,1)S(1)} %dynamic-slice.4), channel_id=1, replica_groups=mesh['ctx'=16,'fsdp'=8] {'ctx'}, use_global_device_ids=true, to_apply=%region_15.16 | all-reduce | flops 512 | bytes 2048 | tf_op jit(solution)/shard_map/psum | solution.py:289
  2182.5 2.7 fusion.46
  2185.2 180.1 %all-reduce.7.cloned.1.call-done = (bf16[320,2048]{1,0:T(8,128)(2,1)}, bf16[256,2048]{1,0:T(8,128)(2,1)}, bf16[2,704,2048]{2,1,0:T(8,128)(2,1)}, bf16[2048,704]{0,1:T(8,128)(2,1)}) async-done(((bf16[320,2048]{1,0:T(8,128)(2,1)}, bf16[256,2048]{1,0:T(8,128)(2,1)}, bf16[2,704,2048]{2,1,0:T(8,128)(2,1)}, bf16[2048,704]{0,1:T(8,128)(2,1)}), (bf16[320,2048]{1,0:T(8,128)(2,1)}, bf16[256,2048]{1,0:T(8,128)(2,1)}, ...) | async-done | bytes 11010064 | tf_op jit(solution)/shard_map/psum | solution.py:290
  2365.4 3.3 convert_element_type.226
  2370.2 6.0 convert_element_type.231
  2376.2 3.3 convert_element_type.234
  (787 shorter events, 368.7 us)
Async XLA Ops:
  7.2 129.7 %all-gather.6.cloned.1.call-start = ((), (), s32[]{:S(2)}) async-start(), calls=%async_computation.4 | async-start | bytes 11796480 | tf_op jit(solution)/shard_map/all_gather | solution.py:91
  7.9 258.4 %all-gather.8.cloned.1.call-start = ((), (), s32[]{:S(2)}) async-start(), calls=%async_computation.5 | async-start | bytes 9437184 | tf_op jit(solution)/shard_map/all_gather | solution.py:92
  8.7 694.4 %all-gather.10.cloned.1.call-start = ((), (), s32[]{:S(2)}) async-start(), calls=%async_computation.6 | async-start | bytes 51904512 | tf_op jit(solution)/shard_map/all_gather | solution.py:172
  9.4 933.1 %all-gather.12.cloned.1.call-start = ((), (), s32[]{:S(2)}) async-start(), calls=%async_computation.7 | async-start | bytes 25952256 | tf_op jit(solution)/shard_map/all_gather | solution.py:173
  10.0 1338.4 %reduce-scatter.7.cloned.1.call-start = ((), (), s32[]{:S(2)}) async-start(), calls=%async_computation.9 | async-start | bytes 9437184 | tf_op jit(solution)/shard_map/reduce_scatter | solution.py:277
  158.6 7.4 collective-permute-start
  166.0 8.0 collective-permute-start
  179.4 8.0 collective-permute-start
  192.5 7.5 collective-permute-start
  200.0 8.0 collective-permute-start
  208.2 9.2 collective-permute-start
  217.4 9.2 collective-permute-start
  226.7 9.2 collective-permute-start
  227.4 8.6 collective-permute-start.1
  993.7 415.8 %reduce-scatter.5.cloned.1.call-start = ((), (), s32[]{:S(2)}) async-start(), calls=%async_computation.8 | async-start | bytes 11796480 | tf_op jit(solution)/shard_map/reduce_scatter | solution.py:274
  995.4 17.9 collective-permute-start.2
  997.5 15.8 collective-permute-start.3
  1014.2 17.6 collective-permute-start.2
  1017.5 14.3 collective-permute-start.3
  1032.7 19.2 collective-permute-start.2
  1036.0 15.9 collective-permute-start.3
  1052.7 16.3 collective-permute-start.2
  1056.1 13.0 collective-permute-start.3
  1070.0 16.6 collective-permute-start.2
  1073.3 13.3 collective-permute-start.3
  1087.4 17.3 collective-permute-start.2
  1090.6 14.1 collective-permute-start.3
  1105.6 17.0 collective-permute-start.2
  1108.9 13.7 collective-permute-start.3
  1123.5 16.2 collective-permute-start.2
  1126.0 13.6 collective-permute-start.3
  1140.5 16.2 collective-permute-start.2
  1142.7 14.0 collective-permute-start.3
  1157.6 16.2 collective-permute-start.2
  1160.7 13.1 collective-permute-start.3
  1174.7 16.8 collective-permute-start.2
  1177.9 13.6 collective-permute-start.3
  1192.3 15.9 collective-permute-start.2
  1195.5 12.7 collective-permute-start.3
  1209.1 17.3 collective-permute-start.2
  1212.3 14.1 collective-permute-start.3
  1227.3 16.2 collective-permute-start.2
  1230.5 13.0 collective-permute-start.3
  1244.4 16.2 collective-permute-start.2
  1247.6 13.0 collective-permute-start.3
  1278.3 376.9 %reduce-scatter.11.cloned.1.call-start = ((), (), s32[]{:S(2)}) async-start(), calls=%async_computation.11 | async-start | bytes 25952256 | tf_op jit(solution)/shard_map/reduce_scatter | solution.py:182
  1291.2 819.0 %reduce-scatter.9.cloned.1.call-start = ((), (), s32[]{:S(2)}) async-start(), calls=%async_computation.10 | async-start | bytes 51904512 | tf_op jit(solution)/shard_map/reduce_scatter | solution.py:179
  1348.1 1017.3 %all-reduce.7.cloned.1.call-start = ((), (), s32[]{:S(2)}) async-start(), calls=%async_computation.12 | async-start | bytes 22020096 | tf_op jit(solution)/shard_map/psum | solution.py:290
  (129 other events, 2303.0 us)
Sparse Core Ops, SparseCore 0:
  10.3 126.5 all-gather.5
  139.2 116.0 all-gather.7
  257.7 445.3 all-gather.9
  705.2 237.3 all-gather.11
  993.8 123.2 reduce-scatter.6
  1278.4 131.0 reduce-scatter.4
  1414.0 241.1 reduce-scatter.10
  1659.7 450.4 reduce-scatter.8
  2113.0 252.2 all-reduce.6
where the time goes:
time: 2400 us; the launch traced here: 2390 us
  waiting for transfers between devices  1720 us (72%)
  matrix products  250 us (10%)
  other arithmetic  129 us (5%)
  local copies, waits for them, and re-layouts  107 us (4%)
  starting transfers between devices  92 us (4%)
  blocking collectives  75.3 us (3%)
    reduce_scatter x1, waiting for transfers between devices, body(): lax.psum_scatter(gate_up_term.astype(jnp.bfloat16), 'fsdp', scatter_dimen...  455 us
    all_gather x1, waiting for transfers between devices, body(): lax.all_gather(w_gate_up, 'fsdp', axis=1, tiled=True)  427 us
    reduce_scatter x1, waiting for transfers between devices, body(): lax.psum_scatter(down_term.astype(jnp.bfloat16), 'fsdp', scatter_dimensio...  246 us
    all_gather x1, waiting for transfers between devices, body(): lax.all_gather(w_down, 'fsdp', axis=1, tiled=True)  211 us
    psum x1, waiting for transfers between devices, body(): lax.psum(qkv_share.astype(jnp.bfloat16), 'ctx').astype(jnp.float32)  180 us
    all_gather x1, waiting for transfers between devices, body(): lax.all_gather(w_qkv, 'fsdp', axis=0, tiled=True)  102 us
    ppermute x92, starting transfers between devices, passed_along(): return lax.ppermute(block, axis, route)  91.4 us
    reduce_scatter x1, waiting for transfers between devices, body(): lax.psum_scatter(grad_qkv_term.astype(jnp.bfloat16), 'fsdp', scatter_dime...  61.2 us
  transfers between devices with their start and end apart: 101, of which 52 were waited for; matrix products, arithmetic and copies ran while one was open for 17% of the time, Pallas kernels for 0%

commit v1 on v0

v1 whole, which is shorter than its diff:
```python
import jax
import jax.numpy as jnp
from jax import lax
from jax.experimental import pallas as pl
from jax.experimental.pallas import tpu as pltpu
from jax.sharding import Mesh
from jax.sharding import PartitionSpec as P

D = 2048
H = 32
KV = 4
HD = 64
FF = 5632
TOK = 128
HALF = 64
FF_DEV = 704
Q_DEV = 256
EPSILON = 1e-05
FILLER = -1e30
AXES = ("z", "xl", "c", "y", "xh")
ANY = pl.BlockSpec(memory_space=pl.ANY)
VMEM = pl.BlockSpec(memory_space=pltpu.VMEM)
BF16 = jnp.bfloat16
F32 = jnp.float32


class Place:
    def __init__(self):
        self.z, self.xl, self.c, self.y, self.xh = (lax.axis_index(a) for a in AXES)

    def at(self, dz=0, dy=0, core=None, xl=None, xh=None, y=None):
        z = lax.rem(self.z + dz + 4, 4) if dz else self.z
        y = (lax.rem(self.y + dy + 4, 4) if dy else self.y) if y is None else y
        return (
            z,
            self.xl if xl is None else xl,
            self.c if core is None else core,
            y,
            self.xh if xh is None else xh,
        )


class Edges:
    def __init__(self, send, recv):
        self.send, self.recv, self.count, self.started = send, recv, 0, []

    def copy(self, src, dst, device, start=True):
        i = self.count
        self.count += 1
        d = pltpu.make_async_remote_copy(
            src_ref=src,
            dst_ref=dst,
            send_sem=self.send.at[i],
            recv_sem=self.recv.at[i],
            device_id=device,
            device_id_type=pl.DeviceIdType.MESH,
        )
        self.started.append(d)
        if start:
            d.start()
        return d

    def finish(self):
        for d in self.started:
            d.wait_send()


def greet(devices):
    barrier = pltpu.get_barrier_semaphore()
    for device in devices:
        pl.semaphore_signal(
            barrier, inc=1, device_id=device, device_id_type=pl.DeviceIdType.MESH
        )
    pl.semaphore_wait(barrier, len(devices))


def group_members(me):
    found = [me.at(core=1 - me.c)]
    for dy in (1, 2, 3):
        found += [me.at(dy=dy), me.at(dy=dy, core=1 - me.c)]
    return found


class RingGather:
    def __init__(self, me, edges, own, out):
        self.me, self.edges, self.out = me, edges, out
        self.core = me.at(core=1 - me.c)
        self.up, self.down = me.at(dy=1), me.at(dy=-1)
        a, b = pl.ds(0, HALF), pl.ds(HALF, HALF)
        self.a, self.b = a, b
        mine = self.slot(0)
        self.up_a = edges.copy(own.at[a], out.at[mine, a], self.up)
        self.down_b = edges.copy(own.at[b], out.at[mine, b], self.down)
        self.up_b = edges.copy(own.at[b], out.at[mine, b], self.up)
        self.down_a = edges.copy(own.at[a], out.at[mine, a], self.down)
        self.to_core = [edges.copy(own, out.at[mine], self.core)]

    def slot(self, dy):
        return 2 * lax.rem(self.me.y + dy + 4, 4) + self.me.c

    def pass_core(self, dy, part):
        ref = self.out.at[self.slot(dy), part]
        self.to_core.append(self.edges.copy(ref, ref, self.core))

    def relay(self):
        out = self.out
        self.up_a.wait_recv()
        ref = out.at[self.slot(-1), self.a]
        self.on_a = self.edges.copy(ref, ref, self.up)
        self.down_b.wait_recv()
        ref = out.at[self.slot(1), self.b]
        self.on_b = self.edges.copy(ref, ref, self.down)
        self.pass_core(-1, self.a)
        self.pass_core(1, self.b)

    def rest(self):
        self.up_b.wait_recv()
        self.pass_core(-1, self.b)
        self.down_a.wait_recv()
        self.pass_core(1, self.a)
        self.on_a.wait_recv()
        self.pass_core(2, self.a)
        self.on_b.wait_recv()
        self.pass_core(2, self.b)
        for d in self.to_core:
            d.wait_recv()


GATHER_EDGES = 13


class RingScatter:
    def __init__(self, me, edges, parts, got, both, relayed, last):
        self.me, self.edges, self.parts = me, edges, parts
        self.got, self.both, self.relayed, self.last = got, both, relayed, last
        self.up, self.down = me.at(dy=1), me.at(dy=-1)
        self.from_core = {}
        for k in (2, 1, 3, 0):
            row = 2 * lax.rem(me.y + k, 4) + 1 - me.c
            self.from_core[k] = edges.copy(
                parts.at[row], got.at[k], me.at(core=1 - me.c)
            )

    def add_core(self, k):
        self.from_core[k].wait_recv()
        row = 2 * lax.rem(self.me.y + k, 4) + self.me.c
        self.both[k] = (
            self.parts[row].astype(F32) + self.got[k].astype(F32)
        ).astype(BF16)

    def first(self):
        a, b = pl.ds(0, HALF), pl.ds(HALF, HALF)
        e, both = self.edges, self.both
        self.add_core(2)
        self.r_a = e.copy(both.at[2, a], self.relayed.at[0], self.up)
        self.r_b = e.copy(both.at[2, b], self.relayed.at[1], self.down)
        self.add_core(1)
        self.u_b = e.copy(both.at[1, b], self.last.at[0, b], self.up)
        self.add_core(3)
        self.d_a = e.copy(both.at[3, a], self.last.at[1, a], self.down)
        self.add_core(0)

    def second(self):
        a, b = pl.ds(0, HALF), pl.ds(HALF, HALF)
        e, both = self.edges, self.both
        self.r_a.wait_recv()
        both[1, a] = (both[1, a].astype(F32) + self.relayed[0].astype(F32)).astype(BF16)
        self.u_a = e.copy(both.at[1, a], self.last.at[0, a], self.up)
        self.r_b.wait_recv()
        both[3, b] = (both[3, b].astype(F32) + self.relayed[1].astype(F32)).astype(BF16)
        self.d_b = e.copy(both.at[3, b], self.last.at[1, b], self.down)

    def total(self, out):
        for d in (self.u_b, self.d_a, self.u_a, self.d_b):
            d.wait_recv()
        out[...] = (
            self.both[0].astype(F32)
            + self.last[0].astype(F32)
            + self.last[1].astype(F32)
        )


SCATTER_EDGES = 10


def scatter_scratch():
    return [
        pltpu.VMEM((4, TOK, D), BF16),
        pltpu.VMEM((4, TOK, D), BF16),
        pltpu.VMEM((2, HALF, D), BF16),
        pltpu.VMEM((2, TOK, D), BF16),
    ]


def sems(n):
    return [pltpu.SemaphoreType.DMA((n,)), pltpu.SemaphoreType.DMA((n,))]


def shape(dims, dtype=BF16):
    return jax.ShapeDtypeStruct(dims, dtype)


def remote_params(number):
    return pltpu.CompilerParams(
        collective_id=number, has_side_effects=True, vmem_limit_bytes=48 * 2**20
    )


def block_place(block):
    is_kv = block >= 32
    other = block - 32
    rank = block // 4
    y = jnp.where(is_kv, lax.rem(other + 32, 4), rank // 2)
    core = jnp.where(is_kv, other // 4, lax.rem(rank, 2))
    return y, core, jnp.where(is_kv, 4, lax.rem(block, 4))


def own_block(me, j):
    if j == 4:
        return 32 + 4 * me.c + me.y
    return 4 * (2 * me.y + me.c) + j


def send_block(me, src, dst, send_sem, recv_sem, target, stays):
    @pl.when(stays)
    def _():
        pltpu.make_async_copy(src, dst, recv_sem).start()

    @pl.when(jnp.logical_not(stays))
    def _():
        pltpu.make_async_remote_copy(
            src_ref=src,
            dst_ref=dst,
            send_sem=send_sem,
            recv_sem=recv_sem,
            device_id=target,
            device_id_type=pl.DeviceIdType.MESH,
        ).start()


def wait_sent(src, send_sem, stays):
    @pl.when(jnp.logical_not(stays))
    def _():
        pltpu.make_async_copy(src, src, send_sem).wait()


def wait_got(dst, recv_sem):
    pltpu.make_async_copy(dst, dst, recv_sem).wait()


def opening_kernel(
    x, pos, wqkv, wout, wgu, wdn,
    xs, poss, wq, wo, gu, dn,
    send, recv, qs, qr, os_, orr, ws, wr, local,
):
    me = Place()
    partner = {"xl": 1 - me.xl, "xh": 1 - me.xh}
    members = group_members(me)
    others = [
        me.at(y=lax.rem(me.y + dy, 4), core=core, **partner)
        for dy in range(4)
        for core in (0, 1)
    ]
    depth = [me.at(dz=dz) for dz in (1, 2, 3)]
    greet(members + others + depth)
    edges = Edges(send, recv)
    keep = pltpu.make_async_copy(x, xs.at[2 * me.y + me.c], local.at[0])
    keep.start()
    keep_pos = pltpu.make_async_copy(pos, poss.at[2 * me.y + me.c], local.at[1])
    keep_pos.start()
    pos_copies = [edges.copy(pos, poss.at[2 * me.y + me.c], m) for m in members]
    ring = RingGather(me, edges, x, xs)

    own = 2 * me.y + me.xh
    own_column = me.c == 0
    to_xl = jnp.where(own_column, me.xl, 1 - me.xl)
    to_xh = jnp.where(own_column, me.xh, 1 - me.xh)
    blocks = []
    for i in range(5):
        y, core, slot = block_place(5 * own + i)
        stays = own_column & (y == me.y) & (core == me.c)
        src = wqkv.at[pl.ds(64 * i, 64)]
        send_block(
            me, src, wq.at[slot], qs.at[i], qr.at[slot], (me.z, to_xl, core, y, to_xh), stays
        )
        blocks.append((src, qs.at[i], stays))
    swap = me.c != me.xh
    rows_gu, rows_dn = 2 * FF_DEV // 4, D // 4
    gu_mine = pl.ds(rows_gu * me.z, rows_gu)
    dn_mine = pl.ds(rows_dn * me.z, rows_dn)
    across = me.at(core=1 - me.c, **partner)

    def over(src, dst, i, device):
        return pltpu.make_async_remote_copy(
            src_ref=src,
            dst_ref=dst,
            send_sem=ws.at[i],
            recv_sem=wr.at[i],
            device_id=device,
            device_id_type=pl.DeviceIdType.MESH,
        )

    @pl.when(swap)
    def _():
        over(wgu.at[gu_mine], gu.at[gu_mine], 0, across).start()
        over(wdn.at[dn_mine], dn.at[dn_mine], 1, across).start()

    @pl.when(jnp.logical_not(swap))
    def _():
        pltpu.make_async_copy(wgu, gu, local.at[2]).start()
        pltpu.make_async_copy(wdn, dn, local.at[3]).start()

    ring.relay()
    for i in range(8):
        dy, other = i // 2, i % 2
        y = lax.rem(me.y + dy, 4)
        core = me.c if other == 0 else 1 - me.c
        stays = own_column if i == 0 else me.c < 0
        src = wout.at[:, pl.ds(pl.multiple_of(Q_DEV * (2 * y + core), Q_DEV), Q_DEV)]
        dst = wo.at[own]
        send_block(
            me, src, dst, os_.at[i], orr.at[own], (me.z, to_xl, core, y, to_xh), stays
        )
        blocks.append((src, os_.at[i], stays))
    ring.rest()

    @pl.when(swap)
    def _():
        over(wgu.at[gu_mine], gu.at[gu_mine], 0, across).wait_recv()
        for k in (1, 2, 3):
            over(gu.at[gu_mine], gu.at[gu_mine], 2 * k, me.at(dz=k)).start()
        over(wdn.at[dn_mine], dn.at[dn_mine], 1, across).wait_recv()
        for k in (1, 2, 3):
            over(dn.at[dn_mine], dn.at[dn_mine], 2 * k + 1, me.at(dz=k)).start()
        over(wgu.at[gu_mine], gu.at[gu_mine], 0, across).wait_send()
        over(wdn.at[dn_mine], dn.at[dn_mine], 1, across).wait_send()
        for k in (1, 2, 3):
            over(gu.at[gu_mine], gu.at[gu_mine], 2 * k, me.at(dz=k)).wait()
            over(dn.at[dn_mine], dn.at[dn_mine], 2 * k + 1, me.at(dz=k)).wait()

    @pl.when(jnp.logical_not(swap))
    def _():
        pltpu.make_async_copy(wgu, gu, local.at[2]).wait()
        pltpu.make_async_copy(wdn, dn, local.at[3]).wait()

    for d in pos_copies:
        d.wait_recv()
    for i in range(5):
        wait_got(wq.at[i], qr.at[i])
    for i in range(8):
        wait_got(wo.at[i], orr.at[i])
    for src, sem, stays in blocks:
        wait_sent(src, sem, stays)
    edges.finish()
    keep.wait()
    keep_pos.wait()


def opening(x, pos, wqkv, wout, wgu, wdn):
    return pl.pallas_call(
        opening_kernel,
        out_shape=(
            shape((8, TOK, D)),
            shape((8, 8, TOK), jnp.int32),
            shape((5, 64, D)),
            shape((8, 256, Q_DEV)),
            shape((2 * FF_DEV, D)),
            shape((D, FF_DEV)),
        ),
        in_specs=[ANY] * 6,
        out_specs=(ANY,) * 6,
        scratch_shapes=sems(7 + GATHER_EDGES) + sems(5) + sems(8) + sems(8)
        + [pltpu.SemaphoreType.DMA((4,))],
        compiler_params=remote_params(0),
        name="opening",
    )(x, pos, wqkv, wout, wgu, wdn)


def chips_in_sequence(me):
    return [(dz, dl) for dz in range(4) for dl in (0, 1)][1:]


def keys_kernel(kv, pos, cot, kvs, poss, cots, send, recv, local):
    me = Place()
    core = me.at(core=1 - me.c)
    far = [
        me.at(dz=dz, xl=(1 - me.xl) if dl else me.xl) for dz, dl in chips_in_sequence(me)
    ]
    greet(far + [core, me.at(dy=1), me.at(dy=-1)])
    edges = Edges(send, recv)
    chip = 2 * me.z + me.xl
    keeps = [
        pltpu.make_async_copy(kv, kvs.at[me.c, chip], local.at[0]),
        pltpu.make_async_copy(pos, poss.at[chip], local.at[1]),
        pltpu.make_async_copy(cot, cots.at[2 * me.y + me.c], local.at[2]),
    ]
    for d in keeps:
        d.start()
    pos_copies = [edges.copy(pos, poss.at[chip], d) for d in far]
    kv_copies = [edges.copy(kv, kvs.at[me.c, chip], d) for d in far]
    over = [edges.copy(kv, kvs.at[me.c, chip], core)]
    ring = RingGather(me, edges, cot, cots)
    ring.relay()
    for (dz, dl), d in zip(chips_in_sequence(me), kv_copies):
        d.wait_recv()
        source = 2 * lax.rem(me.z - dz + 4, 4) + ((1 - me.xl) if dl else me.xl)
        ref = kvs.at[me.c, source]
        over.append(edges.copy(ref, ref, core))
    ring.rest()
    for d in over + pos_copies:
        d.wait_recv()
    edges.finish()
    for d in keeps:
        d.wait()


def exchange_keys(kv, pos, cot):
    return pl.pallas_call(
        keys_kernel,
        out_shape=(
            shape((2, 8, 512, 128)),
            shape((8, 8, 8, TOK), jnp.int32),
            shape((8, TOK, D)),
        ),
        in_specs=[ANY] * 3,
        out_specs=(ANY,) * 3,
        scratch_shapes=sems(7 + 7 + 8 + GATHER_EDGES) + [pltpu.SemaphoreType.DMA((3,))],
        compiler_params=remote_params(1),
        name="exchange_keys",
    )(kv, pos, cot)


def split_heads(rows):
    return jnp.concatenate([rows[:, HD * h : HD * (h + 1)] for h in range(4)], axis=0)


def join_heads(rows):
    return jnp.concatenate([rows[64 * h : 64 * (h + 1), :] for h in range(4)], axis=1)


def dot_last(a, b):
    return lax.dot_general(a, b, (((1,), (1,)), ((), ())), preferred_element_type=F32)


def dot_first(a, b):
    return lax.dot_general(a, b, (((0,), (0,)), ((), ())), preferred_element_type=F32)


def dot(a, b):
    return lax.dot_general(a, b, (((1,), (0,)), ((), ())), preferred_element_type=F32)


TILE = 256


def sort_keys(runs, seq, kv_ref, keys, values):
    for j in range(32):
        chip, core, u = j // 4, (j // 2) % 2, j % 2
        to = pl.ds(pl.multiple_of(runs[seq * 32 + j] * 64, 64), 64)
        rows, lanes = slice(64 * u, 64 * u + 64), slice(HD * core, HD * core + HD)
        keys[to, :] = kv_ref[0, chip, rows, lanes]
        values[to, :] = kv_ref[1, chip, rows, lanes]


def allowed_tile(tile, run):
    key = lax.broadcasted_iota(jnp.int32, (TILE, 256), 0) + tile * TILE
    query = lax.rem(lax.broadcasted_iota(jnp.int32, (TILE, 256), 1), 64) + run * 64
    return key <= query


def attend_kernel(key_runs, query_runs, q_ref, kv_ref, att_ref, ot_ref, lse_ref, keys, values):
    seq = pl.program_id(0)
    sort_keys(key_runs, seq, kv_ref, keys, values)

    def one_run(r, _):
        run = query_runs[seq * 4 + r]
        rows = pl.ds(pl.multiple_of(r * 64, 64), 64)
        query = split_heads(q_ref[rows, :])
        last = run // 4

        def tile_step(tile, carried, masked):
            high, total, acc = carried
            at = pl.ds(pl.multiple_of(tile * TILE, TILE), TILE)
            scores = dot_last(keys[at, :], query)
            if masked:
                allowed = allowed_tile(tile, run)
                scores = jnp.where(allowed, scores, FILLER)
            new_high = jnp.maximum(high, jnp.max(scores, axis=0, keepdims=True))
            weights = jnp.exp(scores - new_high)
            scale = jnp.exp(high - new_high)
            total = total * scale + jnp.sum(weights, axis=0, keepdims=True)
            acc = acc * scale + dot_first(values[at, :], weights.astype(BF16))
            return new_high, total, acc

        start = (
            jnp.full((1, 256), FILLER, F32),
            jnp.zeros((1, 256), F32),
            jnp.zeros((HD, 256), F32),
        )
        carried = lax.fori_loop(0, last, lambda t, s: tile_step(t, s, False), start)
        high, total, acc = tile_step(last, carried, True)
        out = acc / total
        ot_ref[r] = out
        lse_ref[r] = high + jnp.log(total)
        att_ref[rows, :] = join_heads(out.T).astype(BF16)
        return 0

    lax.fori_loop(0, 4, one_run, 0)


def attend(key_runs, query_runs, q, kv):
    return pl.pallas_call(
        attend_kernel,
        out_shape=(shape((1024, 256)), shape((16, HD, 256), F32), shape((16, 1, 256), F32)),
        grid_spec=pltpu.PrefetchScalarGridSpec(
            num_scalar_prefetch=2,
            grid=(4,),
            in_specs=[
                pl.BlockSpec((256, 256), lambda i, *_: (i, 0)),
                pl.BlockSpec((2, 8, 128, 128), lambda i, *_: (0, 0, i, 0)),
            ],
            out_specs=[
                pl.BlockSpec((256, 256), lambda i, *_: (i, 0)),
                pl.BlockSpec((4, HD, 256), lambda i, *_: (i, 0, 0)),
                pl.BlockSpec((4, 1, 256), lambda i, *_: (i, 0, 0)),
            ],
            scratch_shapes=[pltpu.VMEM((2048, HD), BF16), pltpu.VMEM((2048, HD), BF16)],
        ),
        compiler_params=pltpu.CompilerParams(vmem_limit_bytes=40 * 2**20),
        name="attend",
    )(key_runs, query_runs, q, kv)


def attend_back_kernel(
    key_runs, query_runs, q_ref, kv_ref, da_ref, ot_ref, lse_ref,
    dq_ref, dkv_ref, keys, values, dkeys, dvalues,
):
    seq = pl.program_id(0)
    sort_keys(key_runs, seq, kv_ref, keys, values)
    dkeys[...] = jnp.zeros_like(dkeys)
    dvalues[...] = jnp.zeros_like(dvalues)

    def one_run(r, _):
        run = query_runs[seq * 4 + r]
        rows = pl.ds(pl.multiple_of(r * 64, 64), 64)
        query = split_heads(q_ref[rows, :])
        grad = split_heads(da_ref[rows, :])
        lse = lse_ref[r]
        delta = jnp.sum(grad.astype(F32).T * ot_ref[r], axis=0, keepdims=True)
        last = run // 4

        def tile_step(tile, dq, masked):
            at = pl.ds(pl.multiple_of(tile * TILE, TILE), TILE)
            key = keys[at, :]
            probs = jnp.exp(dot_last(key, query) - lse)
            if masked:
                probs = jnp.where(allowed_tile(tile, run), probs, 0.0)
            grad_probs = dot_last(values[at, :], grad)
            grad_scores = (probs * (grad_probs - delta)).astype(BF16)
            dvalues[at, :] += dot(probs.astype(BF16), grad)
            dkeys[at, :] += dot(grad_scores, query)
            return dq + dot_first(key, grad_scores)

        dq = lax.fori_loop(
            0, last, lambda t, s: tile_step(t, s, False), jnp.zeros((HD, 256), F32)
        )
        dq = tile_step(last, dq, True)
        dq_ref[rows, :] = join_heads((dq * 0.125).T)
        return 0

    lax.fori_loop(0, 4, one_run, 0)
    for j in range(32):
        chip, core, u = j // 4, (j // 2) % 2, j % 2
        at = pl.ds(pl.multiple_of(key_runs[seq * 32 + j] * 64, 64), 64)
        rows, lanes = slice(64 * u, 64 * u + 64), slice(HD * core, HD * core + HD)
        dkv_ref[0, chip, rows, lanes] = dkeys[at, :].astype(BF16)
        dkv_ref[1, chip, rows, lanes] = dvalues[at, :].astype(BF16)


def attend_back(key_runs, query_runs, q, kv, grad, ot, lse):
    return pl.pallas_call(
        attend_back_kernel,
        out_shape=(shape((1024, 256), F32), shape((2, 8, 512, 128))),
        grid_spec=pltpu.PrefetchScalarGridSpec(
            num_scalar_prefetch=2,
            grid=(4,),
            in_specs=[
                pl.BlockSpec((256, 256), lambda i, *_: (i, 0)),
                pl.BlockSpec((2, 8, 128, 128), lambda i, *_: (0, 0, i, 0)),
                pl.BlockSpec((256, 256), lambda i, *_: (i, 0)),
                pl.BlockSpec((4, HD, 256), lambda i, *_: (i, 0, 0)),
                pl.BlockSpec((4, 1, 256), lambda i, *_: (i, 0, 0)),
            ],
            out_specs=[
                pl.BlockSpec((256, 256), lambda i, *_: (i, 0)),
                pl.BlockSpec((2, 8, 128, 128), lambda i, *_: (0, 0, i, 0)),
            ],
            scratch_shapes=[
                pltpu.VMEM((2048, HD), BF16),
                pltpu.VMEM((2048, HD), BF16),
                pltpu.VMEM((2048, HD), F32),
                pltpu.VMEM((2048, HD), F32),
            ],
        ),
        compiler_params=pltpu.CompilerParams(vmem_limit_bytes=40 * 2**20),
        name="attend_back",
    )(key_runs, query_runs, q, kv, grad, ot, lse)


def gather_kernel(x, xs, send, recv, local):
    me = Place()
    greet([me.at(core=1 - me.c), me.at(dy=1), me.at(dy=-1)])
    edges = Edges(send, recv)
    keep = pltpu.make_async_copy(x, xs.at[2 * me.y + me.c], local)
    keep.start()
    ring = RingGather(me, edges, x, xs)
    ring.relay()
    ring.rest()
    edges.finish()
    keep.wait()


def gather_group(x, number, name):
    return pl.pallas_call(
        gather_kernel,
        out_shape=shape((8, TOK, D)),
        in_specs=[ANY],
        out_specs=ANY,
        scratch_shapes=sems(GATHER_EDGES) + [pltpu.SemaphoreType.DMA],
        compiler_params=remote_params(number),
        name=name,
    )(x)


def scatter_kernel(parts, out, got, both, relayed, last, send, recv):
    me = Place()
    greet([me.at(core=1 - me.c), me.at(dy=1), me.at(dy=-1)])
    edges = Edges(send, recv)
    ring = RingScatter(me, edges, parts, got, both, relayed, last)
    ring.first()
    ring.second()
    ring.total(out)
    edges.finish()


def scatter_group(parts, number, name):
    return pl.pallas_call(
        scatter_kernel,
        out_shape=shape((TOK, D), F32),
        in_specs=[VMEM],
        out_specs=VMEM,
        scratch_shapes=scatter_scratch() + sems(SCATTER_EDGES),
        compiler_params=remote_params(number),
        name=name,
    )(parts)


def scatter_two_kernel(
    parts_a, parts_b, out_a, out_b, g1, b1, r1, l1, g2, b2, r2, l2, send, recv
):
    me = Place()
    greet([me.at(core=1 - me.c), me.at(dy=1), me.at(dy=-1)])
    edges = Edges(send, recv)
    ring_a = RingScatter(me, edges, parts_a, g1, b1, r1, l1)
    ring_b = RingScatter(me, edges, parts_b, g2, b2, r2, l2)
    ring_a.first()
    ring_b.first()
    ring_a.second()
    ring_b.second()
    ring_a.total(out_a)
    ring_b.total(out_b)
    edges.finish()


def scatter_two(parts_a, parts_b, number, name):
    return pl.pallas_call(
        scatter_two_kernel,
        out_shape=(shape((TOK, D), F32),) * 2,
        in_specs=[VMEM] * 2,
        out_specs=(VMEM,) * 2,
        scratch_shapes=scatter_scratch() * 2 + sems(2 * SCATTER_EDGES),
        compiler_params=remote_params(number),
        name=name,
    )(parts_a, parts_b)


def key_grads_kernel(dkv, gwo, out, rows, got, both, last, send, recv, os_, orr, load):
    me = Place()
    core = me.at(core=1 - me.c)
    far = [
        me.at(dz=dz, xl=(1 - me.xl) if dl else me.xl) for dz, dl in chips_in_sequence(me)
    ]
    greet(far + group_members(me))
    edges = Edges(send, recv)
    order = []
    for dz, dl in chips_in_sequence(me) + [(0, 0)]:
        chip = 2 * lax.rem(me.z + dz, 4) + ((1 - me.xl) if dl else me.xl)
        order.append((chip, edges.copy(dkv.at[1 - me.c, chip], got.at[chip], core)))
    own = 2 * me.y + me.c
    sent = []
    for i in range(8):
        dy, other = i // 2, i % 2
        y = lax.rem(me.y + dy, 4)
        to_core = me.c if other == 0 else 1 - me.c
        src = gwo.at[2 * y + to_core]
        dst = rows.at[:, pl.ds(pl.multiple_of(Q_DEV * own, Q_DEV), Q_DEV)]
        if i == 0:
            pltpu.make_async_copy(src, dst, orr.at[own]).start()
        else:
            d = pltpu.make_async_remote_copy(
                src_ref=src,
                dst_ref=dst,
                send_sem=os_.at[i],
                recv_sem=orr.at[own],
                device_id=me.at(dy=dy, core=to_core),
                device_id_type=pl.DeviceIdType.MESH,
            )
            d.start()
            sent.append(d)
    far_copies = []
    for i, (chip, d) in enumerate(order):
        d.wait_recv()
        both[chip] = (dkv[me.c, chip].astype(F32) + got[chip].astype(F32)).astype(BF16)
        if i < 7:
            far_copies.append(edges.copy(both.at[chip], last.at[i], far[i]))
    total = both[2 * me.z + me.xl].astype(F32)
    for i, d in enumerate(far_copies):
        d.wait_recv()
        total = total + last[i].astype(F32)
    out[...] = total
    for i in range(8):
        wait_got(rows.at[:, pl.ds(Q_DEV * i, Q_DEV)], orr.at[i])
    for d in sent:
        d.wait_send()
    edges.finish()


def sum_key_grads(dkv, gwo):
    return pl.pallas_call(
        key_grads_kernel,
        out_shape=(shape((512, 128), F32), shape((256, D))),
        in_specs=[VMEM, ANY],
        out_specs=(VMEM, ANY),
        scratch_shapes=[
            pltpu.VMEM((8, 512, 128), BF16),
            pltpu.VMEM((8, 512, 128), BF16),
            pltpu.VMEM((7, 512, 128), BF16),
        ]
        + sems(15)
        + sems(8)
        + [pltpu.SemaphoreType.DMA],
        compiler_params=remote_params(2),
        name="sum_key_grads",
    )(dkv, gwo)


def closing_kernel(parts, gwq, out, rows, got, both, relayed, last, send, recv, qs, qr):
    me = Place()
    greet(group_members(me))
    edges = Edges(send, recv)
    ring = RingScatter(me, edges, parts, got, both, relayed, last)
    sent = []
    for j in range(5):
        block = own_block(me, j)
        owner, slot = block // 5, lax.rem(block, 5)
        y, core = owner // 2, lax.rem(owner, 2)
        stays = (y == me.y) & (core == me.c)
        src = gwq.at[j]
        send_block(
            me, src, rows.at[slot], qs.at[j], qr.at[slot], me.at(y=y, core=core), stays
        )
        sent.append((src, qs.at[j], stays))
    ring.first()
    ring.second()
    ring.total(out)
    for i in range(5):
        wait_got(rows.at[i], qr.at[i])
    for src, sem, stays in sent:
        wait_sent(src, sem, stays)
    edges.finish()


def closing(parts, gwq):
    return pl.pallas_call(
        closing_kernel,
        out_shape=(shape((TOK, D), F32), shape((5, 64, D))),
        in_specs=[VMEM, ANY],
        out_specs=(VMEM, ANY),
        scratch_shapes=scatter_scratch() + sems(SCATTER_EDGES) + sems(5),
        compiler_params=remote_params(3),
        name="closing",
    )(parts, gwq)


def rotate(rows, cosine, sine):
    turned = jnp.concatenate([-rows[..., HD // 2 :], rows[..., : HD // 2]], axis=-1)
    return rows * cosine + turned * sine


def norm_back(grad_norm, normal, inverse):
    return inverse * (grad_norm - normal * jnp.mean(grad_norm * normal, axis=-1, keepdims=True))


def reduce_grads(parts):
    rows, width = parts.shape
    shares = parts.reshape(16, rows // 16, width)
    share = lax.psum_scatter(shares, ("z", "xl", "xh"), scatter_dimension=0, tiled=True)
    route = []
    for z in range(4):
        for xl in range(2):
            for c in range(2):
                for y in range(4):
                    for xh in range(2):
                        here = (((z * 2 + xl) * 2 + c) * 4 + y) * 2 + xh
                        there = (((z * 2 + xl) * 2 + xh) * 4 + y) * 2 + c
                        route.append((here, there))
    share = lax.ppermute(share, AXES, route)
    full = lax.all_gather(share, ("z", "xl", "c"), axis=0, tiled=True)
    return full.reshape(rows, width).astype(F32)


def body(hidden, positions, gain_attn, w_qkv, w_out, gain_mlp, w_gate_up, w_down, cotangent):
    tokens = hidden[0].astype(F32)
    core = lax.axis_index("c")
    gain_one = gain_attn.astype(F32)
    gain_two = gain_mlp.astype(F32)
    inverse_one = lax.rsqrt(jnp.mean(tokens * tokens, axis=-1, keepdims=True) + EPSILON)
    normal_one = tokens * inverse_one
    input_one = (normal_one * gain_one).astype(BF16)
    xs, poss, wq, wo, gu, dn = opening(
        input_one,
        jnp.broadcast_to(positions, (8, TOK)),
        w_qkv,
        w_out,
        w_gate_up.reshape(2 * FF_DEV, D),
        w_down,
    )
    xs = xs.reshape(1024, D)
    wq = wq.reshape(320, D)
    wo = wo.reshape(D, Q_DEV)
    places = poss[:, 0, :].reshape(1024)

    steps_half = jnp.arange(HD // 2, dtype=F32)
    inverse = jnp.power(10000.0, steps_half * (-2.0 / HD))
    turning = places.astype(F32)[:, None] * inverse[None, :]
    cosine, sine = jnp.cos(turning), jnp.sin(turning)
    cosine = jnp.concatenate([cosine, cosine], axis=-1)
    sine = jnp.concatenate([sine, sine], axis=-1)
    kv_cosine = jnp.where(core == 0, cosine, 1.0)
    kv_sine = jnp.where(core == 0, sine, 0.0)

    projected = dot_last(xs, wq)
    query = rotate(
        projected[:, :Q_DEV].reshape(1024, 4, HD), cosine[:, None, :], sine[:, None, :]
    )
    query = (query.astype(BF16) * 0.125).astype(BF16).reshape(1024, Q_DEV)
    kv = rotate(projected[:, Q_DEV:], kv_cosine, kv_sine).astype(BF16)
    kv = kv.reshape(4, 2, TOK, HD).transpose(0, 2, 1, 3).reshape(512, 128)
    kvs, places_all, cots = exchange_keys(kv, poss, cotangent[0])
    cots = cots.reshape(1024, D)
    key_runs = (
        places_all[:, :, 0, ::64].reshape(8, 4, 2, 2).transpose(1, 0, 2, 3).reshape(128) // 64
    )
    query_runs = places.reshape(16, 64)[:, 0] // 64
    att, ot, lse = attend(key_runs, query_runs, query, kvs)
    parts = dot_last(att, wo).astype(BF16)
    middle = tokens + scatter_group(parts.reshape(8, TOK, D), 4, "sum_attended")
    inverse_two = lax.rsqrt(jnp.mean(middle * middle, axis=-1, keepdims=True) + EPSILON)
    normal_two = middle * inverse_two
    input_two = (normal_two * gain_two).astype(BF16)
    x2 = gather_group(input_two, 5, "gather_two").reshape(1024, D)

    gate = dot_last(x2, gu[:FF_DEV])
    upward = dot_last(x2, gu[FF_DEV:])
    grad_active = dot(cots, dn)
    sigmoid = jax.nn.sigmoid(gate)
    swish = gate * sigmoid
    active = (swish * upward).astype(BF16)
    grad_upward = (grad_active * swish).astype(BF16)
    grad_gate = (grad_active * upward * sigmoid * (1.0 + gate * (1.0 - sigmoid))).astype(BF16)
    branch_parts = dot_last(active, dn).astype(BF16).reshape(8, TOK, D)
    grad_two_parts = (dot(grad_gate, gu[:FF_DEV]) + dot(grad_upward, gu[FF_DEV:])).astype(BF16)
    grad_gu = jnp.concatenate([dot_first(grad_gate, x2), dot_first(grad_upward, x2)]).astype(BF16)
    grad_dn = dot_first(cots, active).astype(BF16)
    branch, grad_two = scatter_two(
        branch_parts, grad_two_parts.reshape(8, TOK, D), 6, "sum_mlp"
    )
    output = (middle + branch).astype(BF16)
    grad_gain_two = jnp.sum(normal_two * grad_two, axis=0)
    grad_output = cotangent[0].astype(F32)
    grad_middle = grad_output + norm_back(grad_two * gain_two, normal_two, inverse_two)
    gb = gather_group(grad_middle.astype(BF16), 7, "gather_branch").reshape(1024, D)
    grad_att = dot(gb, wo).astype(BF16)
    grad_wo = dot_first(gb, att).astype(BF16)
    dq, dkv = attend_back(key_runs, query_runs, query, kvs, grad_att, ot, lse)
    dkv, wo_rows = sum_key_grads(dkv, grad_wo.reshape(8, 256, Q_DEV))
    dq = rotate(dq.reshape(1024, 4, HD), cosine[:, None, :], -sine[:, None, :])
    dkv = dkv.reshape(4, TOK, 2, HD).transpose(0, 2, 1, 3).reshape(1024, HD)
    dkv = rotate(dkv, kv_cosine, -kv_sine)
    grad_projected = jnp.concatenate([dq.reshape(1024, Q_DEV), dkv], axis=1).astype(BF16)
    grad_one_parts = dot(grad_projected, wq).astype(BF16).reshape(8, TOK, D)
    grad_wq = dot_first(grad_projected, xs).astype(BF16).reshape(5, 64, D)
    grad_one, wq_rows = closing(grad_one_parts, grad_wq)
    grad_gain_one = jnp.sum(normal_one * grad_one, axis=0)
    grad_tokens = grad_middle + norm_back(grad_one * gain_one, normal_one, inverse_one)

    gains = jnp.stack([grad_gain_one, grad_gain_two])
    gains = lax.psum(gains, AXES)
    owner = 2 * lax.axis_index("y") + lax.axis_index("xh")
    gains = lax.dynamic_slice_in_dim(gains, owner * 256, 256, axis=1)
    return (
        output[None],
        grad_tokens[None],
        gains[0],
        reduce_grads(wq_rows.reshape(320, D)),
        reduce_grads(wo_rows),
        gains[1],
        reduce_grads(grad_gu).reshape(2, FF_DEV, D),
        reduce_grads(grad_dn),
    )


def solution(mesh):
    fine = Mesh(mesh.devices.reshape(4, 2, 2, 4, 2), AXES)
    ctx, fsdp = ("z", "xl", "c"), ("y", "xh")
    weight = P(fsdp, None)
    return jax.shard_map(
        body,
        mesh=fine,
        in_specs=(
            P(fsdp, ctx, None),
            P(fsdp, ctx),
            P(),
            weight,
            weight,
            P(),
            P(None, fsdp, None),
            P(None, fsdp),
            P(fsdp, ctx, None),
        ),
        out_specs=(
            P(fsdp, ctx, None),
            P(fsdp, ctx, None),
            P(fsdp),
            weight,
            weight,
            P(fsdp),
            P(None, fsdp, None),
            P(None, fsdp),
        ),
        check_vma=False,
    )
```

time: 2400 us -> 1170 us (0.49)
  waiting for transfers between devices: 1720 us -> 347 us
  Pallas kernels: 0 us -> 544 us
  matrix products: 250 us -> 68.5 us
  other arithmetic: 129 us -> 44.5 us
  local copies, waits for them, and re-layouts: 107 us -> 31.9 us
  starting transfers between devices: 92 us -> 42.9 us
    all_gather x4, waiting for transfers between devices: 741 us -> 59.3 us  [reduce_grads(): full = lax.all_gather(share, ('z', 'xl', 'c'), axis=0, tiled=True)]
    pallas_call x0 -> x10, Pallas kernels: none -> 544 us  [the longest x1 210 us: exchange_keys(): pl.pallas_call(keys_kernel, out_shape=(shape((2, 8, 512, 128)), shape((8,...]
    reduce_scatter x4, waiting for transfers between devices: 762 us -> 272 us  [reduce_grads(): lax.psum_scatter(shares, ('z', 'xl', 'xh'), scatter_dimension=0, tiled=True)]
    dot_general x127 -> x15, matrix products: 250 us -> 68.5 us  [the longest x5 28.1 us: dot_last(): lax.dot_general(a, b, (((1,), (1,)), ((), ())), preferred_element_type=F32)]
    psum x1 -> x0, waiting for transfers between devices: 180 us -> none  [body(): lax.psum(qkv_share.astype(jnp.bfloat16), 'ctx').astype(jnp.float32)]
    ppermute x92 -> x4, starting transfers between devices: 91.4 us -> 42.3 us  [reduce_grads(): share = lax.ppermute(share, AXES, route)]
    convert_element_type x73 -> x8, other arithmetic: 61.1 us -> 19 us  [the longest x3 16.5 us: reduce_grads(): return full.reshape(rows, width).astype(F32)]
    while x135 -> x0, local copies, waits for them, and re-layouts: 40.6 us -> none
  transfers between devices with their start and end apart: 101 -> 12, of which waited for: 52 -> 10; matrix products, arithmetic and copies ran while one was open for 17% -> 5% of each run, Pallas kernels for 0% -> 3%
where the time goes in v1:
time: 1170 us; the launch traced here: 1160 us
  Pallas kernels  544 us (46%)
  waiting for transfers between devices  347 us (30%)
  matrix products  68.5 us (6%)
  blocking collectives  63.8 us (5%)
  other arithmetic  44.5 us (4%)
  starting transfers between devices  42.9 us (4%)
  local copies, waits for them, and re-layouts  31.9 us (3%)
  between operations  15.3 us (1%)
    reduce_scatter x4, waiting for transfers between devices, reduce_grads(): lax.psum_scatter(shares, ('z', 'xl', 'xh'), scatter_dimension=0, tiled=True)  272 us
    pallas_call x1, Pallas kernels, exchange_keys(): pl.pallas_call(keys_kernel, out_shape=(shape((2, 8, 512, 128)), shape((8,...  210 us
    pallas_call x1, Pallas kernels, opening(): pl.pallas_call(opening_kernel, out_shape=(shape((8, TOK, D)), shape((8, 8...  91.8 us
    psum x1, blocking collectives, body(): gains = lax.psum(gains, AXES)  63.8 us
    all_gather x4, waiting for transfers between devices, reduce_grads(): full = lax.all_gather(share, ('z', 'xl', 'c'), axis=0, tiled=True)  59.3 us
    pallas_call x2, Pallas kernels, gather_group(): pl.pallas_call(gather_kernel, out_shape=shape((8, TOK, D)), in_specs=[ANY...  46.9 us
    pallas_call x1, Pallas kernels, scatter_two(): pl.pallas_call(scatter_two_kernel, out_shape=(shape((TOK, D), F32),) * 2,...  42.9 us
    ppermute x4, starting transfers between devices, reduce_grads(): share = lax.ppermute(share, AXES, route)  42.3 us
  transfers between devices with their start and end apart: 12, of which 10 were waited for; matrix products, arithmetic and copies ran while one was open for 5% of the time, Pallas kernels for 3%

profile of v1, /device:TPU:9, one launch (start us, length us, event | category | flops | bytes accessed | tf_op | source)
XLA Modules:
  0.0 1157.9 jit_solution(16097211203858247069)
XLA Ops:
  9.2 4.7 copy.93.wdn
  15.2 91.8 %opening.1 = (bf16[8,128,2048]{2,1,0:T(8,128)(2,1)}, s32[8,8,128]{2,1,0:T(8,128)S(1)}, bf16[5,64,2048]{2,1,0:T(8,128)(2,1)S(1)}, bf16[8,256,256]{2,1,0:T(8,128)(...) custom-call(bf16[128,2048]{1,0:T(8,128)(2,1)S(1)} %fusion.13.x, s32[8,128]{1,0:T(8,128)S(1)} %broadcast_in_dim.16.pos, ...), custom_call_target="tpu_custom_call" | custom-call | tf_op jit(solution)/shard_map/opening/pallas_call | solution.py:360
  107.0 5.4 fusion.32
  114.8 3.0 multiply_sine_fusion
  117.8 3.3 fusion.29
  121.5 209.9 %exchange_keys.1 = (bf16[2,8,512,128]{3,2,1,0:T(8,128)(2,1)S(1)}, s32[8,8,8,128]{3,2,1,0:T(8,128)S(1)}, bf16[8,128,2048]{2,1,0:T(8,128)(2,1)}) custom-call(bf16[512,128]{1,0:T(8,128)(2,1)S(1)} %copy.98.kv, s32[8,8,128]{2,1,0:T(8,128)S(1)} %get-tuple-element.30.pos, bf16[128,2048]{1,0:T(8,128)(2,1)S(1)} %bitcast.113), custom_call_target="tpu_custom_call" | custom-call | tf_op jit(solution)/shard_map/exchange_keys/pallas_call | solution.py:418
  343.1 2.2 fusion.21.q_ref
  345.2 34.3 %attend.1 = (bf16[1024,256]{1,0:T(8,128)(2,1)S(1)}, f32[16,64,256]{2,1,0:T(8,128)S(1)}, f32[16,1,256]{2,1,0:T(1,128)S(1)}) custom-call(s32[128]{0:T(128)S(1)} %and_select_fusion.1.key_runs, s32[16]{0:T(128)S(1)} %and_select_fusion.query_runs, bf16[1024,256]{1,0:T(8,128)(2,1)S(1)} %fusion.21.q_ref, bf16[2,8,512,128]{3,2,1,0:T(8,128)(2,1)S(1)} %get-tuple-element.32.kv_ref), custom_call_target="tpu_custom_call" | custom-call | tf_op jit(solution)/shard_map/attend/pallas_call | solution.py:512
  380.9 21.9 %sum_attended.1 = f32[128,2048]{1,0:T(8,128)S(1)} custom-call(bf16[8,128,2048]{2,1,0:T(8,128)(2,1)S(1)} %bitcast.112), custom_call_target="tpu_custom_call" | custom-call | tf_op jit(solution)/shard_map/sum_attended/pallas_call | solution.py:647
  403.2 23.5 %gather_two.1 = bf16[8,128,2048]{2,1,0:T(8,128)(2,1)S(1)} custom-call(bf16[128,2048]{1,0:T(8,128)(2,1)S(1)} %multiply_convert_fusion.3.x), custom_call_target="tpu_custom_call" | custom-call | tf_op jit(solution)/shard_map/gather_two/pallas_call | solution.py:624
  426.7 8.1 fusion.6
  434.8 6.7 fusion.2
  441.5 7.9 multiply_convert_fusion
  449.4 6.7 convolution_convert_fusion.1
  456.2 3.5 fusion.4
  459.7 5.3 add_convert_fusion
  465.0 42.9 %sum_mlp.1 = (f32[128,2048]{1,0:T(8,128)S(1)}, f32[128,2048]{1,0:T(8,128)S(1)}) custom-call(bf16[8,128,2048]{2,1,0:T(8,128)(2,1)} %bitcast.132, bf16[8,128,2048]{2,1,0:T(8,128)(2,1)} %bitcast.134), custom_call_target="tpu_custom_call" | custom-call | tf_op jit(solution)/shard_map/sum_mlp/pallas_call | solution.py:676
  509.4 23.4 %gather_branch.1 = bf16[8,128,2048]{2,1,0:T(8,128)(2,1)S(1)} custom-call(bf16[128,2048]{1,0:T(8,128)(2,1)S(1)} %fusion.30.x), custom_call_target="tpu_custom_call" | custom-call | tf_op jit(solution)/shard_map/gather_branch/pallas_call | solution.py:624
  535.4 35.4 %attend_back.1 = (f32[1024,256]{1,0:T(8,128)S(1)}, bf16[2,8,512,128]{3,2,1,0:T(8,128)(2,1)S(1)}) custom-call(s32[128]{0:T(128)S(1)} %and_select_fusion.1.key_runs, s32[16]{0:T(128)S(1)} %and_select_fusion.query_runs, bf16[1024,256]{1,0:T(8,128)(2,1)S(1)} %fusion.21.q_ref, bf16[2,8,512,128]{3,2,1,0:T(8,128)(2,1)S(1)} %get-tuple-element.32.kv_ref, ...), custom_call_target="tpu_custom_call" | custom-call | tf_op jit(solution)/shard_map/attend_back/pallas_call | solution.py:581
  571.7 29.0 %sum_key_grads.1 = (f32[512,128]{1,0:T(8,128)S(1)}, bf16[256,2048]{1,0:T(8,128)(2,1)}) custom-call(bf16[2,8,512,128]{3,2,1,0:T(8,128)(2,1)S(1)} %get-tuple-element.43.dkv, bf16[8,256,256]{2,1,0:T(8,128)(2,1)S(1)} %bitcast.123), custom_call_target="tpu_custom_call" | custom-call | tf_op jit(solution)/shard_map/sum_key_grads/pallas_call | solution.py:739
  605.1 2.5 copy.111
  610.1 4.4 convolution_convert_fusion
  616.0 32.3 %closing.1 = (f32[128,2048]{1,0:T(8,128)S(1)}, bf16[5,64,2048]{2,1,0:T(8,128)(2,1)S(1)}) custom-call(bf16[8,128,2048]{2,1,0:T(8,128)(2,1)} %bitcast.133, bf16[5,64,2048]{2,1,0:T(8,128)(2,1)S(1)} %bitcast.120), custom_call_target="tpu_custom_call" | custom-call | tf_op jit(solution)/shard_map/closing/pallas_call | solution.py:784
  649.7 5.8 fusion.8
  655.5 2.3 copy.124
  658.2 6.0 convolution_convert_fusion.4
  664.1 3.4 convolution_convert_fusion.5
  667.5 3.2 pad_maximum_fusion
  670.8 3.1 reduce-scatter.7.cloned.1.call-done
  674.0 16.4 %collective-permute-start.1 = (bf16[1,16,2048]{2,1,0:T(8,128)(2,1)}, bf16[1,16,2048]{2,1,0:T(8,128)(2,1)S(1)}, u32[]{:S(2)}, u32[]{:S(2)}) collective-permute-start(bf16[1,16,2048]{2,1,0:T(8,128)(2,1)} %reduce-scatter.7.cloned.1.call-done), channel_id=1, source_target_pairs={{0,0},{1,8},{2,2},{3,10},{4,4},{5,12},{6,6},{7,14},{8,1},{9,9},{10... | collective-permute-start | bytes 196616 | tf_op jit(solution)/shard_map/ppermute | solution.py:817
  690.4 2.1 collective-permute-done.1
  693.2 64.3 %reduce-scatter.5.cloned.1.call-done = bf16[1,20,2048]{2,1,0:T(8,128)(2,1)} async-done(((bf16[16,20,2048]{2,1,0:T(8,128)(2,1)}), bf16[1,20,2048]{2,1,0:T(8,128)(2,1)}) %reduce-scatter.5.cloned.1.call-update) | async-done | bytes 81936 | tf_op jit(solution)/shard_map/reduce_scatter | solution.py:807
  757.6 10.5 collective-permute-start
  768.1 2.5 collective-permute-done
  771.3 79.8 %reduce-scatter.11.cloned.1.call-done = bf16[1,128,704]{1,2,0:T(8,128)(2,1)} async-done(((bf16[16,128,704]{1,2,0:T(8,128)(2,1)}), bf16[1,128,704]{1,2,0:T(8,128)(2,1)}) %reduce-scatter.11.cloned.1.call-update) | async-done | bytes 180240 | tf_op jit(solution)/shard_map/reduce_scatter | solution.py:807
  851.2 12.1 %collective-permute-start.3 = (bf16[1,128,704]{1,2,0:T(8,128)(2,1)}, bf16[1,128,704]{1,2,0:T(8,128)(2,1)S(1)}, u32[]{:S(2)}, u32[]{:S(2)}) collective-permute-start(bf16[1,128,704]{1,2,0:T(8,128)(2,1)} %reduce-scatter.11.cloned.1.call-done), channel_id=1, source_target_pairs={{0,0},{1,8},{2,2},{3,10},{4,4},{5,12},{6,6},{7,14},{8,1},{9,9},{10... | collective-permute-start | bytes 540680 | tf_op jit(solution)/shard_map/ppermute | solution.py:817
  863.2 3.4 collective-permute-done.3
  867.4 124.9 %reduce-scatter.9.cloned.1.call-done = bf16[1,88,2048]{2,1,0:T(8,128)(2,1)} async-done(((bf16[16,88,2048]{2,1,0:T(8,128)(2,1)}), bf16[1,88,2048]{2,1,0:T(8,128)(2,1)}) %reduce-scatter.9.cloned.1.call-update) | async-done | bytes 360464 | tf_op jit(solution)/shard_map/reduce_scatter | solution.py:807
  992.2 3.3 collective-permute-start.2
  995.5 7.2 collective-permute-done.2
  1003.8 63.8 %psum.7 = f32[2,2048]{1,0:T(2,128)S(1)} all-reduce(f32[2,2048]{1,0:T(2,128)S(1)} %pad_maximum_fusion.6), channel_id=1, replica_groups=mesh['z'=4,'xl'=2,'c'=2,'y'=4,'xh'=2] {'z','xl','c','y','xh'}, use_global_device_ids=true, to_apply=%region_6.7 | all-reduce | flops 4096 | bytes 32768 | tf_op jit(solution)/shard_map/psum | solution.py:908
  1068.3 3.1 fusion.18
  1071.4 2.8 bitcast_convert_fusion.1
  1074.2 3.4 reshape.201
  1077.6 21.4 %all-gather.11.cloned.1.call-done = bf16[16,128,704]{1,2,0:T(8,128)(2,1)} async-done(((bf16[1,128,704]{1,2,0:T(8,128)(2,1)}), bf16[16,128,704]{1,2,0:T(8,128)(2,1)}) %all-gather.11.cloned.1.call-update) | async-done | bytes 2883600 | tf_op jit(solution)/shard_map/all_gather | solution.py:818
  1099.0 5.1 copy_bitcast_fusion
  1104.1 37.9 %all-gather.9.cloned.1.call-done = bf16[16,88,2048]{2,1,0:T(8,128)(2,1)} async-done(((bf16[1,88,2048]{2,1,0:T(8,128)(2,1)}), bf16[16,88,2048]{2,1,0:T(8,128)(2,1)}) %all-gather.9.cloned.1.call-update) | async-done | bytes 5767184 | tf_op jit(solution)/shard_map/all_gather | solution.py:818
  1142.0 8.7 bitcast_convert_fusion
  (149 shorter events, 38.2 us)
Async XLA Ops:
  7.2 666.8 %reduce-scatter.7.cloned.1.call-start = ((), (), s32[]{:S(2)}) async-start(), calls=%async_computation.6 | async-start | bytes 1114112 | tf_op jit(solution)/shard_map/reduce_scatter | solution.py:807
  9.2 6.0 copy-start.29
  9.2 6.0 copy-start.7
  9.2 6.0 copy-start.11
  107.0 5.4 copy-start.9
  107.0 5.4 copy-start.12
  112.4 8.7 copy-start.19
  117.8 3.7 copy-start.20
  117.8 3.7 copy-start
  343.0 36.5 %copy-start.17 = (f32[1024,256]{1,0:T(8,128)}, f32[1024,256]{1,0:T(8,128)S(1)}, u32[]{:S(2)}) copy-start(f32[1024,256]{1,0:T(8,128)S(1)} %copy.104) | copy-start | bytes 3145732
  343.0 36.5 %copy-start.10 = (bf16[8,256,256]{2,1,0:T(8,128)(2,1)S(1)}, bf16[8,256,256]{2,1,0:T(8,128)(2,1)}, u32[]{:S(2)}) copy-start(bf16[8,256,256]{2,1,0:T(8,128)(2,1)} %copy-done.9) | copy-start | bytes 3145732
  380.9 21.9 %copy-start.15 = (bf16[1,128,2048]{2,1,0:T(8,128)(2,1)S(1)}, bf16[1,128,2048]{2,1,0:T(8,128)(2,1)}, u32[]{:S(2)}) copy-start(bf16[1,128,2048]{2,1,0:T(8,128)(2,1)} %param.9) | copy-start | bytes 1572868
  380.9 22.2 %copy-start.28 = (bf16[2048]{0:T(1024)(128)(2,1)S(1)}, bf16[2048]{0:T(1024)(128)(2,1)}, u32[]{:S(2)}) copy-start(bf16[2048]{0:T(1024)(128)(2,1)} %param.14) | copy-start | bytes 12292
  403.0 105.3 %copy-start.14 = (f32[128,2048]{1,0:T(8,128)}, f32[128,2048]{1,0:T(8,128)S(1)}, u32[]{:S(2)}) copy-start(f32[128,2048]{1,0:T(8,128)S(1)} %get-tuple-element.53) | copy-start | bytes 3145732
  426.7 8.1 copy-start.5
  434.8 6.7 copy-start.31
  434.8 6.7 copy-start.32
  434.8 21.3 %slice-start = ((s8[5767168]{0:T(1024)(128)(4,1)}), s8[1572864]{0:T(1024)(128)(4,1)S(1)}, s32[]{:S(2)}) async-start(s8[5767168]{0:T(1024)(128)(4,1)} %bitcast.151), calls=%async_computation.12 | async-start | bytes 3145728
  441.5 14.6 %slice-start.1 = ((s8[5767168]{0:T(1024)(128)(4,1)}), s8[4194304]{0:T(1024)(128)(4,1)S(1)}, s32[]{:S(2)}) async-start(s8[5767168]{0:T(1024)(128)(4,1)} %bitcast.151), calls=%async_computation.13 | async-start | bytes 8388608
  449.4 6.7 copy-start.33
  456.2 3.6 copy-start.35
  465.0 44.0 %copy-start.1 = (bf16[1,128,2048]{2,1,0:T(8,128)(2,1)S(1)}, bf16[1,128,2048]{2,1,0:T(8,128)(2,1)}, u32[]{:S(2)}) copy-start(bf16[1,128,2048]{2,1,0:T(8,128)(2,1)} %param.17) | copy-start | bytes 1572868
  508.0 1.1 copy-start.8
  570.8 1.0 copy-start.3
  571.7 29.5 %copy-start.4 = (f32[1024,256]{1,0:T(8,128)S(1)}, f32[1024,256]{1,0:T(8,128)}, u32[]{:S(2)}) copy-start(f32[1024,256]{1,0:T(8,128)} %copy-done.3) | copy-start | bytes 3145732
  600.7 1.9 copy-start.23
  600.7 156.8 %reduce-scatter.5.cloned.1.call-start = ((), (), s32[]{:S(2)}) async-start(), calls=%async_computation.4 | async-start | bytes 1671168 | tf_op jit(solution)/shard_map/reduce_scatter | solution.py:807
  604.0 3.8 copy-start.21
  607.6 2.2 copy-start.18
  607.6 2.2 copy-start.22
  607.9 2.2 copy-start.13
  610.1 4.4 copy-start.30
  649.6 201.5 %reduce-scatter.11.cloned.1.call-start = ((), (), s32[]{:S(2)}) async-start(), calls=%async_computation.10 | async-start | bytes 3063808 | tf_op jit(solution)/shard_map/reduce_scatter | solution.py:807
  657.8 334.4 %reduce-scatter.9.cloned.1.call-start = ((), (), s32[]{:S(2)}) async-start(), calls=%async_computation.8 | async-start | bytes 6127616 | tf_op jit(solution)/shard_map/reduce_scatter | solution.py:807
  658.1 6.0 copy-start.6
  658.1 6.0 copy-start.34
  670.8 332.7 %copy-start.16 = (bf16[1,128,2048]{2,1,0:T(8,128)(2,1)S(1)}, bf16[1,128,2048]{2,1,0:T(8,128)(2,1)}, u32[]{:S(2)}) copy-start(bf16[1,128,2048]{2,1,0:T(8,128)(2,1)} %param.9) | copy-start | bytes 1572868
  670.8 397.5 %copy-start.2 = (bf16[1,128,2048]{2,1,0:T(8,128)(2,1)S(1)}, bf16[1,128,2048]{2,1,0:T(8,128)(2,1)}, u32[]{:S(2)}) copy-start(bf16[1,128,2048]{2,1,0:T(8,128)(2,1)} %param.17) | copy-start | bytes 1572868
  670.8 400.6 %all-gather.7.cloned.1.call-start = ((), (), s32[]{:S(2)}) async-start(), calls=%async_computation.7 | async-start | bytes 1114112 | tf_op jit(solution)/shard_map/all_gather | solution.py:818
  674.0 18.6 %collective-permute-start.1 = (bf16[1,16,2048]{2,1,0:T(8,128)(2,1)}, bf16[1,16,2048]{2,1,0:T(8,128)(2,1)S(1)}, u32[]{:S(2)}, u32[]{:S(2)}) collective-permute-start(bf16[1,16,2048]{2,1,0:T(8,128)(2,1)} %reduce-scatter.7.cloned.1.call-done), channel_id=1, source_target_pairs={{0,0},{1,8},{2,2},{3,10},{4,4},{5,12},{6,6},{7,14},{8,1},{9,9},{10... | collective-permute-start | bytes 196616 | tf_op jit(solution)/shard_map/ppermute | solution.py:817
  693.2 381.0 %all-gather.5.cloned.1.call-start = ((), (), s32[]{:S(2)}) async-start(), calls=%async_computation.5 | async-start | bytes 1671168 | tf_op jit(solution)/shard_map/all_gather | solution.py:818
  757.6 13.0 %collective-permute-start = (bf16[1,20,2048]{2,1,0:T(8,128)(2,1)}, bf16[1,20,2048]{2,1,0:T(8,128)(2,1)S(1)}, u32[]{:S(2)}, u32[]{:S(2)}) collective-permute-start(bf16[1,20,2048]{2,1,0:T(8,128)(2,1)} %reduce-scatter.5.cloned.1.call-done), channel_id=1, source_target_pairs={{0,0},{1,8},{2,2},{3,10},{4,4},{5,12},{6,6},{7,14},{8,1},{9,9},{10... | collective-permute-start | bytes 245768 | tf_op jit(solution)/shard_map/ppermute | solution.py:817
  771.3 327.7 %all-gather.11.cloned.1.call-start = ((), (), s32[]{:S(2)}) async-start(), calls=%async_computation.11 | async-start | bytes 3063808 | tf_op jit(solution)/shard_map/all_gather | solution.py:818
  851.2 15.5 %collective-permute-start.3 = (bf16[1,128,704]{1,2,0:T(8,128)(2,1)}, bf16[1,128,704]{1,2,0:T(8,128)(2,1)S(1)}, u32[]{:S(2)}, u32[]{:S(2)}) collective-permute-start(bf16[1,128,704]{1,2,0:T(8,128)(2,1)} %reduce-scatter.11.cloned.1.call-done), channel_id=1, source_target_pairs={{0,0},{1,8},{2,2},{3,10},{4,4},{5,12},{6,6},{7,14},{8,1},{9,9},{10... | collective-permute-start | bytes 540680 | tf_op jit(solution)/shard_map/ppermute | solution.py:817
  866.6 0.7 copy-start.25
  867.3 274.7 %all-gather.9.cloned.1.call-start = ((), (), s32[]{:S(2)}) async-start(), calls=%async_computation.9 | async-start | bytes 6127616 | tf_op jit(solution)/shard_map/all_gather | solution.py:818
  992.2 10.4 collective-permute-start.2
  1002.7 0.7 copy-start.24
  (2 other events, 1.3 us)
Sparse Core Ops, SparseCore 0:
  600.9 73.0 reduce-scatter.6
  677.0 80.4 reduce-scatter.4
  760.6 90.5 reduce-scatter.10
  854.0 138.1 reduce-scatter.8
  993.8 32.6 all-gather.6
  1028.6 33.0 all-gather.4
  1063.4 35.4 all-gather.10
  1101.3 40.6 all-gather.8

commit v2 on v1

v2 whole, which is shorter than its diff:
```python
import jax
import jax.numpy as jnp
import numpy as np
from jax import lax
from jax.experimental import pallas as pl
from jax.experimental.pallas import tpu as pltpu
from jax.sharding import Mesh
from jax.sharding import PartitionSpec as P

D = 2048
H = 32
KV = 4
HD = 64
FF = 5632
TOK = 128
HALF = 64
FF_DEV = 704
Q_DEV = 256
EPSILON = 1e-05
FILLER = -1e30
AXES = ("z", "xl", "c", "y", "xh")
ANY = pl.BlockSpec(memory_space=pl.ANY)
VMEM = pl.BlockSpec(memory_space=pltpu.VMEM)
BF16 = jnp.bfloat16
F32 = jnp.float32


class Place:
    def __init__(self):
        self.z, self.xl, self.c, self.y, self.xh = (lax.axis_index(a) for a in AXES)

    def at(self, dz=0, dy=0, core=None, xl=None, xh=None, y=None):
        z = lax.rem(self.z + dz + 4, 4) if dz else self.z
        y = (lax.rem(self.y + dy + 4, 4) if dy else self.y) if y is None else y
        return (
            z,
            self.xl if xl is None else xl,
            self.c if core is None else core,
            y,
            self.xh if xh is None else xh,
        )


class Edges:
    def __init__(self, send, recv):
        self.send, self.recv, self.count, self.started = send, recv, 0, []

    def copy(self, src, dst, device, start=True):
        i = self.count
        self.count += 1
        d = pltpu.make_async_remote_copy(
            src_ref=src,
            dst_ref=dst,
            send_sem=self.send.at[i],
            recv_sem=self.recv.at[i],
            device_id=device,
            device_id_type=pl.DeviceIdType.MESH,
        )
        self.started.append(d)
        if start:
            d.start()
        return d

    def finish(self):
        for d in self.started:
            d.wait_send()


def greet(devices):
    barrier = pltpu.get_barrier_semaphore()
    for device in devices:
        pl.semaphore_signal(
            barrier, inc=1, device_id=device, device_id_type=pl.DeviceIdType.MESH
        )
    pl.semaphore_wait(barrier, len(devices))


def group_members(me):
    found = [me.at(core=1 - me.c)]
    for dy in (1, 2, 3):
        found += [me.at(dy=dy), me.at(dy=dy, core=1 - me.c)]
    return found


class RingGather:
    def __init__(self, me, edges, own, out):
        self.me, self.edges, self.out = me, edges, out
        self.core = me.at(core=1 - me.c)
        self.up, self.down = me.at(dy=1), me.at(dy=-1)
        a, b = pl.ds(0, HALF), pl.ds(HALF, HALF)
        self.a, self.b = a, b
        mine = self.slot(0)
        self.up_a = edges.copy(own.at[a], out.at[mine, a], self.up)
        self.down_b = edges.copy(own.at[b], out.at[mine, b], self.down)
        self.up_b = edges.copy(own.at[b], out.at[mine, b], self.up)
        self.down_a = edges.copy(own.at[a], out.at[mine, a], self.down)
        self.to_core = [edges.copy(own, out.at[mine], self.core)]

    def slot(self, dy):
        return 2 * lax.rem(self.me.y + dy + 4, 4) + self.me.c

    def pass_core(self, dy, part):
        ref = self.out.at[self.slot(dy), part]
        self.to_core.append(self.edges.copy(ref, ref, self.core))

    def relay(self):
        out = self.out
        self.up_a.wait_recv()
        ref = out.at[self.slot(-1), self.a]
        self.on_a = self.edges.copy(ref, ref, self.up)
        self.down_b.wait_recv()
        ref = out.at[self.slot(1), self.b]
        self.on_b = self.edges.copy(ref, ref, self.down)
        self.pass_core(-1, self.a)
        self.pass_core(1, self.b)

    def rest(self):
        self.up_b.wait_recv()
        self.pass_core(-1, self.b)
        self.down_a.wait_recv()
        self.pass_core(1, self.a)
        self.on_a.wait_recv()
        self.pass_core(2, self.a)
        self.on_b.wait_recv()
        self.pass_core(2, self.b)
        for d in self.to_core:
            d.wait_recv()


GATHER_EDGES = 13


class RingScatter:
    def __init__(self, me, edges, parts, got, both, relayed, last):
        self.me, self.edges, self.parts = me, edges, parts
        self.got, self.both, self.relayed, self.last = got, both, relayed, last
        self.up, self.down = me.at(dy=1), me.at(dy=-1)
        self.from_core = {}
        for k in (2, 1, 3, 0):
            row = 2 * lax.rem(me.y + k, 4) + 1 - me.c
            self.from_core[k] = edges.copy(
                parts.at[row], got.at[k], me.at(core=1 - me.c)
            )

    def add_core(self, k):
        self.from_core[k].wait_recv()
        row = 2 * lax.rem(self.me.y + k, 4) + self.me.c
        self.both[k] = (
            self.parts[row].astype(F32) + self.got[k].astype(F32)
        ).astype(BF16)

    def first(self):
        a, b = pl.ds(0, HALF), pl.ds(HALF, HALF)
        e, both = self.edges, self.both
        self.add_core(2)
        self.r_a = e.copy(both.at[2, a], self.relayed.at[0], self.up)
        self.r_b = e.copy(both.at[2, b], self.relayed.at[1], self.down)
        self.add_core(1)
        self.u_b = e.copy(both.at[1, b], self.last.at[0, b], self.up)
        self.add_core(3)
        self.d_a = e.copy(both.at[3, a], self.last.at[1, a], self.down)
        self.add_core(0)

    def second(self):
        a, b = pl.ds(0, HALF), pl.ds(HALF, HALF)
        e, both = self.edges, self.both
        self.r_a.wait_recv()
        both[1, a] = (both[1, a].astype(F32) + self.relayed[0].astype(F32)).astype(BF16)
        self.u_a = e.copy(both.at[1, a], self.last.at[0, a], self.up)
        self.r_b.wait_recv()
        both[3, b] = (both[3, b].astype(F32) + self.relayed[1].astype(F32)).astype(BF16)
        self.d_b = e.copy(both.at[3, b], self.last.at[1, b], self.down)

    def total(self, out):
        for d in (self.u_b, self.d_a, self.u_a, self.d_b):
            d.wait_recv()
        out[...] = (
            self.both[0].astype(F32)
            + self.last[0].astype(F32)
            + self.last[1].astype(F32)
        )


SCATTER_EDGES = 10


def scatter_scratch():
    return [
        pltpu.VMEM((4, TOK, D), BF16),
        pltpu.VMEM((4, TOK, D), BF16),
        pltpu.VMEM((2, HALF, D), BF16),
        pltpu.VMEM((2, TOK, D), BF16),
    ]


def sems(n):
    return [pltpu.SemaphoreType.DMA((n,)), pltpu.SemaphoreType.DMA((n,))]


def shape(dims, dtype=BF16):
    return jax.ShapeDtypeStruct(dims, dtype)


def remote_params(number):
    return pltpu.CompilerParams(
        collective_id=number, has_side_effects=True, vmem_limit_bytes=48 * 2**20
    )


def block_place(block):
    is_kv = block >= 32
    other = block - 32
    rank = block // 4
    y = jnp.where(is_kv, lax.rem(other + 32, 4), rank // 2)
    core = jnp.where(is_kv, other // 4, lax.rem(rank, 2))
    return y, core, jnp.where(is_kv, 4, lax.rem(block, 4))


def own_block(me, j):
    if j == 4:
        return 32 + 4 * me.c + me.y
    return 4 * (2 * me.y + me.c) + j


def send_block(me, src, dst, send_sem, recv_sem, target, stays):
    @pl.when(stays)
    def _():
        pltpu.make_async_copy(src, dst, recv_sem).start()

    @pl.when(jnp.logical_not(stays))
    def _():
        pltpu.make_async_remote_copy(
            src_ref=src,
            dst_ref=dst,
            send_sem=send_sem,
            recv_sem=recv_sem,
            device_id=target,
            device_id_type=pl.DeviceIdType.MESH,
        ).start()


def wait_sent(src, send_sem, stays):
    @pl.when(jnp.logical_not(stays))
    def _():
        pltpu.make_async_copy(src, src, send_sem).wait()


def wait_got(dst, recv_sem):
    pltpu.make_async_copy(dst, dst, recv_sem).wait()


def x_of(me):
    return 2 * me.xh + me.xl


def around(me, dz, dx):
    x = lax.rem(x_of(me) + dx, 4)
    return me.at(dz=dz, xl=lax.rem(x, 2), xh=x // 2)


STEPS = [(dz, dx) for dz in range(4) for dx in range(4)][1:]


class SumOfSixteen:
    def __init__(self, me, src, piece, own, got, send, recv, local):
        self.me, self.src, self.piece, self.own, self.got = me, src, piece, own, got
        self.send, self.recv = send, recv
        self.keep = pltpu.make_async_copy(
            src.at[piece(4 * me.z + x_of(me))], own, local
        )
        self.keep.start()
        for k, (dz, dx) in enumerate(STEPS):
            to = 4 * lax.rem(me.z + dz, 4) + lax.rem(x_of(me) + dx, 4)
            self.copy(src.at[piece(to)], k, around(me, dz, dx)).start()

    def copy(self, src, k, device):
        return pltpu.make_async_remote_copy(
            src_ref=src,
            dst_ref=self.got.at[k],
            send_sem=self.send.at[k],
            recv_sem=self.recv,
            device_id=device,
            device_id_type=pl.DeviceIdType.MESH,
        )

    def total(self):
        self.keep.wait()
        pltpu.make_async_copy(self.got, self.got, self.recv).wait()
        total = self.own[...].astype(F32)
        for k in range(15):
            total = total + self.got[k].astype(F32)
        return total

    def finish(self):
        for k in range(15):
            src = self.src.at[self.piece(0)]
            pltpu.make_async_copy(src, src, self.send.at[k]).wait()


def same(me, z, xl, core, y, xh):
    return (z == me.z) & (xl == me.xl) & (core == me.c) & (y == me.y) & (xh == me.xh)


class Deliver:
    def __init__(self, me, send, recv):
        self.me, self.send, self.recv, self.sent = me, send, recv, []

    def to_owner(self, src, dst, core, y, xh):
        me = self.me
        for dz in range(4):
            for dl in (0, 1):
                z = lax.rem(me.z + dz, 4)
                xl = 1 - me.xl if dl else me.xl
                stays = same(me, z, xl, core, y, xh)
                sem = self.send.at[len(self.sent)]
                send_block(me, src, dst, sem, self.recv, (z, xl, core, y, xh), stays)
                self.sent.append((src, sem, stays))

    def finish(self):
        for src, sem, stays in self.sent:
            wait_sent(src, sem, stays)


def opening_kernel(x, pos, wqkv, xs, poss, wq, send, recv, qs, qr, local):
    me = Place()
    partner = {"xl": 1 - me.xl, "xh": 1 - me.xh}
    members = group_members(me)
    others = [
        me.at(y=lax.rem(me.y + dy, 4), core=core, **partner)
        for dy in range(4)
        for core in (0, 1)
    ]
    greet(members + others)
    edges = Edges(send, recv)
    own_rank = 2 * me.y + me.c
    keep = pltpu.make_async_copy(x, xs.at[own_rank], local.at[0])
    keep.start()
    keep_pos = pltpu.make_async_copy(pos, poss.at[own_rank], local.at[1])
    keep_pos.start()
    pos_copies = [edges.copy(pos, poss.at[own_rank], m) for m in members]
    ring = RingGather(me, edges, x, xs)

    own = 2 * me.y + me.xh
    own_column = me.c == 0
    to_xl = jnp.where(own_column, me.xl, 1 - me.xl)
    to_xh = jnp.where(own_column, me.xh, 1 - me.xh)
    blocks = []
    for i in range(5):
        y, core, slot = block_place(5 * own + i)
        stays = own_column & (y == me.y) & (core == me.c)
        src = wqkv.at[pl.ds(64 * i, 64)]
        send_block(
            me, src, wq.at[slot], qs.at[i], qr.at[slot], (me.z, to_xl, core, y, to_xh), stays
        )
        blocks.append((src, qs.at[i], stays))
    ring.relay()
    ring.rest()
    for d in pos_copies:
        d.wait_recv()
    for i in range(5):
        wait_got(wq.at[i], qr.at[i])
    for src, sem, stays in blocks:
        wait_sent(src, sem, stays)
    edges.finish()
    keep.wait()
    keep_pos.wait()


def opening(x, pos, wqkv):
    return pl.pallas_call(
        opening_kernel,
        out_shape=(
            shape((8, TOK, D)),
            shape((8, 8, TOK), jnp.int32),
            shape((5, 64, D)),
        ),
        in_specs=[ANY] * 3,
        out_specs=(ANY,) * 3,
        scratch_shapes=sems(7 + GATHER_EDGES) + sems(5) + [pltpu.SemaphoreType.DMA((2,))],
        compiler_params=remote_params(0),
        name="opening",
    )(x, pos, wqkv)


def rotary_table():
    steps = np.arange(HD // 2, dtype=np.float32)
    inverse = np.power(np.float32(10000.0), steps * np.float32(-2.0 / HD)).astype(np.float32)
    turning = np.arange(2048, dtype=np.float32)[:, None] * inverse[None, :]
    cosine, sine = np.cos(turning), np.sin(turning)
    return np.concatenate([cosine, cosine, -sine, sine], axis=1).astype(np.float32)


def halves_swapped(rows):
    return jnp.concatenate([rows[:, HD // 2 :], rows[:, : HD // 2]], axis=1)


def rotate(rows, table, back=False):
    turned = halves_swapped(rows) * table[:, HD:]
    return rows * table[:, :HD] + (-turned if back else turned)


def table_rows(table_ref, run):
    return table_ref[pl.ds(pl.multiple_of(run * 64, 64), 64), :]


def project_kernel(runs, core, xs_ref, wq_ref, table_ref, q_ref, kv_ref):
    seq = pl.program_id(0)
    projected = dot_last(xs_ref[...], wq_ref[...])
    is_key = core[0] == 0
    for r in range(4):
        table = table_rows(table_ref, runs[seq * 4 + r])
        rows = projected[64 * r : 64 * r + 64]
        heads = [rotate(rows[:, HD * h : HD * h + HD], table) for h in range(4)]
        query = jnp.concatenate(heads, axis=1).astype(BF16)
        q_ref[64 * r : 64 * r + 64, :] = (query.astype(F32) * 0.125).astype(BF16)
        plain = rows[:, Q_DEV:]
        kv = jnp.where(is_key, rotate(plain, table), plain)
        half, u = r // 2, r % 2
        kv_ref[64 * u : 64 * u + 64, HD * half : HD * half + HD] = kv.astype(BF16)


def whole(dims):
    return pl.BlockSpec(dims, lambda i, *_: (0,) * len(dims))


def project(runs, core, xs, wq, table):
    return pl.pallas_call(
        project_kernel,
        out_shape=(shape((1024, Q_DEV)), shape((512, 128))),
        grid_spec=pltpu.PrefetchScalarGridSpec(
            num_scalar_prefetch=2,
            grid=(4,),
            in_specs=[
                pl.BlockSpec((256, D), lambda i, *_: (i, 0)),
                whole((320, D)),
                whole((2048, 128)),
            ],
            out_specs=[
                pl.BlockSpec((256, Q_DEV), lambda i, *_: (i, 0)),
                pl.BlockSpec((128, 128), lambda i, *_: (i, 0)),
            ],
        ),
        compiler_params=pltpu.CompilerParams(vmem_limit_bytes=40 * 2**20),
        name="project",
    )(runs, core, xs, wq, table)


def project_back_kernel(runs, core, dq_ref, dkv_ref, xs_ref, wq_ref, table_ref, parts_ref, gwq_ref, acc):
    seq = pl.program_id(0)
    is_key = core[0] == 0
    kv = []
    for r in range(4):
        table = table_rows(table_ref, runs[seq * 4 + r])
        half, u = r // 2, r % 2
        plain = dkv_ref[64 * u : 64 * u + 64, HD * half : HD * half + HD]
        kv.append(jnp.where(is_key, rotate(plain, table, back=True), plain))
    grads = jnp.concatenate([dq_ref[...], jnp.concatenate(kv, axis=0).astype(BF16)], axis=1)
    parts_ref[...] = dot(grads, wq_ref[...]).astype(BF16)
    term = dot_first(grads, xs_ref[...])

    @pl.when(seq == 0)
    def _():
        acc[...] = term

    @pl.when(seq > 0)
    def _():
        acc[...] += term

    @pl.when(seq == 3)
    def _():
        gwq_ref[...] = acc[...].astype(BF16)


def project_back(runs, core, dq, dkv, xs, wq, table):
    return pl.pallas_call(
        project_back_kernel,
        out_shape=(shape((1024, D)), shape((320, D))),
        grid_spec=pltpu.PrefetchScalarGridSpec(
            num_scalar_prefetch=2,
            grid=(4,),
            in_specs=[
                pl.BlockSpec((256, Q_DEV), lambda i, *_: (i, 0)),
                pl.BlockSpec((128, 128), lambda i, *_: (i, 0)),
                pl.BlockSpec((256, D), lambda i, *_: (i, 0)),
                whole((320, D)),
                whole((2048, 128)),
            ],
            out_specs=[
                pl.BlockSpec((256, D), lambda i, *_: (i, 0)),
                whole((320, D)),
            ],
            scratch_shapes=[pltpu.VMEM((320, D), F32)],
        ),
        compiler_params=pltpu.CompilerParams(vmem_limit_bytes=40 * 2**20),
        name="project_back",
    )(runs, core, dq, dkv, xs, wq, table)


def chips_in_sequence(me):
    return [(dz, dl) for dz in range(4) for dl in (0, 1)][1:]


def keys_kernel(
    kv, pos, cot, wout, kvs, poss, cots, wo, send, recv, os_, orr, local
):
    me = Place()
    partner = {"xl": 1 - me.xl, "xh": 1 - me.xh}
    core = me.at(core=1 - me.c)
    far = [
        me.at(dz=dz, xl=(1 - me.xl) if dl else me.xl) for dz, dl in chips_in_sequence(me)
    ]
    others = [
        me.at(y=lax.rem(me.y + dy, 4), core=c, **partner) for dy in range(4) for c in (0, 1)
    ]
    greet(far + group_members(me) + others)
    edges = Edges(send, recv)
    chip = 2 * me.z + me.xl
    keeps = [
        pltpu.make_async_copy(kv, kvs.at[me.c, chip], local.at[0]),
        pltpu.make_async_copy(pos, poss.at[chip], local.at[1]),
        pltpu.make_async_copy(cot, cots.at[2 * me.y + me.c], local.at[2]),
    ]
    for d in keeps:
        d.start()
    pos_copies = [edges.copy(pos, poss.at[chip], d) for d in far]
    kv_copies = [edges.copy(kv, kvs.at[me.c, chip], d) for d in far]
    over = [edges.copy(kv, kvs.at[me.c, chip], core)]
    ring = RingGather(me, edges, cot, cots)

    own = 2 * me.y + me.xh
    own_column = me.c == 0
    to_xl = jnp.where(own_column, me.xl, 1 - me.xl)
    to_xh = jnp.where(own_column, me.xh, 1 - me.xh)
    blocks = []
    for i in range(8):
        dy, other = i // 2, i % 2
        y = lax.rem(me.y + dy, 4)
        to_core = me.c if other == 0 else 1 - me.c
        stays = own_column if i == 0 else me.c < 0
        src = wout.at[:, pl.ds(pl.multiple_of(Q_DEV * (2 * y + to_core), Q_DEV), Q_DEV)]
        target = (me.z, to_xl, to_core, y, to_xh)
        send_block(me, src, wo.at[own], os_.at[i], orr.at[own], target, stays)
        blocks.append((src, os_.at[i], stays))
    ring.relay()
    for (dz, dl), d in zip(chips_in_sequence(me), kv_copies):
        d.wait_recv()
        source = 2 * lax.rem(me.z - dz + 4, 4) + ((1 - me.xl) if dl else me.xl)
        ref = kvs.at[me.c, source]
        over.append(edges.copy(ref, ref, core))
    ring.rest()
    for d in over + pos_copies:
        d.wait_recv()
    for i in range(8):
        wait_got(wo.at[i], orr.at[i])
    for src, sem, stays in blocks:
        wait_sent(src, sem, stays)
    edges.finish()
    for d in keeps:
        d.wait()


def exchange_keys(kv, pos, cot, wout):
    return pl.pallas_call(
        keys_kernel,
        out_shape=(
            shape((2, 8, 512, 128)),
            shape((8, 8, 8, TOK), jnp.int32),
            shape((8, TOK, D)),
            shape((8, 256, Q_DEV)),
        ),
        in_specs=[ANY] * 4,
        out_specs=(ANY,) * 4,
        scratch_shapes=sems(7 + 7 + 8 + GATHER_EDGES)
        + sems(8)
        + [pltpu.SemaphoreType.DMA((3,))],
        compiler_params=remote_params(1),
        name="exchange_keys",
    )(kv, pos, cot, wout)


def split_heads(rows):
    return jnp.concatenate([rows[:, HD * h : HD * (h + 1)] for h in range(4)], axis=0)


def join_heads(rows):
    return jnp.concatenate([rows[64 * h : 64 * (h + 1), :] for h in range(4)], axis=1)


def dot_last(a, b):
    return lax.dot_general(a, b, (((1,), (1,)), ((), ())), preferred_element_type=F32)


def dot_first(a, b):
    return lax.dot_general(a, b, (((0,), (0,)), ((), ())), preferred_element_type=F32)


def dot(a, b):
    return lax.dot_general(a, b, (((1,), (0,)), ((), ())), preferred_element_type=F32)


TILE = 256
WIDE = 4


def sort_keys(runs, seq, kv_ref, keys, values):
    for j in range(32):
        chip, core, u = j // 4, (j // 2) % 2, j % 2
        to = pl.ds(pl.multiple_of(runs[seq * 32 + j] * 64, 64), 64)
        rows, lanes = slice(64 * u, 64 * u + 64), slice(HD * core, HD * core + HD)
        keys[to, :] = kv_ref[0, chip, rows, lanes]
        values[to, :] = kv_ref[1, chip, rows, lanes]


def allowed_tile(tile, run):
    key = lax.broadcasted_iota(jnp.int32, (TILE, 256), 0) + tile * TILE
    query = lax.rem(lax.broadcasted_iota(jnp.int32, (TILE, 256), 1), 64) + run * 64
    return key <= query


def tile_rows(tile):
    return pl.ds(pl.multiple_of(tile * TILE, TILE), TILE)


def attend_kernel(
    key_runs, query_runs, q_ref, kv_ref, att_ref, ot_ref, lse_ref, keys, values, high_ref, total_ref, acc_ref
):
    seq = pl.program_id(0)
    sort_keys(key_runs, seq, kv_ref, keys, values)

    def one_run(r, _):
        run = query_runs[seq * 4 + r]
        rows = pl.ds(pl.multiple_of(r * 64, 64), 64)
        query = split_heads(q_ref[rows, :])
        last = run // 4
        high_ref[...] = jnp.full((1, 256), FILLER, F32)
        total_ref[...] = jnp.zeros((1, 256), F32)
        acc_ref[...] = jnp.zeros((HD, 256), F32)

        def tiles(first, count, masked):
            scores = []
            for k in range(count):
                score = dot_last(keys[tile_rows(first + k), :], query)
                if masked and k == count - 1:
                    score = jnp.where(allowed_tile(first + k, run), score, FILLER)
                scores.append(score)
            high = high_ref[...]
            new_high = high
            for score in scores:
                new_high = jnp.maximum(new_high, jnp.max(score, axis=0, keepdims=True))
            scale = jnp.exp(high - new_high)
            total = total_ref[...] * scale
            acc = acc_ref[...] * scale
            for k, score in enumerate(scores):
                weights = jnp.exp(score - new_high)
                total = total + jnp.sum(weights, axis=0, keepdims=True)
                acc = acc + dot_first(values[tile_rows(first + k), :], weights.astype(BF16))
            high_ref[...] = new_high
            total_ref[...] = total
            acc_ref[...] = acc

        @pl.when(last >= WIDE)
        def _():
            tiles(0, WIDE, False)

        start = (last // WIDE) * WIDE
        for n in range(WIDE):

            @pl.when(last - start == n)
            def _():
                tiles(start, n + 1, True)

        total = total_ref[...]
        out = acc_ref[...] / total
        ot_ref[r] = out
        lse_ref[r] = high_ref[...] + jnp.log(total)
        att_ref[rows, :] = join_heads(out.T).astype(BF16)
        return 0

    lax.fori_loop(0, 4, one_run, 0)


def attend(key_runs, query_runs, q, kv):
    return pl.pallas_call(
        attend_kernel,
        out_shape=(shape((1024, 256)), shape((16, HD, 256), F32), shape((16, 1, 256), F32)),
        grid_spec=pltpu.PrefetchScalarGridSpec(
            num_scalar_prefetch=2,
            grid=(4,),
            in_specs=[
                pl.BlockSpec((256, 256), lambda i, *_: (i, 0)),
                pl.BlockSpec((2, 8, 128, 128), lambda i, *_: (0, 0, i, 0)),
            ],
            out_specs=[
                pl.BlockSpec((256, 256), lambda i, *_: (i, 0)),
                pl.BlockSpec((4, HD, 256), lambda i, *_: (i, 0, 0)),
                pl.BlockSpec((4, 1, 256), lambda i, *_: (i, 0, 0)),
            ],
            scratch_shapes=[
                pltpu.VMEM((2048, HD), BF16),
                pltpu.VMEM((2048, HD), BF16),
                pltpu.VMEM((1, 256), F32),
                pltpu.VMEM((1, 256), F32),
                pltpu.VMEM((HD, 256), F32),
            ],
        ),
        compiler_params=pltpu.CompilerParams(vmem_limit_bytes=40 * 2**20),
        name="attend",
    )(key_runs, query_runs, q, kv)


def attend_back_kernel(
    key_runs, query_runs, q_ref, kv_ref, da_ref, ot_ref, lse_ref, table_ref,
    dq_ref, dkv_ref, keys, values, dkeys, dvalues, dq_acc,
):
    seq = pl.program_id(0)
    sort_keys(key_runs, seq, kv_ref, keys, values)
    dkeys[...] = jnp.zeros_like(dkeys)
    dvalues[...] = jnp.zeros_like(dvalues)

    def one_run(r, _):
        run = query_runs[seq * 4 + r]
        rows = pl.ds(pl.multiple_of(r * 64, 64), 64)
        query = split_heads(q_ref[rows, :])
        grad = split_heads(da_ref[rows, :])
        lse = lse_ref[r]
        delta = jnp.sum(grad.astype(F32).T * ot_ref[r], axis=0, keepdims=True)
        last = run // 4
        dq_acc[...] = jnp.zeros((HD, 256), F32)

        def tiles(first, count, masked):
            dq = dq_acc[...]
            for k in range(count):
                at = tile_rows(first + k)
                key = keys[at, :]
                probs = jnp.exp(dot_last(key, query) - lse)
                if masked and k == count - 1:
                    probs = jnp.where(allowed_tile(first + k, run), probs, 0.0)
                grad_probs = dot_last(values[at, :], grad)
                grad_scores = (probs * (grad_probs - delta)).astype(BF16)
                dvalues[at, :] += dot(probs.astype(BF16), grad)
                dkeys[at, :] += dot(grad_scores, query)
                dq = dq + dot_first(key, grad_scores)
            dq_acc[...] = dq

        @pl.when(last >= WIDE)
        def _():
            tiles(0, WIDE, False)

        start = (last // WIDE) * WIDE
        for n in range(WIDE):

            @pl.when(last - start == n)
            def _():
                tiles(start, n + 1, True)

        table = table_rows(table_ref, run)
        dq = (dq_acc[...] * 0.125).T
        heads = [rotate(dq[64 * h : 64 * h + 64], table, back=True) for h in range(4)]
        dq_ref[rows, :] = jnp.concatenate(heads, axis=1).astype(BF16)
        return 0

    lax.fori_loop(0, 4, one_run, 0)
    for j in range(32):
        chip, core, u = j // 4, (j // 2) % 2, j % 2
        at = pl.ds(pl.multiple_of(key_runs[seq * 32 + j] * 64, 64), 64)
        rows, lanes = slice(64 * u, 64 * u + 64), slice(HD * core, HD * core + HD)
        dkv_ref[0, chip, rows, lanes] = dkeys[at, :].astype(BF16)
        dkv_ref[1, chip, rows, lanes] = dvalues[at, :].astype(BF16)


def attend_back(key_runs, query_runs, q, kv, grad, ot, lse, table):
    return pl.pallas_call(
        attend_back_kernel,
        out_shape=(shape((1024, 256)), shape((2, 8, 512, 128))),
        grid_spec=pltpu.PrefetchScalarGridSpec(
            num_scalar_prefetch=2,
            grid=(4,),
            in_specs=[
                pl.BlockSpec((256, 256), lambda i, *_: (i, 0)),
                pl.BlockSpec((2, 8, 128, 128), lambda i, *_: (0, 0, i, 0)),
                pl.BlockSpec((256, 256), lambda i, *_: (i, 0)),
                pl.BlockSpec((4, HD, 256), lambda i, *_: (i, 0, 0)),
                pl.BlockSpec((4, 1, 256), lambda i, *_: (i, 0, 0)),
                whole((2048, 128)),
            ],
            out_specs=[
                pl.BlockSpec((256, 256), lambda i, *_: (i, 0)),
                pl.BlockSpec((2, 8, 128, 128), lambda i, *_: (0, 0, i, 0)),
            ],
            scratch_shapes=[
                pltpu.VMEM((2048, HD), BF16),
                pltpu.VMEM((2048, HD), BF16),
                pltpu.VMEM((2048, HD), F32),
                pltpu.VMEM((2048, HD), F32),
                pltpu.VMEM((HD, 256), F32),
            ],
        ),
        compiler_params=pltpu.CompilerParams(vmem_limit_bytes=40 * 2**20),
        name="attend_back",
    )(key_runs, query_runs, q, kv, grad, ot, lse, table)


ROWS = 16


def in_chunks(step):
    def one(i, _):
        step(pl.ds(pl.multiple_of(i * ROWS, ROWS), ROWS))
        return 0

    lax.fori_loop(0, TOK // ROWS, one, 0)


def mean_last(rows):
    return jnp.mean(rows, axis=-1, keepdims=True)


def middle_kernel(
    parts, tokens, gain, middle, xs, got, both, relayed, last, total, low, send, recv, local
):
    me = Place()
    greet([me.at(core=1 - me.c), me.at(dy=1), me.at(dy=-1)])
    edges = Edges(send, recv)
    ring = RingScatter(me, edges, parts, got, both, relayed, last)
    ring.first()
    ring.second()
    ring.total(total)

    def norm(at):
        rows = tokens[at, :].astype(F32) + total[at, :]
        middle[at, :] = rows
        normal = rows * lax.rsqrt(mean_last(rows * rows) + EPSILON)
        low[at, :] = (normal * gain[...]).astype(BF16)

    in_chunks(norm)
    keep = pltpu.make_async_copy(low, xs.at[2 * me.y + me.c], local)
    keep.start()
    gather = RingGather(me, edges, low, xs)
    gather.relay()
    gather.rest()
    edges.finish()
    keep.wait()


def to_middle(parts, tokens, gain):
    return pl.pallas_call(
        middle_kernel,
        out_shape=(shape((TOK, D), F32), shape((8, TOK, D))),
        in_specs=[VMEM] * 3,
        out_specs=(VMEM, ANY),
        scratch_shapes=scatter_scratch()
        + [pltpu.VMEM((TOK, D), F32), pltpu.VMEM((TOK, D), BF16)]
        + sems(SCATTER_EDGES + GATHER_EDGES)
        + [pltpu.SemaphoreType.DMA],
        compiler_params=remote_params(2),
        name="to_middle",
    )(parts, tokens, gain)


class SumOfFour:
    def __init__(self, me, along_z, src, piece, own, got, send, recv, local):
        self.src, self.piece, self.own, self.got = src, piece, own, got
        self.send, self.recv = send, recv
        here = me.z if along_z else x_of(me)
        self.keep = pltpu.make_async_copy(src.at[piece(here)], own, local)
        self.keep.start()
        for k in (1, 2, 3):
            device = around(me, k, 0) if along_z else around(me, 0, k)
            pltpu.make_async_remote_copy(
                src_ref=src.at[piece(lax.rem(here + k, 4))],
                dst_ref=got.at[k - 1],
                send_sem=send.at[k - 1],
                recv_sem=recv,
                device_id=device,
                device_id_type=pl.DeviceIdType.MESH,
            ).start()

    def total(self, out, rows):
        self.keep.wait()
        pltpu.make_async_copy(self.got, self.got, self.recv).wait()
        own, got = self.own, self.got

        def one(i, _):
            at = pl.ds(pl.multiple_of(i * rows, rows), rows)
            total = own[at, :].astype(F32)
            for k in range(3):
                total = total + got[k, at, :].astype(F32)
            out[at, :] = total.astype(BF16)
            return 0

        lax.fori_loop(0, out.shape[0] // rows, one, 0)

    def finish(self):
        for k in range(3):
            src = self.src.at[self.piece(0)]
            pltpu.make_async_copy(src, src, self.send.at[k]).wait()


def columns(width):
    return lambda i: (slice(None), pl.ds(pl.multiple_of(i * width, width), width))


def row_block(height, start=0):
    return lambda i: (pl.ds(pl.multiple_of(start + i * height, height), height), slice(None))


def mlp_back_kernel(
    branch_parts, grad_parts, middle, cot, gain, ggate, gup, gdn,
    output, grad_middle, gain_grad, gbs, gate_out, up_out, top_out, low_out,
    g1, b1, r1, l1, g2, b2, r2, l2, total, low,
    gate_own, gate_got, up_own, up_got, top_own, top_got, low_own, low_got,
    gate_q, up_q, top_q, low_q,
    gate_own2, gate_got2, up_own2, up_got2, top_own2, top_got2, low_own2, low_got2,
    send, recv, qs, qr, ql, local,
):
    me = Place()
    greet(
        [me.at(core=1 - me.c), me.at(dy=1), me.at(dy=-1)]
        + [around(me, k, 0) for k in (1, 2, 3)]
        + [around(me, 0, k) for k in (1, 2, 3)]
    )
    edges = Edges(send, recv)
    ring = RingScatter(me, edges, grad_parts, g2, b2, r2, l2)

    def quarter(i, along_z, src, piece, own, got):
        return SumOfFour(
            me, along_z, src, piece, own, got, qs.at[i], qr.at[i], ql.at[i]
        )

    gate_sum = quarter(0, True, ggate, columns(512), gate_own, gate_got)
    up_sum = quarter(1, False, gup, columns(512), up_own, up_got)
    top_sum = quarter(2, True, gdn, row_block(256), top_own, top_got)
    low_sum = quarter(3, False, gdn, row_block(256, 1024), low_own, low_got)
    ring.first()
    ring.second()
    ring.total(total)
    gain_grad[...] = jnp.zeros_like(gain_grad)

    def back(at):
        rows = middle[at, :]
        inverse = lax.rsqrt(mean_last(rows * rows) + EPSILON)
        normal = rows * inverse
        grad = total[at, :]
        gain_grad[...] += jnp.sum(normal * grad, axis=0, keepdims=True)
        scaled = grad * gain[...]
        result = cot[at, :].astype(F32) + inverse * (
            scaled - normal * mean_last(scaled * normal)
        )
        grad_middle[at, :] = result
        low[at, :] = result.astype(BF16)

    in_chunks(back)
    keep = pltpu.make_async_copy(low, gbs.at[2 * me.y + me.c], local)
    keep.start()
    gather = RingGather(me, edges, low, gbs)
    branch = RingScatter(me, edges, branch_parts, g1, b1, r1, l1)
    gather.relay()
    branch.first()
    gate_sum.total(gate_q, 64)
    up_sum.total(up_q, 64)
    top_sum.total(top_q, 64)
    low_sum.total(low_q, 64)
    branch.second()
    gate_two = quarter(4, False, gate_q, columns(128), gate_own2, gate_got2)
    up_two = quarter(5, True, up_q, columns(128), up_own2, up_got2)
    top_two = quarter(6, False, top_q, row_block(64), top_own2, top_got2)
    low_two = quarter(7, True, low_q, row_block(64), low_own2, low_got2)
    gather.rest()
    branch.total(total)

    def out(at):
        output[at, :] = (middle[at, :] + total[at, :]).astype(BF16)

    in_chunks(out)
    gate_two.total(gate_out, 64)
    up_two.total(up_out, 64)
    top_two.total(top_out, 64)
    low_two.total(low_out, 64)
    for d in (gate_sum, up_sum, top_sum, low_sum, gate_two, up_two, top_two, low_two):
        d.finish()
    edges.finish()
    keep.wait()


def mlp_back(branch_parts, grad_parts, middle, cot, gain, ggate, gup, gdn):
    def own_and_got(rows, width):
        return [pltpu.VMEM((rows, width), BF16), pltpu.VMEM((3, rows, width), BF16)]

    return pl.pallas_call(
        mlp_back_kernel,
        out_shape=(
            shape((TOK, D)),
            shape((TOK, D), F32),
            shape((1, D), F32),
            shape((8, TOK, D)),
            shape((FF_DEV, 128)),
            shape((FF_DEV, 128)),
            shape((64, FF_DEV)),
            shape((64, FF_DEV)),
        ),
        in_specs=[VMEM] * 5 + [ANY] * 3,
        out_specs=(VMEM, VMEM, VMEM, ANY, VMEM, VMEM, VMEM, VMEM),
        scratch_shapes=scatter_scratch() * 2
        + [pltpu.VMEM((TOK, D), F32), pltpu.VMEM((TOK, D), BF16)]
        + own_and_got(FF_DEV, 512) * 2
        + own_and_got(256, FF_DEV) * 2
        + [pltpu.VMEM((FF_DEV, 512), BF16)] * 2
        + [pltpu.VMEM((256, FF_DEV), BF16)] * 2
        + own_and_got(FF_DEV, 128) * 2
        + own_and_got(64, FF_DEV) * 2
        + sems(2 * SCATTER_EDGES + GATHER_EDGES)
        + [
            pltpu.SemaphoreType.DMA((8, 3)),
            pltpu.SemaphoreType.DMA((8,)),
            pltpu.SemaphoreType.DMA((8,)),
            pltpu.SemaphoreType.DMA,
        ],
        compiler_params=remote_params(3),
        name="mlp_back",
    )(branch_parts, grad_parts, middle, cot, gain, ggate, gup, gdn)


def key_grads_kernel(
    dkv, gwo, out, wo_out, got, both, last, wo_own, wo_got, wo_piece, wo_all,
    send, recv, ws, wr, local, ds, dr,
):
    me = Place()
    core = me.at(core=1 - me.c)
    far = [
        me.at(dz=dz, xl=(1 - me.xl) if dl else me.xl) for dz, dl in chips_in_sequence(me)
    ]
    wide = [around(me, dz, dx) for dz, dx in STEPS]
    greet(far + wide + group_members(me))
    edges = Edges(send, recv)
    order = []
    for dz, dl in chips_in_sequence(me) + [(0, 0)]:
        chip = 2 * lax.rem(me.z + dz, 4) + ((1 - me.xl) if dl else me.xl)
        order.append((chip, edges.copy(dkv.at[1 - me.c, chip], got.at[chip], core)))
    far_copies = []
    for i, (chip, d) in enumerate(order):
        d.wait_recv()
        both[chip] = (dkv[me.c, chip].astype(F32) + got[chip].astype(F32)).astype(BF16)
        if i < 7:
            far_copies.append(edges.copy(both.at[chip], last.at[i], far[i]))
    wo_sum = SumOfSixteen(me, gwo, row_block(128), wo_own, wo_got, ws, wr, local)
    total = both[2 * me.z + me.xl].astype(F32)
    for i, d in enumerate(far_copies):
        d.wait_recv()
        total = total + last[i].astype(F32)
    out[...] = total
    wo_piece[...] = wo_sum.total().astype(BF16)
    deliver = Deliver(me, ds, dr)
    rank = 2 * me.y + me.c
    dst = wo_all.at[
        pl.ds(pl.multiple_of(128 * me.xl, 128), 128),
        pl.ds(pl.multiple_of(Q_DEV * rank, Q_DEV), Q_DEV),
    ]
    deliver.to_owner(wo_piece, dst, me.y // 2, me.z, me.xh)
    half = wo_all.at[:, pl.ds(pl.multiple_of(1024 * me.c, 1024), 1024)]
    wait_got(half, dr)
    edges.copy(half, half, core).wait_recv()
    wo_out[...] = wo_all[...].astype(F32)
    wo_sum.finish()
    deliver.finish()
    edges.finish()


def sum_key_grads(dkv, gwo):
    return pl.pallas_call(
        key_grads_kernel,
        out_shape=(shape((512, 128), F32), shape((256, D), F32)),
        in_specs=[VMEM, ANY],
        out_specs=(VMEM, VMEM),
        scratch_shapes=[
            pltpu.VMEM((8, 512, 128), BF16),
            pltpu.VMEM((8, 512, 128), BF16),
            pltpu.VMEM((7, 512, 128), BF16),
            pltpu.VMEM((128, Q_DEV), BF16),
            pltpu.VMEM((15, 128, Q_DEV), BF16),
            pltpu.VMEM((128, Q_DEV), BF16),
            pltpu.VMEM((256, D), BF16),
        ]
        + sems(16)
        + [
            pltpu.SemaphoreType.DMA((15,)),
            pltpu.SemaphoreType.DMA,
            pltpu.SemaphoreType.DMA,
            pltpu.SemaphoreType.DMA((8,)),
            pltpu.SemaphoreType.DMA,
        ],
        compiler_params=remote_params(4),
        name="sum_key_grads",
    )(dkv, gwo)


def closing_kernel(
    parts, gwq, tokens, gain, grad_middle, gain_two,
    grad_tokens, gains, wq_out,
    got, both, relayed, last, total, wq_own, wq_got, wq_piece, wq_all,
    mine, near, near_sum, owners,
    send, recv, ws, wr, local, ds, dr, gs, gr, hs, hr,
):
    me = Place()
    members = group_members(me)
    greet(members + [around(me, dz, dx) for dz, dx in STEPS])
    edges = Edges(send, recv)
    ring = RingScatter(me, edges, parts, got, both, relayed, last)
    wq_sum = SumOfSixteen(me, gwq, columns(128), wq_own, wq_got, ws, wr, local)
    ring.first()
    ring.second()
    wq_piece[...] = wq_sum.total().astype(BF16)
    deliver = Deliver(me, ds, dr)
    piece = 4 * me.z + x_of(me)
    for j in range(5):
        block = own_block(me, j)
        owner, slot = block // 5, lax.rem(block, 5)
        dst = wq_all.at[
            pl.ds(pl.multiple_of(64 * slot, 64), 64),
            pl.ds(pl.multiple_of(128 * piece, 128), 128),
        ]
        deliver.to_owner(
            wq_piece.at[pl.ds(64 * j, 64)], dst, me.z // 2, owner // 2, lax.rem(owner, 2)
        )
    ring.total(total)
    mine[...] = jnp.zeros_like(mine)
    mine[1:2, :] = gain_two[...]

    def back(at):
        rows = tokens[at, :].astype(F32)
        inverse = lax.rsqrt(mean_last(rows * rows) + EPSILON)
        normal = rows * inverse
        grad = total[at, :]
        mine[0:1, :] += jnp.sum(normal * grad, axis=0, keepdims=True)
        scaled = grad * gain[...]
        grad_tokens[at, :] = grad_middle[at, :] + inverse * (
            scaled - normal * mean_last(scaled * normal)
        )

    in_chunks(back)

    def slice_of(rank):
        return mine.at[:, pl.ds(pl.multiple_of(256 * rank, 256), 256)]

    near_copies = []
    for k in range(1, 8):
        dy, other = k // 2, k % 2
        y = lax.rem(me.y + dy, 4)
        to_core = 1 - me.c if other else me.c
        d = pltpu.make_async_remote_copy(
            src_ref=slice_of(2 * y + to_core),
            dst_ref=near.at[k - 1],
            send_sem=gs.at[k - 1],
            recv_sem=gr,
            device_id=me.at(y=y, core=to_core),
            device_id_type=pl.DeviceIdType.MESH,
        )
        d.start()
        near_copies.append(d)
    own = mine[:, pl.ds(pl.multiple_of(256 * (2 * me.y + me.c), 256), 256)]
    wait_got(near, gr)
    for k in range(7):
        own = own + near[k]
    near_sum[...] = own
    far = Deliver(me, hs, hr)
    for to_core in (0, 1):
        far.to_owner(near_sum, owners.at[piece], to_core, me.y, me.c)

    half = wq_all.at[:, pl.ds(pl.multiple_of(1024 * me.c, 1024), 1024)]
    wait_got(half, dr)
    over = edges.copy(half, half, me.at(core=1 - me.c))
    wait_got(owners, hr)
    sum_all = owners[0]
    for k in range(1, 16):
        sum_all = sum_all + owners[k]
    gains[...] = sum_all
    over.wait_recv()
    wq_out[...] = wq_all[...].astype(F32)
    wq_sum.finish()
    deliver.finish()
    for d in near_copies:
        d.wait_send()
    far.finish()
    edges.finish()


def closing(parts, gwq, tokens, gain, grad_middle, gain_two):
    return pl.pallas_call(
        closing_kernel,
        out_shape=(
            shape((TOK, D), F32),
            shape((8, 256), F32),
            shape((320, D), F32),
        ),
        in_specs=[VMEM, ANY] + [VMEM] * 4,
        out_specs=(VMEM,) * 3,
        scratch_shapes=scatter_scratch()
        + [
            pltpu.VMEM((TOK, D), F32),
            pltpu.VMEM((320, 128), BF16),
            pltpu.VMEM((15, 320, 128), BF16),
            pltpu.VMEM((320, 128), BF16),
            pltpu.VMEM((320, D), BF16),
            pltpu.VMEM((8, D), F32),
            pltpu.VMEM((7, 8, 256), F32),
            pltpu.VMEM((8, 256), F32),
            pltpu.VMEM((16, 8, 256), F32),
        ]
        + sems(SCATTER_EDGES + 1)
        + [
            pltpu.SemaphoreType.DMA((15,)),
            pltpu.SemaphoreType.DMA,
            pltpu.SemaphoreType.DMA,
            pltpu.SemaphoreType.DMA((40,)),
            pltpu.SemaphoreType.DMA,
            pltpu.SemaphoreType.DMA((7,)),
            pltpu.SemaphoreType.DMA,
            pltpu.SemaphoreType.DMA((16,)),
            pltpu.SemaphoreType.DMA,
        ],
        compiler_params=remote_params(5),
        name="closing",
    )(parts, gwq, tokens, gain, grad_middle, gain_two)


def route(step):
    pairs = []
    for z in range(4):
        for xl in range(2):
            for c in range(2):
                for y in range(4):
                    for xh in range(2):
                        here = (((z * 2 + xl) * 2 + c) * 4 + y) * 2 + xh
                        z_to, xl_to, c_to, y_to, xh_to = step(z, xl, c, y, xh)
                        there = (((z_to * 2 + xl_to) * 2 + c_to) * 4 + y_to) * 2 + xh_to
                        pairs.append((here, there))
    return pairs


def to_worker(z, xl, c, y, xh):
    return (z, xl, c, y, xh) if c == xh else (z, 1 - xl, 1 - c, y, 1 - xh)


def to_owner(z, xl, c, y, xh):
    return (z, xl, xh, y, c)


def worker_shard(shard):
    rows = shard.shape[0] // 4
    mine = lax.dynamic_slice_in_dim(shard, lax.axis_index("z") * rows, rows)
    mine = lax.ppermute(mine, AXES, route(to_worker))
    return lax.all_gather(mine, "z", axis=0, tiled=True)


def gather_owned(piece):
    piece = lax.ppermute(piece, AXES, route(to_owner))
    return lax.all_gather(piece, ("z", "xl", "c"), axis=0).reshape((4, 2, 2) + piece.shape)


def body(hidden, positions, gain_attn, w_qkv, w_out, gain_mlp, w_gate_up, w_down, cotangent):
    core = lax.axis_index("c").reshape(1)
    gain_one = gain_attn.astype(F32).reshape(1, D)
    gain_two = gain_mlp.astype(F32).reshape(1, D)
    tokens = hidden[0].astype(F32)
    inverse_one = lax.rsqrt(jnp.mean(tokens * tokens, axis=-1, keepdims=True) + EPSILON)
    input_one = (tokens * inverse_one * gain_one).astype(BF16)
    table = jnp.asarray(rotary_table())
    xs, poss, wq = opening(input_one, jnp.broadcast_to(positions, (8, TOK)), w_qkv)
    gu = worker_shard(w_gate_up.reshape(2 * FF_DEV, D))
    dn = worker_shard(w_down)
    xs = xs.reshape(1024, D)
    wq = wq.reshape(320, D)
    query_runs = poss[:, 0, ::64].reshape(16) // 64
    query, kv = project(query_runs, core, xs, wq, table)
    kvs, places, cots, wo = exchange_keys(kv, poss, cotangent[0], w_out)
    cots = cots.reshape(1024, D)
    wo = wo.reshape(D, Q_DEV)
    key_runs = (
        places[:, :, 0, ::64].reshape(8, 4, 2, 2).transpose(1, 0, 2, 3).reshape(128) // 64
    )
    att, ot, lse = attend(key_runs, query_runs, query, kvs)
    parts = dot_last(att, wo).astype(BF16)
    middle, x2 = to_middle(parts.reshape(8, TOK, D), hidden[0], gain_two)
    x2 = x2.reshape(1024, D)

    gate = dot_last(x2, gu[:FF_DEV])
    upward = dot_last(x2, gu[FF_DEV:])
    grad_active = dot(cots, dn)
    sigmoid = jax.nn.sigmoid(gate)
    swish = gate * sigmoid
    active = (swish * upward).astype(BF16)
    grad_upward = (grad_active * swish).astype(BF16)
    grad_gate = (grad_active * upward * sigmoid * (1.0 + gate * (1.0 - sigmoid))).astype(BF16)
    branch_parts = dot_last(active, dn).astype(BF16).reshape(8, TOK, D)
    grad_parts = (dot(grad_gate, gu[:FF_DEV]) + dot(grad_upward, gu[FF_DEV:])).astype(BF16)
    ggate = dot_first(grad_gate, x2).astype(BF16)
    gup = dot_first(grad_upward, x2).astype(BF16)
    gdn = dot_first(cots, active).astype(BF16)
    output, grad_middle, gain_grad, gbs, gate_piece, up_piece, top_piece, low_piece = mlp_back(
        branch_parts, grad_parts.reshape(8, TOK, D), middle, cotangent[0], gain_two,
        ggate, gup, gdn,
    )
    gb = gbs.reshape(1024, D)
    grad_att = dot(gb, wo).astype(BF16)
    grad_wo = dot_first(gb, att).astype(BF16)
    grad_gu = gather_owned(jnp.stack([gate_piece, up_piece]))
    grad_dn = gather_owned(jnp.stack([top_piece, low_piece]))
    dq, dkv = attend_back(key_runs, query_runs, query, kvs, grad_att, ot, lse, table)
    dkv, grad_w_out = sum_key_grads(dkv, grad_wo)
    one_parts, gwq = project_back(query_runs, core, dq, dkv, xs, wq, table)
    grad_tokens, gains, grad_w_qkv = closing(
        one_parts.reshape(8, TOK, D), gwq, hidden[0], gain_one, grad_middle, gain_grad
    )

    gate_full = grad_gu[:, :, :, 0].transpose(3, 0, 2, 1, 4).reshape(FF_DEV, D)
    up_full = grad_gu[:, :, :, 1].transpose(3, 2, 1, 0, 4).reshape(FF_DEV, D)
    top_full = grad_dn[:, :, :, 0].transpose(0, 2, 1, 3, 4).reshape(1024, FF_DEV)
    low_full = grad_dn[:, :, :, 1].transpose(2, 1, 0, 3, 4).reshape(1024, FF_DEV)
    return (
        output[None],
        grad_tokens[None],
        gains[0],
        grad_w_qkv,
        grad_w_out,
        gains[1],
        jnp.stack([gate_full, up_full]).astype(F32),
        jnp.concatenate([top_full, low_full]).astype(F32),
    )


def solution(mesh):
    fine = Mesh(mesh.devices.reshape(4, 2, 2, 4, 2), AXES)
    ctx, fsdp = ("z", "xl", "c"), ("y", "xh")
    weight = P(fsdp, None)
    return jax.shard_map(
        body,
        mesh=fine,
        in_specs=(
            P(fsdp, ctx, None),
            P(fsdp, ctx),
            P(),
            weight,
            weight,
            P(),
            P(None, fsdp, None),
            P(None, fsdp),
            P(fsdp, ctx, None),
        ),
        out_specs=(
            P(fsdp, ctx, None),
            P(fsdp, ctx, None),
            P(fsdp),
            weight,
            weight,
            P(fsdp),
            P(None, fsdp, None),
            P(None, fsdp),
        ),
        check_vma=False,
    )
```

time: 1170 us -> 614 us (0.52)
  waiting for transfers between devices: 347 us -> 36.9 us
  Pallas kernels: 544 us -> 387 us
  blocking collectives: 63.8 us -> 0 us
  local copies, waits for them, and re-layouts: 31.9 us -> 76.6 us
  other arithmetic: 44.5 us -> 13.2 us
  starting transfers between devices: 42.9 us -> 19.4 us
    reduce_scatter x4 -> x0, waiting for transfers between devices: 272 us -> none  [reduce_grads(): lax.psum_scatter(shares, ('z', 'xl', 'xh'), scatter_dimension=0, tiled=True)]
    pallas_call x1, Pallas kernels: 210 us -> 43.3 us  [exchange_keys(): pl.pallas_call(keys_kernel, out_shape=(shape((2, 8, 512, 128)), shape((8,...]
    psum x1 -> x0, blocking collectives: 63.8 us -> none  [body(): gains = lax.psum(gains, AXES)]
    all_gather x4, waiting for transfers between devices: 59.3 us -> 0.01 us  [the longest x2 0.01 us: worker_shard(): return lax.all_gather(mine, 'z', axis=0, tiled=True)]
    pallas_call x1, Pallas kernels: 91.8 us -> 34.6 us  [opening(): pl.pallas_call(opening_kernel, out_shape=(shape((8, TOK, D)), shape((8, 8...]
    pallas_call x1, Pallas kernels: 29 us -> 69.9 us  [sum_key_grads(): pl.pallas_call(key_grads_kernel, out_shape=(shape((512, 128), F32), shape...]
    pallas_call x6, Pallas kernels: 179 us -> 217 us  [the longest x1 71.9 us: mlp_back(): pl.pallas_call(mlp_back_kernel, out_shape=(shape((TOK, D)), shape((TOK, D...]
    unnamed x79 -> x107, local copies, waits for them, and re-layouts: 9.35 us -> 35 us
  transfers between devices with their start and end apart: 12 -> 8, of which waited for: 10 -> 4; matrix products, arithmetic and copies ran while one was open for 5% -> 6% of each run, Pallas kernels for 3% -> 52%
where the time goes in v2:
time: 614 us; the launch traced here: 607 us
  Pallas kernels  387 us (63%)
  local copies, waits for them, and re-layouts  76.6 us (12%)
  matrix products  59.2 us (10%)
  waiting for transfers between devices  36.9 us (6%)
  starting transfers between devices  19.4 us (3%)
  between operations  14.6 us (2%)
  other arithmetic  13.2 us (2%)
    pallas_call x1, Pallas kernels, mlp_back(): pl.pallas_call(mlp_back_kernel, out_shape=(shape((TOK, D)), shape((TOK, D...  71.9 us
    pallas_call x1, Pallas kernels, sum_key_grads(): pl.pallas_call(key_grads_kernel, out_shape=(shape((512, 128), F32), shape...  69.9 us
    pallas_call x1, Pallas kernels, closing(): pl.pallas_call(closing_kernel, out_shape=(shape((TOK, D), F32), shape((8,...  51 us
    pallas_call x1, Pallas kernels, to_middle(): pl.pallas_call(middle_kernel, out_shape=(shape((TOK, D), F32), shape((8,...  49.6 us
    pallas_call x1, Pallas kernels, exchange_keys(): pl.pallas_call(keys_kernel, out_shape=(shape((2, 8, 512, 128)), shape((8,...  43.3 us
    unnamed x107, local copies, waits for them, and re-layouts  35 us
    pallas_call x1, Pallas kernels, opening(): pl.pallas_call(opening_kernel, out_shape=(shape((8, TOK, D)), shape((8, 8...  34.6 us
    pallas_call x1, Pallas kernels, attend_back(): pl.pallas_call(attend_back_kernel, out_shape=(shape((1024, 256)), shape((...  33.1 us
  transfers between devices with their start and end apart: 8, of which 4 were waited for; matrix products, arithmetic and copies ran while one was open for 6% of the time, Pallas kernels for 52%

profile of v2, /device:TPU:9, one launch (start us, length us, event | category | flops | bytes accessed | tf_op | source)
XLA Modules:
  0.0 607.1 jit_solution(218607413813276030)
XLA Ops:
  7.2 1.8 copy-done
  9.1 5.1 collective-permute-start.1
  14.2 9.0 %collective-permute-done.1 = bf16[512,704]{0,1:T(8,128)(2,1)S(1)} collective-permute-done((bf16[512,704]{0,1:T(8,128)(2,1)S(1)}, bf16[512,704]{0,1:T(8,128)(2,1)S(1)}, u32[]{:S(2)}, u32[]{:S(2)}) %collective-permute-start.1) | collective-permute-done | bytes 720928 | tf_op jit(solution)/shard_map/ppermute | solution.py:1250
  24.1 1.5 constant_dynamic-slice_fusion.1
  25.6 5.0 collective-permute-start
  30.6 17.1 %collective-permute-done = bf16[352,2048]{1,0:T(8,128)(2,1)} collective-permute-done((bf16[352,2048]{1,0:T(8,128)(2,1)S(1)}, bf16[352,2048]{1,0:T(8,128)(2,1)}, u32[]{:S(2)}, u32[]{:S(2)}) %collective-permute-start) | collective-permute-done | bytes 1441824 | tf_op jit(solution)/shard_map/ppermute | solution.py:1250
  49.5 34.6 %opening.1 = (bf16[8,128,2048]{2,1,0:T(8,128)(2,1)}, s32[8,8,128]{2,1,0:T(8,128)S(1)}, bf16[5,64,2048]{2,1,0:T(8,128)(2,1)S(1)}) custom-call(bf16[128,2048]{1,0:T(8,128)(2,1)S(1)} %fusion.10.x, s32[8,128]{1,0:T(8,128)S(1)} %broadcast_in_dim.15.pos, bf16[320,2048]{1,0:T(8,128)(2,1)S(1)} %copy-done.16), custom_call_target="tpu_custom_call" | custom-call | tf_op jit(solution)/shard_map/opening/pallas_call | solution.py:370
  85.5 2.2 copy-done.2
  87.8 4.5 project.1
  92.3 43.3 %exchange_keys.1 = (bf16[2,8,512,128]{3,2,1,0:T(8,128)(2,1)S(1)}, s32[8,8,8,128]{3,2,1,0:T(8,128)S(1)}, bf16[8,128,2048]{2,1,0:T(8,128)(2,1)}, bf16[8,256,256]{2,1,0:T(8,128)(2,1)S(1)}) custom-call(bf16[512,128]{1,0:T(8,128)(2,1)S(1)} %get-tuple-element.42.kv, s32[8,8,128]{2,1,0:T(8,128)S(1)} %get-tuple-element.39.pos, bf16[128,2048]{1,0:T(8,128)(2,1)S(1)} %bitcast.77, ...), custom_call_target="tpu_custom_call" | custom-call | tf_op jit(solution)/shard_map/exchange_keys/pallas_call | solution.py:563
  138.6 3.5 slice.33
  142.5 1.6 copy-done.7
  144.1 22.7 %attend.1 = (bf16[1024,256]{1,0:T(8,128)(2,1)S(1)}, f32[16,64,256]{2,1,0:T(8,128)S(1)}, f32[16,1,256]{2,1,0:T(1,128)S(1)}) custom-call(s32[128]{0:T(128)S(1)} %and_select_fusion.key_runs, s32[16]{0:T(128)S(1)} %and_select_fusion.1.runs.query_runs, bf16[1024,256]{1,0:T(8,128)(2,1)S(1)} %get-tuple-element.44.q_ref, bf16[2,8,512,128]{3,2,1,0:T(8,128)(2,1)S(1)} %copy-done.7), custom_call_target="tpu_custom_call" | custom-call | tf_op jit(solution)/shard_map/attend/pallas_call | solution.py:683
  166.8 3.3 convolution_convert_fusion.1
  170.1 49.6 %to_middle.1 = (f32[128,2048]{1,0:T(8,128)S(1)}, bf16[8,128,2048]{2,1,0:T(8,128)(2,1)S(1)}) custom-call(bf16[8,128,2048]{2,1,0:T(8,128)(2,1)} %bitcast.94, bf16[128,2048]{1,0:T(8,128)(2,1)S(1)} %bitcast.72, f32[1,2048]{1,0:T(1,128)S(1)} %bitcast.88), custom_call_target="tpu_custom_call" | custom-call | tf_op jit(solution)/shard_map/to_middle/pallas_call | solution.py:846
  220.7 2.0 copy-done.31
  222.8 7.8 %fusion.13 = f32[1024,704]{0,1:T(8,128)} fusion(bf16[1024,2048]{1,0:T(8,128)(2,1)} %bitcast.110, bf16[2048,704]{0,1:T(8,128)(2,1)} %all-gather.9.cloned.1.call-done), kind=kOutput, calls=%fused_computation.44 | convolution fusion | flops 2952790016 | bytes 9961472 | tf_op jit(solution)/shard_map/dot_general | solution.py:598
  230.6 6.0 fusion.3
  237.4 5.8 multiply_convert_fusion.1
  244.4 4.6 convolution_convert_fusion.2
  249.0 4.6 copy.43.gdn
  253.6 7.5 %convolution_convert_fusion.4.ggate = bf16[704,2048]{1,0:T(8,128)(2,1)} fusion(bf16[1024,704]{0,1:T(8,128)(2,1)} %get-tuple-element.96, bf16[1024,2048]{1,0:T(8,128)(2,1)} %bitcast.91), kind=kOutput, calls=%fused_computation.6 | convolution fusion | flops 2954231808 | bytes 8519680 | tf_op jit(solution)/shard_map/dot_general | solution.py:594
  261.2 4.6 convolution_convert_fusion.3.gup
  265.8 5.0 convolution_convert_fusion
  270.8 3.5 fusion.1
  274.4 5.7 add_convert_fusion
  280.1 71.9 %mlp_back.1 = (bf16[128,2048]{1,0:T(8,128)(2,1)S(1)}, f32[128,2048]{1,0:T(8,128)S(1)}, f32[1,2048]{1,0:T(1,128)S(1)}, bf16[8,128,2048]{2,1,0:T(8,128)(2,1)}, bf1...) custom-call(bf16[8,128,2048]{2,1,0:T(8,128)(2,1)} %bitcast.98, ...), custom_call_target="tpu_custom_call" | custom-call | tf_op jit(solution)/shard_map/mlp_back/pallas_call | solution.py:989
  355.1 4.6 collective-permute-start.3
  359.7 4.0 collective-permute-done.3
  364.9 4.6 collective-permute-start.2
  369.5 6.8 %collective-permute-done.2 = bf16[2,704,128]{2,1,0:T(8,128)(2,1)} collective-permute-done((bf16[2,704,128]{2,1,0:T(8,128)(2,1)S(1)}, bf16[2,704,128]{2,1,0:T(8,128)(2,1)}, u32[]{:S(2)}, u32[]{:S(2)}) %collective-permute-start.2) | collective-permute-done | bytes 360480 | tf_op jit(solution)/shard_map/ppermute | solution.py:1255
  376.3 4.0 convolution_convert_fusion.6.da_ref
  380.3 33.1 %attend_back.1 = (bf16[1024,256]{1,0:T(8,128)(2,1)S(1)}, bf16[2,8,512,128]{3,2,1,0:T(8,128)(2,1)S(1)}) custom-call(s32[128]{0:T(128)S(1)} %and_select_fusion.key_runs, s32[16]{0:T(128)S(1)} %and_select_fusion.1.runs.query_runs, bf16[1024,256]{1,0:T(8,128)(2,1)S(1)} %get-tuple-element.44.q_ref, bf16[2,8,512,128]{3,2,1,0:T(8,128)(2,1)S(1)} %copy-done.8, ...), custom_call_target="tpu_custom_call" | custom-call | tf_op jit(solution)/shard_map/attend_back/pallas_call | solution.py:772
  413.4 1.3 convolution_convert_fusion.5.gwo
  414.8 69.9 %sum_key_grads.1 = (f32[512,128]{1,0:T(8,128)S(1)}, f32[256,2048]{1,0:T(8,128)S(1)}) custom-call(bf16[2,8,512,128]{3,2,1,0:T(8,128)(2,1)S(1)} %get-tuple-element.56.dkv, bf16[2048,256]{1,0:T(8,128)(2,1)S(1)} %convolution_convert_fusion.5.gwo), custom_call_target="tpu_custom_call" | custom-call | tf_op jit(solution)/shard_map/sum_key_grads/pallas_call | solution.py:1069
  486.1 6.5 %project_back.1 = (bf16[1024,2048]{1,0:T(8,128)(2,1)S(1)}, bf16[320,2048]{1,0:T(8,128)(2,1)S(1)}) custom-call(s32[16]{0:T(128)S(1)} %and_select_fusion.1.runs.query_runs, s32[1]{0:T(128)} %bitcast.2.core, bf16[1024,256]{1,0:T(8,128)(2,1)S(1)} %get-tuple-element.55.dq_ref, f32[512,128]{1,0:T(8,128)S(1)} %get-tuple-element.57.dkv_ref, ...), custom_call_target="tpu_custom_call" | custom-call | tf_op jit(solution)/shard_map/project_back/pallas_call | solution.py:475
  492.6 2.0 copy-done.9
  494.6 51.0 %closing.1 = (f32[128,2048]{1,0:T(8,128)S(1)}, f32[8,256]{1,0:T(8,128)S(1)}, f32[320,2048]{1,0:T(8,128)}) custom-call(bf16[8,128,2048]{2,1,0:T(8,128)(2,1)} %bitcast.76, bf16[320,2048]{1,0:T(8,128)(2,1)S(1)} %get-tuple-element.59.gwq, bf16[128,2048]{1,0:T(8,128)(2,1)S(1)} %bitcast.73, f32[1,2048]{1,0:T(1,128)S(1)} %bitcast.87, f32[128,2048]{1,0:T(8,128)S(1)} %copy-done.20, ...), custom_call_target="tpu_custom_call" | custom-call | tf_op jit(solution)/shard_map/closing/pallas_call | solution.py:1187
  546.2 2.1 fusion.11
  548.5 3.2 maximum_convert_fusion.1
  551.7 6.4 %copy.48 = f32[2048,704]{0,1:T(8,128)} copy(f32[2048,704]{1,0:T(8,128)} %maximum_convert_fusion.1) | data formatting | bytes 11534336
  558.0 4.8 slice_bitcast_fusion.1
  562.8 4.6 copy.44
  567.4 7.4 %stack_reshape.6 = bf16[1,704,2048]{2,1,0:T(8,128)(2,1)} reshape(bf16[704,4,2,2,128]{4,3,2,1,0:T(2,128)(2,1)} %copy.44) | data formatting | bytes 5767168 | tf_op jit(solution)/shard_map/stack;reshape | solution.py:1325
  574.9 5.6 copy.45
  580.4 5.8 stack_reshape.7
  586.2 7.9 %maximum_convert_fusion = f32[2,704,2048]{2,1,0:T(8,128)} fusion(bf16[1,704,2048]{2,1,0:T(8,128)(2,1)} %stack_reshape.7, bf16[1,704,2048]{2,1,0:T(8,128)(2,1)} %stack_reshape.6), kind=kLoop, calls=%fused_computation.1 | loop fusion | flops 5767168 | bytes 17301504 | tf_op jit(solution)/shard_map/convert_element_type | solution.py:1325
  596.5 1.5 copy.57
  (132 shorter events, 21.7 us)
Async XLA Ops:
  7.2 1.8 copy-start
  7.2 215.6 %all-gather.9.cloned.1.call-start = ((), (), s32[]{:S(2)}) async-start(), calls=%async_computation.1 | async-start | bytes 3604480 | tf_op jit(solution)/shard_map/all_gather | solution.py:1251
  9.1 38.7 %copy-start.36 = (bf16[2048]{0:T(1024)(128)(2,1)S(1)}, bf16[2048]{0:T(1024)(128)(2,1)}, u32[]{:S(2)}) copy-start(bf16[2048]{0:T(1024)(128)(2,1)} %param.12) | copy-start | bytes 12292
  9.1 38.7 %copy-start.37 = (bf16[2048]{0:T(1024)(128)(2,1)S(1)}, bf16[2048]{0:T(1024)(128)(2,1)}, u32[]{:S(2)}) copy-start(bf16[2048]{0:T(1024)(128)(2,1)} %param.15) | copy-start | bytes 12292
  9.1 38.7 %copy-start.5 = (bf16[1,128,2048]{2,1,0:T(8,128)(2,1)S(1)}, bf16[1,128,2048]{2,1,0:T(8,128)(2,1)}, u32[]{:S(2)}) copy-start(bf16[1,128,2048]{2,1,0:T(8,128)(2,1)} %param.10) | copy-start | bytes 1572868
  9.1 14.0 %collective-permute-start.1 = (bf16[512,704]{0,1:T(8,128)(2,1)S(1)}, bf16[512,704]{0,1:T(8,128)(2,1)S(1)}, u32[]{:S(2)}, u32[]{:S(2)}) collective-permute-start(bf16[512,704]{0,1:T(8,128)(2,1)S(1)} %constant_dynamic-slice_fusion), channel_id=1, source_target_pairs={{0,0},{1,24},{2,2},{3,26},{4,4},{5,28},{6,6},{7,30},{8,17},{9,9},{... | collective-permute-start | bytes 2162696 | tf_op jit(solution)/shard_map/ppermute | solution.py:1250
  24.0 206.6 %all-gather.7.cloned.1.call-start = ((), (), s32[]{:S(2)}) async-start(), calls=%async_computation | async-start | bytes 7208960 | tf_op jit(solution)/shard_map/all_gather | solution.py:1251
  24.1 24.1 %copy-start.38 = (s32[1,128]{1,0:T(1,128)S(1)}, s32[1,128]{1,0:T(1,128)}, u32[]{:S(2)}) copy-start(s32[1,128]{1,0:T(1,128)} %param.11) | copy-start | bytes 1540
  25.6 60.0 %copy-start.4 = (f32[2048,128]{1,0:T(8,128)S(1)}, f32[2048,128]{1,0:T(8,128)}, u32[]{:S(2)}) copy-start(f32[2048,128]{1,0:T(8,128)} %constant.56.clone.table_ref) | copy-start | bytes 3145732
  25.6 22.1 %collective-permute-start = (bf16[352,2048]{1,0:T(8,128)(2,1)S(1)}, bf16[352,2048]{1,0:T(8,128)(2,1)}, u32[]{:S(2)}, u32[]{:S(2)}) collective-permute-start(bf16[352,2048]{1,0:T(8,128)(2,1)S(1)} %constant_dynamic-slice_fusion.1), channel_id=1, source_target_pairs={{0,0},{1,24},{2,2},{3,26},{4,4},{5,28},{6,6},{7,30},{8,17},{9,9},{... | collective-permute-start | bytes 4325384 | tf_op jit(solution)/shard_map/ppermute | solution.py:1250
  47.7 498.5 %all-gather.13.cloned.1.call-start = ((), (), s32[]{:S(2)}) async-start(), calls=%async_computation.3 | async-start | bytes 3342336 | tf_op jit(solution)/shard_map/all_gather | solution.py:1256
  48.2 1.3 copy-start.16
  85.5 2.2 copy-start.2
  87.8 4.5 copy-start.10
  87.8 4.5 copy-start.23
  135.6 1.3 copy-start.6
  142.5 1.6 copy-start.7
  144.1 22.8 %copy-start.18 = (bf16[8,256,256]{2,1,0:T(8,128)(2,1)S(1)}, bf16[8,256,256]{2,1,0:T(8,128)(2,1)}, u32[]{:S(2)}) copy-start(bf16[8,256,256]{2,1,0:T(8,128)(2,1)} %copy-done.17) | copy-start | bytes 3145732
  166.8 3.3 copy-start.14
  166.8 3.3 copy-start.24
  220.7 2.0 copy-start.31
  230.6 6.0 copy-start.32
  230.6 6.0 copy-start.39
  230.6 6.8 %copy-start.43 = (f32[1024,704]{0,1:T(8,128)S(1)}, f32[1024,704]{0,1:T(8,128)}, u32[]{:S(2)}) copy-start(f32[1024,704]{0,1:T(8,128)} %fusion.13) | copy-start | bytes 8650756
  237.4 7.0 %copy-start.41 = (bf16[8,128,2048]{2,1,0:T(8,128)(2,1)S(1)}, bf16[8,128,2048]{2,1,0:T(8,128)(2,1)}, u32[]{:S(2)}) copy-start(bf16[8,128,2048]{2,1,0:T(8,128)(2,1)} %get-tuple-element.49) | copy-start | bytes 12582916
  253.6 7.5 %copy-start.33 = (bf16[8,128,2048]{2,1,0:T(8,128)(2,1)S(1)}, bf16[8,128,2048]{2,1,0:T(8,128)(2,1)}, u32[]{:S(2)}) copy-start(bf16[8,128,2048]{2,1,0:T(8,128)(2,1)} %copy-done.31) | copy-start | bytes 12582916
  253.6 7.5 %copy-start.44 = (bf16[1024,704]{0,1:T(8,128)(2,1)S(1)}, bf16[1024,704]{0,1:T(8,128)(2,1)}, u32[]{:S(2)}) copy-start(bf16[1024,704]{0,1:T(8,128)(2,1)} %get-tuple-element.97) | copy-start | bytes 4325380
  261.2 4.6 copy-start.42
  261.2 4.6 copy-start.47
  261.2 9.7 %slice-start = ((s8[5767168]{0:T(1024)(128)(4,1)}), s8[4194304]{0:T(1024)(128)(4,1)S(1)}, s32[]{:S(2)}) async-start(s8[5767168]{0:T(1024)(128)(4,1)} %bitcast.106), calls=%async_computation.4 | async-start | bytes 8388608
  265.8 5.0 slice-start.1
  270.8 3.5 copy-start.45
  274.4 5.7 copy-start.11
  274.4 5.7 copy-start.22
  355.1 8.6 %collective-permute-start.3 = (bf16[2,64,704]{2,1,0:T(8,128)(2,1)S(1)}, bf16[2,64,704]{2,1,0:T(8,128)(2,1)}, u32[]{:S(2)}, u32[]{:S(2)}) collective-permute-start(bf16[2,64,704]{2,1,0:T(8,128)(2,1)S(1)} %pad_maximum_fusion.1), channel_id=1, source_target_pairs={{0,0},{1,8},{2,2},{3,10},{4,4},{5,12},{6,6},{7,14},{8,1},{9,9},{10... | collective-permute-start | bytes 540680 | tf_op jit(solution)/shard_map/ppermute | solution.py:1255
  363.8 194.3 %all-gather.11.cloned.1.call-start = ((), (), s32[]{:S(2)}) async-start(), calls=%async_computation.2 | async-start | bytes 6127616 | tf_op jit(solution)/shard_map/all_gather | solution.py:1256
  364.9 11.4 %collective-permute-start.2 = (bf16[2,704,128]{2,1,0:T(8,128)(2,1)S(1)}, bf16[2,704,128]{2,1,0:T(8,128)(2,1)}, u32[]{:S(2)}, u32[]{:S(2)}) collective-permute-start(bf16[2,704,128]{2,1,0:T(8,128)(2,1)S(1)} %pad_maximum_fusion), channel_id=1, source_target_pairs={{0,0},{1,8},{2,2},{3,10},{4,4},{5,12},{6,6},{7,14},{8,1},{9,9},{10... | collective-permute-start | bytes 1081352 | tf_op jit(solution)/shard_map/ppermute | solution.py:1255
  376.3 4.0 copy-start.8
  376.3 4.0 copy-start.25
  380.2 33.2 %copy-start.15 = (bf16[1024,256]{1,0:T(8,128)(2,1)S(1)}, bf16[1024,256]{1,0:T(8,128)(2,1)}, u32[]{:S(2)}) copy-start(bf16[1024,256]{1,0:T(8,128)(2,1)} %copy-done.14) | copy-start | bytes 1572868
  380.2 33.2 %copy-start.40 = (bf16[8,128,2048]{2,1,0:T(8,128)(2,1)S(1)}, bf16[8,128,2048]{2,1,0:T(8,128)(2,1)}, u32[]{:S(2)}) copy-start(bf16[8,128,2048]{2,1,0:T(8,128)(2,1)} %get-tuple-element.52) | copy-start | bytes 12582916
  413.4 72.6 %copy-start.3 = (bf16[8,128,2048]{2,1,0:T(8,128)(2,1)S(1)}, bf16[8,128,2048]{2,1,0:T(8,128)(2,1)}, u32[]{:S(2)}) copy-start(bf16[8,128,2048]{2,1,0:T(8,128)(2,1)} %get-tuple-element.40) | copy-start | bytes 12582916
  486.1 8.5 %copy-start.20 = (f32[128,2048]{1,0:T(8,128)S(1)}, f32[128,2048]{1,0:T(8,128)}, u32[]{:S(2)}) copy-start(f32[128,2048]{1,0:T(8,128)} %copy-done.19) | copy-start | bytes 3145732
  492.6 2.0 copy-start.9
  586.2 7.9 %copy-start.27 = (bf16[128,2048]{1,0:T(8,128)(2,1)S(1)}, bf16[128,2048]{1,0:T(8,128)(2,1)}, u32[]{:S(2)}) copy-start(bf16[128,2048]{1,0:T(8,128)(2,1)} %copy-done.26) | copy-start | bytes 1572868
  594.2 2.3 copy-start.34
  596.5 2.5 copy-start.13
  596.5 3.9 copy-start.1
  (10 other events, 9.1 us)
Sparse Core Ops, SparseCore 0:
  24.1 39.4 all-gather.8
  65.3 75.6 all-gather.6
  363.9 35.3 all-gather.12
  400.8 85.5 all-gather.10

commit v3 on v2

--- a/solution.py
+++ b/solution.py
@@ -61,6 +61,11 @@
             d.start()
         return d
 
+    def sent(self, copies):
+        for d in copies:
+            d.wait_send()
+        self.started = [d for d in self.started if all(d is not e for e in copies)]
+
     def finish(self):
         for d in self.started:
             d.wait_send()
@@ -114,56 +119,77 @@
         self.pass_core(-1, self.a)
         self.pass_core(1, self.b)
 
-    def rest(self):
+    def near(self):
         self.up_b.wait_recv()
         self.pass_core(-1, self.b)
         self.down_a.wait_recv()
         self.pass_core(1, self.a)
+
+    def far(self):
         self.on_a.wait_recv()
         self.pass_core(2, self.a)
         self.on_b.wait_recv()
         self.pass_core(2, self.b)
-        for d in self.to_core:
+
+    def from_core(self, first, last):
+        for d in self.to_core[first:last]:
             d.wait_recv()
 
+    def rest(self):
+        self.near()
+        self.far()
+        self.from_core(0, 7)
+
 
 GATHER_EDGES = 13
 
 
 class RingScatter:
-    def __init__(self, me, edges, parts, got, both, relayed, last):
+    def __init__(self, me, edges, parts, scratch):
         self.me, self.edges, self.parts = me, edges, parts
-        self.got, self.both, self.relayed, self.last = got, both, relayed, last
+        self.got, self.both, self.relayed, self.last = scratch
         self.up, self.down = me.at(dy=1), me.at(dy=-1)
-        self.from_core = {}
+        self.cores = {}
+        self.a, self.b = pl.ds(0, HALF), pl.ds(HALF, HALF)
+
+    def send_core(self, k):
+        row = 2 * lax.rem(self.me.y + k, 4) + 1 - self.me.c
+        core = self.me.at(core=1 - self.me.c)
+        self.cores[k] = self.edges.copy(self.parts.at[row], self.got.at[k], core)
+
+    def add_core(self, k):
+        self.cores[k].wait_recv()
+        row = 2 * lax.rem(self.me.y + k, 4) + self.me.c
+
+        def add(at):
+            self.both[k, at] = (
+                self.parts[row, at].astype(F32) + self.got[k, at].astype(F32)
+            ).astype(BF16)
+
+        in_chunks(add)
+
+    def far(self):
+        self.add_core(2)
+        e, both = self.edges, self.both
+        self.r_a = e.copy(both.at[2, self.a], self.relayed.at[0], self.up)
+        self.r_b = e.copy(both.at[2, self.b], self.relayed.at[1], self.down)
+
+    def near(self):
+        e, both = self.edges, self.both
+        self.add_core(1)
+        self.u_b = e.copy(both.at[1, self.b], self.last.at[0, self.b], self.up)
+        self.add_core(3)
+        self.d_a = e.copy(both.at[3, self.a], self.last.at[1, self.a], self.down)
+
+    def first(self):
         for k in (2, 1, 3, 0):
-            row = 2 * lax.rem(me.y + k, 4) + 1 - me.c
-            self.from_core[k] = edges.copy(
-                parts.at[row], got.at[k], me.at(core=1 - me.c)
-            )
-
-    def add_core(self, k):
-        self.from_core[k].wait_recv()
-        row = 2 * lax.rem(self.me.y + k, 4) + self.me.c
-        self.both[k] = (
-            self.parts[row].astype(F32) + self.got[k].astype(F32)
-        ).astype(BF16)
-
-    def first(self):
-        a, b = pl.ds(0, HALF), pl.ds(HALF, HALF)
-        e, both = self.edges, self.both
-        self.add_core(2)
-        self.r_a = e.copy(both.at[2, a], self.relayed.at[0], self.up)
-        self.r_b = e.copy(both.at[2, b], self.relayed.at[1], self.down)
-        self.add_core(1)
-        self.u_b = e.copy(both.at[1, b], self.last.at[0, b], self.up)
-        self.add_core(3)
-        self.d_a = e.copy(both.at[3, a], self.last.at[1, a], self.down)
+            self.send_core(k)
+        self.far()
+        self.near()
         self.add_core(0)
 
     def second(self):
-        a, b = pl.ds(0, HALF), pl.ds(HALF, HALF)
-        e, both = self.edges, self.both
+        a, b, e, both = self.a, self.b, self.edges, self.both
         self.r_a.wait_recv()
         both[1, a] = (both[1, a].astype(F32) + self.relayed[0].astype(F32)).astype(BF16)
         self.u_a = e.copy(both.at[1, a], self.last.at[0, a], self.up)
@@ -171,14 +197,20 @@
         both[3, b] = (both[3, b].astype(F32) + self.relayed[1].astype(F32)).astype(BF16)
         self.d_b = e.copy(both.at[3, b], self.last.at[1, b], self.down)
 
-    def total(self, out):
+    def arrived(self):
         for d in (self.u_b, self.d_a, self.u_a, self.d_b):
             d.wait_recv()
-        out[...] = (
-            self.both[0].astype(F32)
-            + self.last[0].astype(F32)
-            + self.last[1].astype(F32)
+
+    def rows(self, at):
+        return (
+            self.both[0, at].astype(F32)
+            + self.last[0, at].astype(F32)
+            + self.last[1, at].astype(F32)
         )
+
+    def release(self):
+        ring = [self.r_a, self.r_b, self.u_b, self.d_a, self.u_a, self.d_b]
+        self.edges.sent(ring + list(self.cores.values()))
 
 
 SCATTER_EDGES = 10
@@ -321,7 +353,9 @@
             wait_sent(src, sem, stays)
 
 
-def opening_kernel(x, pos, wqkv, xs, poss, wq, send, recv, qs, qr, local):
+def opening_kernel(
+    x, pos, wqkv, wgu, wdn, xs, poss, wq, wswap, send, recv, qs, qr, ws, wr, local
+):
     me = Place()
     partner = {"xl": 1 - me.xl, "xh": 1 - me.xh}
     members = group_members(me)
@@ -353,8 +387,21 @@
             me, src, wq.at[slot], qs.at[i], qr.at[slot], (me.z, to_xl, core, y, to_xh), stays
         )
         blocks.append((src, qs.at[i], stays))
+    swaps = swap_copies(me, wgu, wdn, wswap, ws, wr)
+
+    @pl.when(me.c != me.xh)
+    def _():
+        for d in swaps:
+            d.start()
+
     ring.relay()
     ring.rest()
+
+    @pl.when(me.c != me.xh)
+    def _():
+        for d in swaps:
+            d.wait()
+
     for d in pos_copies:
         d.wait_recv()
     for i in range(5):
@@ -366,20 +413,48 @@
     keep_pos.wait()
 
 
-def opening(x, pos, wqkv):
+GU_QUARTER = 2 * FF_DEV // 4
+DN_QUARTER = FF_DEV // 4
+QUARTER = GU_QUARTER + DN_QUARTER
+
+
+def swap_copies(me, wgu, wdn, wswap, send, recv):
+    found = []
+    across = me.at(core=1 - me.c, xl=1 - me.xl, xh=1 - me.xh)
+    for i, (src, rows, start) in enumerate(
+        ((wgu, GU_QUARTER, 0), (wdn, DN_QUARTER, GU_QUARTER))
+    ):
+        found.append(
+            pltpu.make_async_remote_copy(
+                src_ref=src.at[pl.ds(pl.multiple_of(rows * me.z, 16), rows)],
+                dst_ref=wswap.at[pl.ds(start, rows)],
+                send_sem=send.at[i],
+                recv_sem=recv.at[i],
+                device_id=across,
+                device_id_type=pl.DeviceIdType.MESH,
+            )
+        )
+    return found
+
+
+def opening(x, pos, wqkv, wgu, wdn):
     return pl.pallas_call(
         opening_kernel,
         out_shape=(
             shape((8, TOK, D)),
             shape((8, 8, TOK), jnp.int32),
             shape((5, 64, D)),
+            shape((QUARTER, D)),
         ),
-        in_specs=[ANY] * 3,
-        out_specs=(ANY,) * 3,
-        scratch_shapes=sems(7 + GATHER_EDGES) + sems(5) + [pltpu.SemaphoreType.DMA((2,))],
+        in_specs=[ANY] * 5,
+        out_specs=(ANY,) * 4,
+        scratch_shapes=sems(7 + GATHER_EDGES)
+        + sems(5)
+        + sems(2)
+        + [pltpu.SemaphoreType.DMA((2,))],
         compiler_params=remote_params(0),
         name="opening",
-    )(x, pos, wqkv)
+    )(x, pos, wqkv, wgu, wdn)
 
 
 def rotary_table():
@@ -501,7 +576,7 @@
 
 
 def keys_kernel(
-    kv, pos, cot, wout, kvs, poss, cots, wo, send, recv, os_, orr, local
+    kv, pos, cot, wout, wswap, kvs, poss, cots, wo, wnear, send, recv, os_, orr, ws, wr, local
 ):
     me = Place()
     partner = {"xl": 1 - me.xl, "xh": 1 - me.xh}
@@ -512,9 +587,21 @@
     others = [
         me.at(y=lax.rem(me.y + dy, 4), core=c, **partner) for dy in range(4) for c in (0, 1)
     ]
+    depth = [me.at(dz=1), me.at(dz=-1)]
     greet(far + group_members(me) + others)
     edges = Edges(send, recv)
     chip = 2 * me.z + me.xl
+    steps = [
+        pltpu.make_async_remote_copy(
+            src_ref=wswap,
+            dst_ref=wnear.at[i],
+            send_sem=ws.at[i],
+            recv_sem=wr.at[i],
+            device_id=depth[i],
+            device_id_type=pl.DeviceIdType.MESH,
+        )
+        for i in range(2)
+    ]
     keeps = [
         pltpu.make_async_copy(kv, kvs.at[me.c, chip], local.at[0]),
         pltpu.make_async_copy(pos, poss.at[chip], local.at[1]),
@@ -541,6 +628,12 @@
         target = (me.z, to_xl, to_core, y, to_xh)
         send_block(me, src, wo.at[own], os_.at[i], orr.at[own], target, stays)
         blocks.append((src, os_.at[i], stays))
+
+    @pl.when(me.c != me.xh)
+    def _():
+        for d in steps:
+            d.start()
+
     ring.relay()
     for (dz, dl), d in zip(chips_in_sequence(me), kv_copies):
         d.wait_recv()
@@ -554,12 +647,18 @@
         wait_got(wo.at[i], orr.at[i])
     for src, sem, stays in blocks:
         wait_sent(src, sem, stays)
+
+    @pl.when(me.c != me.xh)
+    def _():
+        for d in steps:
+            d.wait()
+
     edges.finish()
     for d in keeps:
         d.wait()
 
 
-def exchange_keys(kv, pos, cot, wout):
+def exchange_keys(kv, pos, cot, wout, wswap):
     return pl.pallas_call(
         keys_kernel,
         out_shape=(
@@ -567,15 +666,17 @@
             shape((8, 8, 8, TOK), jnp.int32),
             shape((8, TOK, D)),
             shape((8, 256, Q_DEV)),
+            shape((2, QUARTER, D)),
         ),
-        in_specs=[ANY] * 4,
-        out_specs=(ANY,) * 4,
+        in_specs=[ANY] * 5,
+        out_specs=(ANY,) * 5,
         scratch_shapes=sems(7 + 7 + 8 + GATHER_EDGES)
         + sems(8)
+        + sems(2)
         + [pltpu.SemaphoreType.DMA((3,))],
         compiler_params=remote_params(1),
         name="exchange_keys",
-    )(kv, pos, cot, wout)
+    )(kv, pos, cot, wout, wswap)
 
 
 def split_heads(rows):
@@ -815,234 +916,407 @@
     return jnp.mean(rows, axis=-1, keepdims=True)
 
 
-def middle_kernel(
-    parts, tokens, gain, middle, xs, got, both, relayed, last, total, low, send, recv, local
+PART = 3 * FF_DEV // 2
+PART_HALF = PART // 2
+
+
+class RingSum:
+    def __init__(self, me, edges, along_z, src, start, width, step, relayed, last):
+        self.edges, self.src, self.start, self.width, self.step = edges, src, start, width, step
+        self.relayed, self.last = relayed, last
+        self.here = me.z if along_z else x_of(me)
+        self.up = around(me, 1, 0) if along_z else around(me, 0, 1)
+        self.down = around(me, -1, 0) if along_z else around(me, 0, 3)
+        self.a, self.b = pl.ds(0, PART_HALF), pl.ds(PART_HALF, PART_HALF)
+
+    def columns(self, k):
+        at = self.width * lax.rem(self.here + k, 4)
+        return pl.ds(pl.multiple_of(at, self.width), self.width)
+
+    def piece(self, k, half):
+        rows = pl.ds(self.start + PART_HALF * half, PART_HALF)
+        return self.src.at[rows, self.columns(k)]
+
+    def far(self):
+        self.r_a = self.edges.copy(self.piece(2, 0), self.relayed.at[0], self.up)
+        self.r_b = self.edges.copy(self.piece(2, 1), self.relayed.at[1], self.down)
+
+    def near_up(self):
+        self.u_b = self.edges.copy(self.piece(1, 1), self.last.at[0, self.b], self.up)
+
+    def near_down(self):
+        self.d_a = self.edges.copy(self.piece(3, 0), self.last.at[1, self.a], self.down)
+
+    def add(self, k, half):
+        step, start, cols = self.step, self.start + PART_HALF * half, self.columns(k)
+
+        def one(i, _):
+            at = pl.ds(pl.multiple_of(start + i * step, 16), step)
+            from_ = pl.ds(pl.multiple_of(i * step, 16), step)
+            self.src[at, cols] = (
+                self.src[at, cols].astype(F32) + self.relayed[half, from_, :].astype(F32)
+            ).astype(BF16)
+            return 0
+
+        lax.fori_loop(0, PART_HALF // step, one, 0)
+
+    def second(self):
+        self.r_a.wait_recv()
+        self.add(1, 0)
+        self.u_a = self.edges.copy(self.piece(1, 0), self.last.at[0, self.a], self.up)
+        self.r_b.wait_recv()
+        self.add(3, 1)
+        self.d_b = self.edges.copy(self.piece(3, 1), self.last.at[1, self.b], self.down)
+
+    def total(self, out):
+        for d in (self.u_b, self.d_a, self.u_a, self.d_b):
+            d.wait_recv()
+        step, cols = self.step, self.columns(0)
+
+        def one(i, _):
+            at = pl.ds(pl.multiple_of(self.start + i * step, 16), step)
+            from_ = pl.ds(pl.multiple_of(i * step, 16), step)
+            out[from_, :] = (
+                self.src[at, cols].astype(F32)
+                + self.last[0, from_, :].astype(F32)
+                + self.last[1, from_, :].astype(F32)
+            ).astype(BF16)
+            return 0
+
+        lax.fori_loop(0, PART // step, one, 0)
+
+
+SUM_EDGES = 6
+
+
+def feed_forward_kernel(
+    parts, tokens, gain, cots, wgu, wdn, wswap, wnear,
+    output, grad_middle, gain_grad, gbs, z_out, x_out,
+    xs, p, c, gp, w, act_t, gate_t, up_t, act, dgate, dup, middle, low,
+    g1, b1, r1, l1, g2, b2, r2, l2,
+    z_relayed, z_last, x_relayed, x_last, z_q, x_q,
+    z_relayed2, z_last2, x_relayed2, x_last2,
+    send, recv, fs, fr, local,
 ):
     me = Place()
-    greet([me.at(core=1 - me.c), me.at(dy=1), me.at(dy=-1)])
+    core = me.at(core=1 - me.c)
+    greet(
+        [core, me.at(dy=1), me.at(dy=-1)]
+        + [around(me, k, 0) for k in (1, 2, 3)]
+        + [around(me, 0, 1), around(me, 0, 3)]
+    )
     edges = Edges(send, recv)
-    ring = RingScatter(me, edges, parts, got, both, relayed, last)
+    mine = 2 * me.y + me.c
+    moved = me.c != me.xh
+    load_p = pltpu.make_async_copy(parts, p, local.at[0])
+    load_c = pltpu.make_async_copy(cots, c, local.at[1])
+    load_p.start()
+    load_c.start()
+
+    def w_rows(dz):
+        z = lax.rem(me.z + dz + 4, 4)
+        return (
+            pl.ds(pl.multiple_of(GU_QUARTER * z, 16), GU_QUARTER),
+            pl.ds(pl.multiple_of(2 * FF_DEV + DN_QUARTER * z, 16), DN_QUARTER),
+        )
+
+    gu_part, dn_part = pl.ds(0, GU_QUARTER), pl.ds(GU_QUARTER, DN_QUARTER)
+    kept = [
+        pltpu.make_async_copy(wgu, w.at[pl.ds(0, 2 * FF_DEV)], local.at[2]),
+        pltpu.make_async_copy(wdn, w.at[pl.ds(2 * FF_DEV, FF_DEV)], local.at[3]),
+    ]
+    near_w = []
+    for i, (src, dz) in enumerate(((wswap, 0), (wnear.at[0], -1), (wnear.at[1], 1))):
+        gu_rows, dn_rows = w_rows(dz)
+        near_w.append(pltpu.make_async_copy(src.at[gu_part], w.at[gu_rows], local.at[4 + 2 * i]))
+        near_w.append(pltpu.make_async_copy(src.at[dn_part], w.at[dn_rows], local.at[5 + 2 * i]))
+    far_w = [
+        pltpu.make_async_remote_copy(
+            src_ref=wswap.at[part],
+            dst_ref=w.at[rows],
+            send_sem=fs.at[i],
+            recv_sem=fr.at[i],
+            device_id=me.at(dz=2),
+            device_id_type=pl.DeviceIdType.MESH,
+        )
+        for i, (part, rows) in enumerate(zip((gu_part, dn_part), w_rows(0)))
+    ]
+
+    @pl.when(moved)
+    def _():
+        for d in far_w + near_w:
+            d.start()
+
+    @pl.when(jnp.logical_not(moved))
+    def _():
+        for d in kept:
+            d.start()
+
+    load_p.wait()
+    ring = RingScatter(me, edges, p, (g1, b1, r1, l1))
     ring.first()
     ring.second()
-    ring.total(total)
+    ring.arrived()
 
     def norm(at):
-        rows = tokens[at, :].astype(F32) + total[at, :]
+        rows = tokens[at, :].astype(F32) + ring.rows(at)
         middle[at, :] = rows
         normal = rows * lax.rsqrt(mean_last(rows * rows) + EPSILON)
         low[at, :] = (normal * gain[...]).astype(BF16)
 
     in_chunks(norm)
-    keep = pltpu.make_async_copy(low, xs.at[2 * me.y + me.c], local)
+    keep = pltpu.make_async_copy(low, xs.at[mine], local.at[10])
     keep.start()
     gather = RingGather(me, edges, low, xs)
+    ring.release()
+
+    @pl.when(moved)
+    def _():
+        for d in near_w:
+            d.wait()
+        for d in far_w:
+            d.wait()
+
+    @pl.when(jnp.logical_not(moved))
+    def _():
+        for d in kept:
+            d.wait()
+
+    load_c.wait()
+    keep.wait()
+
+    def compute(pair):
+        at = pl.ds(2 * pair, 2)
+        x = xs[at].reshape(2 * TOK, D)
+        g = c[at].reshape(2 * TOK, D)
+        here = pl.ds(pl.multiple_of(2 * TOK * pair, 2 * TOK), 2 * TOK)
+        for n0, n1 in ((0, 256), (256, 512), (512, FF_DEV)):
+            gate = dot_last(x, w[n0:n1, :])
+            upward = dot_last(x, w[FF_DEV + n0 : FF_DEV + n1, :])
+            grad = dot_last(g, w[2 * FF_DEV + n0 : 2 * FF_DEV + n1, :])
+            sigmoid = 1.0 / (1.0 + jnp.exp(-gate))
+            swish = gate * sigmoid
+            active = swish * upward
+            grad_up = grad * swish
+            grad_gate = grad * upward * sigmoid * (1.0 + gate * (1.0 - sigmoid))
+            act[:, n0:n1] = active.astype(BF16)
+            dup[:, n0:n1] = grad_up.astype(BF16)
+            dgate[:, n0:n1] = grad_gate.astype(BF16)
+            act_t[n0:n1, here] = active.T.astype(BF16)
+            up_t[n0:n1, here] = grad_up.T.astype(BF16)
+            gate_t[n0:n1, here] = grad_gate.T.astype(BF16)
+
+        def block(i, _):
+            cols = pl.ds(pl.multiple_of(512 * i, 512), 512)
+            branch = dot(act[...], w[2 * FF_DEV :, cols])
+            p[at, :, cols] = branch.astype(BF16).reshape(2, TOK, 512)
+            grads = dot(dgate[...], w[:FF_DEV, cols]) + dot(dup[...], w[FF_DEV : 2 * FF_DEV, cols])
+            gp[at, :, cols] = grads.astype(BF16).reshape(2, TOK, 512)
+            return 0
+
+        lax.fori_loop(0, 4, block, 0)
+
+    def pair(k):
+        return lax.rem(me.y + k, 4)
+
+    two = RingScatter(me, edges, gp, (g1, b1, r1, l1))
+    gather.from_core(0, 1)
+    compute(pair(0))
+    two.send_core(0)
     gather.relay()
-    gather.rest()
-    edges.finish()
-    keep.wait()
-
-
-def to_middle(parts, tokens, gain):
-    return pl.pallas_call(
-        middle_kernel,
-        out_shape=(shape((TOK, D), F32), shape((8, TOK, D))),
-        in_specs=[VMEM] * 3,
-        out_specs=(VMEM, ANY),
-        scratch_shapes=scatter_scratch()
-        + [pltpu.VMEM((TOK, D), F32), pltpu.VMEM((TOK, D), BF16)]
-        + sems(SCATTER_EDGES + GATHER_EDGES)
-        + [pltpu.SemaphoreType.DMA],
-        compiler_params=remote_params(2),
-        name="to_middle",
-    )(parts, tokens, gain)
-
-
-class SumOfFour:
-    def __init__(self, me, along_z, src, piece, own, got, send, recv, local):
-        self.src, self.piece, self.own, self.got = src, piece, own, got
-        self.send, self.recv = send, recv
-        here = me.z if along_z else x_of(me)
-        self.keep = pltpu.make_async_copy(src.at[piece(here)], own, local)
-        self.keep.start()
-        for k in (1, 2, 3):
-            device = around(me, k, 0) if along_z else around(me, 0, k)
-            pltpu.make_async_remote_copy(
-                src_ref=src.at[piece(lax.rem(here + k, 4))],
-                dst_ref=got.at[k - 1],
-                send_sem=send.at[k - 1],
-                recv_sem=recv,
-                device_id=device,
-                device_id_type=pl.DeviceIdType.MESH,
-            ).start()
-
-    def total(self, out, rows):
-        self.keep.wait()
-        pltpu.make_async_copy(self.got, self.got, self.recv).wait()
-        own, got = self.own, self.got
-
-        def one(i, _):
-            at = pl.ds(pl.multiple_of(i * rows, rows), rows)
-            total = own[at, :].astype(F32)
-            for k in range(3):
-                total = total + got[k, at, :].astype(F32)
-            out[at, :] = total.astype(BF16)
-            return 0
-
-        lax.fori_loop(0, out.shape[0] // rows, one, 0)
-
-    def finish(self):
-        for k in range(3):
-            src = self.src.at[self.piece(0)]
-            pltpu.make_async_copy(src, src, self.send.at[k]).wait()
-
-
-def columns(width):
-    return lambda i: (slice(None), pl.ds(pl.multiple_of(i * width, width), width))
-
-
-def row_block(height, start=0):
-    return lambda i: (pl.ds(pl.multiple_of(start + i * height, height), height), slice(None))
-
-
-def mlp_back_kernel(
-    branch_parts, grad_parts, middle, cot, gain, ggate, gup, gdn,
-    output, grad_middle, gain_grad, gbs, gate_out, up_out, top_out, low_out,
-    g1, b1, r1, l1, g2, b2, r2, l2, total, low,
-    gate_own, gate_got, up_own, up_got, top_own, top_got, low_own, low_got,
-    gate_q, up_q, top_q, low_q,
-    gate_own2, gate_got2, up_own2, up_got2, top_own2, top_got2, low_own2, low_got2,
-    send, recv, qs, qr, ql, local,
-):
-    me = Place()
-    greet(
-        [me.at(core=1 - me.c), me.at(dy=1), me.at(dy=-1)]
-        + [around(me, k, 0) for k in (1, 2, 3)]
-        + [around(me, 0, k) for k in (1, 2, 3)]
-    )
-    edges = Edges(send, recv)
-    ring = RingScatter(me, edges, grad_parts, g2, b2, r2, l2)
-
-    def quarter(i, along_z, src, piece, own, got):
-        return SumOfFour(
-            me, along_z, src, piece, own, got, qs.at[i], qr.at[i], ql.at[i]
-        )
-
-    gate_sum = quarter(0, True, ggate, columns(512), gate_own, gate_got)
-    up_sum = quarter(1, False, gup, columns(512), up_own, up_got)
-    top_sum = quarter(2, True, gdn, row_block(256), top_own, top_got)
-    low_sum = quarter(3, False, gdn, row_block(256, 1024), low_own, low_got)
-    ring.first()
-    ring.second()
-    ring.total(total)
+    gather.near()
+    gather.from_core(1, 5)
+
+    def sides(i, _):
+        compute(pair(1 + 2 * i))
+        return 0
+
+    lax.fori_loop(0, 2, sides, 0)
+    two.send_core(1)
+    two.send_core(3)
+    gather.far()
+    two.near()
+    gather.from_core(5, 7)
+    compute(pair(2))
+    two.send_core(2)
+    two.add_core(0)
+
+    z_sum = RingSum(me, edges, True, w, 0, 512, 48, z_relayed, z_last)
+    x_sum = RingSum(me, edges, False, w, PART, 512, 48, x_relayed, x_last)
+    split = PART - FF_DEV
+
+    def z_task(k):
+        cols = z_sum.columns(k)
+        x = xs[:, :, cols].reshape(8 * TOK, 512)
+        w[:FF_DEV, cols] = dot(gate_t[...], x).astype(BF16)
+        w[FF_DEV:PART, cols] = dot(up_t[:split, :], x).astype(BF16)
+
+    def x_task(k):
+        cols = x_sum.columns(k)
+        x = xs[:, :, cols].reshape(8 * TOK, 512)
+        g = c[:, :, cols].reshape(8 * TOK, 512)
+        w[PART : 2 * FF_DEV, cols] = dot(up_t[split:, :], x).astype(BF16)
+        w[2 * FF_DEV :, cols] = dot(act_t[...], g).astype(BF16)
+
+    two.far()
+    z_task(2)
+    z_sum.far()
+    x_task(2)
+    x_sum.far()
+    z_task(1)
+    z_sum.near_up()
+    x_task(1)
+    x_sum.near_up()
+    two.second()
+    z_task(3)
+    z_sum.near_down()
+    x_task(3)
+    x_sum.near_down()
+    z_task(0)
+    x_task(0)
+    two.arrived()
     gain_grad[...] = jnp.zeros_like(gain_grad)
 
     def back(at):
         rows = middle[at, :]
         inverse = lax.rsqrt(mean_last(rows * rows) + EPSILON)
         normal = rows * inverse
-        grad = total[at, :]
+        grad = two.rows(at)
         gain_grad[...] += jnp.sum(normal * grad, axis=0, keepdims=True)
         scaled = grad * gain[...]
-        result = cot[at, :].astype(F32) + inverse * (
+        result = c[mine, at].astype(F32) + inverse * (
             scaled - normal * mean_last(scaled * normal)
         )
         grad_middle[at, :] = result
         low[at, :] = result.astype(BF16)
 
+    edges.sent([gather.up_a, gather.up_b, gather.down_a, gather.down_b, gather.to_core[0]])
     in_chunks(back)
-    keep = pltpu.make_async_copy(low, gbs.at[2 * me.y + me.c], local)
+    keep = pltpu.make_async_copy(low, gbs.at[mine], local.at[10])
     keep.start()
     gather = RingGather(me, edges, low, gbs)
-    branch = RingScatter(me, edges, branch_parts, g1, b1, r1, l1)
+    branch = RingScatter(me, edges, p, (g2, b2, r2, l2))
+    for k in (2, 1, 3, 0):
+        branch.send_core(k)
+    z_sum.second()
+    x_sum.second()
     gather.relay()
-    branch.first()
-    gate_sum.total(gate_q, 64)
-    up_sum.total(up_q, 64)
-    top_sum.total(top_q, 64)
-    low_sum.total(low_q, 64)
+    branch.far()
+    branch.near()
+    branch.add_core(0)
+    z_sum.total(z_q)
+    z_two = RingSum(me, edges, False, z_q, 0, 128, 176, z_relayed2, z_last2)
+    z_two.far()
+    z_two.near_up()
+    z_two.near_down()
+    x_sum.total(x_q)
+    x_two = RingSum(me, edges, True, x_q, 0, 128, 176, x_relayed2, x_last2)
+    x_two.far()
+    x_two.near_up()
+    x_two.near_down()
+    gather.near()
+    gather.far()
     branch.second()
-    gate_two = quarter(4, False, gate_q, columns(128), gate_own2, gate_got2)
-    up_two = quarter(5, True, up_q, columns(128), up_own2, up_got2)
-    top_two = quarter(6, False, top_q, row_block(64), top_own2, top_got2)
-    low_two = quarter(7, True, low_q, row_block(64), low_own2, low_got2)
-    gather.rest()
-    branch.total(total)
+    z_two.second()
+    x_two.second()
+    gather.from_core(0, 7)
+    branch.arrived()
 
     def out(at):
-        output[at, :] = (middle[at, :] + total[at, :]).astype(BF16)
+        output[at, :] = (middle[at, :] + branch.rows(at)).astype(BF16)
 
     in_chunks(out)
-    gate_two.total(gate_out, 64)
-    up_two.total(up_out, 64)
-    top_two.total(top_out, 64)
-    low_two.total(low_out, 64)
-    for d in (gate_sum, up_sum, top_sum, low_sum, gate_two, up_two, top_two, low_two):
-        d.finish()
+    z_two.total(z_out)
+    x_two.total(x_out)
     edges.finish()
     keep.wait()
 
 
-def mlp_back(branch_parts, grad_parts, middle, cot, gain, ggate, gup, gdn):
-    def own_and_got(rows, width):
-        return [pltpu.VMEM((rows, width), BF16), pltpu.VMEM((3, rows, width), BF16)]
+def feed_forward(parts, tokens, gain, cots, wgu, wdn, wswap, wnear):
+    block = pltpu.VMEM((8, TOK, D), BF16)
+    turned = pltpu.VMEM((FF_DEV, 8 * TOK), BF16)
+    pair = pltpu.VMEM((2 * TOK, FF_DEV), BF16)
+
+    def ring(width):
+        return [
+            pltpu.VMEM((2, PART_HALF, width), BF16),
+            pltpu.VMEM((2, PART, width), BF16),
+        ] * 2
 
     return pl.pallas_call(
-        mlp_back_kernel,
+        feed_forward_kernel,
         out_shape=(
             shape((TOK, D)),
             shape((TOK, D), F32),
             shape((1, D), F32),
             shape((8, TOK, D)),
-            shape((FF_DEV, 128)),
-            shape((FF_DEV, 128)),
-            shape((64, FF_DEV)),
-            shape((64, FF_DEV)),
+            shape((PART, 128)),
+            shape((PART, 128)),
         ),
-        in_specs=[VMEM] * 5 + [ANY] * 3,
-        out_specs=(VMEM, VMEM, VMEM, ANY, VMEM, VMEM, VMEM, VMEM),
-        scratch_shapes=scatter_scratch() * 2
+        in_specs=[ANY, VMEM, VMEM] + [ANY] * 5,
+        out_specs=(VMEM, VMEM, VMEM, ANY, VMEM, VMEM),
+        scratch_shapes=[block] * 4
+        + [pltpu.VMEM((3 * FF_DEV, D), BF16)]
+        + [turned] * 3
+        + [pair] * 3
         + [pltpu.VMEM((TOK, D), F32), pltpu.VMEM((TOK, D), BF16)]
-        + own_and_got(FF_DEV, 512) * 2
-        + own_and_got(256, FF_DEV) * 2
-        + [pltpu.VMEM((FF_DEV, 512), BF16)] * 2
-        + [pltpu.VMEM((256, FF_DEV), BF16)] * 2
-        + own_and_got(FF_DEV, 128) * 2
-        + own_and_got(64, FF_DEV) * 2
-        + sems(2 * SCATTER_EDGES + GATHER_EDGES)
-        + [
-            pltpu.SemaphoreType.DMA((8, 3)),
-            pltpu.SemaphoreType.DMA((8,)),
-            pltpu.SemaphoreType.DMA((8,)),
-            pltpu.SemaphoreType.DMA,
-        ],
-        compiler_params=remote_params(3),
-        name="mlp_back",
-    )(branch_parts, grad_parts, middle, cot, gain, ggate, gup, gdn)
+        + scatter_scratch() * 2
+        + ring(512)
+        + [pltpu.VMEM((PART, 512), BF16)] * 2
+        + ring(128)
+        + sems(3 * SCATTER_EDGES + 2 * GATHER_EDGES + 4 * SUM_EDGES)
+        + sems(2)
+        + [pltpu.SemaphoreType.DMA((11,))],
+        compiler_params=pltpu.CompilerParams(
+            collective_id=2, has_side_effects=True, vmem_limit_bytes=62 * 2**20
+        ),
+        name="feed_forward",
+    )(parts, tokens, gain, cots, wgu, wdn, wswap, wnear)
+
+
+def columns(width):
+    return lambda i: (slice(None), pl.ds(pl.multiple_of(i * width, width), width))
+
+
+def row_block(height, start=0):
+    return lambda i: (pl.ds(pl.multiple_of(start + i * height, height), height), slice(None))
+
+
+def plane_devices(me):
+    found = [me.at(core=1 - me.c)]
+    for dz, dx in STEPS:
+        z, xl, core, y, xh = around(me, dz, dx)
+        found += [(z, xl, core, y, xh), (z, xl, 1 - core, y, xh)]
+    return found
 
 
 def key_grads_kernel(
-    dkv, gwo, out, wo_out, got, both, last, wo_own, wo_got, wo_piece, wo_all,
-    send, recv, ws, wr, local, ds, dr,
+    dkv, gwo, z_piece, out, wo_out, z_all, got, both, last, wo_own, wo_got, wo_piece, wo_all,
+    send, recv, ws, wr, local, ds, dr, zs, zr,
 ):
     me = Place()
     core = me.at(core=1 - me.c)
     far = [
         me.at(dz=dz, xl=(1 - me.xl) if dl else me.xl) for dz, dl in chips_in_sequence(me)
     ]
-    wide = [around(me, dz, dx) for dz, dx in STEPS]
-    greet(far + wide + group_members(me))
+    greet(plane_devices(me) + group_members(me)[1:])
     edges = Edges(send, recv)
     order = []
     for dz, dl in chips_in_sequence(me) + [(0, 0)]:
         chip = 2 * lax.rem(me.z + dz, 4) + ((1 - me.xl) if dl else me.xl)
         order.append((chip, edges.copy(dkv.at[1 - me.c, chip], got.at[chip], core)))
+    wo_sum = SumOfSixteen(me, gwo, row_block(128), wo_own, wo_got, ws, wr, local)
     far_copies = []
     for i, (chip, d) in enumerate(order):
         d.wait_recv()
         both[chip] = (dkv[me.c, chip].astype(F32) + got[chip].astype(F32)).astype(BF16)
         if i < 7:
             far_copies.append(edges.copy(both.at[chip], last.at[i], far[i]))
-    wo_sum = SumOfSixteen(me, gwo, row_block(128), wo_own, wo_got, ws, wr, local)
+    place = 4 * me.z + x_of(me)
+    z_deliver = Deliver(me, zs, zr)
+    z_deliver.to_owner(
+        z_piece, z_all.at[columns(128)(place)], me.z // 2, me.y, me.c
+    )
     total = both[2 * me.z + me.xl].astype(F32)
     for i, d in enumerate(far_copies):
         d.wait_recv()
@@ -1058,19 +1332,25 @@
     deliver.to_owner(wo_piece, dst, me.y // 2, me.z, me.xh)
     half = wo_all.at[:, pl.ds(pl.multiple_of(1024 * me.c, 1024), 1024)]
     wait_got(half, dr)
-    edges.copy(half, half, core).wait_recv()
-    wo_out[...] = wo_all[...].astype(F32)
+    over = edges.copy(half, half, core)
+    half = z_all.at[:, pl.ds(pl.multiple_of(1024 * me.c, 1024), 1024)]
+    wait_got(half, zr)
+    z_over = edges.copy(half, half, core)
+    over.wait_recv()
+    wo_out[...] = wo_all[...]
+    z_over.wait_recv()
     wo_sum.finish()
     deliver.finish()
+    z_deliver.finish()
     edges.finish()
 
 
-def sum_key_grads(dkv, gwo):
+def sum_key_grads(dkv, gwo, z_piece):
     return pl.pallas_call(
         key_grads_kernel,
-        out_shape=(shape((512, 128), F32), shape((256, D), F32)),
-        in_specs=[VMEM, ANY],
-        out_specs=(VMEM, VMEM),
+        out_shape=(shape((512, 128), F32), shape((256, D)), shape((PART, D))),
+        in_specs=[VMEM, ANY, VMEM],
+        out_specs=(VMEM, VMEM, ANY),
         scratch_shapes=[
             pltpu.VMEM((8, 512, 128), BF16),
             pltpu.VMEM((8, 512, 128), BF16),
@@ -1080,33 +1360,42 @@
             pltpu.VMEM((128, Q_DEV), BF16),
             pltpu.VMEM((256, D), BF16),
         ]
-        + sems(16)
+        + sems(17)
         + [
             pltpu.SemaphoreType.DMA((15,)),
             pltpu.SemaphoreType.DMA,
             pltpu.SemaphoreType.DMA,
             pltpu.SemaphoreType.DMA((8,)),
             pltpu.SemaphoreType.DMA,
+            pltpu.SemaphoreType.DMA((8,)),
+            pltpu.SemaphoreType.DMA,
         ],
         compiler_params=remote_params(4),
         name="sum_key_grads",
-    )(dkv, gwo)
+    )(dkv, gwo, z_piece)
 
 
 def closing_kernel(
-    parts, gwq, tokens, gain, grad_middle, gain_two,
-    grad_tokens, gains, wq_out,
-    got, both, relayed, last, total, wq_own, wq_got, wq_piece, wq_all,
+    parts, gwq, tokens, gain, grad_middle, gain_two, x_piece,
+    grad_tokens, gains, wq_out, x_all,
+    got, both, relayed, last, wq_own, wq_got, wq_piece, wq_all,
     mine, near, near_sum, owners,
-    send, recv, ws, wr, local, ds, dr, gs, gr, hs, hr,
+    send, recv, ws, wr, local, ds, dr, gs, gr, hs, hr, xs_, xr,
 ):
     me = Place()
-    members = group_members(me)
-    greet(members + [around(me, dz, dx) for dz, dx in STEPS])
+    greet(plane_devices(me) + group_members(me)[1:])
     edges = Edges(send, recv)
-    ring = RingScatter(me, edges, parts, got, both, relayed, last)
+    ring = RingScatter(me, edges, parts, (got, both, relayed, last))
+    for k in (2, 1, 3, 0):
+        ring.send_core(k)
     wq_sum = SumOfSixteen(me, gwq, columns(128), wq_own, wq_got, ws, wr, local)
-    ring.first()
+    ring.far()
+    ring.near()
+    ring.add_core(0)
+    x_deliver = Deliver(me, xs_, xr)
+    x_deliver.to_owner(
+        x_piece, x_all.at[columns(128)(4 * x_of(me) + me.z)], me.xh, me.y, me.c
+    )
     ring.second()
     wq_piece[...] = wq_sum.total().astype(BF16)
     deliver = Deliver(me, ds, dr)
@@ -1121,7 +1410,7 @@
         deliver.to_owner(
             wq_piece.at[pl.ds(64 * j, 64)], dst, me.z // 2, owner // 2, lax.rem(owner, 2)
         )
-    ring.total(total)
+    ring.arrived()
     mine[...] = jnp.zeros_like(mine)
     mine[1:2, :] = gain_two[...]
 
@@ -1129,7 +1418,7 @@
         rows = tokens[at, :].astype(F32)
         inverse = lax.rsqrt(mean_last(rows * rows) + EPSILON)
         normal = rows * inverse
-        grad = total[at, :]
+        grad = ring.rows(at)
         mine[0:1, :] += jnp.sum(normal * grad, axis=0, keepdims=True)
         scaled = grad * gain[...]
         grad_tokens[at, :] = grad_middle[at, :] + inverse * (
@@ -1173,29 +1462,34 @@
     for k in range(1, 16):
         sum_all = sum_all + owners[k]
     gains[...] = sum_all
+    half = x_all.at[:, pl.ds(pl.multiple_of(1024 * me.c, 1024), 1024)]
+    wait_got(half, xr)
+    x_over = edges.copy(half, half, me.at(core=1 - me.c))
     over.wait_recv()
-    wq_out[...] = wq_all[...].astype(F32)
+    wq_out[...] = wq_all[...]
+    x_over.wait_recv()
     wq_sum.finish()
     deliver.finish()
+    x_deliver.finish()
     for d in near_copies:
         d.wait_send()
     far.finish()
     edges.finish()
 
 
-def closing(parts, gwq, tokens, gain, grad_middle, gain_two):
+def closing(parts, gwq, tokens, gain, grad_middle, gain_two, x_piece):
     return pl.pallas_call(
         closing_kernel,
         out_shape=(
             shape((TOK, D), F32),
             shape((8, 256), F32),
-            shape((320, D), F32),
+            shape((320, D)),
+            shape((PART, D)),
         ),
-        in_specs=[VMEM, ANY] + [VMEM] * 4,
-        out_specs=(VMEM,) * 3,
+        in_specs=[VMEM, ANY] + [VMEM] * 5,
+        out_specs=(VMEM,) * 3 + (ANY,),
         scratch_shapes=scatter_scratch()
         + [
-            pltpu.VMEM((TOK, D), F32),
             pltpu.VMEM((320, 128), BF16),
             pltpu.VMEM((15, 320, 128), BF16),
             pltpu.VMEM((320, 128), BF16),
@@ -1205,7 +1499,7 @@
             pltpu.VMEM((8, 256), F32),
             pltpu.VMEM((16, 8, 256), F32),
         ]
-        + sems(SCATTER_EDGES + 1)
+        + sems(SCATTER_EDGES + 2)
         + [
             pltpu.SemaphoreType.DMA((15,)),
             pltpu.SemaphoreType.DMA,
@@ -1216,44 +1510,47 @@
             pltpu.SemaphoreType.DMA,
             pltpu.SemaphoreType.DMA((16,)),
             pltpu.SemaphoreType.DMA,
+            pltpu.SemaphoreType.DMA((8,)),
+            pltpu.SemaphoreType.DMA,
         ],
         compiler_params=remote_params(5),
         name="closing",
-    )(parts, gwq, tokens, gain, grad_middle, gain_two)
-
-
-def route(step):
-    pairs = []
-    for z in range(4):
-        for xl in range(2):
-            for c in range(2):
-                for y in range(4):
-                    for xh in range(2):
-                        here = (((z * 2 + xl) * 2 + c) * 4 + y) * 2 + xh
-                        z_to, xl_to, c_to, y_to, xh_to = step(z, xl, c, y, xh)
-                        there = (((z_to * 2 + xl_to) * 2 + c_to) * 4 + y_to) * 2 + xh_to
-                        pairs.append((here, there))
-    return pairs
-
-
-def to_worker(z, xl, c, y, xh):
-    return (z, xl, c, y, xh) if c == xh else (z, 1 - xl, 1 - c, y, 1 - xh)
-
-
-def to_owner(z, xl, c, y, xh):
-    return (z, xl, xh, y, c)
-
-
-def worker_shard(shard):
-    rows = shard.shape[0] // 4
-    mine = lax.dynamic_slice_in_dim(shard, lax.axis_index("z") * rows, rows)
-    mine = lax.ppermute(mine, AXES, route(to_worker))
-    return lax.all_gather(mine, "z", axis=0, tiled=True)
-
-
-def gather_owned(piece):
-    piece = lax.ppermute(piece, AXES, route(to_owner))
-    return lax.all_gather(piece, ("z", "xl", "c"), axis=0).reshape((4, 2, 2) + piece.shape)
+    )(parts, gwq, tokens, gain, grad_middle, gain_two, x_piece)
+
+
+def widen_kernel(z_ref, x_ref, gu_ref, dn_ref):
+    i = pl.program_id(0)
+
+    @pl.when(i < 3)
+    def _():
+        gu_ref[...] = z_ref[...].astype(F32)
+
+    @pl.when(i == 3)
+    def _():
+        gu_ref[...] = x_ref[...].astype(F32)
+
+    @pl.when(i > 3)
+    def _():
+        dn_ref[...] = x_ref[...].astype(F32)
+
+
+def widen(z_all, x_all):
+    rows = PART // 3
+    return pl.pallas_call(
+        widen_kernel,
+        out_shape=(shape((2 * FF_DEV, D), F32), shape((FF_DEV, D), F32)),
+        grid=(6,),
+        in_specs=[
+            pl.BlockSpec((rows, D), lambda i: (jnp.minimum(i, 2), 0)),
+            pl.BlockSpec((rows, D), lambda i: (jnp.maximum(i - 3, 0), 0)),
+        ],
+        out_specs=(
+            pl.BlockSpec((rows, D), lambda i: (jnp.minimum(i, 3), 0)),
+            pl.BlockSpec((rows, D), lambda i: (jnp.maximum(i - 4, 0), 0)),
+        ),
+        compiler_params=pltpu.CompilerParams(vmem_limit_bytes=40 * 2**20),
+        name="widen",
+    )(z_all, x_all)
 
 
 def body(hidden, positions, gain_attn, w_qkv, w_out, gain_mlp, w_gate_up, w_down, cotangent):
@@ -1264,66 +1561,50 @@
     inverse_one = lax.rsqrt(jnp.mean(tokens * tokens, axis=-1, keepdims=True) + EPSILON)
     input_one = (tokens * inverse_one * gain_one).astype(BF16)
     table = jnp.asarray(rotary_table())
-    xs, poss, wq = opening(input_one, jnp.broadcast_to(positions, (8, TOK)), w_qkv)
-    gu = worker_shard(w_gate_up.reshape(2 * FF_DEV, D))
-    dn = worker_shard(w_down)
+    wgu = w_gate_up.reshape(2 * FF_DEV, D)
+    wdn = w_down.T
+    xs, poss, wq, wswap = opening(
+        input_one, jnp.broadcast_to(positions, (8, TOK)), w_qkv, wgu, wdn
+    )
     xs = xs.reshape(1024, D)
     wq = wq.reshape(320, D)
     query_runs = poss[:, 0, ::64].reshape(16) // 64
     query, kv = project(query_runs, core, xs, wq, table)
-    kvs, places, cots, wo = exchange_keys(kv, poss, cotangent[0], w_out)
-    cots = cots.reshape(1024, D)
+    kvs, places, cots, wo, wnear = exchange_keys(kv, poss, cotangent[0], w_out, wswap)
     wo = wo.reshape(D, Q_DEV)
     key_runs = (
         places[:, :, 0, ::64].reshape(8, 4, 2, 2).transpose(1, 0, 2, 3).reshape(128) // 64
     )
     att, ot, lse = attend(key_runs, query_runs, query, kvs)
-    parts = dot_last(att, wo).astype(BF16)
-    middle, x2 = to_middle(parts.reshape(8, TOK, D), hidden[0], gain_two)
-    x2 = x2.reshape(1024, D)
-
-    gate = dot_last(x2, gu[:FF_DEV])
-    upward = dot_last(x2, gu[FF_DEV:])
-    grad_active = dot(cots, dn)
-    sigmoid = jax.nn.sigmoid(gate)
-    swish = gate * sigmoid
-    active = (swish * upward).astype(BF16)
-    grad_upward = (grad_active * swish).astype(BF16)
-    grad_gate = (grad_active * upward * sigmoid * (1.0 + gate * (1.0 - sigmoid))).astype(BF16)
-    branch_parts = dot_last(active, dn).astype(BF16).reshape(8, TOK, D)
-    grad_parts = (dot(grad_gate, gu[:FF_DEV]) + dot(grad_upward, gu[FF_DEV:])).astype(BF16)
-    ggate = dot_first(grad_gate, x2).astype(BF16)
-    gup = dot_first(grad_upward, x2).astype(BF16)
-    gdn = dot_first(cots, active).astype(BF16)
-    output, grad_middle, gain_grad, gbs, gate_piece, up_piece, top_piece, low_piece = mlp_back(
-        branch_parts, grad_parts.reshape(8, TOK, D), middle, cotangent[0], gain_two,
-        ggate, gup, gdn,
+    parts = dot_last(att, wo).astype(BF16).reshape(8, TOK, D)
+    output, grad_middle, gain_grad, gbs, z_piece, x_piece = feed_forward(
+        parts, hidden[0], gain_two, cots, wgu, wdn, wswap, wnear
     )
     gb = gbs.reshape(1024, D)
     grad_att = dot(gb, wo).astype(BF16)
     grad_wo = dot_first(gb, att).astype(BF16)
-    grad_gu = gather_owned(jnp.stack([gate_piece, up_piece]))
-    grad_dn = gather_owned(jnp.stack([top_piece, low_piece]))
     dq, dkv = attend_back(key_runs, query_runs, query, kvs, grad_att, ot, lse, table)
-    dkv, grad_w_out = sum_key_grads(dkv, grad_wo)
+    dkv, grad_w_out, z_all = sum_key_grads(dkv, grad_wo, z_piece)
     one_parts, gwq = project_back(query_runs, core, dq, dkv, xs, wq, table)
-    grad_tokens, gains, grad_w_qkv = closing(
-        one_parts.reshape(8, TOK, D), gwq, hidden[0], gain_one, grad_middle, gain_grad
+    grad_tokens, gains, grad_w_qkv, x_all = closing(
+        one_parts.reshape(8, TOK, D),
+        gwq,
+        hidden[0],
+        gain_one,
+        grad_middle,
+        gain_grad,
+        x_piece,
     )
-
-    gate_full = grad_gu[:, :, :, 0].transpose(3, 0, 2, 1, 4).reshape(FF_DEV, D)
-    up_full = grad_gu[:, :, :, 1].transpose(3, 2, 1, 0, 4).reshape(FF_DEV, D)
-    top_full = grad_dn[:, :, :, 0].transpose(0, 2, 1, 3, 4).reshape(1024, FF_DEV)
-    low_full = grad_dn[:, :, :, 1].transpose(2, 1, 0, 3, 4).reshape(1024, FF_DEV)
+    grad_gu, grad_dn = widen(z_all, x_all)
     return (
         output[None],
         grad_tokens[None],
         gains[0],
-        grad_w_qkv,
-        grad_w_out,
+        grad_w_qkv.astype(F32),
+        grad_w_out.astype(F32),
         gains[1],
-        jnp.stack([gate_full, up_full]).astype(F32),
-        jnp.concatenate([top_full, low_full]).astype(F32),
+        grad_gu.reshape(2, FF_DEV, D),
+        grad_dn.T,
     )
 
 

time: 614 us -> 485 us (0.79)
  local copies, waits for them, and re-layouts: 76.6 us -> 22 us
  Pallas kernels: 387 us -> 439 us
  matrix products: 59.2 us -> 10.1 us
  waiting for transfers between devices: 36.9 us -> 0 us
  starting transfers between devices: 19.4 us -> 0 us
  between operations: 14.6 us -> 1.43 us
    ppermute x4 -> x0, waiting for transfers between devices: 36.8 us -> none  [the longest x2 26 us: worker_shard(): mine = lax.ppermute(mine, AXES, route(to_worker))]
    dot_general x4 -> x1, matrix products: 21 us -> 1.25 us  [dot(): lax.dot_general(a, b, (((1,), (0,)), ((), ())), preferred_element_type=F32)]
    ppermute x4 -> x0, starting transfers between devices: 19.3 us -> none  [the longest x2 10.1 us: worker_shard(): mine = lax.ppermute(mine, AXES, route(to_worker))]
    pallas_call x1, Pallas kernels: 51 us -> 68.2 us  [closing(): pl.pallas_call(closing_kernel, out_shape=(shape((TOK, D), F32), shape((8,...]
    unnamed x107 -> x62, local copies, waits for them, and re-layouts: 35 us -> 18.9 us
    pallas_call x1, Pallas kernels: 69.9 us -> 85.2 us  [sum_key_grads(): pl.pallas_call(key_grads_kernel, out_shape=(shape((512, 128), F32), shape...]
    dot_general x4 -> x1, matrix products: 20.1 us -> 5.1 us  [dot_last(): lax.dot_general(a, b, (((1,), (1,)), ((), ())), preferred_element_type=F32)]
    transpose x3 -> x0, local copies, waits for them, and re-layouts: 15 us -> none  [the longest x2 9.37 us: body(): gate_full = grad_gu[:, :, :, 0].transpose(3, 0, 2, 1, 4).reshape(FF_DEV, D)]
  transfers between devices with their start and end apart: 8 -> 0, of which waited for: 4 -> 0; matrix products, arithmetic and copies ran while one was open for 6% -> 0% of each run, Pallas kernels for 52% -> 0%
where the time goes in v3:
time: 485 us; the launch traced here: 480 us
  Pallas kernels  439 us (91%)
  local copies, waits for them, and re-layouts  22 us (5%)
  matrix products  10.1 us (2%)
  other arithmetic  7.8 us (2%)
    pallas_call x1, Pallas kernels, feed_forward(): pl.pallas_call(feed_forward_kernel, out_shape=(shape((TOK, D)), shape((TO...  119 us
    pallas_call x1, Pallas kernels, sum_key_grads(): pl.pallas_call(key_grads_kernel, out_shape=(shape((512, 128), F32), shape...  85.2 us
    pallas_call x1, Pallas kernels, closing(): pl.pallas_call(closing_kernel, out_shape=(shape((TOK, D), F32), shape((8,...  68.2 us
    pallas_call x1, Pallas kernels, exchange_keys(): pl.pallas_call(keys_kernel, out_shape=(shape((2, 8, 512, 128)), shape((8,...  46.1 us
    pallas_call x1, Pallas kernels, opening(): pl.pallas_call(opening_kernel, out_shape=(shape((8, TOK, D)), shape((8, 8...  43.8 us
    pallas_call x1, Pallas kernels, attend_back(): pl.pallas_call(attend_back_kernel, out_shape=(shape((1024, 256)), shape((...  34.7 us
    pallas_call x1, Pallas kernels, attend(): pl.pallas_call(attend_kernel, out_shape=(shape((1024, 256)), shape((16, H...  23.8 us
    unnamed x62, local copies, waits for them, and re-layouts  18.9 us

profile of v3, /device:TPU:9, one launch (start us, length us, event | category | flops | bytes accessed | tf_op | source)
XLA Modules:
  0.0 480.4 jit_solution(5637906039964960621)
XLA Ops:
  0.6 0.7 convert_element_type.26
  1.3 1.2 fusion
  2.6 1.2 fusion.2.x
  3.8 0.7 broadcast_in_dim.15.pos
  4.5 1.3 copy-done.14
  5.8 43.8 %opening.1 = (bf16[8,128,2048]{2,1,0:T(8,128)(2,1)}, s32[8,8,128]{2,1,0:T(8,128)S(1)}, bf16[5,64,2048]{2,1,0:T(8,128)(2,1)S(1)}, bf16[528,2048]{1,0:T(8,128)(2,1)S(1)}) custom-call(bf16[128,2048]{1,0:T(8,128)(2,1)S(1)} %fusion.2.x, s32[8,128]{1,0:T(8,128)S(1)} %broadcast_in_dim.15.pos, bf16[320,2048]{1,0:T(8,128)(2,1)S(1)} %copy-done.14, ...), custom_call_target="tpu_custom_call" | custom-call | tf_op jit(solution)/shard_map/opening/pallas_call | solution.py:441
  49.6 1.3 copy-done.3
  51.0 0.1 slice.12
  51.0 0.6 broadcast.37
  51.7 0.7 reduce.3
  52.3 0.1 reshape_squeeze.6
  52.4 2.2 copy-done
  54.6 4.5 project.1
  59.1 0.0 copy-start.17
  59.1 1.2 copy-done.17
  60.3 1.0 copy-done.21
  61.4 46.1 %exchange_keys.1 = (bf16[2,8,512,128]{3,2,1,0:T(8,128)(2,1)S(1)}, s32[8,8,8,128]{3,2,1,0:T(8,128)S(1)}, bf16[8,128,2048]{2,1,0:T(8,128)(2,1)}, bf16[8,256,256]{2,1,0:T(8,128)(2,1)S(1)}, bf16[2,528,2048]{2,1,0:T(8,128)(2,1)}) custom-call(bf16[512,128]{1,0:T(8,128)(2,1)S(1)} %get-tuple-element.44.kv, s32[8,8,128]{2,1,0:T(8,128)S(1)} %get-tuple-element.41.pos, ...), custom_call_target="tpu_custom_call" | custom-call | tf_op jit(solution)/shard_map/exchange_keys/pallas_call | solution.py:662
  107.5 0.0 copy-start.5
  107.5 1.3 copy-done.5
  108.8 1.0 copy-done.15
  109.8 0.7 slice.13
  110.5 0.1 copy.20
  110.6 0.1 copy.21
  110.7 0.1 reshape.67
  110.9 0.0 copy-start.6
  110.9 1.6 copy-done.6
  112.5 23.8 %attend.1 = (bf16[1024,256]{1,0:T(8,128)(2,1)S(1)}, f32[16,64,256]{2,1,0:T(8,128)S(1)}, f32[16,1,256]{2,1,0:T(1,128)S(1)}) custom-call(s32[128]{0:T(128)S(1)} %and_select_fusion.key_runs, s32[16]{0:T(128)S(1)} %and_select_fusion.1.runs.query_runs, bf16[1024,256]{1,0:T(8,128)(2,1)S(1)} %get-tuple-element.47.q_ref, bf16[2,8,512,128]{3,2,1,0:T(8,128)(2,1)S(1)} %copy-done.6), custom_call_target="tpu_custom_call" | custom-call | tf_op jit(solution)/shard_map/attend/pallas_call | solution.py:784
  136.3 5.1 %convolution_convert_fusion = bf16[1024,2048]{1,0:T(8,128)(2,1)} fusion(bf16[1024,256]{1,0:T(8,128)(2,1)S(1)} %get-tuple-element.49, bf16[2048,256]{1,0:T(8,128)(2,1)} %bitcast.38), kind=kOutput, calls=%fused_computation | convolution fusion | flops 1075838976 | bytes 5767168 | tf_op jit(solution)/shard_map/dot_general | solution.py:691
  141.4 0.6 reshape.76
  142.0 119.0 %feed_forward.1 = (bf16[128,2048]{1,0:T(8,128)(2,1)}, f32[128,2048]{1,0:T(8,128)}, f32[1,2048]{1,0:T(1,128)}, bf16[8,128,2048]{2,1,0:T(8,128)(2,1)}, bf16[1056,1...) custom-call(bf16[8,128,2048]{2,1,0:T(8,128)(2,1)} %bitcast.43, bf16[128,2048]{1,0:T(8,128)(2,1)} %bitcast.33, ...), custom_call_target="tpu_custom_call" | custom-call | tf_op jit(solution)/shard_map/feed_forward/pallas_call | solution.py:1246
  261.1 3.8 convolution_convert_fusion.1.gwo
  264.9 0.1 copy-done.29
  265.0 1.2 convolution_convert_fusion.2.da_ref
  266.3 0.3 copy-done.7
  266.6 0.3 copy-done.20
  266.9 34.7 %attend_back.1 = (bf16[1024,256]{1,0:T(8,128)(2,1)S(1)}, bf16[2,8,512,128]{3,2,1,0:T(8,128)(2,1)S(1)}) custom-call(s32[128]{0:T(128)S(1)} %and_select_fusion.key_runs, s32[16]{0:T(128)S(1)} %and_select_fusion.1.runs.query_runs, bf16[1024,256]{1,0:T(8,128)(2,1)S(1)} %get-tuple-element.47.q_ref, bf16[2,8,512,128]{3,2,1,0:T(8,128)(2,1)S(1)} %copy-done.7, ...), custom_call_target="tpu_custom_call" | custom-call | tf_op jit(solution)/shard_map/attend_back/pallas_call | solution.py:873
  301.6 85.2 %sum_key_grads.1 = (f32[512,128]{1,0:T(8,128)S(1)}, bf16[256,2048]{1,0:T(8,128)(2,1)S(1)}, bf16[1056,2048]{1,0:T(8,128)(2,1)}) custom-call(bf16[2,8,512,128]{3,2,1,0:T(8,128)(2,1)S(1)} %get-tuple-element.58.dkv, bf16[2048,256]{1,0:T(8,128)(2,1)S(1)} %convolution_convert_fusion.1.gwo, bf16[1056,128]{1,0:T(8,128)(2,1)S(1)} %copy-done.25), custom_call_target="tpu_custom_call" | custom-call | tf_op jit(solution)/shard_map/sum_key_grads/pallas_call | solution.py:1349
  386.9 1.1 copy-done.23
  388.1 6.3 %project_back.1 = (bf16[1024,2048]{1,0:T(8,128)(2,1)S(1)}, bf16[320,2048]{1,0:T(8,128)(2,1)S(1)}) custom-call(s32[16]{0:T(128)S(1)} %and_select_fusion.1.runs.query_runs, s32[1]{0:T(128)} %bitcast.4.core, bf16[1024,256]{1,0:T(8,128)(2,1)S(1)} %copy-done.23, f32[512,128]{1,0:T(8,128)S(1)} %get-tuple-element.60.dkv_ref, bf16[1024,2048]{1,0:T(8,128)(2,1)S(1)} %bitcast.32, ...), custom_call_target="tpu_custom_call" | custom-call | tf_op jit(solution)/shard_map/project_back/pallas_call | solution.py:550
  394.4 2.0 copy-done.12
  396.5 68.2 %closing.1 = (f32[128,2048]{1,0:T(8,128)S(1)}, f32[8,256]{1,0:T(8,128)S(1)}, bf16[320,2048]{1,0:T(8,128)(2,1)S(1)}, bf16[1056,2048]{1,0:T(8,128)(2,1)}) custom-call(bf16[8,128,2048]{2,1,0:T(8,128)(2,1)} %bitcast.37, bf16[320,2048]{1,0:T(8,128)(2,1)S(1)} %get-tuple-element.62.gwq, bf16[128,2048]{1,0:T(8,128)(2,1)S(1)} %bitcast.34, f32[1,2048]{1,0:T(1,128)S(1)} %bitcast.42, ...), custom_call_target="tpu_custom_call" | custom-call | tf_op jit(solution)/shard_map/closing/pallas_call | solution.py:1481
  464.7 2.2 copy-done.11
  466.9 7.3 %widen.1 = (f32[1408,2048]{1,0:T(8,128)}, f32[704,2048]{1,0:T(8,128)}) custom-call(bf16[1056,2048]{1,0:T(8,128)(2,1)S(1)} %copy-done.10, bf16[1056,2048]{1,0:T(8,128)(2,1)S(1)} %copy-done.11), custom_call_target="tpu_custom_call" | custom-call | tf_op jit(solution)/shard_map/widen/pallas_call | solution.py:1539
  474.3 1.8 convert_element_type.31
  476.0 0.6 fusion.3
  476.6 1.6 convert_element_type.32
  478.2 0.8 copy.24
  479.0 1.0 copy.25
  (46 shorter events, 0.1 us)
Async XLA Ops:
  4.5 1.3 copy-start.14
  5.8 46.6 %copy-start.2 = (f32[2048,128]{1,0:T(8,128)S(1)}, f32[2048,128]{1,0:T(8,128)}, u32[]{:S(2)}) copy-start(f32[2048,128]{1,0:T(8,128)} %constant.40.clone.table_ref) | copy-start | bytes 3145732
  49.6 1.3 copy-start.3
  51.0 56.5 %copy-start.8 = (bf16[5,64,2048]{2,1,0:T(8,128)(2,1)}, bf16[5,64,2048]{2,1,0:T(8,128)(2,1)S(1)}, u32[]{:S(2)}) copy-start(bf16[5,64,2048]{2,1,0:T(8,128)(2,1)S(1)} %get-tuple-element.43) | copy-start | bytes 3932164
  52.4 2.2 copy-start
  59.1 1.2 copy-start.17
  60.3 1.0 copy-start.21
  107.5 1.3 copy-start.5
  108.8 1.0 copy-start.15
  110.9 1.6 copy-start.6
  136.3 5.1 %copy-start.13 = (bf16[1024,256]{1,0:T(8,128)(2,1)}, bf16[1024,256]{1,0:T(8,128)(2,1)S(1)}, u32[]{:S(2)}) copy-start(bf16[1024,256]{1,0:T(8,128)(2,1)S(1)} %get-tuple-element.49) | copy-start | bytes 1572868
  136.3 5.1 %copy-start.19 = (f32[16,64,256]{2,1,0:T(8,128)}, f32[16,64,256]{2,1,0:T(8,128)S(1)}, u32[]{:S(2)}) copy-start(f32[16,64,256]{2,1,0:T(8,128)S(1)} %get-tuple-element.55.ot_ref) | copy-start | bytes 3145732
  136.3 5.1 %copy-start.28 = (bf16[2048]{0:T(1024)(128)(2,1)S(1)}, bf16[2048]{0:T(1024)(128)(2,1)}, u32[]{:S(2)}) copy-start(bf16[2048]{0:T(1024)(128)(2,1)} %param.15) | copy-start | bytes 12292
  261.1 3.8 copy-start.16
  261.1 3.9 copy-start.29
  265.0 1.6 copy-start.7
  265.0 1.9 copy-start.20
  266.3 35.3 %copy-start.25 = (bf16[1056,128]{1,0:T(8,128)(2,1)S(1)}, bf16[1056,128]{1,0:T(8,128)(2,1)}, u32[]{:S(2)}) copy-start(bf16[1056,128]{1,0:T(8,128)(2,1)} %get-tuple-element.59.z_piece) | copy-start | bytes 811012
  266.9 120.0 %copy-start.1 = (bf16[8,128,2048]{2,1,0:T(8,128)(2,1)S(1)}, bf16[8,128,2048]{2,1,0:T(8,128)(2,1)}, u32[]{:S(2)}) copy-start(bf16[8,128,2048]{2,1,0:T(8,128)(2,1)} %get-tuple-element.42) | copy-start | bytes 12582916
  266.9 120.1 %copy-start.9 = (bf16[5,64,2048]{2,1,0:T(8,128)(2,1)S(1)}, bf16[5,64,2048]{2,1,0:T(8,128)(2,1)}, u32[]{:S(2)}) copy-start(bf16[5,64,2048]{2,1,0:T(8,128)(2,1)} %copy-done.8) | copy-start | bytes 3932164
  301.6 85.3 %copy-start.22 = (bf16[1024,256]{1,0:T(8,128)(2,1)}, bf16[1024,256]{1,0:T(8,128)(2,1)S(1)}, u32[]{:S(2)}) copy-start(bf16[1024,256]{1,0:T(8,128)(2,1)S(1)} %get-tuple-element.57.dq_ref) | copy-start | bytes 1572868
  301.6 94.9 %copy-start.24 = (bf16[1056,128]{1,0:T(8,128)(2,1)S(1)}, bf16[1056,128]{1,0:T(8,128)(2,1)}, u32[]{:S(2)}) copy-start(bf16[1056,128]{1,0:T(8,128)(2,1)} %get-tuple-element.65.x_piece) | copy-start | bytes 811012
  301.6 94.8 %copy-start.26 = (f32[1,2048]{1,0:T(1,128)S(1)}, f32[1,2048]{1,0:T(1,128)}, u32[]{:S(2)}) copy-start(f32[1,2048]{1,0:T(1,128)} %get-tuple-element.64.gain_two) | copy-start | bytes 24580
  386.9 9.6 %copy-start.4 = (bf16[1,128,2048]{2,1,0:T(8,128)(2,1)S(1)}, bf16[1,128,2048]{2,1,0:T(8,128)(2,1)}, u32[]{:S(2)}) copy-start(bf16[1,128,2048]{2,1,0:T(8,128)(2,1)} %param.10) | copy-start | bytes 1572868
  386.9 9.6 %copy-start.18 = (f32[128,2048]{1,0:T(8,128)S(1)}, f32[128,2048]{1,0:T(8,128)}, u32[]{:S(2)}) copy-start(f32[128,2048]{1,0:T(8,128)} %get-tuple-element.63.grad_middle) | copy-start | bytes 3145732
  386.9 1.2 copy-start.23
  394.4 2.0 copy-start.12
  396.5 68.2 %copy-start.10 = (bf16[1056,2048]{1,0:T(8,128)(2,1)S(1)}, bf16[1056,2048]{1,0:T(8,128)(2,1)}, u32[]{:S(2)}) copy-start(bf16[1056,2048]{1,0:T(8,128)(2,1)} %get-tuple-element.70.z_ref) | copy-start | bytes 12976132
  464.7 2.2 copy-start.11
  474.2 3.9 copy-start.27

commit v4 on v3

--- a/solution.py
+++ b/solution.py
@@ -1,6 +1,5 @@
 import jax
 import jax.numpy as jnp
-import numpy as np
 from jax import lax
 from jax.experimental import pallas as pl
 from jax.experimental.pallas import tpu as pltpu
@@ -353,64 +352,42 @@
             wait_sent(src, sem, stays)
 
 
-def opening_kernel(
-    x, pos, wqkv, wgu, wdn, xs, poss, wq, wswap, send, recv, qs, qr, ws, wr, local
-):
-    me = Place()
-    partner = {"xl": 1 - me.xl, "xh": 1 - me.xh}
-    members = group_members(me)
-    others = [
-        me.at(y=lax.rem(me.y + dy, 4), core=core, **partner)
-        for dy in range(4)
-        for core in (0, 1)
-    ]
-    greet(members + others)
-    edges = Edges(send, recv)
-    own_rank = 2 * me.y + me.c
-    keep = pltpu.make_async_copy(x, xs.at[own_rank], local.at[0])
-    keep.start()
-    keep_pos = pltpu.make_async_copy(pos, poss.at[own_rank], local.at[1])
-    keep_pos.start()
-    pos_copies = [edges.copy(pos, poss.at[own_rank], m) for m in members]
-    ring = RingGather(me, edges, x, xs)
-
-    own = 2 * me.y + me.xh
-    own_column = me.c == 0
-    to_xl = jnp.where(own_column, me.xl, 1 - me.xl)
-    to_xh = jnp.where(own_column, me.xh, 1 - me.xh)
-    blocks = []
-    for i in range(5):
-        y, core, slot = block_place(5 * own + i)
-        stays = own_column & (y == me.y) & (core == me.c)
-        src = wqkv.at[pl.ds(64 * i, 64)]
-        send_block(
-            me, src, wq.at[slot], qs.at[i], qr.at[slot], (me.z, to_xl, core, y, to_xh), stays
-        )
-        blocks.append((src, qs.at[i], stays))
-    swaps = swap_copies(me, wgu, wdn, wswap, ws, wr)
-
-    @pl.when(me.c != me.xh)
-    def _():
-        for d in swaps:
-            d.start()
-
-    ring.relay()
-    ring.rest()
-
-    @pl.when(me.c != me.xh)
-    def _():
-        for d in swaps:
-            d.wait()
-
-    for d in pos_copies:
-        d.wait_recv()
-    for i in range(5):
-        wait_got(wq.at[i], qr.at[i])
-    for src, sem, stays in blocks:
-        wait_sent(src, sem, stays)
-    edges.finish()
-    keep.wait()
-    keep_pos.wait()
+def rotary_rows(places):
+    steps = jnp.arange(HD // 2, dtype=F32)
+    inverse = jnp.power(10000.0, steps * (-2.0 / HD))
+    turning = places.astype(F32)[:, None] * inverse[None, :]
+    rows = jnp.concatenate([jnp.cos(turning), jnp.sin(turning)], axis=1)
+    return rows.reshape(2, 64, HD).transpose(1, 0, 2).reshape(64, 2 * HD)
+
+
+def halves_swapped(rows):
+    return jnp.concatenate([rows[:, HD // 2 :], rows[:, : HD // 2]], axis=1)
+
+
+def rotate(rows, table, back=False):
+    turned = halves_swapped(rows) * table[:, HD:]
+    return rows * table[:, :HD] + (-turned if back else turned)
+
+
+def rotary_of(rows, u):
+    cosine = rows[:, HD * u : HD * u + HD // 2]
+    sine = rows[:, HD * u + HD // 2 : HD * u + HD]
+    return jnp.concatenate([cosine, cosine, -sine, sine], axis=1)
+
+
+ROWS = 16
+
+
+def in_chunks(step, rows=TOK):
+    def one(i, _):
+        step(pl.ds(pl.multiple_of(i * ROWS, ROWS), ROWS))
+        return 0
+
+    lax.fori_loop(0, rows // ROWS, one, 0)
+
+
+def mean_last(rows):
+    return jnp.mean(rows, axis=-1, keepdims=True)
 
 
 GU_QUARTER = 2 * FF_DEV // 4
@@ -437,200 +414,170 @@
     return found
 
 
-def opening(x, pos, wqkv, wgu, wdn):
-    return pl.pallas_call(
-        opening_kernel,
-        out_shape=(
-            shape((8, TOK, D)),
-            shape((8, 8, TOK), jnp.int32),
-            shape((5, 64, D)),
-            shape((QUARTER, D)),
-        ),
-        in_specs=[ANY] * 5,
-        out_specs=(ANY,) * 4,
-        scratch_shapes=sems(7 + GATHER_EDGES)
-        + sems(5)
-        + sems(2)
-        + [pltpu.SemaphoreType.DMA((2,))],
-        compiler_params=remote_params(0),
-        name="opening",
-    )(x, pos, wqkv, wgu, wdn)
-
-
-def rotary_table():
-    steps = np.arange(HD // 2, dtype=np.float32)
-    inverse = np.power(np.float32(10000.0), steps * np.float32(-2.0 / HD)).astype(np.float32)
-    turning = np.arange(2048, dtype=np.float32)[:, None] * inverse[None, :]
-    cosine, sine = np.cos(turning), np.sin(turning)
-    return np.concatenate([cosine, cosine, -sine, sine], axis=1).astype(np.float32)
-
-
-def halves_swapped(rows):
-    return jnp.concatenate([rows[:, HD // 2 :], rows[:, : HD // 2]], axis=1)
-
-
-def rotate(rows, table, back=False):
-    turned = halves_swapped(rows) * table[:, HD:]
-    return rows * table[:, :HD] + (-turned if back else turned)
-
-
-def table_rows(table_ref, run):
-    return table_ref[pl.ds(pl.multiple_of(run * 64, 64), 64), :]
-
-
-def project_kernel(runs, core, xs_ref, wq_ref, table_ref, q_ref, kv_ref):
-    seq = pl.program_id(0)
-    projected = dot_last(xs_ref[...], wq_ref[...])
-    is_key = core[0] == 0
-    for r in range(4):
-        table = table_rows(table_ref, runs[seq * 4 + r])
-        rows = projected[64 * r : 64 * r + 64]
-        heads = [rotate(rows[:, HD * h : HD * h + HD], table) for h in range(4)]
-        query = jnp.concatenate(heads, axis=1).astype(BF16)
-        q_ref[64 * r : 64 * r + 64, :] = (query.astype(F32) * 0.125).astype(BF16)
-        plain = rows[:, Q_DEV:]
-        kv = jnp.where(is_key, rotate(plain, table), plain)
-        half, u = r // 2, r % 2
-        kv_ref[64 * u : 64 * u + 64, HD * half : HD * half + HD] = kv.astype(BF16)
-
-
-def whole(dims):
-    return pl.BlockSpec(dims, lambda i, *_: (0,) * len(dims))
-
-
-def project(runs, core, xs, wq, table):
-    return pl.pallas_call(
-        project_kernel,
-        out_shape=(shape((1024, Q_DEV)), shape((512, 128))),
-        grid_spec=pltpu.PrefetchScalarGridSpec(
-            num_scalar_prefetch=2,
-            grid=(4,),
-            in_specs=[
-                pl.BlockSpec((256, D), lambda i, *_: (i, 0)),
-                whole((320, D)),
-                whole((2048, 128)),
-            ],
-            out_specs=[
-                pl.BlockSpec((256, Q_DEV), lambda i, *_: (i, 0)),
-                pl.BlockSpec((128, 128), lambda i, *_: (i, 0)),
-            ],
-        ),
-        compiler_params=pltpu.CompilerParams(vmem_limit_bytes=40 * 2**20),
-        name="project",
-    )(runs, core, xs, wq, table)
-
-
-def project_back_kernel(runs, core, dq_ref, dkv_ref, xs_ref, wq_ref, table_ref, parts_ref, gwq_ref, acc):
-    seq = pl.program_id(0)
-    is_key = core[0] == 0
-    kv = []
-    for r in range(4):
-        table = table_rows(table_ref, runs[seq * 4 + r])
-        half, u = r // 2, r % 2
-        plain = dkv_ref[64 * u : 64 * u + 64, HD * half : HD * half + HD]
-        kv.append(jnp.where(is_key, rotate(plain, table, back=True), plain))
-    grads = jnp.concatenate([dq_ref[...], jnp.concatenate(kv, axis=0).astype(BF16)], axis=1)
-    parts_ref[...] = dot(grads, wq_ref[...]).astype(BF16)
-    term = dot_first(grads, xs_ref[...])
-
-    @pl.when(seq == 0)
-    def _():
-        acc[...] = term
-
-    @pl.when(seq > 0)
-    def _():
-        acc[...] += term
-
-    @pl.when(seq == 3)
-    def _():
-        gwq_ref[...] = acc[...].astype(BF16)
-
-
-def project_back(runs, core, dq, dkv, xs, wq, table):
-    return pl.pallas_call(
-        project_back_kernel,
-        out_shape=(shape((1024, D)), shape((320, D))),
-        grid_spec=pltpu.PrefetchScalarGridSpec(
-            num_scalar_prefetch=2,
-            grid=(4,),
-            in_specs=[
-                pl.BlockSpec((256, Q_DEV), lambda i, *_: (i, 0)),
-                pl.BlockSpec((128, 128), lambda i, *_: (i, 0)),
-                pl.BlockSpec((256, D), lambda i, *_: (i, 0)),
-                whole((320, D)),
-                whole((2048, 128)),
-            ],
-            out_specs=[
-                pl.BlockSpec((256, D), lambda i, *_: (i, 0)),
-                whole((320, D)),
-            ],
-            scratch_shapes=[pltpu.VMEM((320, D), F32)],
-        ),
-        compiler_params=pltpu.CompilerParams(vmem_limit_bytes=40 * 2**20),
-        name="project_back",
-    )(runs, core, dq, dkv, xs, wq, table)
-
-
 def chips_in_sequence(me):
     return [(dz, dl) for dz in range(4) for dl in (0, 1)][1:]
 
 
-def keys_kernel(
-    kv, pos, cot, wout, wswap, kvs, poss, cots, wo, wnear, send, recv, os_, orr, ws, wr, local
+def begin_kernel(
+    tokens, gain, pos, trig, wqkv, wgu, wdn, cot, wout,
+    q, kv_table, trigs, xs_out, wq_out, poss, kvs, places, cots, wo, wswap, wnear,
+    low, xs, wq, kv,
+    send, recv, qs, qr, os_, orr, ws, wr, ns, nr, local,
 ):
     me = Place()
     partner = {"xl": 1 - me.xl, "xh": 1 - me.xh}
     core = me.at(core=1 - me.c)
+    members = group_members(me)
+    others = [
+        me.at(y=lax.rem(me.y + dy, 4), core=c, **partner) for dy in range(4) for c in (0, 1)
+    ]
     far = [
         me.at(dz=dz, xl=(1 - me.xl) if dl else me.xl) for dz, dl in chips_in_sequence(me)
     ]
-    others = [
-        me.at(y=lax.rem(me.y + dy, 4), core=c, **partner) for dy in range(4) for c in (0, 1)
-    ]
-    depth = [me.at(dz=1), me.at(dz=-1)]
-    greet(far + group_members(me) + others)
+    greet(members + others + far)
     edges = Edges(send, recv)
+    mine = 2 * me.y + me.c
     chip = 2 * me.z + me.xl
-    steps = [
-        pltpu.make_async_remote_copy(
-            src_ref=wswap,
-            dst_ref=wnear.at[i],
-            send_sem=ws.at[i],
-            recv_sem=wr.at[i],
-            device_id=depth[i],
-            device_id_type=pl.DeviceIdType.MESH,
-        )
-        for i in range(2)
-    ]
-    keeps = [
-        pltpu.make_async_copy(kv, kvs.at[me.c, chip], local.at[0]),
-        pltpu.make_async_copy(pos, poss.at[chip], local.at[1]),
-        pltpu.make_async_copy(cot, cots.at[2 * me.y + me.c], local.at[2]),
-    ]
-    for d in keeps:
-        d.start()
-    pos_copies = [edges.copy(pos, poss.at[chip], d) for d in far]
-    kv_copies = [edges.copy(kv, kvs.at[me.c, chip], d) for d in far]
-    over = [edges.copy(kv, kvs.at[me.c, chip], core)]
-    ring = RingGather(me, edges, cot, cots)
-
+
+    spread = pl.ds(pl.multiple_of(512 * me.z, 512), 512)
+    spread_rows = pl.ds(pl.multiple_of(64 * me.z, 64), 64)
     own = 2 * me.y + me.xh
     own_column = me.c == 0
     to_xl = jnp.where(own_column, me.xl, 1 - me.xl)
     to_xh = jnp.where(own_column, me.xh, 1 - me.xh)
     blocks = []
+    for i in range(5):
+        y, to_core, slot = block_place(5 * own + i)
+        stays = own_column & (y == me.y) & (to_core == me.c)
+        src = wqkv.at[pl.ds(64 * i, 64), spread]
+        dst = wq.at[pl.ds(pl.multiple_of(64 * slot, 64), 64), spread]
+        target = (me.z, to_xl, to_core, y, to_xh)
+        send_block(me, src, dst, qs.at[i], qr.at[slot], target, stays)
+        blocks.append((src, qs.at[i], stays))
+
+    def norm(at):
+        rows = tokens[at, :].astype(F32)
+        inverse = lax.rsqrt(mean_last(rows * rows) + EPSILON)
+        low[at, :] = (rows * inverse * gain[...]).astype(BF16)
+
+    in_chunks(norm)
+    keep = pltpu.make_async_copy(low, xs.at[mine], local.at[0])
+    keep.start()
+    keep_pos = pltpu.make_async_copy(pos, poss.at[mine], local.at[1])
+    keep_pos.start()
+    pos_copies = [edges.copy(pos, poss.at[mine], m) for m in members]
+    trigs[mine] = trig[...]
+    trig_copies = [edges.copy(trig, trigs.at[mine], me.at(dy=k)) for k in (1, 2, 3)]
+    trig_over = [edges.copy(trig, trigs.at[mine], core)]
+    ring = RingGather(me, edges, low, xs)
+    moved = me.c != me.xh
+    swaps = swap_copies(me, wgu, wdn, wswap, ws, wr)
+
+    @pl.when(moved)
+    def _():
+        for d in swaps:
+            d.start()
+
+    for i in range(5):
+        wait_got(wq.at[pl.ds(64 * i, 64), spread], qr.at[i])
+    wq_copies = [
+        edges.copy(wq.at[:, spread], wq.at[:, spread], me.at(dz=k)) for k in (1, 3, 2)
+    ]
+    for k, d in zip((1, 2, 3), trig_copies):
+        d.wait_recv()
+        ref = trigs.at[2 * lax.rem(me.y - k + 4, 4) + me.c]
+        trig_over.append(edges.copy(ref, ref, core))
+    ring.relay()
+    keep_pos.wait()
+    for d in pos_copies + trig_over:
+        d.wait_recv()
+    keep.wait()
+    for d in wq_copies:
+        d.wait_recv()
+    wq_save = pltpu.make_async_copy(wq, wq_out, local.at[2])
+    wq_save.start()
+    is_key = me.c == 0
+
+    def compute(pair):
+        at = pl.ds(2 * pair, 2)
+        projected = dot_last(xs[at].reshape(2 * TOK, D), wq[...])
+        for r in range(4):
+            half, u = r // 2, r % 2
+            rows = rotary_of(trigs[2 * pair + half], u)
+            values = projected[64 * r : 64 * r + 64]
+            heads = [rotate(values[:, HD * h : HD * h + HD], rows) for h in range(4)]
+            query = jnp.concatenate(heads, axis=1).astype(BF16)
+            to = pl.ds(pl.multiple_of(2 * TOK * pair + 64 * r, 64), 64)
+            q[to, :] = (query.astype(F32) * 0.125).astype(BF16)
+            rows = jnp.concatenate(
+                [
+                    jnp.where(is_key, rows[:, :HD], 1.0),
+                    jnp.where(is_key, rows[:, HD:], 0.0),
+                ],
+                axis=1,
+            )
+            to = pl.ds(pl.multiple_of(TOK * pair + 64 * u, 64), 64)
+            lanes = slice(HD * half, HD * half + HD)
+            kv[to, lanes] = rotate(values[:, Q_DEV:], rows).astype(BF16)
+            kv_table[0, to, lanes] = rows[:, :HD]
+            kv_table[1, to, lanes] = rows[:, HD:]
+
+    def pair(k):
+        return lax.rem(me.y + k, 4)
+
+    ring.from_core(0, 1)
+    compute(pair(0))
+    ring.near()
+    ring.from_core(1, 5)
+
+    def sides(i, _):
+        compute(pair(1 + 2 * i))
+        return 0
+
+    lax.fori_loop(0, 2, sides, 0)
+    ring.far()
+    ring.from_core(5, 7)
+    compute(pair(2))
+
+    keeps = [
+        pltpu.make_async_copy(kv, kvs.at[me.c, chip], local.at[0]),
+        pltpu.make_async_copy(poss, places.at[chip], local.at[1]),
+        pltpu.make_async_copy(xs, xs_out, local.at[4]),
+        pltpu.make_async_copy(cot, cots.at[mine], local.at[5]),
+    ]
+    for d in keeps:
+        d.start()
+    pos_copies = [edges.copy(poss, places.at[chip], d) for d in far]
+    kv_copies = [edges.copy(kv, kvs.at[me.c, chip], d) for d in far]
+    over = [edges.copy(kv, kvs.at[me.c, chip], core)]
+    ring = RingGather(me, edges, cot, cots)
     for i in range(8):
         dy, other = i // 2, i % 2
         y = lax.rem(me.y + dy, 4)
         to_core = me.c if other == 0 else 1 - me.c
         stays = own_column if i == 0 else me.c < 0
-        src = wout.at[:, pl.ds(pl.multiple_of(Q_DEV * (2 * y + to_core), Q_DEV), Q_DEV)]
+        cols = pl.ds(pl.multiple_of(Q_DEV * (2 * y + to_core), Q_DEV), Q_DEV)
+        src = wout.at[spread_rows, cols]
+        dst = wo.at[own, spread_rows]
         target = (me.z, to_xl, to_core, y, to_xh)
-        send_block(me, src, wo.at[own], os_.at[i], orr.at[own], target, stays)
+        send_block(me, src, dst, os_.at[i], orr.at[own], target, stays)
         blocks.append((src, os_.at[i], stays))
-
-    @pl.when(me.c != me.xh)
+    steps = [
+        pltpu.make_async_remote_copy(
+            src_ref=wswap,
+            dst_ref=wnear.at[i],
+            send_sem=ns.at[i],
+            recv_sem=nr.at[i],
+            device_id=me.at(dz=1 - 2 * i),
+            device_id_type=pl.DeviceIdType.MESH,
+        )
+        for i in range(2)
+    ]
+
+    @pl.when(moved)
     def _():
+        for d in swaps:
+            d.wait()
         for d in steps:
             d.start()
 
@@ -640,43 +587,60 @@
         source = 2 * lax.rem(me.z - dz + 4, 4) + ((1 - me.xl) if dl else me.xl)
         ref = kvs.at[me.c, source]
         over.append(edges.copy(ref, ref, core))
+    for i in range(8):
+        wait_got(wo.at[i, spread_rows], orr.at[i])
+    ref = wo.at[:, spread_rows]
+    wo_copies = [edges.copy(ref, ref, me.at(dz=k)) for k in (1, 3, 2)]
     ring.rest()
-    for d in over + pos_copies:
+    for d in over + pos_copies + wo_copies:
         d.wait_recv()
-    for i in range(8):
-        wait_got(wo.at[i], orr.at[i])
     for src, sem, stays in blocks:
         wait_sent(src, sem, stays)
 
-    @pl.when(me.c != me.xh)
+    @pl.when(moved)
     def _():
         for d in steps:
             d.wait()
 
     edges.finish()
-    for d in keeps:
+    for d in keeps + [wq_save]:
         d.wait()
 
 
-def exchange_keys(kv, pos, cot, wout, wswap):
+def begin(tokens, gain, pos, trig, wqkv, wgu, wdn, cot, wout):
     return pl.pallas_call(
-        keys_kernel,
+        begin_kernel,
         out_shape=(
+            shape((1024, Q_DEV)),
+            shape((2, 512, 128), F32),
+            shape((8, 64, 128), F32),
+            shape((8, TOK, D)),
+            shape((320, D)),
+            shape((8, 8, TOK), jnp.int32),
             shape((2, 8, 512, 128)),
             shape((8, 8, 8, TOK), jnp.int32),
             shape((8, TOK, D)),
             shape((8, 256, Q_DEV)),
+            shape((QUARTER, D)),
             shape((2, QUARTER, D)),
         ),
-        in_specs=[ANY] * 5,
-        out_specs=(ANY,) * 5,
-        scratch_shapes=sems(7 + 7 + 8 + GATHER_EDGES)
+        in_specs=[VMEM, VMEM, VMEM, VMEM] + [ANY] * 5,
+        out_specs=(VMEM, VMEM, VMEM) + (ANY,) * 9,
+        scratch_shapes=[
+            pltpu.VMEM((TOK, D), BF16),
+            pltpu.VMEM((8, TOK, D), BF16),
+            pltpu.VMEM((320, D), BF16),
+            pltpu.VMEM((512, 128), BF16),
+        ]
+        + sems(7 + 7 + 6 + 2 * GATHER_EDGES + 7 + 7 + 8)
+        + sems(5)
         + sems(8)
         + sems(2)
-        + [pltpu.SemaphoreType.DMA((3,))],
-        compiler_params=remote_params(1),
-        name="exchange_keys",
-    )(kv, pos, cot, wout, wswap)
+        + sems(2)
+        + [pltpu.SemaphoreType.DMA((6,))],
+        compiler_params=remote_params(0),
+        name="begin",
+    )(tokens, gain, pos, trig, wqkv, wgu, wdn, cot, wout)
 
 
 def split_heads(rows):
@@ -810,7 +774,7 @@
 
 
 def attend_back_kernel(
-    key_runs, query_runs, q_ref, kv_ref, da_ref, ot_ref, lse_ref, table_ref,
+    key_runs, query_runs, q_ref, kv_ref, da_ref, ot_ref, lse_ref, trig_ref,
     dq_ref, dkv_ref, keys, values, dkeys, dvalues, dq_acc,
 ):
     seq = pl.program_id(0)
@@ -854,7 +818,10 @@
             def _():
                 tiles(start, n + 1, True)
 
-        table = table_rows(table_ref, run)
+        pair_rows = trig_ref[r // 2]
+        table = jnp.where(
+            lax.rem(r, 2) == 0, rotary_of(pair_rows, 0), rotary_of(pair_rows, 1)
+        )
         dq = (dq_acc[...] * 0.125).T
         heads = [rotate(dq[64 * h : 64 * h + 64], table, back=True) for h in range(4)]
         dq_ref[rows, :] = jnp.concatenate(heads, axis=1).astype(BF16)
@@ -869,7 +836,7 @@
         dkv_ref[1, chip, rows, lanes] = dvalues[at, :].astype(BF16)
 
 
-def attend_back(key_runs, query_runs, q, kv, grad, ot, lse, table):
+def attend_back(key_runs, query_runs, q, kv, grad, ot, lse, trigs):
     return pl.pallas_call(
         attend_back_kernel,
         out_shape=(shape((1024, 256)), shape((2, 8, 512, 128))),
@@ -882,7 +849,7 @@
                 pl.BlockSpec((256, 256), lambda i, *_: (i, 0)),
                 pl.BlockSpec((4, HD, 256), lambda i, *_: (i, 0, 0)),
                 pl.BlockSpec((4, 1, 256), lambda i, *_: (i, 0, 0)),
-                whole((2048, 128)),
+                pl.BlockSpec((2, 64, 128), lambda i, *_: (i, 0, 0)),
             ],
             out_specs=[
                 pl.BlockSpec((256, 256), lambda i, *_: (i, 0)),
@@ -898,22 +865,7 @@
         ),
         compiler_params=pltpu.CompilerParams(vmem_limit_bytes=40 * 2**20),
         name="attend_back",
-    )(key_runs, query_runs, q, kv, grad, ot, lse, table)
-
-
-ROWS = 16
-
-
-def in_chunks(step):
-    def one(i, _):
-        step(pl.ds(pl.multiple_of(i * ROWS, ROWS), ROWS))
-        return 0
-
-    lax.fori_loop(0, TOK // ROWS, one, 0)
-
-
-def mean_last(rows):
-    return jnp.mean(rows, axis=-1, keepdims=True)
+    )(key_runs, query_runs, q, kv, grad, ot, lse, trigs)
 
 
 PART = 3 * FF_DEV // 2
@@ -921,20 +873,21 @@
 
 
 class RingSum:
-    def __init__(self, me, edges, along_z, src, start, width, step, relayed, last):
+    def __init__(self, me, edges, along_z, src, start, rows, width, step, relayed, last):
         self.edges, self.src, self.start, self.width, self.step = edges, src, start, width, step
+        self.rows, self.half = rows, rows // 2
         self.relayed, self.last = relayed, last
         self.here = me.z if along_z else x_of(me)
         self.up = around(me, 1, 0) if along_z else around(me, 0, 1)
         self.down = around(me, -1, 0) if along_z else around(me, 0, 3)
-        self.a, self.b = pl.ds(0, PART_HALF), pl.ds(PART_HALF, PART_HALF)
+        self.a, self.b = pl.ds(0, self.half), pl.ds(self.half, self.half)
 
     def columns(self, k):
         at = self.width * lax.rem(self.here + k, 4)
         return pl.ds(pl.multiple_of(at, self.width), self.width)
 
     def piece(self, k, half):
-        rows = pl.ds(self.start + PART_HALF * half, PART_HALF)
+        rows = pl.ds(self.start + self.half * half, self.half)
         return self.src.at[rows, self.columns(k)]
 
     def far(self):
@@ -948,7 +901,7 @@
         self.d_a = self.edges.copy(self.piece(3, 0), self.last.at[1, self.a], self.down)
 
     def add(self, k, half):
-        step, start, cols = self.step, self.start + PART_HALF * half, self.columns(k)
+        step, start, cols = self.step, self.start + self.half * half, self.columns(k)
 
         def one(i, _):
             at = pl.ds(pl.multiple_of(start + i * step, 16), step)
@@ -958,7 +911,7 @@
             ).astype(BF16)
             return 0
 
-        lax.fori_loop(0, PART_HALF // step, one, 0)
+        lax.fori_loop(0, self.half // step, one, 0)
 
     def second(self):
         self.r_a.wait_recv()
@@ -983,7 +936,7 @@
             ).astype(BF16)
             return 0
 
-        lax.fori_loop(0, PART // step, one, 0)
+        lax.fori_loop(0, self.rows // step, one, 0)
 
 
 SUM_EDGES = 6
@@ -1141,8 +1094,8 @@
     two.send_core(2)
     two.add_core(0)
 
-    z_sum = RingSum(me, edges, True, w, 0, 512, 48, z_relayed, z_last)
-    x_sum = RingSum(me, edges, False, w, PART, 512, 48, x_relayed, x_last)
+    z_sum = RingSum(me, edges, True, w, 0, PART, 512, 48, z_relayed, z_last)
+    x_sum = RingSum(me, edges, False, w, PART, PART, 512, 48, x_relayed, x_last)
     split = PART - FF_DEV
 
     def z_task(k):
@@ -1205,12 +1158,12 @@
     branch.near()
     branch.add_core(0)
     z_sum.total(z_q)
-    z_two = RingSum(me, edges, False, z_q, 0, 128, 176, z_relayed2, z_last2)
+    z_two = RingSum(me, edges, False, z_q, 0, PART, 128, 176, z_relayed2, z_last2)
     z_two.far()
     z_two.near_up()
     z_two.near_down()
     x_sum.total(x_q)
-    x_two = RingSum(me, edges, True, x_q, 0, 128, 176, x_relayed2, x_last2)
+    x_two = RingSum(me, edges, True, x_q, 0, PART, 128, 176, x_relayed2, x_last2)
     x_two.far()
     x_two.near_up()
     x_two.near_down()
@@ -1290,10 +1243,186 @@
     return found
 
 
-def key_grads_kernel(
-    dkv, gwo, z_piece, out, wo_out, z_all, got, both, last, wo_own, wo_got, wo_piece, wo_all,
-    send, recv, ws, wr, local, ds, dr, zs, zr,
+def swapped_pairs(rows):
+    return jnp.concatenate([halves_swapped(rows[:, :HD]), halves_swapped(rows[:, HD:])], axis=1)
+
+
+class RingBlocks:
+    def __init__(self, me, edges, ref, columns):
+        self.me, self.edges, self.ref, self.columns = me, edges, ref, columns
+        rows = ref.shape[0]
+        self.halves = (pl.ds(0, rows // 2), pl.ds(rows // 2, rows // 2))
+        self.up, self.down = me.at(dz=1), me.at(dz=-1)
+        self.up_a = self.send(0, 0, self.up)
+        self.down_b = self.send(0, 1, self.down)
+        self.up_b = self.send(0, 1, self.up)
+        self.down_a = self.send(0, 0, self.down)
+
+    def block(self, dz):
+        return self.ref.at[:, self.columns(lax.rem(self.me.z + dz + 4, 4))]
+
+    def send(self, dz, half, device):
+        cols = self.columns(lax.rem(self.me.z + dz + 4, 4))
+        ref = self.ref.at[self.halves[half], cols]
+        return self.edges.copy(ref, ref, device)
+
+    def relay(self):
+        self.up_a.wait_recv()
+        self.on_a = self.send(-1, 0, self.up)
+        self.down_b.wait_recv()
+        self.on_b = self.send(1, 1, self.down)
+
+    def near(self):
+        self.up_b.wait_recv()
+        self.down_a.wait_recv()
+
+    def far(self):
+        self.on_a.wait_recv()
+        self.on_b.wait_recv()
+
+
+class PlaneGather:
+    def __init__(self, me, edges, z_piece, x_piece, z_all, x_all, send, recv):
+        self.me, self.edges, self.z_all, self.x_all = me, edges, z_all, x_all
+        self.send, self.recv, self.z_piece, self.x_piece = send, recv, z_piece, x_piece
+        self.stays = me.c == me.xh
+        self.core = me.at(core=1 - me.c)
+        self.side = me.at(xl=1 - me.xl)
+        across = me.at(core=1 - me.c, xl=1 - me.xl, xh=1 - me.xh)
+        x = x_of(me)
+        self.held = jnp.where(self.stays, x, 3 - x)
+        for i, (piece, ref, at) in enumerate(
+            ((z_piece, z_all, 4 * me.z + x), (x_piece, x_all, 4 * x + me.z))
+        ):
+            dst = ref.at[columns(128)(at)]
+            send_block(me, piece, dst, send.at[i], recv.at[i], across, self.stays)
+
+    def z_columns(self, z):
+        return pl.ds(pl.multiple_of(512 * z + 256 * self.me.c, 256), 256)
+
+    def x_columns(self, z):
+        return pl.ds(pl.multiple_of(512 * self.held + 128 * z, 128), 128)
+
+    def sideways(self):
+        own = self.z_all.at[columns(128)(4 * self.me.z + self.held)]
+        wait_got(own, self.recv.at[0])
+        self.z_side = self.edges.copy(own, own, self.side)
+        own = self.x_all.at[:, self.x_columns(self.me.z)]
+        wait_got(own, self.recv.at[1])
+        self.x_ring = RingBlocks(self.me, self.edges, self.x_all, self.x_columns)
+        self.x_side = [self.edges.copy(own, own, self.side)]
+
+    def along(self):
+        self.z_side.wait_recv()
+        self.z_ring = RingBlocks(self.me, self.edges, self.z_all, self.z_columns)
+        own = self.z_ring.block(0)
+        self.over = [self.edges.copy(own, own, self.core)]
+        self.x_ring.relay()
+
+    def to_side(self, dz):
+        ref = self.x_ring.block(dz)
+        self.x_side.append(self.edges.copy(ref, ref, self.side))
+
+    def to_core(self, dz):
+        ref = self.z_ring.block(dz)
+        self.over.append(self.edges.copy(ref, ref, self.core))
+
+    def near(self):
+        self.x_ring.near()
+        self.to_side(1)
+        self.to_side(-1)
+        self.z_ring.relay()
+        self.x_ring.far()
+        self.to_side(2)
+
+    def far(self):
+        self.z_ring.near()
+        self.to_core(1)
+        self.to_core(-1)
+        self.z_ring.far()
+        self.to_core(2)
+        for d in self.x_side:
+            d.wait_recv()
+        half = self.x_all.at[:, pl.ds(pl.multiple_of(1024 * self.me.c, 1024), 1024)]
+        self.over.append(self.edges.copy(half, half, self.core))
+
+    def finish(self):
+        for d in self.over:
+            d.wait_recv()
+        wait_sent(self.z_piece, self.send.at[0], self.stays)
+        wait_sent(self.x_piece, self.send.at[1], self.stays)
+
+
+PLANE_EDGES = 1 + 2 * SUM_EDGES + 4 + 5
+
+
+class TwoSums:
+    def __init__(self, me, edges, src, rows, steps, scratch):
+        self.me, self.edges, self.rows, self.steps = me, edges, rows, steps
+        self.q, self.out = scratch[4:6], scratch[10:12]
+        self.scratch = scratch
+        start = (0, rows[0])
+        self.one = [
+            RingSum(
+                me, edges, i == 0, src, start[i], rows[i], 512, steps[0][i],
+                scratch[2 * i], scratch[2 * i + 1],
+            )
+            for i in (0, 1)
+        ]
+        for ring in self.one:
+            ring.far()
+            ring.near_up()
+            ring.near_down()
+
+    def second(self):
+        for ring in self.one:
+            ring.second()
+
+    def cross(self):
+        self.two = []
+        for i in (0, 1):
+            self.one[i].total(self.q[i])
+            ring = RingSum(
+                self.me, self.edges, i == 1, self.q[i], 0, self.rows[i], 128,
+                self.steps[1][i], self.scratch[6 + 2 * i], self.scratch[7 + 2 * i],
+            )
+            ring.far()
+            ring.near_up()
+            ring.near_down()
+            self.two.append(ring)
+
+    def fourth(self):
+        for ring in self.two:
+            ring.second()
+
+    def total(self):
+        for i in (0, 1):
+            self.two[i].total(self.out[i])
+
+
+def two_sums_scratch(rows):
+    found = []
+    for r in rows:
+        found += [pltpu.VMEM((2, r // 2, 512), BF16), pltpu.VMEM((2, r, 512), BF16)]
+    found += [pltpu.VMEM((r, 512), BF16) for r in rows]
+    for r in rows:
+        found += [pltpu.VMEM((2, r // 2, 128), BF16), pltpu.VMEM((2, r, 128), BF16)]
+    return found + [pltpu.VMEM((r, 128), BF16) for r in rows]
+
+
+WQ_ROWS = (128, 192)
+WO_ROWS = (128, 128)
+
+
+def ending_kernel(
+    dkv, dq, kv_table, wq, tokens, gain, grad_middle, gain_two, z_piece, x_piece, gwo_in, xs_in,
+    grad_tokens, gains, wq_out, wo_out, z_all, x_all,
+    kv_got, kv_both, kv_last, dkv_low, xs, grads, grads_t, parts, gwq, gwo,
+    got, both, relayed, last, wq_all, wo_all, mine, near, near_sum, owners,
+    *rest,
 ):
+    wq_scratch, wo_scratch = rest[:12], rest[12:24]
+    (send, recv, ds, dr, es, er, ps, pr, gs, gr, hs, hr, local) = rest[24:]
     me = Place()
     core = me.at(core=1 - me.c)
     far = [
@@ -1301,115 +1430,105 @@
     ]
     greet(plane_devices(me) + group_members(me)[1:])
     edges = Edges(send, recv)
+    place = 4 * me.z + x_of(me)
+    turned = 4 * x_of(me) + me.z
+    rank = 2 * me.y + me.c
+    load_x = pltpu.make_async_copy(xs_in, xs, local.at[0])
+    load_x.start()
+    load_wo = pltpu.make_async_copy(gwo_in, gwo, local.at[1])
+    load_wo.start()
+
     order = []
     for dz, dl in chips_in_sequence(me) + [(0, 0)]:
         chip = 2 * lax.rem(me.z + dz, 4) + ((1 - me.xl) if dl else me.xl)
-        order.append((chip, edges.copy(dkv.at[1 - me.c, chip], got.at[chip], core)))
-    wo_sum = SumOfSixteen(me, gwo, row_block(128), wo_own, wo_got, ws, wr, local)
+        order.append((chip, edges.copy(dkv.at[1 - me.c, chip], kv_got.at[chip], core)))
+    plane = PlaneGather(me, edges, z_piece, x_piece, z_all, x_all, ps, pr)
     far_copies = []
     for i, (chip, d) in enumerate(order):
         d.wait_recv()
-        both[chip] = (dkv[me.c, chip].astype(F32) + got[chip].astype(F32)).astype(BF16)
+        kv_both[chip] = (dkv[me.c, chip].astype(F32) + kv_got[chip].astype(F32)).astype(BF16)
         if i < 7:
-            far_copies.append(edges.copy(both.at[chip], last.at[i], far[i]))
-    place = 4 * me.z + x_of(me)
-    z_deliver = Deliver(me, zs, zr)
-    z_deliver.to_owner(
-        z_piece, z_all.at[columns(128)(place)], me.z // 2, me.y, me.c
-    )
-    total = both[2 * me.z + me.xl].astype(F32)
-    for i, d in enumerate(far_copies):
+            far_copies.append(edges.copy(kv_both.at[chip], kv_last.at[i], far[i]))
+    load_wo.wait()
+    wo_sum = TwoSums(me, edges, gwo, WO_ROWS, ((64, 64), (64, 64)), wo_scratch)
+    plane.sideways()
+
+    def query_part(i, _):
+        at = pl.ds(pl.multiple_of(2 * TOK * i, 2 * TOK), 2 * TOK)
+        rows = dq[at, :]
+        grads[at, :Q_DEV] = rows
+        grads_t[:Q_DEV, at] = rows.astype(F32).T.astype(BF16)
+        return 0
+
+    lax.fori_loop(0, 4, query_part, 0)
+    plane.along()
+    wo_sum.second()
+    for d in far_copies:
         d.wait_recv()
-        total = total + last[i].astype(F32)
-    out[...] = total
-    wo_piece[...] = wo_sum.total().astype(BF16)
-    deliver = Deliver(me, ds, dr)
-    rank = 2 * me.y + me.c
-    dst = wo_all.at[
-        pl.ds(pl.multiple_of(128 * me.xl, 128), 128),
-        pl.ds(pl.multiple_of(Q_DEV * rank, Q_DEV), Q_DEV),
-    ]
-    deliver.to_owner(wo_piece, dst, me.y // 2, me.z, me.xh)
-    half = wo_all.at[:, pl.ds(pl.multiple_of(1024 * me.c, 1024), 1024)]
-    wait_got(half, dr)
-    over = edges.copy(half, half, core)
-    half = z_all.at[:, pl.ds(pl.multiple_of(1024 * me.c, 1024), 1024)]
-    wait_got(half, zr)
-    z_over = edges.copy(half, half, core)
-    over.wait_recv()
-    wo_out[...] = wo_all[...]
-    z_over.wait_recv()
-    wo_sum.finish()
-    deliver.finish()
-    z_deliver.finish()
-    edges.finish()
-
-
-def sum_key_grads(dkv, gwo, z_piece):
-    return pl.pallas_call(
-        key_grads_kernel,
-        out_shape=(shape((512, 128), F32), shape((256, D)), shape((PART, D))),
-        in_specs=[VMEM, ANY, VMEM],
-        out_specs=(VMEM, VMEM, ANY),
-        scratch_shapes=[
-            pltpu.VMEM((8, 512, 128), BF16),
-            pltpu.VMEM((8, 512, 128), BF16),
-            pltpu.VMEM((7, 512, 128), BF16),
-            pltpu.VMEM((128, Q_DEV), BF16),
-            pltpu.VMEM((15, 128, Q_DEV), BF16),
-            pltpu.VMEM((128, Q_DEV), BF16),
-            pltpu.VMEM((256, D), BF16),
+
+    def kv_total(at):
+        total = kv_both[2 * me.z + me.xl, at].astype(F32)
+        for i in range(7):
+            total = total + kv_last[i, at].astype(F32)
+        dkv_low[at, :] = (
+            total * kv_table[0, at, :] - swapped_pairs(total) * kv_table[1, at, :]
+        )
+
+    in_chunks(kv_total, 512)
+    for i in range(4):
+        for half in (0, 1):
+            rows = dkv_low[TOK * i : TOK * (i + 1), HD * half : HD * half + HD]
+            at = slice(TOK * (2 * i + half), TOK * (2 * i + half + 1))
+            grads[at, Q_DEV:] = rows.astype(BF16)
+            grads_t[Q_DEV:, at] = rows.T.astype(BF16)
+
+    load_x.wait()
+
+    def weight_block(i, _):
+        cols = pl.ds(pl.multiple_of(512 * i, 512), 512)
+        term = dot(grads_t[...], xs[:, :, cols].reshape(8 * TOK, 512))
+        gwq[:, cols] = term.astype(BF16)
+        return 0
+
+    lax.fori_loop(0, 4, weight_block, 0)
+    wq_sum = TwoSums(me, edges, gwq, WQ_ROWS, ((64, 48), (64, 96)), wq_scratch)
+    ring = RingScatter(me, edges, parts, (got, both, relayed, last))
+
+    def part(k):
+        pair = lax.rem(me.y + k, 4)
+        rows = grads[pl.ds(pl.multiple_of(2 * TOK * pair, 2 * TOK), 2 * TOK), :]
+
+        def block(i, _):
+            cols = pl.ds(pl.multiple_of(512 * i, 512), 512)
+            term = dot(rows, wq[:, cols]).astype(BF16)
+            parts[pl.ds(2 * pair, 2), :, cols] = term.reshape(2, TOK, 512)
+            return 0
+
+        lax.fori_loop(0, 4, block, 0)
+        ring.send_core(k)
+
+    part(2)
+    part(1)
+    ring.far()
+    part(3)
+    ring.near()
+    part(0)
+    ring.add_core(0)
+    wq_sum.second()
+    wo_sum.cross()
+    plane.near()
+    ring.second()
+    wq_sum.cross()
+    wo_sum.fourth()
+    wo_sum.total()
+    wo_deliver = Deliver(me, es, er)
+    for i, at in enumerate((place, turned)):
+        dst = wo_all.at[
+            pl.ds(pl.multiple_of(Q_DEV * rank + 128 * i, 128), 128),
+            pl.ds(pl.multiple_of(128 * lax.rem(at, 2), 128), 128),
         ]
-        + sems(17)
-        + [
-            pltpu.SemaphoreType.DMA((15,)),
-            pltpu.SemaphoreType.DMA,
-            pltpu.SemaphoreType.DMA,
-            pltpu.SemaphoreType.DMA((8,)),
-            pltpu.SemaphoreType.DMA,
-            pltpu.SemaphoreType.DMA((8,)),
-            pltpu.SemaphoreType.DMA,
-        ],
-        compiler_params=remote_params(4),
-        name="sum_key_grads",
-    )(dkv, gwo, z_piece)
-
-
-def closing_kernel(
-    parts, gwq, tokens, gain, grad_middle, gain_two, x_piece,
-    grad_tokens, gains, wq_out, x_all,
-    got, both, relayed, last, wq_own, wq_got, wq_piece, wq_all,
-    mine, near, near_sum, owners,
-    send, recv, ws, wr, local, ds, dr, gs, gr, hs, hr, xs_, xr,
-):
-    me = Place()
-    greet(plane_devices(me) + group_members(me)[1:])
-    edges = Edges(send, recv)
-    ring = RingScatter(me, edges, parts, (got, both, relayed, last))
-    for k in (2, 1, 3, 0):
-        ring.send_core(k)
-    wq_sum = SumOfSixteen(me, gwq, columns(128), wq_own, wq_got, ws, wr, local)
-    ring.far()
-    ring.near()
-    ring.add_core(0)
-    x_deliver = Deliver(me, xs_, xr)
-    x_deliver.to_owner(
-        x_piece, x_all.at[columns(128)(4 * x_of(me) + me.z)], me.xh, me.y, me.c
-    )
-    ring.second()
-    wq_piece[...] = wq_sum.total().astype(BF16)
-    deliver = Deliver(me, ds, dr)
-    piece = 4 * me.z + x_of(me)
-    for j in range(5):
-        block = own_block(me, j)
-        owner, slot = block // 5, lax.rem(block, 5)
-        dst = wq_all.at[
-            pl.ds(pl.multiple_of(64 * slot, 64), 64),
-            pl.ds(pl.multiple_of(128 * piece, 128), 128),
-        ]
-        deliver.to_owner(
-            wq_piece.at[pl.ds(64 * j, 64)], dst, me.z // 2, owner // 2, lax.rem(owner, 2)
-        )
+        wo_deliver.to_owner(wo_sum.out[i], dst, me.y // 2, at // 4, lax.rem(at // 2, 2))
+    wq_sum.fourth()
     ring.arrived()
     mine[...] = jnp.zeros_like(mine)
     mine[1:2, :] = gain_two[...]
@@ -1427,8 +1546,8 @@
 
     in_chunks(back)
 
-    def slice_of(rank):
-        return mine.at[:, pl.ds(pl.multiple_of(256 * rank, 256), 256)]
+    def slice_of(member):
+        return mine.at[:, pl.ds(pl.multiple_of(256 * member, 256), 256)]
 
     near_copies = []
     for k in range(1, 8):
@@ -1445,77 +1564,94 @@
         )
         d.start()
         near_copies.append(d)
-    own = mine[:, pl.ds(pl.multiple_of(256 * (2 * me.y + me.c), 256), 256)]
+    wq_sum.total()
+    wq_deliver = Deliver(me, ds, dr)
+    for j in range(5):
+        block = own_block(me, j)
+        owner, slot = block // 5, lax.rem(block, 5)
+        at = place if j < 2 else turned
+        piece = wq_sum.out[0] if j < 2 else wq_sum.out[1]
+        dst = wq_all.at[
+            pl.ds(pl.multiple_of(64 * slot, 64), 64),
+            pl.ds(pl.multiple_of(128 * at, 128), 128),
+        ]
+        src = piece.at[pl.ds(64 * (j if j < 2 else j - 2), 64)]
+        wq_deliver.to_owner(src, dst, at // 8, owner // 2, lax.rem(owner, 2))
+    own = mine[:, pl.ds(pl.multiple_of(256 * rank, 256), 256)]
     wait_got(near, gr)
     for k in range(7):
         own = own + near[k]
     near_sum[...] = own
-    far = Deliver(me, hs, hr)
+    gain_deliver = Deliver(me, hs, hr)
     for to_core in (0, 1):
-        far.to_owner(near_sum, owners.at[piece], to_core, me.y, me.c)
-
-    half = wq_all.at[:, pl.ds(pl.multiple_of(1024 * me.c, 1024), 1024)]
-    wait_got(half, dr)
-    over = edges.copy(half, half, me.at(core=1 - me.c))
+        gain_deliver.to_owner(near_sum, owners.at[place], to_core, me.y, me.c)
+    plane.far()
+
+    half = pl.ds(pl.multiple_of(1024 * me.c, 1024), 1024)
+    over = []
+    for ref, sem in ((wo_all.at[half], er), (wq_all.at[:, half], dr)):
+        wait_got(ref, sem)
+        over.append(edges.copy(ref, ref, core))
     wait_got(owners, hr)
     sum_all = owners[0]
     for k in range(1, 16):
         sum_all = sum_all + owners[k]
     gains[...] = sum_all
-    half = x_all.at[:, pl.ds(pl.multiple_of(1024 * me.c, 1024), 1024)]
-    wait_got(half, xr)
-    x_over = edges.copy(half, half, me.at(core=1 - me.c))
-    over.wait_recv()
+    for d in over:
+        d.wait_recv()
+    wo_out[...] = wo_all[...]
     wq_out[...] = wq_all[...]
-    x_over.wait_recv()
-    wq_sum.finish()
-    deliver.finish()
-    x_deliver.finish()
+    plane.finish()
+    for d in (wo_deliver, wq_deliver, gain_deliver):
+        d.finish()
     for d in near_copies:
         d.wait_send()
-    far.finish()
     edges.finish()
 
 
-def closing(parts, gwq, tokens, gain, grad_middle, gain_two, x_piece):
+def ending(dkv, dq, kv_table, wq, tokens, gain, grad_middle, gain_two, z_piece, x_piece, gwo, xs):
+    many = pltpu.SemaphoreType.DMA
     return pl.pallas_call(
-        closing_kernel,
+        ending_kernel,
         out_shape=(
             shape((TOK, D), F32),
             shape((8, 256), F32),
             shape((320, D)),
+            shape((D, 256)),
+            shape((PART, D)),
             shape((PART, D)),
         ),
-        in_specs=[VMEM, ANY] + [VMEM] * 5,
-        out_specs=(VMEM,) * 3 + (ANY,),
-        scratch_shapes=scatter_scratch()
+        in_specs=[VMEM] * 10 + [ANY] * 2,
+        out_specs=(VMEM,) * 4 + (ANY,) * 2,
+        scratch_shapes=[
+            pltpu.VMEM((8, 512, 128), BF16),
+            pltpu.VMEM((8, 512, 128), BF16),
+            pltpu.VMEM((7, 512, 128), BF16),
+            pltpu.VMEM((512, 128), F32),
+            pltpu.VMEM((8, TOK, D), BF16),
+            pltpu.VMEM((1024, 320), BF16),
+            pltpu.VMEM((320, 1024), BF16),
+            pltpu.VMEM((8, TOK, D), BF16),
+            pltpu.VMEM((320, D), BF16),
+            pltpu.VMEM((256, D), BF16),
+        ]
+        + scatter_scratch()
         + [
-            pltpu.VMEM((320, 128), BF16),
-            pltpu.VMEM((15, 320, 128), BF16),
-            pltpu.VMEM((320, 128), BF16),
             pltpu.VMEM((320, D), BF16),
+            pltpu.VMEM((D, 256), BF16),
             pltpu.VMEM((8, D), F32),
             pltpu.VMEM((7, 8, 256), F32),
             pltpu.VMEM((8, 256), F32),
             pltpu.VMEM((16, 8, 256), F32),
         ]
-        + sems(SCATTER_EDGES + 2)
-        + [
-            pltpu.SemaphoreType.DMA((15,)),
-            pltpu.SemaphoreType.DMA,
-            pltpu.SemaphoreType.DMA,
-            pltpu.SemaphoreType.DMA((40,)),
-            pltpu.SemaphoreType.DMA,
-            pltpu.SemaphoreType.DMA((7,)),
-            pltpu.SemaphoreType.DMA,
-            pltpu.SemaphoreType.DMA((16,)),
-            pltpu.SemaphoreType.DMA,
-            pltpu.SemaphoreType.DMA((8,)),
-            pltpu.SemaphoreType.DMA,
-        ],
-        compiler_params=remote_params(5),
-        name="closing",
-    )(parts, gwq, tokens, gain, grad_middle, gain_two, x_piece)
+        + two_sums_scratch(WQ_ROWS)
+        + two_sums_scratch(WO_ROWS)
+        + sems(15 + SCATTER_EDGES + PLANE_EDGES + 8 * SUM_EDGES + 2)
+        + [many((40,)), many, many((16,)), many, many((2,)), many((2,))]
+        + [many((7,)), many, many((16,)), many, many((2,))],
+        compiler_params=remote_params(3),
+        name="ending",
+    )(dkv, dq, kv_table, wq, tokens, gain, grad_middle, gain_two, z_piece, x_piece, gwo, xs)
 
 
 def widen_kernel(z_ref, x_ref, gu_ref, dn_ref):
@@ -1554,24 +1690,23 @@
 
 
 def body(hidden, positions, gain_attn, w_qkv, w_out, gain_mlp, w_gate_up, w_down, cotangent):
-    core = lax.axis_index("c").reshape(1)
     gain_one = gain_attn.astype(F32).reshape(1, D)
     gain_two = gain_mlp.astype(F32).reshape(1, D)
-    tokens = hidden[0].astype(F32)
-    inverse_one = lax.rsqrt(jnp.mean(tokens * tokens, axis=-1, keepdims=True) + EPSILON)
-    input_one = (tokens * inverse_one * gain_one).astype(BF16)
-    table = jnp.asarray(rotary_table())
     wgu = w_gate_up.reshape(2 * FF_DEV, D)
     wdn = w_down.T
-    xs, poss, wq, wswap = opening(
-        input_one, jnp.broadcast_to(positions, (8, TOK)), w_qkv, wgu, wdn
+    query, kv_table, trigs, xs, wq, poss, kvs, places, cots, wo, wswap, wnear = begin(
+        hidden[0],
+        gain_one,
+        jnp.broadcast_to(positions, (8, TOK)),
+        rotary_rows(positions[0]),
+        w_qkv,
+        wgu,
+        wdn,
+        cotangent[0],
+        w_out,
     )
-    xs = xs.reshape(1024, D)
-    wq = wq.reshape(320, D)
+    wo = wo.reshape(D, Q_DEV)
     query_runs = poss[:, 0, ::64].reshape(16) // 64
-    query, kv = project(query_runs, core, xs, wq, table)
-    kvs, places, cots, wo, wnear = exchange_keys(kv, poss, cotangent[0], w_out, wswap)
-    wo = wo.reshape(D, Q_DEV)
     key_runs = (
         places[:, :, 0, ::64].reshape(8, 4, 2, 2).transpose(1, 0, 2, 3).reshape(128) // 64
     )
@@ -1582,18 +1717,21 @@
     )
     gb = gbs.reshape(1024, D)
     grad_att = dot(gb, wo).astype(BF16)
-    grad_wo = dot_first(gb, att).astype(BF16)
-    dq, dkv = attend_back(key_runs, query_runs, query, kvs, grad_att, ot, lse, table)
-    dkv, grad_w_out, z_all = sum_key_grads(dkv, grad_wo, z_piece)
-    one_parts, gwq = project_back(query_runs, core, dq, dkv, xs, wq, table)
-    grad_tokens, gains, grad_w_qkv, x_all = closing(
-        one_parts.reshape(8, TOK, D),
-        gwq,
+    grad_wo = dot_first(att, gb).astype(BF16)
+    dq, dkv = attend_back(key_runs, query_runs, query, kvs, grad_att, ot, lse, trigs)
+    grad_tokens, gains, grad_w_qkv, grad_w_out, z_all, x_all = ending(
+        dkv,
+        dq,
+        kv_table,
+        wq,
         hidden[0],
         gain_one,
         grad_middle,
         gain_grad,
+        z_piece,
         x_piece,
+        grad_wo,
+        xs,
     )
     grad_gu, grad_dn = widen(z_all, x_all)
     return (
@@ -1601,7 +1739,7 @@
         grad_tokens[None],
         gains[0],
         grad_w_qkv.astype(F32),
-        grad_w_out.astype(F32),
+        grad_w_out.T.astype(F32),
         gains[1],
         grad_gu.reshape(2, FF_DEV, D),
         grad_dn.T,

time: 485 us -> 431 us (0.89)
  Pallas kernels: 439 us -> 389 us
    pallas_call x6 -> x2, Pallas kernels: 254 us -> 203 us  [the longest x1 116 us: ending(): pl.pallas_call(ending_kernel, out_shape=(shape((TOK, D), F32), shape((8,...]
    unnamed x62 -> x41, local copies, waits for them, and re-layouts: 18.9 us -> 15.3 us
where the time goes in v4:
time: 431 us; the launch traced here: 425 us
  Pallas kernels  389 us (90%)
  local copies, waits for them, and re-layouts  18.5 us (4%)
  matrix products  9.45 us (2%)
  other arithmetic  6.82 us (2%)
    pallas_call x1, Pallas kernels, feed_forward(): pl.pallas_call(feed_forward_kernel, out_shape=(shape((TOK, D)), shape((TO...  123 us
    pallas_call x1, Pallas kernels, ending(): pl.pallas_call(ending_kernel, out_shape=(shape((TOK, D), F32), shape((8,...  116 us
    pallas_call x1, Pallas kernels, begin(): pl.pallas_call(begin_kernel, out_shape=(shape((1024, Q_DEV)), shape((2, 5...  87.1 us
    pallas_call x1, Pallas kernels, attend_back(): pl.pallas_call(attend_back_kernel, out_shape=(shape((1024, 256)), shape((...  33.2 us
    pallas_call x1, Pallas kernels, attend(): pl.pallas_call(attend_kernel, out_shape=(shape((1024, 256)), shape((16, H...  22.3 us
    unnamed x41, local copies, waits for them, and re-layouts  15.3 us

profile of v4, /device:TPU:9, one launch (start us, length us, event | category | flops | bytes accessed | tf_op | source)
XLA Modules:
  0.0 425.1 jit_solution(14696393089945570842)
XLA Ops:
  0.6 0.7 convert_reduce_fusion
  1.3 0.1 convert_element_type.31
  1.4 0.7 broadcast_in_dim.16.pos
  2.1 0.7 reshape.92
  2.8 1.3 reshape.94
  4.0 0.2 multiply_cosine_fusion
  4.3 0.1 copy.29.trig
  4.3 0.0 copy-start.2
  4.3 1.0 copy-done.2
  5.4 1.2 copy-done.8
  6.6 1.0 copy-done.13
  7.6 87.1 %begin.1 = (bf16[1024,256]{1,0:T(8,128)(2,1)S(1)}, f32[2,512,128]{2,1,0:T(8,128)S(1)}, f32[8,64,128]{2,1,0:T(8,128)S(1)}, bf16[8,128,2048]{2,1,0:T(8,128)(2,1)},...) custom-call(bf16[128,2048]{1,0:T(8,128)(2,1)S(1)} %bitcast.31, ...), custom_call_target="tpu_custom_call" | custom-call | tf_op jit(solution)/shard_map/begin/pallas_call | solution.py:611
  94.7 0.0 copy-start.7
  94.7 1.0 copy-done.7
  95.8 0.7 slice.12
  96.5 0.1 copy.26
  96.6 0.1 slice.13
  96.7 0.5 broadcast.48
  97.2 0.7 reduce.7
  97.9 0.1 reshape_squeeze.7
  98.0 0.1 copy.27
  98.1 0.1 reshape.85
  98.3 1.6 copy-done
  99.9 22.3 %attend.1 = (bf16[1024,256]{1,0:T(8,128)(2,1)S(1)}, f32[16,64,256]{2,1,0:T(8,128)S(1)}, f32[16,1,256]{2,1,0:T(1,128)S(1)}) custom-call(s32[128]{0:T(128)S(1)} %and_select_fusion.1.key_runs, s32[16]{0:T(128)S(1)} %and_select_fusion.query_runs, bf16[1024,256]{1,0:T(8,128)(2,1)S(1)} %get-tuple-element.41.q_ref, bf16[2,8,512,128]{3,2,1,0:T(8,128)(2,1)S(1)} %copy-done), custom_call_target="tpu_custom_call" | custom-call | tf_op jit(solution)/shard_map/attend/pallas_call | solution.py:748
  122.2 0.0 copy-start.11
  122.2 3.3 convolution_convert_fusion
  125.5 123.2 %feed_forward.1 = (bf16[128,2048]{1,0:T(8,128)(2,1)}, f32[128,2048]{1,0:T(8,128)}, f32[1,2048]{1,0:T(1,128)}, bf16[8,128,2048]{2,1,0:T(8,128)(2,1)}, bf16[1056,1...) custom-call(bf16[8,128,2048]{2,1,0:T(8,128)(2,1)} %bitcast.39, bf16[128,2048]{1,0:T(8,128)(2,1)} %bitcast.30, ...), custom_call_target="tpu_custom_call" | custom-call | tf_op jit(solution)/shard_map/feed_forward/pallas_call | solution.py:1199
  248.8 3.9 convolution_convert_fusion.2.da_ref
  252.7 0.0 copy-start.12
  252.7 0.0 copy-start.3
  252.7 0.0 copy-start.10
  252.7 0.0 copy-start.14
  252.7 0.0 copy-start.15
  252.7 0.0 copy-start.16
  252.8 2.3 convolution_convert_fusion.1.gwo_in
  255.0 33.2 %attend_back.1 = (bf16[1024,256]{1,0:T(8,128)(2,1)S(1)}, bf16[2,8,512,128]{3,2,1,0:T(8,128)(2,1)S(1)}) custom-call(s32[128]{0:T(128)S(1)} %and_select_fusion.1.key_runs, s32[16]{0:T(128)S(1)} %and_select_fusion.query_runs, bf16[1024,256]{1,0:T(8,128)(2,1)S(1)} %get-tuple-element.41.q_ref, bf16[2,8,512,128]{3,2,1,0:T(8,128)(2,1)S(1)} %copy-done.1, ...), custom_call_target="tpu_custom_call" | custom-call | tf_op jit(solution)/shard_map/attend_back/pallas_call | solution.py:840
  288.2 0.0 copy-start.6
  288.2 1.3 copy-done.6
  289.6 115.8 %ending.1 = (f32[128,2048]{1,0:T(8,128)S(1)}, f32[8,256]{1,0:T(8,128)S(1)}, bf16[320,2048]{1,0:T(8,128)(2,1)}, bf16[2048,256]{1,0:T(8,128)(2,1)S(1)}, bf16[1056,...) custom-call(bf16[2,8,512,128]{3,2,1,0:T(8,128)(2,1)} %copy-done.6, bf16[1024,256]{1,0:T(8,128)(2,1)S(1)} %get-tuple-element.54.dq, ...), custom_call_target="tpu_custom_call" | custom-call | tf_op jit(solution)/shard_map/ending/pallas_call | solution.py:1614
  405.4 0.6 fusion
  406.0 0.2 convert_bitcast_fusion
  406.1 1.8 copy.28
  407.9 3.1 convert_element_type.35
  411.1 2.2 copy-done.4
  413.3 2.2 copy-done.5
  415.5 7.3 %widen.1 = (f32[1408,2048]{1,0:T(8,128)}, f32[704,2048]{1,0:T(8,128)}) custom-call(bf16[1056,2048]{1,0:T(8,128)(2,1)S(1)} %copy-done.4, bf16[1056,2048]{1,0:T(8,128)(2,1)S(1)} %copy-done.5), custom_call_target="tpu_custom_call" | custom-call | tf_op jit(solution)/shard_map/widen/pallas_call | solution.py:1675
  422.8 0.8 copy.32
  423.6 1.0 copy.33
  (24 shorter events, 0.1 us)
Async XLA Ops:
  4.3 1.1 copy-start.2
  5.4 1.2 copy-start.8
  6.6 1.0 copy-start.13
  94.7 1.1 copy-start.7
  95.8 29.7 %copy-start.9 = (bf16[8,256,256]{2,1,0:T(8,128)(2,1)}, bf16[8,256,256]{2,1,0:T(8,128)(2,1)S(1)}, u32[]{:S(2)}) copy-start(bf16[8,256,256]{2,1,0:T(8,128)(2,1)S(1)} %get-tuple-element.44) | copy-start | bytes 3145732
  98.3 1.6 copy-start
  122.2 3.3 copy-start.11
  248.8 3.9 copy-start.18
  252.7 2.3 copy-start.1
  252.7 2.3 copy-start.12
  252.7 36.8 %copy-start.3 = (bf16[1,128,2048]{2,1,0:T(8,128)(2,1)S(1)}, bf16[1,128,2048]{2,1,0:T(8,128)(2,1)}, u32[]{:S(2)}) copy-start(bf16[1,128,2048]{2,1,0:T(8,128)(2,1)} %param.9) | copy-start | bytes 1572868
  252.7 36.8 %copy-start.10 = (f32[128,2048]{1,0:T(8,128)S(1)}, f32[128,2048]{1,0:T(8,128)}, u32[]{:S(2)}) copy-start(f32[128,2048]{1,0:T(8,128)} %get-tuple-element.57.grad_middle) | copy-start | bytes 3145732
  252.7 36.8 %copy-start.14 = (bf16[1056,128]{1,0:T(8,128)(2,1)S(1)}, bf16[1056,128]{1,0:T(8,128)(2,1)}, u32[]{:S(2)}) copy-start(bf16[1056,128]{1,0:T(8,128)(2,1)} %get-tuple-element.59.z_piece) | copy-start | bytes 811012
  252.7 36.8 %copy-start.15 = (bf16[1056,128]{1,0:T(8,128)(2,1)S(1)}, bf16[1056,128]{1,0:T(8,128)(2,1)}, u32[]{:S(2)}) copy-start(bf16[1056,128]{1,0:T(8,128)(2,1)} %get-tuple-element.60.x_piece) | copy-start | bytes 811012
  252.7 36.8 %copy-start.16 = (f32[1,2048]{1,0:T(1,128)S(1)}, f32[1,2048]{1,0:T(1,128)}, u32[]{:S(2)}) copy-start(f32[1,2048]{1,0:T(1,128)} %get-tuple-element.58.gain_two) | copy-start | bytes 24580
  288.2 1.3 copy-start.6
  411.1 2.2 copy-start.4
  413.3 2.2 copy-start.5
  415.5 7.3 %copy-start.17 = (bf16[128,2048]{1,0:T(8,128)(2,1)S(1)}, bf16[128,2048]{1,0:T(8,128)(2,1)}, u32[]{:S(2)}) copy-start(bf16[128,2048]{1,0:T(8,128)(2,1)} %get-tuple-element.48) | copy-start | bytes 1572868

commit v5 on v4

--- a/solution.py
+++ b/solution.py
@@ -71,12 +71,18 @@
 
 
 def greet(devices):
-    barrier = pltpu.get_barrier_semaphore()
     for device in devices:
         pl.semaphore_signal(
-            barrier, inc=1, device_id=device, device_id_type=pl.DeviceIdType.MESH
+            pltpu.get_barrier_semaphore(),
+            inc=1,
+            device_id=device,
+            device_id_type=pl.DeviceIdType.MESH,
         )
-    pl.semaphore_wait(barrier, len(devices))
+    return len(devices)
+
+
+def met(count):
+    pl.semaphore_wait(pltpu.get_barrier_semaphore(), count)
 
 
 def group_members(me):
@@ -420,9 +426,9 @@
 
 def begin_kernel(
     tokens, gain, pos, trig, wqkv, wgu, wdn, cot, wout,
-    q, kv_table, trigs, xs_out, wq_out, poss, kvs, places, cots, wo, wswap, wnear,
+    q, kv_table, trigs, xs_out, wq_out, poss, kvs, places, cots, wo, wswap,
     low, xs, wq, kv,
-    send, recv, qs, qr, os_, orr, ws, wr, ns, nr, local,
+    send, recv, qs, qr, os_, orr, ws, wr, local,
 ):
     me = Place()
     partner = {"xl": 1 - me.xl, "xh": 1 - me.xh}
@@ -434,10 +440,18 @@
     far = [
         me.at(dz=dz, xl=(1 - me.xl) if dl else me.xl) for dz, dl in chips_in_sequence(me)
     ]
-    greet(members + others + far)
+    signalled = greet(members + others + far)
     edges = Edges(send, recv)
     mine = 2 * me.y + me.c
     chip = 2 * me.z + me.xl
+
+    def norm_rows():
+        def norm(at):
+            rows = tokens[at, :].astype(F32)
+            inverse = lax.rsqrt(mean_last(rows * rows) + EPSILON)
+            low[at, :] = (rows * inverse * gain[...]).astype(BF16)
+
+        in_chunks(norm)
 
     spread = pl.ds(pl.multiple_of(512 * me.z, 512), 512)
     spread_rows = pl.ds(pl.multiple_of(64 * me.z, 64), 64)
@@ -445,6 +459,8 @@
     own_column = me.c == 0
     to_xl = jnp.where(own_column, me.xl, 1 - me.xl)
     to_xh = jnp.where(own_column, me.xh, 1 - me.xh)
+    norm_rows()
+    met(signalled)
     blocks = []
     for i in range(5):
         y, to_core, slot = block_place(5 * own + i)
@@ -455,12 +471,6 @@
         send_block(me, src, dst, qs.at[i], qr.at[slot], target, stays)
         blocks.append((src, qs.at[i], stays))
 
-    def norm(at):
-        rows = tokens[at, :].astype(F32)
-        inverse = lax.rsqrt(mean_last(rows * rows) + EPSILON)
-        low[at, :] = (rows * inverse * gain[...]).astype(BF16)
-
-    in_chunks(norm)
     keep = pltpu.make_async_copy(low, xs.at[mine], local.at[0])
     keep.start()
     keep_pos = pltpu.make_async_copy(pos, poss.at[mine], local.at[1])
@@ -470,6 +480,17 @@
     trig_copies = [edges.copy(trig, trigs.at[mine], me.at(dy=k)) for k in (1, 2, 3)]
     trig_over = [edges.copy(trig, trigs.at[mine], core)]
     ring = RingGather(me, edges, low, xs)
+    for i in range(8):
+        dy, other = i // 2, i % 2
+        y = lax.rem(me.y + dy, 4)
+        to_core = me.c if other == 0 else 1 - me.c
+        stays = own_column if i == 0 else me.c < 0
+        cols = pl.ds(pl.multiple_of(Q_DEV * (2 * y + to_core), Q_DEV), Q_DEV)
+        src = wout.at[spread_rows, cols]
+        dst = wo.at[own, spread_rows]
+        target = (me.z, to_xl, to_core, y, to_xh)
+        send_block(me, src, dst, os_.at[i], orr.at[own], target, stays)
+        blocks.append((src, os_.at[i], stays))
     moved = me.c != me.xh
     swaps = swap_copies(me, wgu, wdn, wswap, ws, wr)
 
@@ -488,6 +509,10 @@
         ref = trigs.at[2 * lax.rem(me.y - k + 4, 4) + me.c]
         trig_over.append(edges.copy(ref, ref, core))
     ring.relay()
+    for i in range(8):
+        wait_got(wo.at[i, spread_rows], orr.at[i])
+    ref = wo.at[:, spread_rows]
+    wo_copies = [edges.copy(ref, ref, me.at(dz=k)) for k in (1, 3, 2)]
     keep_pos.wait()
     for d in pos_copies + trig_over:
         d.wait_recv()
@@ -551,46 +576,12 @@
     kv_copies = [edges.copy(kv, kvs.at[me.c, chip], d) for d in far]
     over = [edges.copy(kv, kvs.at[me.c, chip], core)]
     ring = RingGather(me, edges, cot, cots)
-    for i in range(8):
-        dy, other = i // 2, i % 2
-        y = lax.rem(me.y + dy, 4)
-        to_core = me.c if other == 0 else 1 - me.c
-        stays = own_column if i == 0 else me.c < 0
-        cols = pl.ds(pl.multiple_of(Q_DEV * (2 * y + to_core), Q_DEV), Q_DEV)
-        src = wout.at[spread_rows, cols]
-        dst = wo.at[own, spread_rows]
-        target = (me.z, to_xl, to_core, y, to_xh)
-        send_block(me, src, dst, os_.at[i], orr.at[own], target, stays)
-        blocks.append((src, os_.at[i], stays))
-    steps = [
-        pltpu.make_async_remote_copy(
-            src_ref=wswap,
-            dst_ref=wnear.at[i],
-            send_sem=ns.at[i],
-            recv_sem=nr.at[i],
-            device_id=me.at(dz=1 - 2 * i),
-            device_id_type=pl.DeviceIdType.MESH,
-        )
-        for i in range(2)
-    ]
-
-    @pl.when(moved)
-    def _():
-        for d in swaps:
-            d.wait()
-        for d in steps:
-            d.start()
-
     ring.relay()
     for (dz, dl), d in zip(chips_in_sequence(me), kv_copies):
         d.wait_recv()
         source = 2 * lax.rem(me.z - dz + 4, 4) + ((1 - me.xl) if dl else me.xl)
         ref = kvs.at[me.c, source]
         over.append(edges.copy(ref, ref, core))
-    for i in range(8):
-        wait_got(wo.at[i, spread_rows], orr.at[i])
-    ref = wo.at[:, spread_rows]
-    wo_copies = [edges.copy(ref, ref, me.at(dz=k)) for k in (1, 3, 2)]
     ring.rest()
     for d in over + pos_copies + wo_copies:
         d.wait_recv()
@@ -599,7 +590,7 @@
 
     @pl.when(moved)
     def _():
-        for d in steps:
+        for d in swaps:
             d.wait()
 
     edges.finish()
@@ -622,10 +613,9 @@
             shape((8, TOK, D)),
             shape((8, 256, Q_DEV)),
             shape((QUARTER, D)),
-            shape((2, QUARTER, D)),
         ),
         in_specs=[VMEM, VMEM, VMEM, VMEM] + [ANY] * 5,
-        out_specs=(VMEM, VMEM, VMEM) + (ANY,) * 9,
+        out_specs=(VMEM, VMEM, VMEM) + (ANY,) * 8,
         scratch_shapes=[
             pltpu.VMEM((TOK, D), BF16),
             pltpu.VMEM((8, TOK, D), BF16),
@@ -636,7 +626,6 @@
         + sems(5)
         + sems(8)
         + sems(2)
-        + sems(2)
         + [pltpu.SemaphoreType.DMA((6,))],
         compiler_params=remote_params(0),
         name="begin",
@@ -676,6 +665,12 @@
         values[to, :] = kv_ref[1, chip, rows, lanes]
 
 
+def turn(rows, turned):
+    for i in range(4):
+        at = slice(512 * i, 512 * (i + 1))
+        turned[:, at] = rows[at, :].astype(F32).T.astype(BF16)
+
+
 def allowed_tile(tile, run):
     key = lax.broadcasted_iota(jnp.int32, (TILE, 256), 0) + tile * TILE
     query = lax.rem(lax.broadcasted_iota(jnp.int32, (TILE, 256), 1), 64) + run * 64
@@ -687,15 +682,17 @@
 
 
 def attend_kernel(
-    key_runs, query_runs, q_ref, kv_ref, att_ref, ot_ref, lse_ref, keys, values, high_ref, total_ref, acc_ref
+    key_runs, query_runs, q_ref, kv_ref, att_ref, ot_ref, lse_ref,
+    keys, values, values_t, high_ref, total_ref, acc_ref,
 ):
     seq = pl.program_id(0)
     sort_keys(key_runs, seq, kv_ref, keys, values)
+    turn(values, values_t)
 
     def one_run(r, _):
         run = query_runs[seq * 4 + r]
         rows = pl.ds(pl.multiple_of(r * 64, 64), 64)
-        query = split_heads(q_ref[rows, :])
+        query = split_heads(q_ref[rows, :]).astype(F32).T.astype(BF16)
         last = run // 4
         high_ref[...] = jnp.full((1, 256), FILLER, F32)
         total_ref[...] = jnp.zeros((1, 256), F32)
@@ -704,7 +701,7 @@
         def tiles(first, count, masked):
             scores = []
             for k in range(count):
-                score = dot_last(keys[tile_rows(first + k), :], query)
+                score = dot(keys[tile_rows(first + k), :], query)
                 if masked and k == count - 1:
                     score = jnp.where(allowed_tile(first + k, run), score, FILLER)
                 scores.append(score)
@@ -718,7 +715,7 @@
             for k, score in enumerate(scores):
                 weights = jnp.exp(score - new_high)
                 total = total + jnp.sum(weights, axis=0, keepdims=True)
-                acc = acc + dot_first(values[tile_rows(first + k), :], weights.astype(BF16))
+                acc = acc + dot(values_t[:, tile_rows(first + k)], weights.astype(BF16))
             high_ref[...] = new_high
             total_ref[...] = total
             acc_ref[...] = acc
@@ -763,6 +760,7 @@
             scratch_shapes=[
                 pltpu.VMEM((2048, HD), BF16),
                 pltpu.VMEM((2048, HD), BF16),
+                pltpu.VMEM((HD, 2048), BF16),
                 pltpu.VMEM((1, 256), F32),
                 pltpu.VMEM((1, 256), F32),
                 pltpu.VMEM((HD, 256), F32),
@@ -775,10 +773,11 @@
 
 def attend_back_kernel(
     key_runs, query_runs, q_ref, kv_ref, da_ref, ot_ref, lse_ref, trig_ref,
-    dq_ref, dkv_ref, keys, values, dkeys, dvalues, dq_acc,
+    dq_ref, dkv_ref, keys, values, keys_t, dkeys, dvalues, dq_acc,
 ):
     seq = pl.program_id(0)
     sort_keys(key_runs, seq, kv_ref, keys, values)
+    turn(keys, keys_t)
     dkeys[...] = jnp.zeros_like(dkeys)
     dvalues[...] = jnp.zeros_like(dvalues)
 
@@ -788,7 +787,10 @@
         query = split_heads(q_ref[rows, :])
         grad = split_heads(da_ref[rows, :])
         lse = lse_ref[r]
-        delta = jnp.sum(grad.astype(F32).T * ot_ref[r], axis=0, keepdims=True)
+        query_t = query.astype(F32).T.astype(BF16)
+        grad_t = grad.astype(F32).T
+        delta = jnp.sum(grad_t * ot_ref[r], axis=0, keepdims=True)
+        grad_t = grad_t.astype(BF16)
         last = run // 4
         dq_acc[...] = jnp.zeros((HD, 256), F32)
 
@@ -797,14 +799,14 @@
             for k in range(count):
                 at = tile_rows(first + k)
                 key = keys[at, :]
-                probs = jnp.exp(dot_last(key, query) - lse)
+                probs = jnp.exp(dot(key, query_t) - lse)
                 if masked and k == count - 1:
                     probs = jnp.where(allowed_tile(first + k, run), probs, 0.0)
-                grad_probs = dot_last(values[at, :], grad)
+                grad_probs = dot(values[at, :], grad_t)
                 grad_scores = (probs * (grad_probs - delta)).astype(BF16)
                 dvalues[at, :] += dot(probs.astype(BF16), grad)
                 dkeys[at, :] += dot(grad_scores, query)
-                dq = dq + dot_first(key, grad_scores)
+                dq = dq + dot(keys_t[:, at], grad_scores)
             dq_acc[...] = dq
 
         @pl.when(last >= WIDE)
@@ -858,6 +860,7 @@
             scratch_shapes=[
                 pltpu.VMEM((2048, HD), BF16),
                 pltpu.VMEM((2048, HD), BF16),
+                pltpu.VMEM((HD, 2048), BF16),
                 pltpu.VMEM((2048, HD), F32),
                 pltpu.VMEM((2048, HD), F32),
                 pltpu.VMEM((HD, 256), F32),
@@ -943,17 +946,17 @@
 
 
 def feed_forward_kernel(
-    parts, tokens, gain, cots, wgu, wdn, wswap, wnear,
-    output, grad_middle, gain_grad, gbs, z_out, x_out,
-    xs, p, c, gp, w, act_t, gate_t, up_t, act, dgate, dup, middle, low,
-    g1, b1, r1, l1, g2, b2, r2, l2,
+    parts, tokens, gain, cots, wgu, wdn, wswap, wnear_up, wnear_down,
+    middle, grad_middle, gain_grad, gbs, z_out, x_out, branch,
+    xs, p, c, gp, w, act_t, gate_t, up_t, act, dgate, dup, low,
+    g1, b1, r1, l1,
     z_relayed, z_last, x_relayed, x_last, z_q, x_q,
     z_relayed2, z_last2, x_relayed2, x_last2,
     send, recv, fs, fr, local,
 ):
     me = Place()
     core = me.at(core=1 - me.c)
-    greet(
+    signalled = greet(
         [core, me.at(dy=1), me.at(dy=-1)]
         + [around(me, k, 0) for k in (1, 2, 3)]
         + [around(me, 0, 1), around(me, 0, 3)]
@@ -979,7 +982,7 @@
         pltpu.make_async_copy(wdn, w.at[pl.ds(2 * FF_DEV, FF_DEV)], local.at[3]),
     ]
     near_w = []
-    for i, (src, dz) in enumerate(((wswap, 0), (wnear.at[0], -1), (wnear.at[1], 1))):
+    for i, (src, dz) in enumerate(((wswap, 0), (wnear_up, -1), (wnear_down, 1))):
         gu_rows, dn_rows = w_rows(dz)
         near_w.append(pltpu.make_async_copy(src.at[gu_part], w.at[gu_rows], local.at[4 + 2 * i]))
         near_w.append(pltpu.make_async_copy(src.at[dn_part], w.at[dn_rows], local.at[5 + 2 * i]))
@@ -994,6 +997,8 @@
         )
         for i, (part, rows) in enumerate(zip((gu_part, dn_part), w_rows(0)))
     ]
+
+    met(signalled)
 
     @pl.when(moved)
     def _():
@@ -1061,8 +1066,8 @@
 
         def block(i, _):
             cols = pl.ds(pl.multiple_of(512 * i, 512), 512)
-            branch = dot(act[...], w[2 * FF_DEV :, cols])
-            p[at, :, cols] = branch.astype(BF16).reshape(2, TOK, 512)
+            term = dot(act[...], w[2 * FF_DEV :, cols])
+            p[at, :, cols] = term.astype(BF16).reshape(2, TOK, 512)
             grads = dot(dgate[...], w[:FF_DEV, cols]) + dot(dup[...], w[FF_DEV : 2 * FF_DEV, cols])
             gp[at, :, cols] = grads.astype(BF16).reshape(2, TOK, 512)
             return 0
@@ -1092,6 +1097,8 @@
     gather.from_core(5, 7)
     compute(pair(2))
     two.send_core(2)
+    save = pltpu.make_async_copy(p, branch, local.at[0])
+    save.start()
     two.add_core(0)
 
     z_sum = RingSum(me, edges, True, w, 0, PART, 512, 48, z_relayed, z_last)
@@ -1148,15 +1155,9 @@
     keep = pltpu.make_async_copy(low, gbs.at[mine], local.at[10])
     keep.start()
     gather = RingGather(me, edges, low, gbs)
-    branch = RingScatter(me, edges, p, (g2, b2, r2, l2))
-    for k in (2, 1, 3, 0):
-        branch.send_core(k)
     z_sum.second()
     x_sum.second()
     gather.relay()
-    branch.far()
-    branch.near()
-    branch.add_core(0)
     z_sum.total(z_q)
     z_two = RingSum(me, edges, False, z_q, 0, PART, 128, 176, z_relayed2, z_last2)
     z_two.far()
@@ -1169,23 +1170,17 @@
     x_two.near_down()
     gather.near()
     gather.far()
-    branch.second()
     z_two.second()
     x_two.second()
     gather.from_core(0, 7)
-    branch.arrived()
-
-    def out(at):
-        output[at, :] = (middle[at, :] + branch.rows(at)).astype(BF16)
-
-    in_chunks(out)
     z_two.total(z_out)
     x_two.total(x_out)
     edges.finish()
     keep.wait()
-
-
-def feed_forward(parts, tokens, gain, cots, wgu, wdn, wswap, wnear):
+    save.wait()
+
+
+def feed_forward(parts, tokens, gain, cots, wgu, wdn, wswap, wnear_up, wnear_down):
     block = pltpu.VMEM((8, TOK, D), BF16)
     turned = pltpu.VMEM((FF_DEV, 8 * TOK), BF16)
     pair = pltpu.VMEM((2 * TOK, FF_DEV), BF16)
@@ -1199,32 +1194,33 @@
     return pl.pallas_call(
         feed_forward_kernel,
         out_shape=(
-            shape((TOK, D)),
+            shape((TOK, D), F32),
             shape((TOK, D), F32),
             shape((1, D), F32),
             shape((8, TOK, D)),
             shape((PART, 128)),
             shape((PART, 128)),
+            shape((8, TOK, D)),
         ),
-        in_specs=[ANY, VMEM, VMEM] + [ANY] * 5,
-        out_specs=(VMEM, VMEM, VMEM, ANY, VMEM, VMEM),
+        in_specs=[ANY, VMEM, VMEM] + [ANY] * 6,
+        out_specs=(VMEM, VMEM, VMEM, ANY, VMEM, VMEM, ANY),
         scratch_shapes=[block] * 4
         + [pltpu.VMEM((3 * FF_DEV, D), BF16)]
         + [turned] * 3
         + [pair] * 3
-        + [pltpu.VMEM((TOK, D), F32), pltpu.VMEM((TOK, D), BF16)]
-        + scatter_scratch() * 2
+        + [pltpu.VMEM((TOK, D), BF16)]
+        + scatter_scratch()
         + ring(512)
         + [pltpu.VMEM((PART, 512), BF16)] * 2
         + ring(128)
-        + sems(3 * SCATTER_EDGES + 2 * GATHER_EDGES + 4 * SUM_EDGES)
+        + sems(2 * SCATTER_EDGES + 2 * GATHER_EDGES + 4 * SUM_EDGES)
         + sems(2)
         + [pltpu.SemaphoreType.DMA((11,))],
         compiler_params=pltpu.CompilerParams(
             collective_id=2, has_side_effects=True, vmem_limit_bytes=62 * 2**20
         ),
         name="feed_forward",
-    )(parts, tokens, gain, cots, wgu, wdn, wswap, wnear)
+    )(parts, tokens, gain, cots, wgu, wdn, wswap, wnear_up, wnear_down)
 
 
 def columns(width):
@@ -1410,38 +1406,59 @@
     return found + [pltpu.VMEM((r, 128), BF16) for r in rows]
 
 
-WQ_ROWS = (128, 192)
-WO_ROWS = (128, 128)
+EARLY_ROWS = (256, 256)
 
 
 def ending_kernel(
-    dkv, dq, kv_table, wq, tokens, gain, grad_middle, gain_two, z_piece, x_piece, gwo_in, xs_in,
-    grad_tokens, gains, wq_out, wo_out, z_all, x_all,
-    kv_got, kv_both, kv_last, dkv_low, xs, grads, grads_t, parts, gwq, gwo,
-    got, both, relayed, last, wq_all, wo_all, mine, near, near_sum, owners,
+    dkv, dq, kv_table, wq, tokens, gain, grad_middle, gain_two, z_piece, x_piece, middle,
+    gwo, xs_in, branch_in,
+    output, grad_tokens, gains, wq_out, wo_out, z_all, x_all,
+    kv_got, kv_both, kv_last, dkv_low, xs, grads, grads_t, parts, branch_parts, early, late,
+    g1, b1, r1, l1, g2, b2, r2, l2,
+    wq_all, wo_all, late_own, late_got, late_piece, mine, near, near_sum, owners,
     *rest,
 ):
-    wq_scratch, wo_scratch = rest[:12], rest[12:24]
-    (send, recv, ds, dr, es, er, ps, pr, gs, gr, hs, hr, local) = rest[24:]
+    early_scratch = rest[:12]
+    (send, recv, ds, dr, es, er, ps, pr, gs, gr, hs, hr, us, ur, local) = rest[12:]
     me = Place()
     core = me.at(core=1 - me.c)
     far = [
         me.at(dz=dz, xl=(1 - me.xl) if dl else me.xl) for dz, dl in chips_in_sequence(me)
     ]
-    greet(plane_devices(me) + group_members(me)[1:])
+    signalled = greet(plane_devices(me) + group_members(me)[1:])
     edges = Edges(send, recv)
     place = 4 * me.z + x_of(me)
     turned = 4 * x_of(me) + me.z
     rank = 2 * me.y + me.c
     load_x = pltpu.make_async_copy(xs_in, xs, local.at[0])
-    load_x.start()
-    load_wo = pltpu.make_async_copy(gwo_in, gwo, local.at[1])
-    load_wo.start()
+    load_branch = pltpu.make_async_copy(branch_in, branch_parts, local.at[1])
+    load_wo = [
+        pltpu.make_async_copy(
+            gwo.at[pl.ds(128 * i, 128)], early.at[pl.ds(256 * i + 128, 128)], local.at[2 + i]
+        )
+        for i in (0, 1)
+    ]
+    for d in [load_x, load_branch] + load_wo:
+        d.start()
+
+    def query_part(i, _):
+        at = pl.ds(pl.multiple_of(2 * TOK * i, 2 * TOK), 2 * TOK)
+        rows = dq[at, :]
+        grads[at, :Q_DEV] = rows
+        grads_t[:Q_DEV, at] = rows.astype(F32).T.astype(BF16)
+        return 0
+
+    lax.fori_loop(0, 4, query_part, 0)
+    met(signalled)
 
     order = []
     for dz, dl in chips_in_sequence(me) + [(0, 0)]:
         chip = 2 * lax.rem(me.z + dz, 4) + ((1 - me.xl) if dl else me.xl)
         order.append((chip, edges.copy(dkv.at[1 - me.c, chip], kv_got.at[chip], core)))
+    load_branch.wait()
+    branch = RingScatter(me, edges, branch_parts, (g2, b2, r2, l2))
+    for k in (2, 1, 3, 0):
+        branch.send_core(k)
     plane = PlaneGather(me, edges, z_piece, x_piece, z_all, x_all, ps, pr)
     far_copies = []
     for i, (chip, d) in enumerate(order):
@@ -1449,20 +1466,24 @@
         kv_both[chip] = (dkv[me.c, chip].astype(F32) + kv_got[chip].astype(F32)).astype(BF16)
         if i < 7:
             far_copies.append(edges.copy(kv_both.at[chip], kv_last.at[i], far[i]))
-    load_wo.wait()
-    wo_sum = TwoSums(me, edges, gwo, WO_ROWS, ((64, 64), (64, 64)), wo_scratch)
+    branch.far()
+    branch.near()
+    load_x.wait()
+
+    def weight_block(i, _):
+        cols = pl.ds(pl.multiple_of(512 * i, 512), 512)
+        rows = xs[:, :, cols].reshape(8 * TOK, 512)
+        early[:128, cols] = dot(grads_t[:128, :], rows).astype(BF16)
+        early[256:384, cols] = dot(grads_t[128:Q_DEV, :], rows).astype(BF16)
+        return 0
+
+    lax.fori_loop(0, 4, weight_block, 0)
+    for d in load_wo:
+        d.wait()
+    early_sum = TwoSums(me, edges, early, EARLY_ROWS, ((64, 64), (128, 128)), early_scratch)
     plane.sideways()
-
-    def query_part(i, _):
-        at = pl.ds(pl.multiple_of(2 * TOK * i, 2 * TOK), 2 * TOK)
-        rows = dq[at, :]
-        grads[at, :Q_DEV] = rows
-        grads_t[:Q_DEV, at] = rows.astype(F32).T.astype(BF16)
-        return 0
-
-    lax.fori_loop(0, 4, query_part, 0)
-    plane.along()
-    wo_sum.second()
+    branch.add_core(0)
+    branch.second()
     for d in far_copies:
         d.wait_recv()
 
@@ -1481,18 +1502,10 @@
             at = slice(TOK * (2 * i + half), TOK * (2 * i + half + 1))
             grads[at, Q_DEV:] = rows.astype(BF16)
             grads_t[Q_DEV:, at] = rows.T.astype(BF16)
-
-    load_x.wait()
-
-    def weight_block(i, _):
-        cols = pl.ds(pl.multiple_of(512 * i, 512), 512)
-        term = dot(grads_t[...], xs[:, :, cols].reshape(8 * TOK, 512))
-        gwq[:, cols] = term.astype(BF16)
-        return 0
-
-    lax.fori_loop(0, 4, weight_block, 0)
-    wq_sum = TwoSums(me, edges, gwq, WQ_ROWS, ((64, 48), (64, 96)), wq_scratch)
-    ring = RingScatter(me, edges, parts, (got, both, relayed, last))
+    early_sum.second()
+    plane.along()
+
+    ring = RingScatter(me, edges, parts, (g1, b1, r1, l1))
 
     def part(k):
         pair = lax.rem(me.y + k, 4)
@@ -1513,22 +1526,50 @@
     part(3)
     ring.near()
     part(0)
+
+    def late_block(i, _):
+        cols = pl.ds(pl.multiple_of(512 * i, 512), 512)
+        rows = xs[:, :, cols].reshape(8 * TOK, 512)
+        late[:, cols] = dot(grads_t[Q_DEV:, :], rows).astype(BF16)
+        return 0
+
+    lax.fori_loop(0, 4, late_block, 0)
+    late_sum = SumOfSixteen(me, late, columns(128), late_own, late_got, us, ur, local.at[4])
     ring.add_core(0)
-    wq_sum.second()
-    wo_sum.cross()
+    early_sum.cross()
     plane.near()
     ring.second()
-    wq_sum.cross()
-    wo_sum.fourth()
-    wo_sum.total()
+    early_sum.fourth()
+    branch.arrived()
+
+    def out(at):
+        output[at, :] = (middle[at, :] + branch.rows(at)).astype(BF16)
+
+    in_chunks(out)
+    late_piece[...] = late_sum.total().astype(BF16)
+    wq_deliver = Deliver(me, ds, dr)
+
+    def deliver_block(j, src, at):
+        block = own_block(me, j)
+        owner, slot = block // 5, lax.rem(block, 5)
+        dst = wq_all.at[
+            pl.ds(pl.multiple_of(64 * slot, 64), 64),
+            pl.ds(pl.multiple_of(128 * at, 128), 128),
+        ]
+        wq_deliver.to_owner(src, dst, at // 8, owner // 2, lax.rem(owner, 2))
+
+    deliver_block(4, late_piece, place)
+    early_sum.total()
     wo_deliver = Deliver(me, es, er)
     for i, at in enumerate((place, turned)):
+        for j in (0, 1):
+            deliver_block(2 * i + j, early_sum.out[i].at[pl.ds(64 * j, 64)], at)
         dst = wo_all.at[
             pl.ds(pl.multiple_of(Q_DEV * rank + 128 * i, 128), 128),
             pl.ds(pl.multiple_of(128 * lax.rem(at, 2), 128), 128),
         ]
-        wo_deliver.to_owner(wo_sum.out[i], dst, me.y // 2, at // 4, lax.rem(at // 2, 2))
-    wq_sum.fourth()
+        src = early_sum.out[i].at[pl.ds(128, 128)]
+        wo_deliver.to_owner(src, dst, me.y // 2, at // 4, lax.rem(at // 2, 2))
     ring.arrived()
     mine[...] = jnp.zeros_like(mine)
     mine[1:2, :] = gain_two[...]
@@ -1564,19 +1605,7 @@
         )
         d.start()
         near_copies.append(d)
-    wq_sum.total()
-    wq_deliver = Deliver(me, ds, dr)
-    for j in range(5):
-        block = own_block(me, j)
-        owner, slot = block // 5, lax.rem(block, 5)
-        at = place if j < 2 else turned
-        piece = wq_sum.out[0] if j < 2 else wq_sum.out[1]
-        dst = wq_all.at[
-            pl.ds(pl.multiple_of(64 * slot, 64), 64),
-            pl.ds(pl.multiple_of(128 * at, 128), 128),
-        ]
-        src = piece.at[pl.ds(64 * (j if j < 2 else j - 2), 64)]
-        wq_deliver.to_owner(src, dst, at // 8, owner // 2, lax.rem(owner, 2))
+    plane.far()
     own = mine[:, pl.ds(pl.multiple_of(256 * rank, 256), 256)]
     wait_got(near, gr)
     for k in range(7):
@@ -1585,7 +1614,6 @@
     gain_deliver = Deliver(me, hs, hr)
     for to_core in (0, 1):
         gain_deliver.to_owner(near_sum, owners.at[place], to_core, me.y, me.c)
-    plane.far()
 
     half = pl.ds(pl.multiple_of(1024 * me.c, 1024), 1024)
     over = []
@@ -1602,6 +1630,7 @@
     wo_out[...] = wo_all[...]
     wq_out[...] = wq_all[...]
     plane.finish()
+    late_sum.finish()
     for d in (wo_deliver, wq_deliver, gain_deliver):
         d.finish()
     for d in near_copies:
@@ -1609,11 +1638,15 @@
     edges.finish()
 
 
-def ending(dkv, dq, kv_table, wq, tokens, gain, grad_middle, gain_two, z_piece, x_piece, gwo, xs):
+def ending(
+    dkv, dq, kv_table, wq, tokens, gain, grad_middle, gain_two, z_piece, x_piece, middle,
+    gwo, xs, branch,
+):
     many = pltpu.SemaphoreType.DMA
     return pl.pallas_call(
         ending_kernel,
         out_shape=(
+            shape((TOK, D)),
             shape((TOK, D), F32),
             shape((8, 256), F32),
             shape((320, D)),
@@ -1621,8 +1654,8 @@
             shape((PART, D)),
             shape((PART, D)),
         ),
-        in_specs=[VMEM] * 10 + [ANY] * 2,
-        out_specs=(VMEM,) * 4 + (ANY,) * 2,
+        in_specs=[VMEM] * 11 + [ANY] * 3,
+        out_specs=(VMEM,) * 5 + (ANY,) * 2,
         scratch_shapes=[
             pltpu.VMEM((8, 512, 128), BF16),
             pltpu.VMEM((8, 512, 128), BF16),
@@ -1632,26 +1665,34 @@
             pltpu.VMEM((1024, 320), BF16),
             pltpu.VMEM((320, 1024), BF16),
             pltpu.VMEM((8, TOK, D), BF16),
-            pltpu.VMEM((320, D), BF16),
-            pltpu.VMEM((256, D), BF16),
+            pltpu.VMEM((8, TOK, D), BF16),
+            pltpu.VMEM((512, D), BF16),
+            pltpu.VMEM((64, D), BF16),
         ]
-        + scatter_scratch()
+        + scatter_scratch() * 2
         + [
             pltpu.VMEM((320, D), BF16),
             pltpu.VMEM((D, 256), BF16),
+            pltpu.VMEM((64, 128), BF16),
+            pltpu.VMEM((15, 64, 128), BF16),
+            pltpu.VMEM((64, 128), BF16),
             pltpu.VMEM((8, D), F32),
             pltpu.VMEM((7, 8, 256), F32),
             pltpu.VMEM((8, 256), F32),
             pltpu.VMEM((16, 8, 256), F32),
         ]
-        + two_sums_scratch(WQ_ROWS)
-        + two_sums_scratch(WO_ROWS)
-        + sems(15 + SCATTER_EDGES + PLANE_EDGES + 8 * SUM_EDGES + 2)
+        + two_sums_scratch(EARLY_ROWS)
+        + sems(15 + 2 * SCATTER_EDGES + PLANE_EDGES + 4 * SUM_EDGES + 2)
         + [many((40,)), many, many((16,)), many, many((2,)), many((2,))]
-        + [many((7,)), many, many((16,)), many, many((2,))],
-        compiler_params=remote_params(3),
+        + [many((7,)), many, many((16,)), many, many((15,)), many, many((5,))],
+        compiler_params=pltpu.CompilerParams(
+            collective_id=3, has_side_effects=True, vmem_limit_bytes=60 * 2**20
+        ),
         name="ending",
-    )(dkv, dq, kv_table, wq, tokens, gain, grad_middle, gain_two, z_piece, x_piece, gwo, xs)
+    )(
+        dkv, dq, kv_table, wq, tokens, gain, grad_middle, gain_two, z_piece, x_piece, middle,
+        gwo, xs, branch,
+    )
 
 
 def widen_kernel(z_ref, x_ref, gu_ref, dn_ref):
@@ -1689,12 +1730,21 @@
     )(z_all, x_all)
 
 
+def route(dz):
+    pairs = []
+    for i in range(128):
+        z, xl, c, y, xh = i // 32, i // 16 % 2, i // 8 % 2, i // 2 % 4, i % 2
+        if c != xh:
+            pairs.append((i, (((((z + dz) % 4) * 2 + xl) * 2 + c) * 4 + y) * 2 + xh))
+    return pairs
+
+
 def body(hidden, positions, gain_attn, w_qkv, w_out, gain_mlp, w_gate_up, w_down, cotangent):
     gain_one = gain_attn.astype(F32).reshape(1, D)
     gain_two = gain_mlp.astype(F32).reshape(1, D)
     wgu = w_gate_up.reshape(2 * FF_DEV, D)
     wdn = w_down.T
-    query, kv_table, trigs, xs, wq, poss, kvs, places, cots, wo, wswap, wnear = begin(
+    query, kv_table, trigs, xs, wq, poss, kvs, places, cots, wo, wswap = begin(
         hidden[0],
         gain_one,
         jnp.broadcast_to(positions, (8, TOK)),
@@ -1710,16 +1760,18 @@
     key_runs = (
         places[:, :, 0, ::64].reshape(8, 4, 2, 2).transpose(1, 0, 2, 3).reshape(128) // 64
     )
+    wnear_up = lax.ppermute(wswap, AXES, route(1))
+    wnear_down = lax.ppermute(wswap, AXES, route(3))
     att, ot, lse = attend(key_runs, query_runs, query, kvs)
     parts = dot_last(att, wo).astype(BF16).reshape(8, TOK, D)
-    output, grad_middle, gain_grad, gbs, z_piece, x_piece = feed_forward(
-        parts, hidden[0], gain_two, cots, wgu, wdn, wswap, wnear
+    middle, grad_middle, gain_grad, gbs, z_piece, x_piece, branch = feed_forward(
+        parts, hidden[0], gain_two, cots, wgu, wdn, wswap, wnear_up, wnear_down
     )
     gb = gbs.reshape(1024, D)
     grad_att = dot(gb, wo).astype(BF16)
     grad_wo = dot_first(att, gb).astype(BF16)
     dq, dkv = attend_back(key_runs, query_runs, query, kvs, grad_att, ot, lse, trigs)
-    grad_tokens, gains, grad_w_qkv, grad_w_out, z_all, x_all = ending(
+    output, grad_tokens, gains, grad_w_qkv, grad_w_out, z_all, x_all = ending(
         dkv,
         dq,
         kv_table,
@@ -1730,8 +1782,10 @@
         gain_grad,
         z_piece,
         x_piece,
+        middle,
         grad_wo,
         xs,
+        branch,
     )
     grad_gu, grad_dn = widen(z_all, x_all)
     return (

time: 431 us -> 403 us (0.935)
  Pallas kernels: 389 us -> 354 us
  starting transfers between devices: 0 us -> 5.44 us
    pallas_call x1, Pallas kernels: 87.1 us -> 63.3 us  [begin(): pl.pallas_call(begin_kernel, out_shape=(shape((1024, Q_DEV)), shape((2, 5...]
    pallas_call x2, Pallas kernels: 239 us -> 230 us  [the longest x1 120 us: feed_forward(): pl.pallas_call(feed_forward_kernel, out_shape=(shape((TOK, D), F32), shap...]
    ppermute x0 -> x2, starting transfers between devices: none -> 5.44 us  [the longest x1 3.29 us: body(): wnear_up = lax.ppermute(wswap, AXES, route(1))]
    unnamed x41 -> x43, local copies, waits for them, and re-layouts: 15.3 us -> 16.9 us
  transfers between devices with their start and end apart: 0 -> 2, of which waited for: 0 -> 0; matrix products, arithmetic and copies ran while one was open for 0% -> 2% of each run, Pallas kernels for 0% -> 6%
where the time goes in v5:
time: 403 us; the launch traced here: 397 us
  Pallas kernels  354 us (88%)
  local copies, waits for them, and re-layouts  20.9 us (5%)
  matrix products  9.45 us (2%)
  other arithmetic  6.04 us (1%)
  starting transfers between devices  5.44 us (1%)
    pallas_call x1, Pallas kernels, feed_forward(): pl.pallas_call(feed_forward_kernel, out_shape=(shape((TOK, D), F32), shap...  120 us
    pallas_call x1, Pallas kernels, ending(): pl.pallas_call(ending_kernel, out_shape=(shape((TOK, D)), shape((TOK, D),...  110 us
    pallas_call x1, Pallas kernels, begin(): pl.pallas_call(begin_kernel, out_shape=(shape((1024, Q_DEV)), shape((2, 5...  63.3 us
    pallas_call x1, Pallas kernels, attend_back(): pl.pallas_call(attend_back_kernel, out_shape=(shape((1024, 256)), shape((...  31.2 us
    pallas_call x1, Pallas kernels, attend(): pl.pallas_call(attend_kernel, out_shape=(shape((1024, 256)), shape((16, H...  21.9 us
    unnamed x43, local copies, waits for them, and re-layouts  16.9 us
  transfers between devices with their start and end apart: 2, of which 0 were waited for; matrix products, arithmetic and copies ran while one was open for 2% of the time, Pallas kernels for 6%

profile of v5, /device:TPU:9, one launch (start us, length us, event | category | flops | bytes accessed | tf_op | source)
XLA Modules:
  0.0 397.1 jit_solution(14394229303460545874)
XLA Ops:
  0.6 0.7 convert_reduce_fusion
  1.3 0.1 convert_element_type.31
  1.4 0.7 reshape.92
  2.1 0.2 multiply_cosine_fusion
  2.3 0.1 copy.29.trig
  2.4 0.7 broadcast_in_dim.16.pos
  3.1 1.0 copy-done.2
  4.1 1.2 copy-done.7
  5.3 1.0 copy-done.11
  6.4 63.3 %begin.1 = (bf16[1024,256]{1,0:T(8,128)(2,1)S(1)}, f32[2,512,128]{2,1,0:T(8,128)S(1)}, f32[8,64,128]{2,1,0:T(8,128)S(1)}, bf16[8,128,2048]{2,1,0:T(8,128)(2,1)},...) custom-call(bf16[128,2048]{1,0:T(8,128)(2,1)S(1)} %bitcast.32, ...), custom_call_target="tpu_custom_call" | custom-call | tf_op jit(solution)/shard_map/begin/pallas_call | solution.py:602
  69.7 0.0 copy-start.6
  69.7 1.0 copy-done.6
  70.7 0.8 copy-done.12
  71.5 2.2 collective-permute-start.1
  73.7 3.3 collective-permute-start
  77.0 0.6 reshape.94
  77.6 0.7 slice.12
  78.3 0.1 copy.26
  78.4 0.1 slice.13
  78.5 0.5 broadcast.48
  79.1 0.7 reduce.7
  79.7 0.1 reshape_squeeze.7
  79.8 0.1 copy.27
  79.9 0.1 reshape.85
  80.1 1.6 copy-done
  81.7 21.9 %attend.1 = (bf16[1024,256]{1,0:T(8,128)(2,1)S(1)}, f32[16,64,256]{2,1,0:T(8,128)S(1)}, f32[16,1,256]{2,1,0:T(1,128)S(1)}) custom-call(s32[128]{0:T(128)S(1)} %and_select_fusion.1.key_runs, s32[16]{0:T(128)S(1)} %and_select_fusion.query_runs, bf16[1024,256]{1,0:T(8,128)(2,1)S(1)} %get-tuple-element.42.q_ref, bf16[2,8,512,128]{3,2,1,0:T(8,128)(2,1)S(1)} %copy-done), custom_call_target="tpu_custom_call" | custom-call | tf_op jit(solution)/shard_map/attend/pallas_call | solution.py:745
  103.6 0.0 copy-start.9
  103.6 3.3 convolution_convert_fusion
  106.9 0.0 collective-permute-done.1.wnear_down
  106.9 0.0 collective-permute-done.wnear_up
  106.9 119.8 %feed_forward.1 = (f32[128,2048]{1,0:T(8,128)}, f32[128,2048]{1,0:T(8,128)}, f32[1,2048]{1,0:T(1,128)}, bf16[8,128,2048]{2,1,0:T(8,128)(2,1)}, bf16[1056,128]{1,...) custom-call(bf16[8,128,2048]{2,1,0:T(8,128)(2,1)} %bitcast.38, bf16[128,2048]{1,0:T(8,128)(2,1)} %bitcast.30, ...), custom_call_target="tpu_custom_call" | custom-call | tf_op jit(solution)/shard_map/feed_forward/pallas_call | solution.py:1194
  226.7 3.9 convolution_convert_fusion.2.da_ref
  230.6 0.0 copy-start.10
  230.7 2.3 convolution_convert_fusion.1.gwo
  232.9 31.2 %attend_back.1 = (bf16[1024,256]{1,0:T(8,128)(2,1)S(1)}, bf16[2,8,512,128]{3,2,1,0:T(8,128)(2,1)S(1)}) custom-call(s32[128]{0:T(128)S(1)} %and_select_fusion.1.key_runs, s32[16]{0:T(128)S(1)} %and_select_fusion.query_runs, bf16[1024,256]{1,0:T(8,128)(2,1)S(1)} %get-tuple-element.42.q_ref, bf16[2,8,512,128]{3,2,1,0:T(8,128)(2,1)S(1)} %copy-done.1, ...), custom_call_target="tpu_custom_call" | custom-call | tf_op jit(solution)/shard_map/attend_back/pallas_call | solution.py:842
  264.1 0.0 copy-start.5
  264.1 1.3 copy-done.5
  265.5 0.8 copy-done.13
  266.3 110.5 %ending.1 = (bf16[128,2048]{1,0:T(8,128)(2,1)}, f32[128,2048]{1,0:T(8,128)}, f32[8,256]{1,0:T(8,128)}, bf16[320,2048]{1,0:T(8,128)(2,1)}, bf16[2048,256]{1,0:T(8...) custom-call(bf16[2,8,512,128]{3,2,1,0:T(8,128)(2,1)} %copy-done.5, bf16[1024,256]{1,0:T(8,128)(2,1)} %copy-done.13, ...), custom_call_target="tpu_custom_call" | custom-call | tf_op jit(solution)/shard_map/ending/pallas_call | solution.py:1646
  376.7 1.4 fusion
  378.1 1.4 convert_bitcast_fusion
  379.5 1.8 copy.28
  381.3 1.8 convert_element_type.35
  383.1 2.2 copy-done.3
  385.4 2.2 copy-done.4
  387.6 7.3 %widen.1 = (f32[1408,2048]{1,0:T(8,128)}, f32[704,2048]{1,0:T(8,128)}) custom-call(bf16[1056,2048]{1,0:T(8,128)(2,1)S(1)} %copy-done.3, bf16[1056,2048]{1,0:T(8,128)(2,1)S(1)} %copy-done.4), custom_call_target="tpu_custom_call" | custom-call | tf_op jit(solution)/shard_map/widen/pallas_call | solution.py:1716
  394.9 0.8 copy.32
  395.7 1.0 copy.33
  (30 shorter events, 0.1 us)
Async XLA Ops:
  2.1 67.6 %copy-start.14 = (f32[2048]{0:T(1024)}, f32[2048]{0:T(1024)S(1)}, u32[]{:S(2)}) copy-start(f32[2048]{0:T(1024)S(1)} %reshape.92) | copy-start | bytes 24580
  3.1 1.0 copy-start.2
  4.1 1.2 copy-start.7
  5.3 1.0 copy-start.11
  6.4 70.6 %copy-start.18 = (bf16[2048]{0:T(1024)(128)(2,1)S(1)}, bf16[2048]{0:T(1024)(128)(2,1)}, u32[]{:S(2)}) copy-start(bf16[2048]{0:T(1024)(128)(2,1)} %param.14) | copy-start | bytes 12292
  69.7 1.1 copy-start.6
  70.7 0.8 copy-start.12
  71.5 35.3 %copy-start.8 = (bf16[8,256,256]{2,1,0:T(8,128)(2,1)}, bf16[8,256,256]{2,1,0:T(8,128)(2,1)S(1)}, u32[]{:S(2)}) copy-start(bf16[8,256,256]{2,1,0:T(8,128)(2,1)S(1)} %get-tuple-element.45) | copy-start | bytes 3145732
  71.5 35.4 %collective-permute-start.1 = (bf16[528,2048]{1,0:T(8,128)(2,1)}, bf16[528,2048]{1,0:T(8,128)(2,1)}, u32[]{:S(2)}, u32[]{:S(2)}) collective-permute-start(bf16[528,2048]{1,0:T(8,128)(2,1)} %get-tuple-element.47.wswap), channel_id=1, source_target_pairs={{1,97},{3,99},{5,101},{7,103},{8,104},{10,106},{12,108},{14,110},{... | collective-permute-start | bytes 6488072 | tf_op jit(solution)/shard_map/ppermute | solution.py:1764
  73.7 33.2 %collective-permute-start = (bf16[528,2048]{1,0:T(8,128)(2,1)}, bf16[528,2048]{1,0:T(8,128)(2,1)}, u32[]{:S(2)}, u32[]{:S(2)}) collective-permute-start(bf16[528,2048]{1,0:T(8,128)(2,1)} %get-tuple-element.47.wswap), channel_id=1, source_target_pairs={{1,33},{3,35},{5,37},{7,39},{8,40},{10,42},{12,44},{14,46},{17,49}... | collective-permute-start | bytes 6488072 | tf_op jit(solution)/shard_map/ppermute | solution.py:1763
  80.1 1.6 copy-start
  103.6 3.3 copy-start.9
  226.7 3.9 copy-start.19
  230.6 2.3 copy-start.1
  230.6 2.3 copy-start.10
  264.1 1.3 copy-start.5
  265.5 0.8 copy-start.13
  376.7 4.6 %copy-start.15 = (bf16[320,2048]{1,0:T(8,128)(2,1)S(1)}, bf16[320,2048]{1,0:T(8,128)(2,1)}, u32[]{:S(2)}) copy-start(bf16[320,2048]{1,0:T(8,128)(2,1)} %get-tuple-element.66) | copy-start | bytes 3932164
  383.1 2.2 copy-start.3
  385.4 2.2 copy-start.4
  387.6 7.3 %copy-start.17 = (bf16[128,2048]{1,0:T(8,128)(2,1)S(1)}, bf16[128,2048]{1,0:T(8,128)(2,1)}, u32[]{:S(2)}) copy-start(bf16[128,2048]{1,0:T(8,128)(2,1)} %get-tuple-element.63) | copy-start | bytes 1572868
  387.6 8.1 %copy-start.16 = (f32[128,2048]{1,0:T(8,128)S(1)}, f32[128,2048]{1,0:T(8,128)}, u32[]{:S(2)}) copy-start(f32[128,2048]{1,0:T(8,128)} %get-tuple-element.64) | copy-start | bytes 3145732

commit v6 on v5

--- a/solution.py
+++ b/solution.py
@@ -93,48 +93,59 @@
 
 
 class RingGather:
-    def __init__(self, me, edges, own, out):
+    def __init__(self, me, edges, own, out, local):
         self.me, self.edges, self.out = me, edges, out
         self.core = me.at(core=1 - me.c)
         self.up, self.down = me.at(dy=1), me.at(dy=-1)
-        a, b = pl.ds(0, HALF), pl.ds(HALF, HALF)
-        self.a, self.b = a, b
-        mine = self.slot(0)
-        self.up_a = edges.copy(own.at[a], out.at[mine, a], self.up)
-        self.down_b = edges.copy(own.at[b], out.at[mine, b], self.down)
-        self.up_b = edges.copy(own.at[b], out.at[mine, b], self.up)
-        self.down_a = edges.copy(own.at[a], out.at[mine, a], self.down)
-        self.to_core = [edges.copy(own, out.at[mine], self.core)]
-
-    def slot(self, dy):
-        return 2 * lax.rem(self.me.y + dy + 4, 4) + self.me.c
-
-    def pass_core(self, dy, part):
-        ref = self.out.at[self.slot(dy), part]
+        a, b = own.at[pl.ds(0, HALF)], own.at[pl.ds(HALF, HALF)]
+        to_a, to_b = self.block(0, 0), self.block(0, 1)
+        self.up_a = edges.copy(a, to_a, self.up)
+        self.down_b = edges.copy(b, to_b, self.down)
+        self.up_b = edges.copy(b, to_b, self.up)
+        self.down_a = edges.copy(a, to_a, self.down)
+        self.to_core = [edges.copy(a, to_a, self.core), edges.copy(b, to_b, self.core)]
+        self.kept = [
+            pltpu.make_async_copy(a, to_a, local.at[0]),
+            pltpu.make_async_copy(b, to_b, local.at[1]),
+        ]
+        for d in self.kept:
+            d.start()
+
+    def block(self, dy, half):
+        y = lax.rem(self.me.y + dy + 4, 4)
+        rows = pl.ds(pl.multiple_of(HALF * self.me.c, HALF), HALF)
+        return self.out.at[2 * y + half, rows]
+
+    def pass_core(self, dy, half):
+        ref = self.block(dy, half)
         self.to_core.append(self.edges.copy(ref, ref, self.core))
 
+    def own(self):
+        for d in self.kept:
+            d.wait()
+        self.from_core(0, 2)
+
     def relay(self):
-        out = self.out
         self.up_a.wait_recv()
-        ref = out.at[self.slot(-1), self.a]
+        ref = self.block(-1, 0)
         self.on_a = self.edges.copy(ref, ref, self.up)
+        self.pass_core(-1, 0)
         self.down_b.wait_recv()
-        ref = out.at[self.slot(1), self.b]
+        ref = self.block(1, 1)
         self.on_b = self.edges.copy(ref, ref, self.down)
-        self.pass_core(-1, self.a)
-        self.pass_core(1, self.b)
+        self.pass_core(1, 1)
 
     def near(self):
         self.up_b.wait_recv()
-        self.pass_core(-1, self.b)
+        self.pass_core(-1, 1)
         self.down_a.wait_recv()
-        self.pass_core(1, self.a)
+        self.pass_core(1, 0)
 
     def far(self):
         self.on_a.wait_recv()
-        self.pass_core(2, self.a)
+        self.pass_core(2, 0)
         self.on_b.wait_recv()
-        self.pass_core(2, self.b)
+        self.pass_core(2, 1)
 
     def from_core(self, first, last):
         for d in self.to_core[first:last]:
@@ -143,10 +154,15 @@
     def rest(self):
         self.near()
         self.far()
-        self.from_core(0, 7)
-
-
-GATHER_EDGES = 13
+        self.own()
+        self.from_core(2, 8)
+
+    def sources(self):
+        return [self.up_a, self.up_b, self.down_a, self.down_b] + self.to_core[:2]
+
+
+GATHER_EDGES = 14
+GROUPS = (((0, 0), (0, 1)), ((3, 0), (1, 1)), ((3, 1), (1, 0)), ((2, 0), (2, 1)))
 
 
 class RingScatter:
@@ -471,15 +487,13 @@
         send_block(me, src, dst, qs.at[i], qr.at[slot], target, stays)
         blocks.append((src, qs.at[i], stays))
 
-    keep = pltpu.make_async_copy(low, xs.at[mine], local.at[0])
-    keep.start()
     keep_pos = pltpu.make_async_copy(pos, poss.at[mine], local.at[1])
     keep_pos.start()
     pos_copies = [edges.copy(pos, poss.at[mine], m) for m in members]
     trigs[mine] = trig[...]
     trig_copies = [edges.copy(trig, trigs.at[mine], me.at(dy=k)) for k in (1, 2, 3)]
     trig_over = [edges.copy(trig, trigs.at[mine], core)]
-    ring = RingGather(me, edges, low, xs)
+    ring = RingGather(me, edges, low, xs, local.at[pl.ds(6, 2)])
     for i in range(8):
         dy, other = i // 2, i % 2
         y = lax.rem(me.y + dy, 4)
@@ -516,66 +530,60 @@
     keep_pos.wait()
     for d in pos_copies + trig_over:
         d.wait_recv()
-    keep.wait()
     for d in wq_copies:
         d.wait_recv()
     wq_save = pltpu.make_async_copy(wq, wq_out, local.at[2])
     wq_save.start()
     is_key = me.c == 0
 
-    def compute(pair):
-        at = pl.ds(2 * pair, 2)
-        projected = dot_last(xs[at].reshape(2 * TOK, D), wq[...])
-        for r in range(4):
-            half, u = r // 2, r % 2
-            rows = rotary_of(trigs[2 * pair + half], u)
-            values = projected[64 * r : 64 * r + 64]
-            heads = [rotate(values[:, HD * h : HD * h + HD], rows) for h in range(4)]
-            query = jnp.concatenate(heads, axis=1).astype(BF16)
-            to = pl.ds(pl.multiple_of(2 * TOK * pair + 64 * r, 64), 64)
-            q[to, :] = (query.astype(F32) * 0.125).astype(BF16)
-            rows = jnp.concatenate(
-                [
-                    jnp.where(is_key, rows[:, :HD], 1.0),
-                    jnp.where(is_key, rows[:, HD:], 0.0),
-                ],
-                axis=1,
-            )
-            to = pl.ds(pl.multiple_of(TOK * pair + 64 * u, 64), 64)
-            lanes = slice(HD * half, HD * half + HD)
-            kv[to, lanes] = rotate(values[:, Q_DEV:], rows).astype(BF16)
-            kv_table[0, to, lanes] = rows[:, :HD]
-            kv_table[1, to, lanes] = rows[:, HD:]
-
-    def pair(k):
-        return lax.rem(me.y + k, 4)
-
-    ring.from_core(0, 1)
-    compute(pair(0))
+    def compute(group):
+        ys = [lax.rem(me.y + dy, 4) for dy, _ in group]
+        rows = [xs[2 * y + u] for y, (_, u) in zip(ys, group)]
+        projected = dot_last(jnp.concatenate(rows, axis=0), wq[...])
+        for i, (y, (_, u)) in enumerate(zip(ys, group)):
+            for half in (0, 1):
+                rows = rotary_of(trigs[2 * y + half], u)
+                at = TOK * i + 64 * half
+                values = projected[at : at + 64]
+                heads = [rotate(values[:, HD * h : HD * h + HD], rows) for h in range(4)]
+                query = jnp.concatenate(heads, axis=1).astype(BF16)
+                to = pl.ds(pl.multiple_of(2 * TOK * y + TOK * u + 64 * half, 64), 64)
+                q[to, :] = (query.astype(F32) * 0.125).astype(BF16)
+                rows = jnp.concatenate(
+                    [
+                        jnp.where(is_key, rows[:, :HD], 1.0),
+                        jnp.where(is_key, rows[:, HD:], 0.0),
+                    ],
+                    axis=1,
+                )
+                to = pl.ds(pl.multiple_of(TOK * y + 64 * u, 64), 64)
+                lanes = slice(HD * half, HD * half + HD)
+                kv[to, lanes] = rotate(values[:, Q_DEV:], rows).astype(BF16)
+                kv_table[0, to, lanes] = rows[:, :HD]
+                kv_table[1, to, lanes] = rows[:, HD:]
+
+    ring.own()
+    compute(GROUPS[0])
     ring.near()
-    ring.from_core(1, 5)
-
-    def sides(i, _):
-        compute(pair(1 + 2 * i))
-        return 0
-
-    lax.fori_loop(0, 2, sides, 0)
+    ring.from_core(2, 4)
+    compute(GROUPS[1])
+    ring.from_core(4, 6)
     ring.far()
-    ring.from_core(5, 7)
-    compute(pair(2))
+    compute(GROUPS[2])
+    ring.from_core(6, 8)
+    compute(GROUPS[3])
 
     keeps = [
         pltpu.make_async_copy(kv, kvs.at[me.c, chip], local.at[0]),
         pltpu.make_async_copy(poss, places.at[chip], local.at[1]),
         pltpu.make_async_copy(xs, xs_out, local.at[4]),
-        pltpu.make_async_copy(cot, cots.at[mine], local.at[5]),
     ]
     for d in keeps:
         d.start()
     pos_copies = [edges.copy(poss, places.at[chip], d) for d in far]
     kv_copies = [edges.copy(kv, kvs.at[me.c, chip], d) for d in far]
     over = [edges.copy(kv, kvs.at[me.c, chip], core)]
-    ring = RingGather(me, edges, cot, cots)
+    ring = RingGather(me, edges, cot, cots, local.at[pl.ds(6, 2)])
     ring.relay()
     for (dz, dl), d in zip(chips_in_sequence(me), kv_copies):
         d.wait_recv()
@@ -626,7 +634,7 @@
         + sems(5)
         + sems(8)
         + sems(2)
-        + [pltpu.SemaphoreType.DMA((6,))],
+        + [pltpu.SemaphoreType.DMA((8,))],
         compiler_params=remote_params(0),
         name="begin",
     )(tokens, gain, pos, trig, wqkv, wgu, wdn, cot, wout)
@@ -766,7 +774,7 @@
                 pltpu.VMEM((HD, 256), F32),
             ],
         ),
-        compiler_params=pltpu.CompilerParams(vmem_limit_bytes=40 * 2**20),
+        compiler_params=pltpu.CompilerParams(vmem_limit_bytes=61 * 2**20),
         name="attend",
     )(key_runs, query_runs, q, kv)
 
@@ -820,10 +828,8 @@
             def _():
                 tiles(start, n + 1, True)
 
-        pair_rows = trig_ref[r // 2]
-        table = jnp.where(
-            lax.rem(r, 2) == 0, rotary_of(pair_rows, 0), rotary_of(pair_rows, 1)
-        )
+        pair_rows = trig_ref[lax.rem(r, 2)]
+        table = jnp.where(r < 2, rotary_of(pair_rows, 0), rotary_of(pair_rows, 1))
         dq = (dq_acc[...] * 0.125).T
         heads = [rotate(dq[64 * h : 64 * h + 64], table, back=True) for h in range(4)]
         dq_ref[rows, :] = jnp.concatenate(heads, axis=1).astype(BF16)
@@ -866,7 +872,7 @@
                 pltpu.VMEM((HD, 256), F32),
             ],
         ),
-        compiler_params=pltpu.CompilerParams(vmem_limit_bytes=40 * 2**20),
+        compiler_params=pltpu.CompilerParams(vmem_limit_bytes=61 * 2**20),
         name="attend_back",
     )(key_runs, query_runs, q, kv, grad, ot, lse, trigs)
 
@@ -876,17 +882,19 @@
 
 
 class RingSum:
-    def __init__(self, me, edges, along_z, src, start, rows, width, step, relayed, last):
+    def __init__(
+        self, me, edges, along_z, src, start, rows, width, step, relayed, last, shift=0
+    ):
         self.edges, self.src, self.start, self.width, self.step = edges, src, start, width, step
         self.rows, self.half = rows, rows // 2
-        self.relayed, self.last = relayed, last
+        self.relayed, self.last, self.shift = relayed, last, shift
         self.here = me.z if along_z else x_of(me)
         self.up = around(me, 1, 0) if along_z else around(me, 0, 1)
         self.down = around(me, -1, 0) if along_z else around(me, 0, 3)
         self.a, self.b = pl.ds(0, self.half), pl.ds(self.half, self.half)
 
     def columns(self, k):
-        at = self.width * lax.rem(self.here + k, 4)
+        at = self.width * lax.rem(self.here + k + self.shift, 4)
         return pl.ds(pl.multiple_of(at, self.width), self.width)
 
     def piece(self, k, half):
@@ -945,10 +953,17 @@
 SUM_EDGES = 6
 
 
+def to_chunks(ref, ys, halves, cols, rows):
+    for i, (y, half) in enumerate(zip(ys, halves)):
+        for core in (0, 1):
+            at = TOK * i + HALF * core
+            ref[2 * y + core, HALF * half : HALF * half + HALF, cols] = rows[at : at + HALF]
+
+
 def feed_forward_kernel(
-    parts, tokens, gain, cots, wgu, wdn, wswap, wnear_up, wnear_down,
-    middle, grad_middle, gain_grad, gbs, z_out, x_out, branch,
-    xs, p, c, gp, w, act_t, gate_t, up_t, act, dgate, dup, low,
+    att, wo, tokens, cot, gain, cots, wgu, wdn, wswap, wnear_up, wnear_down,
+    middle, grad_middle, gain_grad, grad_att, grad_wo, z_out, x_out, branch,
+    xs, p, c, gp, gb, att_t, w, act_t, gate_t, up_t, act, dgate, dup, low,
     g1, b1, r1, l1,
     z_relayed, z_last, x_relayed, x_last, z_q, x_q,
     z_relayed2, z_last2, x_relayed2, x_last2,
@@ -962,11 +977,8 @@
         + [around(me, 0, 1), around(me, 0, 3)]
     )
     edges = Edges(send, recv)
-    mine = 2 * me.y + me.c
     moved = me.c != me.xh
-    load_p = pltpu.make_async_copy(parts, p, local.at[0])
     load_c = pltpu.make_async_copy(cots, c, local.at[1])
-    load_p.start()
     load_c.start()
 
     def w_rows(dz):
@@ -1010,9 +1022,35 @@
         for d in kept:
             d.start()
 
-    load_p.wait()
     ring = RingScatter(me, edges, p, (g1, b1, r1, l1))
-    ring.first()
+
+    def attended_part(k):
+        y = lax.rem(me.y + k, 4)
+        rows = att[pl.ds(pl.multiple_of(2 * TOK * y, 2 * TOK), 2 * TOK), :]
+
+        def block(i, _):
+            cols = pl.ds(pl.multiple_of(512 * i, 512), 512)
+            term = dot_last(rows, wo[cols, :]).astype(BF16)
+            to_chunks(p, (y, y), (0, 1), cols, term)
+            return 0
+
+        lax.fori_loop(0, 4, block, 0)
+        ring.send_core(k)
+
+    attended_part(2)
+    attended_part(1)
+    ring.far()
+    attended_part(3)
+    ring.near()
+    attended_part(0)
+    ring.add_core(0)
+
+    def turn_block(i, _):
+        at = pl.ds(pl.multiple_of(2 * TOK * i, 2 * TOK), 2 * TOK)
+        att_t[:, at] = att[at, :].astype(F32).T.astype(BF16)
+        return 0
+
+    lax.fori_loop(0, 4, turn_block, 0)
     ring.second()
     ring.arrived()
 
@@ -1023,9 +1061,7 @@
         low[at, :] = (normal * gain[...]).astype(BF16)
 
     in_chunks(norm)
-    keep = pltpu.make_async_copy(low, xs.at[mine], local.at[10])
-    keep.start()
-    gather = RingGather(me, edges, low, xs)
+    gather = RingGather(me, edges, low, xs, local.at[pl.ds(10, 2)])
     ring.release()
 
     @pl.when(moved)
@@ -1041,13 +1077,14 @@
             d.wait()
 
     load_c.wait()
-    keep.wait()
-
-    def compute(pair):
-        at = pl.ds(2 * pair, 2)
-        x = xs[at].reshape(2 * TOK, D)
-        g = c[at].reshape(2 * TOK, D)
-        here = pl.ds(pl.multiple_of(2 * TOK * pair, 2 * TOK), 2 * TOK)
+
+    def compute(group):
+        ys = [lax.rem(me.y + dy, 4) for dy, _ in group]
+        halves = [half for _, half in group]
+        blocks = [2 * y + half for y, half in zip(ys, halves)]
+        x = jnp.concatenate([xs[b] for b in blocks], axis=0)
+        g = jnp.concatenate([c[b] for b in blocks], axis=0)
+        here = [pl.ds(pl.multiple_of(TOK * b, TOK), TOK) for b in blocks]
         for n0, n1 in ((0, 256), (256, 512), (512, FF_DEV)):
             gate = dot_last(x, w[n0:n1, :])
             upward = dot_last(x, w[FF_DEV + n0 : FF_DEV + n1, :])
@@ -1060,42 +1097,37 @@
             act[:, n0:n1] = active.astype(BF16)
             dup[:, n0:n1] = grad_up.astype(BF16)
             dgate[:, n0:n1] = grad_gate.astype(BF16)
-            act_t[n0:n1, here] = active.T.astype(BF16)
-            up_t[n0:n1, here] = grad_up.T.astype(BF16)
-            gate_t[n0:n1, here] = grad_gate.T.astype(BF16)
+            for ref, value in ((act_t, active), (up_t, grad_up), (gate_t, grad_gate)):
+                value = value.T.astype(BF16)
+                ref[n0:n1, here[0]] = value[:, :TOK]
+                ref[n0:n1, here[1]] = value[:, TOK:]
 
         def block(i, _):
             cols = pl.ds(pl.multiple_of(512 * i, 512), 512)
             term = dot(act[...], w[2 * FF_DEV :, cols])
-            p[at, :, cols] = term.astype(BF16).reshape(2, TOK, 512)
+            to_chunks(p, ys, halves, cols, term.astype(BF16))
             grads = dot(dgate[...], w[:FF_DEV, cols]) + dot(dup[...], w[FF_DEV : 2 * FF_DEV, cols])
-            gp[at, :, cols] = grads.astype(BF16).reshape(2, TOK, 512)
+            to_chunks(gp, ys, halves, cols, grads.astype(BF16))
             return 0
 
         lax.fori_loop(0, 4, block, 0)
 
-    def pair(k):
-        return lax.rem(me.y + k, 4)
-
     two = RingScatter(me, edges, gp, (g1, b1, r1, l1))
-    gather.from_core(0, 1)
-    compute(pair(0))
+    gather.own()
+    compute(GROUPS[0])
     two.send_core(0)
     gather.relay()
     gather.near()
-    gather.from_core(1, 5)
-
-    def sides(i, _):
-        compute(pair(1 + 2 * i))
-        return 0
-
-    lax.fori_loop(0, 2, sides, 0)
+    gather.from_core(2, 4)
+    compute(GROUPS[1])
+    gather.from_core(4, 6)
+    gather.far()
+    compute(GROUPS[2])
     two.send_core(1)
     two.send_core(3)
-    gather.far()
     two.near()
-    gather.from_core(5, 7)
-    compute(pair(2))
+    gather.from_core(6, 8)
+    compute(GROUPS[3])
     two.send_core(2)
     save = pltpu.make_async_copy(p, branch, local.at[0])
     save.start()
@@ -1144,17 +1176,15 @@
         grad = two.rows(at)
         gain_grad[...] += jnp.sum(normal * grad, axis=0, keepdims=True)
         scaled = grad * gain[...]
-        result = c[mine, at].astype(F32) + inverse * (
+        result = cot[at, :].astype(F32) + inverse * (
             scaled - normal * mean_last(scaled * normal)
         )
         grad_middle[at, :] = result
         low[at, :] = result.astype(BF16)
 
-    edges.sent([gather.up_a, gather.up_b, gather.down_a, gather.down_b, gather.to_core[0]])
+    edges.sent(gather.sources())
     in_chunks(back)
-    keep = pltpu.make_async_copy(low, gbs.at[mine], local.at[10])
-    keep.start()
-    gather = RingGather(me, edges, low, gbs)
+    gather = RingGather(me, edges, low, gb, local.at[pl.ds(10, 2)])
     z_sum.second()
     x_sum.second()
     gather.relay()
@@ -1170,17 +1200,28 @@
     x_two.near_down()
     gather.near()
     gather.far()
+    gather.own()
+    gather.from_core(2, 8)
+
+    def attended_grad(i, _):
+        at = pl.ds(pl.multiple_of(2 * TOK * i, 2 * TOK), 2 * TOK)
+        rows = gb[pl.ds(2 * i, 2)].reshape(2 * TOK, D)
+        grad_att[at, :] = dot(rows, wo[...]).astype(BF16)
+        cols = pl.ds(pl.multiple_of(512 * i, 512), 512)
+        rows = gb[:, :, cols].reshape(8 * TOK, 512)
+        grad_wo[:, cols] = dot(att_t[...], rows).astype(BF16)
+        return 0
+
+    lax.fori_loop(0, 4, attended_grad, 0)
     z_two.second()
     x_two.second()
-    gather.from_core(0, 7)
     z_two.total(z_out)
     x_two.total(x_out)
     edges.finish()
-    keep.wait()
     save.wait()
 
 
-def feed_forward(parts, tokens, gain, cots, wgu, wdn, wswap, wnear_up, wnear_down):
+def feed_forward(att, wo, tokens, cot, gain, cots, wgu, wdn, wswap, wnear_up, wnear_down):
     block = pltpu.VMEM((8, TOK, D), BF16)
     turned = pltpu.VMEM((FF_DEV, 8 * TOK), BF16)
     pair = pltpu.VMEM((2 * TOK, FF_DEV), BF16)
@@ -1197,14 +1238,16 @@
             shape((TOK, D), F32),
             shape((TOK, D), F32),
             shape((1, D), F32),
-            shape((8, TOK, D)),
+            shape((1024, Q_DEV)),
+            shape((Q_DEV, D)),
             shape((PART, 128)),
             shape((PART, 128)),
             shape((8, TOK, D)),
         ),
-        in_specs=[ANY, VMEM, VMEM] + [ANY] * 6,
-        out_specs=(VMEM, VMEM, VMEM, ANY, VMEM, VMEM, ANY),
-        scratch_shapes=[block] * 4
+        in_specs=[VMEM] * 5 + [ANY] * 6,
+        out_specs=(VMEM,) * 7 + (ANY,),
+        scratch_shapes=[block] * 5
+        + [pltpu.VMEM((Q_DEV, 8 * TOK), BF16)]
         + [pltpu.VMEM((3 * FF_DEV, D), BF16)]
         + [turned] * 3
         + [pair] * 3
@@ -1215,12 +1258,12 @@
         + ring(128)
         + sems(2 * SCATTER_EDGES + 2 * GATHER_EDGES + 4 * SUM_EDGES)
         + sems(2)
-        + [pltpu.SemaphoreType.DMA((11,))],
+        + [pltpu.SemaphoreType.DMA((12,))],
         compiler_params=pltpu.CompilerParams(
             collective_id=2, has_side_effects=True, vmem_limit_bytes=62 * 2**20
         ),
         name="feed_forward",
-    )(parts, tokens, gain, cots, wgu, wdn, wswap, wnear_up, wnear_down)
+    )(att, wo, tokens, cot, gain, cots, wgu, wdn, wswap, wnear_up, wnear_down)
 
 
 def columns(width):
@@ -1361,7 +1404,7 @@
         self.one = [
             RingSum(
                 me, edges, i == 0, src, start[i], rows[i], 512, steps[0][i],
-                scratch[2 * i], scratch[2 * i + 1],
+                scratch[2 * i], scratch[2 * i + 1], me.y,
             )
             for i in (0, 1)
         ]
@@ -1428,7 +1471,6 @@
     signalled = greet(plane_devices(me) + group_members(me)[1:])
     edges = Edges(send, recv)
     place = 4 * me.z + x_of(me)
-    turned = 4 * x_of(me) + me.z
     rank = 2 * me.y + me.c
     load_x = pltpu.make_async_copy(xs_in, xs, local.at[0])
     load_branch = pltpu.make_async_copy(branch_in, branch_parts, local.at[1])
@@ -1459,15 +1501,13 @@
     branch = RingScatter(me, edges, branch_parts, (g2, b2, r2, l2))
     for k in (2, 1, 3, 0):
         branch.send_core(k)
-    plane = PlaneGather(me, edges, z_piece, x_piece, z_all, x_all, ps, pr)
     far_copies = []
     for i, (chip, d) in enumerate(order):
         d.wait_recv()
         kv_both[chip] = (dkv[me.c, chip].astype(F32) + kv_got[chip].astype(F32)).astype(BF16)
         if i < 7:
             far_copies.append(edges.copy(kv_both.at[chip], kv_last.at[i], far[i]))
-    branch.far()
-    branch.near()
+    plane = PlaneGather(me, edges, z_piece, x_piece, z_all, x_all, ps, pr)
     load_x.wait()
 
     def weight_block(i, _):
@@ -1481,8 +1521,11 @@
     for d in load_wo:
         d.wait()
     early_sum = TwoSums(me, edges, early, EARLY_ROWS, ((64, 64), (128, 128)), early_scratch)
+    branch.far()
+    branch.near()
     plane.sideways()
     branch.add_core(0)
+    early_sum.second()
     branch.second()
     for d in far_copies:
         d.wait_recv()
@@ -1496,36 +1539,14 @@
         )
 
     in_chunks(kv_total, 512)
-    for i in range(4):
-        for half in (0, 1):
-            rows = dkv_low[TOK * i : TOK * (i + 1), HD * half : HD * half + HD]
-            at = slice(TOK * (2 * i + half), TOK * (2 * i + half + 1))
-            grads[at, Q_DEV:] = rows.astype(BF16)
-            grads_t[Q_DEV:, at] = rows.T.astype(BF16)
-    early_sum.second()
+    for i in range(8):
+        rows = dkv_low[64 * i : 64 * (i + 1), :]
+        rows = jnp.concatenate([rows[:, :HD], rows[:, HD:]], axis=0)
+        at = slice(TOK * i, TOK * (i + 1))
+        grads[at, Q_DEV:] = rows.astype(BF16)
+        grads_t[Q_DEV:, at] = rows.T.astype(BF16)
+
     plane.along()
-
-    ring = RingScatter(me, edges, parts, (g1, b1, r1, l1))
-
-    def part(k):
-        pair = lax.rem(me.y + k, 4)
-        rows = grads[pl.ds(pl.multiple_of(2 * TOK * pair, 2 * TOK), 2 * TOK), :]
-
-        def block(i, _):
-            cols = pl.ds(pl.multiple_of(512 * i, 512), 512)
-            term = dot(rows, wq[:, cols]).astype(BF16)
-            parts[pl.ds(2 * pair, 2), :, cols] = term.reshape(2, TOK, 512)
-            return 0
-
-        lax.fori_loop(0, 4, block, 0)
-        ring.send_core(k)
-
-    part(2)
-    part(1)
-    ring.far()
-    part(3)
-    ring.near()
-    part(0)
 
     def late_block(i, _):
         cols = pl.ds(pl.multiple_of(512 * i, 512), 512)
@@ -1533,20 +1554,34 @@
         late[:, cols] = dot(grads_t[Q_DEV:, :], rows).astype(BF16)
         return 0
 
+    ring = RingScatter(me, edges, parts, (g1, b1, r1, l1))
+
+    def part(k):
+        y = lax.rem(me.y + k, 4)
+        rows = grads[pl.ds(pl.multiple_of(2 * TOK * y, 2 * TOK), 2 * TOK), :]
+
+        def block(i, _):
+            cols = pl.ds(pl.multiple_of(512 * i, 512), 512)
+            to_chunks(parts, (y, y), (0, 1), cols, dot(rows, wq[:, cols]).astype(BF16))
+            return 0
+
+        lax.fori_loop(0, 4, block, 0)
+        ring.send_core(k)
+
+    part(2)
+    part(1)
+    ring.far()
+    part(3)
+    early_sum.cross()
+    ring.near()
     lax.fori_loop(0, 4, late_block, 0)
     late_sum = SumOfSixteen(me, late, columns(128), late_own, late_got, us, ur, local.at[4])
+    part(0)
     ring.add_core(0)
-    early_sum.cross()
+    early_sum.fourth()
+    early_sum.total()
     plane.near()
     ring.second()
-    early_sum.fourth()
-    branch.arrived()
-
-    def out(at):
-        output[at, :] = (middle[at, :] + branch.rows(at)).astype(BF16)
-
-    in_chunks(out)
-    late_piece[...] = late_sum.total().astype(BF16)
     wq_deliver = Deliver(me, ds, dr)
 
     def deliver_block(j, src, at):
@@ -1558,10 +1593,10 @@
         ]
         wq_deliver.to_owner(src, dst, at // 8, owner // 2, lax.rem(owner, 2))
 
-    deliver_block(4, late_piece, place)
-    early_sum.total()
     wo_deliver = Deliver(me, es, er)
-    for i, at in enumerate((place, turned)):
+    early_place = 4 * lax.rem(me.z + me.y, 4) + x_of(me)
+    early_turned = 4 * lax.rem(x_of(me) + me.y, 4) + me.z
+    for i, at in enumerate((early_place, early_turned)):
         for j in (0, 1):
             deliver_block(2 * i + j, early_sum.out[i].at[pl.ds(64 * j, 64)], at)
         dst = wo_all.at[
@@ -1570,6 +1605,14 @@
         ]
         src = early_sum.out[i].at[pl.ds(128, 128)]
         wo_deliver.to_owner(src, dst, me.y // 2, at // 4, lax.rem(at // 2, 2))
+    late_piece[...] = late_sum.total().astype(BF16)
+    deliver_block(4, late_piece, place)
+    branch.arrived()
+
+    def out(at):
+        output[at, :] = (middle[at, :] + branch.rows(at)).astype(BF16)
+
+    in_chunks(out)
     ring.arrived()
     mine[...] = jnp.zeros_like(mine)
     mine[1:2, :] = gain_two[...]
@@ -1695,7 +1738,7 @@
     )
 
 
-def widen_kernel(z_ref, x_ref, gu_ref, dn_ref):
+def widen_kernel(z_ref, x_ref, wq_ref, wo_ref, gu_ref, dn_ref, gq_ref, go_ref):
     i = pl.program_id(0)
 
     @pl.when(i < 3)
@@ -1710,24 +1753,36 @@
     def _():
         dn_ref[...] = x_ref[...].astype(F32)
 
-
-def widen(z_all, x_all):
+    gq_ref[...] = wq_ref[...].astype(F32)
+    go_ref[...] = wo_ref[...].astype(F32).T
+
+
+def widen(z_all, x_all, wq, wo):
     rows = PART // 3
     return pl.pallas_call(
         widen_kernel,
-        out_shape=(shape((2 * FF_DEV, D), F32), shape((FF_DEV, D), F32)),
+        out_shape=(
+            shape((2 * FF_DEV, D), F32),
+            shape((FF_DEV, D), F32),
+            shape((320, D), F32),
+            shape((256, D), F32),
+        ),
         grid=(6,),
         in_specs=[
             pl.BlockSpec((rows, D), lambda i: (jnp.minimum(i, 2), 0)),
             pl.BlockSpec((rows, D), lambda i: (jnp.maximum(i - 3, 0), 0)),
+            pl.BlockSpec((64, D), lambda i: (jnp.minimum(i, 4), 0)),
+            pl.BlockSpec((512, 256), lambda i: (jnp.minimum(i, 3), 0)),
         ],
         out_specs=(
             pl.BlockSpec((rows, D), lambda i: (jnp.minimum(i, 3), 0)),
             pl.BlockSpec((rows, D), lambda i: (jnp.maximum(i - 4, 0), 0)),
+            pl.BlockSpec((64, D), lambda i: (jnp.minimum(i, 4), 0)),
+            pl.BlockSpec((256, 512), lambda i: (0, jnp.minimum(i, 3))),
         ),
-        compiler_params=pltpu.CompilerParams(vmem_limit_bytes=40 * 2**20),
+        compiler_params=pltpu.CompilerParams(vmem_limit_bytes=61 * 2**20),
         name="widen",
-    )(z_all, x_all)
+    )(z_all, x_all, wq, wo)
 
 
 def route(dz):
@@ -1756,20 +1811,16 @@
         w_out,
     )
     wo = wo.reshape(D, Q_DEV)
-    query_runs = poss[:, 0, ::64].reshape(16) // 64
+    query_runs = poss[:, 0, ::64].reshape(4, 2, 2).transpose(0, 2, 1).reshape(16) // 64
     key_runs = (
         places[:, :, 0, ::64].reshape(8, 4, 2, 2).transpose(1, 0, 2, 3).reshape(128) // 64
     )
     wnear_up = lax.ppermute(wswap, AXES, route(1))
     wnear_down = lax.ppermute(wswap, AXES, route(3))
     att, ot, lse = attend(key_runs, query_runs, query, kvs)
-    parts = dot_last(att, wo).astype(BF16).reshape(8, TOK, D)
-    middle, grad_middle, gain_grad, gbs, z_piece, x_piece, branch = feed_forward(
-        parts, hidden[0], gain_two, cots, wgu, wdn, wswap, wnear_up, wnear_down
+    middle, grad_middle, gain_grad, grad_att, grad_wo, z_piece, x_piece, branch = feed_forward(
+        att, wo, hidden[0], cotangent[0], gain_two, cots, wgu, wdn, wswap, wnear_up, wnear_down
     )
-    gb = gbs.reshape(1024, D)
-    grad_att = dot(gb, wo).astype(BF16)
-    grad_wo = dot_first(att, gb).astype(BF16)
     dq, dkv = attend_back(key_runs, query_runs, query, kvs, grad_att, ot, lse, trigs)
     output, grad_tokens, gains, grad_w_qkv, grad_w_out, z_all, x_all = ending(
         dkv,
@@ -1787,13 +1838,13 @@
         xs,
         branch,
     )
-    grad_gu, grad_dn = widen(z_all, x_all)
+    grad_gu, grad_dn, grad_w_qkv, grad_w_out = widen(z_all, x_all, grad_w_qkv, grad_w_out)
     return (
         output[None],
         grad_tokens[None],
         gains[0],
-        grad_w_qkv.astype(F32),
-        grad_w_out.T.astype(F32),
+        grad_w_qkv,
+        grad_w_out,
         gains[1],
         grad_gu.reshape(2, FF_DEV, D),
         grad_dn.T,

time: 403 us -> 390 us (0.968)
  matrix products: 9.45 us -> 0 us
  Pallas kernels: 354 us -> 363 us
  local copies, waits for them, and re-layouts: 20.9 us -> 12.9 us
    dot_general x3 -> x0, matrix products: 9.45 us -> none  [the longest x1 3.89 us: dot(): lax.dot_general(a, b, (((1,), (0,)), ((), ())), preferred_element_type=F32)]
    unnamed x43 -> x26, local copies, waits for them, and re-layouts: 16.9 us -> 9.37 us
    pallas_call x1, Pallas kernels: 110 us -> 104 us  [ending(): pl.pallas_call(ending_kernel, out_shape=(shape((TOK, D)), shape((TOK, D),...]
    pallas_call x1, Pallas kernels: 31.2 us -> 37.3 us  [attend_back(): pl.pallas_call(attend_back_kernel, out_shape=(shape((1024, 256)), shape((...]
    pallas_call x1, Pallas kernels: 7.33 us -> 12.4 us  [widen(): pl.pallas_call(widen_kernel, out_shape=(shape((2 * FF_DEV, D), F32), shap...]
    pallas_call x1, Pallas kernels: 21.9 us -> 26.5 us  [attend(): pl.pallas_call(attend_kernel, out_shape=(shape((1024, 256)), shape((16, H...]
  transfers between devices with their start and end apart: 2 -> 2, of which waited for: 0 -> 0; matrix products, arithmetic and copies ran while one was open for 2% -> 1% of each run, Pallas kernels for 6% -> 7%
where the time goes in v6:
time: 390 us; the launch traced here: 386 us
  Pallas kernels  363 us (93%)
  local copies, waits for them, and re-layouts  12.9 us (3%)
  starting transfers between devices  5.8 us (1%)
    pallas_call x1, Pallas kernels, feed_forward(): pl.pallas_call(feed_forward_kernel, out_shape=(shape((TOK, D), F32), shap...  120 us
    pallas_call x1, Pallas kernels, ending(): pl.pallas_call(ending_kernel, out_shape=(shape((TOK, D)), shape((TOK, D),...  104 us
    pallas_call x1, Pallas kernels, begin(): pl.pallas_call(begin_kernel, out_shape=(shape((1024, Q_DEV)), shape((2, 5...  63.3 us
    pallas_call x1, Pallas kernels, attend_back(): pl.pallas_call(attend_back_kernel, out_shape=(shape((1024, 256)), shape((...  37.3 us
    pallas_call x1, Pallas kernels, attend(): pl.pallas_call(attend_kernel, out_shape=(shape((1024, 256)), shape((16, H...  26.5 us
    pallas_call x1, Pallas kernels, widen(): pl.pallas_call(widen_kernel, out_shape=(shape((2 * FF_DEV, D), F32), shap...  12.4 us
    unnamed x26, local copies, waits for them, and re-layouts  9.37 us
  transfers between devices with their start and end apart: 2, of which 0 were waited for; matrix products, arithmetic and copies ran while one was open for 1% of the time, Pallas kernels for 7%

profile of v6, /device:TPU:9, one launch (start us, length us, event | category | flops | bytes accessed | tf_op | source)
XLA Modules:
  0.0 385.6 jit_solution(9541712145682607333)
XLA Ops:
  0.6 0.7 convert_reduce_fusion
  1.3 0.1 convert_element_type.13
  1.4 0.7 reshape.88
  2.1 0.0 copy-start.8
  2.1 0.2 multiply_cosine_fusion
  2.3 0.1 copy.32.trig
  2.4 0.7 broadcast_in_dim.16.pos
  3.1 0.0 copy-start
  3.1 1.0 copy-done
  4.1 0.0 copy-start.1
  4.1 1.0 copy-done.1
  5.1 0.0 copy-start.4
  5.1 1.2 copy-done.4
  6.4 0.0 copy-start.11
  6.4 63.3 %begin.1 = (bf16[1024,256]{1,0:T(8,128)(2,1)S(1)}, f32[2,512,128]{2,1,0:T(8,128)S(1)}, f32[8,64,128]{2,1,0:T(8,128)S(1)}, bf16[8,128,2048]{2,1,0:T(8,128)(2,1)},...) custom-call(bf16[128,2048]{1,0:T(8,128)(2,1)S(1)} %bitcast.24, ...), custom_call_target="tpu_custom_call" | custom-call | tf_op jit(solution)/shard_map/begin/pallas_call | solution.py:610
  69.7 0.0 copy-done.8
  69.7 0.0 copy-start.2
  69.7 0.8 copy-done.2
  70.5 0.0 copy-start.3
  70.5 1.1 copy-done.3
  71.5 1.0 copy-done.5
  72.5 0.8 copy-done.6
  73.3 0.7 copy-done.7
  74.0 1.9 collective-permute-start.1
  75.9 3.9 %collective-permute-start = (bf16[528,2048]{1,0:T(8,128)(2,1)}, bf16[528,2048]{1,0:T(8,128)(2,1)}, u32[]{:S(2)}, u32[]{:S(2)}) collective-permute-start(bf16[528,2048]{1,0:T(8,128)(2,1)} %get-tuple-element.50.wswap), channel_id=1, source_target_pairs={{1,33},{3,35},{5,37},{7,39},{8,40},{10,42},{12,44},{14,46},{17,49}... | collective-permute-start | bytes 6488072 | tf_op jit(solution)/shard_map/ppermute | solution.py:1818
  79.8 0.0 copy-done.11
  79.8 0.6 reshape.90
  80.4 0.7 slice.12
  81.1 0.1 copy.28
  81.2 0.1 slice.13
  81.3 0.1 copy.33
  81.5 0.1 reshape.83
  81.5 0.1 copy.29
  81.7 0.1 reshape.82
  81.8 0.5 and_select_fusion.query_runs
  82.3 0.5 and_select_fusion.1.key_runs
  82.9 26.5 %attend.1 = (bf16[1024,256]{1,0:T(8,128)(2,1)}, f32[16,64,256]{2,1,0:T(8,128)}, f32[16,1,256]{2,1,0:T(1,128)}) custom-call(s32[128]{0:T(128)} %and_select_fusion.1.key_runs, s32[16]{0:T(128)} %and_select_fusion.query_runs, bf16[1024,256]{1,0:T(8,128)(2,1)} %copy-done.2, bf16[2,8,512,128]{3,2,1,0:T(8,128)(2,1)} %get-tuple-element.46.kv_ref), custom_call_target="tpu_custom_call" | custom-call | tf_op jit(solution)/shard_map/attend/pallas_call | solution.py:753
  109.3 0.0 collective-permute-done.1.wnear_down
  109.3 0.0 collective-permute-done.wnear_up
  109.3 119.7 %feed_forward.1 = (f32[128,2048]{1,0:T(8,128)}, f32[128,2048]{1,0:T(8,128)}, f32[1,2048]{1,0:T(1,128)}, bf16[1024,256]{1,0:T(8,128)(2,1)}, bf16[256,2048]{1,0:T(...) custom-call(bf16[1024,256]{1,0:T(8,128)(2,1)} %get-tuple-element.47.att, ...), custom_call_target="tpu_custom_call" | custom-call | tf_op jit(solution)/shard_map/feed_forward/pallas_call | solution.py:1235
  229.0 37.3 %attend_back.1 = (bf16[1024,256]{1,0:T(8,128)(2,1)}, bf16[2,8,512,128]{3,2,1,0:T(8,128)(2,1)}) custom-call(s32[128]{0:T(128)} %and_select_fusion.1.key_runs, s32[16]{0:T(128)} %and_select_fusion.query_runs, bf16[1024,256]{1,0:T(8,128)(2,1)} %copy-done.2, bf16[2,8,512,128]{3,2,1,0:T(8,128)(2,1)} %get-tuple-element.46.kv_ref, ...), custom_call_target="tpu_custom_call" | custom-call | tf_op jit(solution)/shard_map/attend_back/pallas_call | solution.py:848
  266.3 103.5 %ending.1 = (bf16[128,2048]{1,0:T(8,128)(2,1)}, f32[128,2048]{1,0:T(8,128)}, f32[8,256]{1,0:T(8,128)}, bf16[320,2048]{1,0:T(8,128)(2,1)}, bf16[2048,256]{1,0:T(8...) custom-call(bf16[2,8,512,128]{3,2,1,0:T(8,128)(2,1)} %get-tuple-element.55.dkv, ...), custom_call_target="tpu_custom_call" | custom-call | tf_op jit(solution)/shard_map/ending/pallas_call | solution.py:1689
  369.8 1.3 fusion
  371.2 12.4 %widen.1 = (f32[1408,2048]{1,0:T(8,128)}, f32[704,2048]{1,0:T(8,128)}, f32[320,2048]{1,0:T(8,128)}, f32[256,2048]{1,0:T(8,128)}) custom-call(bf16[1056,2048]{1,0:T(8,128)(2,1)} %get-tuple-element.70.z_ref, bf16[1056,2048]{1,0:T(8,128)(2,1)} %get-tuple-element.71.x_ref, bf16[320,2048]{1,0:T(8,128)(2,1)} %get-tuple-element.72.wq_ref, ...), custom_call_target="tpu_custom_call" | custom-call | tf_op jit(solution)/shard_map/widen/pallas_call | solution.py:1762
  383.6 0.0 copy-done.10
  383.6 0.8 copy.36
  384.4 0.0 copy-done.9
  384.4 1.0 copy.37
  (8 shorter events, 0.0 us)
Async XLA Ops:
  2.1 67.6 %copy-start.8 = (f32[2048]{0:T(1024)}, f32[2048]{0:T(1024)S(1)}, u32[]{:S(2)}) copy-start(f32[2048]{0:T(1024)S(1)} %reshape.88) | copy-start | bytes 24580
  3.1 1.0 copy-start
  4.1 1.0 copy-start.1
  5.1 1.2 copy-start.4
  6.4 73.4 %copy-start.11 = (bf16[2048]{0:T(1024)(128)(2,1)S(1)}, bf16[2048]{0:T(1024)(128)(2,1)}, u32[]{:S(2)}) copy-start(bf16[2048]{0:T(1024)(128)(2,1)} %param.14) | copy-start | bytes 12292
  69.7 0.8 copy-start.2
  70.5 1.1 copy-start.3
  71.5 1.0 copy-start.5
  72.5 0.8 copy-start.6
  73.3 0.7 copy-start.7
  74.0 35.3 %collective-permute-start.1 = (bf16[528,2048]{1,0:T(8,128)(2,1)}, bf16[528,2048]{1,0:T(8,128)(2,1)}, u32[]{:S(2)}, u32[]{:S(2)}) collective-permute-start(bf16[528,2048]{1,0:T(8,128)(2,1)} %get-tuple-element.50.wswap), channel_id=1, source_target_pairs={{1,97},{3,99},{5,101},{7,103},{8,104},{10,106},{12,108},{14,110},{... | collective-permute-start | bytes 6488072 | tf_op jit(solution)/shard_map/ppermute | solution.py:1819
  75.9 33.4 %collective-permute-start = (bf16[528,2048]{1,0:T(8,128)(2,1)}, bf16[528,2048]{1,0:T(8,128)(2,1)}, u32[]{:S(2)}, u32[]{:S(2)}) collective-permute-start(bf16[528,2048]{1,0:T(8,128)(2,1)} %get-tuple-element.50.wswap), channel_id=1, source_target_pairs={{1,33},{3,35},{5,37},{7,39},{8,40},{10,42},{12,44},{14,46},{17,49}... | collective-permute-start | bytes 6488072 | tf_op jit(solution)/shard_map/ppermute | solution.py:1818
  371.2 12.4 %copy-start.10 = (bf16[128,2048]{1,0:T(8,128)(2,1)S(1)}, bf16[128,2048]{1,0:T(8,128)(2,1)}, u32[]{:S(2)}) copy-start(bf16[128,2048]{1,0:T(8,128)(2,1)} %get-tuple-element.67) | copy-start | bytes 1572868
  371.2 13.2 %copy-start.9 = (f32[128,2048]{1,0:T(8,128)S(1)}, f32[128,2048]{1,0:T(8,128)}, u32[]{:S(2)}) copy-start(f32[128,2048]{1,0:T(8,128)} %get-tuple-element.68) | copy-start | bytes 3145732

commit v7 on v6

--- a/solution.py
+++ b/solution.py
@@ -256,7 +256,7 @@
 
 def remote_params(number):
     return pltpu.CompilerParams(
-        collective_id=number, has_side_effects=True, vmem_limit_bytes=48 * 2**20
+        collective_id=number, has_side_effects=True, vmem_limit_bytes=61 * 2**20
     )
 
 
@@ -442,8 +442,8 @@
 
 def begin_kernel(
     tokens, gain, pos, trig, wqkv, wgu, wdn, cot, wout,
-    q, kv_table, trigs, xs_out, wq_out, poss, kvs, places, cots, wo, wswap,
-    low, xs, wq, kv,
+    q, kv_table, trigs, runs, xs_out, wq_out, kvs, places, cots, wo, wswap,
+    low, xs, wq, kv, poss, own_runs,
     send, recv, qs, qr, os_, orr, ws, wr, local,
 ):
     me = Place()
@@ -487,9 +487,17 @@
         send_block(me, src, dst, qs.at[i], qr.at[slot], target, stays)
         blocks.append((src, qs.at[i], stays))
 
-    keep_pos = pltpu.make_async_copy(pos, poss.at[mine], local.at[1])
+    lane = lax.broadcasted_iota(jnp.int32, (8, TOK), 1)
+    first = 4 * me.y + me.c
+    run_numbers = jnp.where(
+        lane == first,
+        jnp.broadcast_to(pos[:, 0:1], (8, TOK)),
+        jnp.where(lane == first + 2, jnp.broadcast_to(pos[:, 64:65], (8, TOK)), 0),
+    )
+    own_runs[...] = lax.shift_right_logical(run_numbers, 6)
+    keep_pos = pltpu.make_async_copy(own_runs, poss.at[mine], local.at[1])
     keep_pos.start()
-    pos_copies = [edges.copy(pos, poss.at[mine], m) for m in members]
+    pos_copies = [edges.copy(own_runs, poss.at[mine], m) for m in members]
     trigs[mine] = trig[...]
     trig_copies = [edges.copy(trig, trigs.at[mine], me.at(dy=k)) for k in (1, 2, 3)]
     trig_over = [edges.copy(trig, trigs.at[mine], core)]
@@ -530,6 +538,10 @@
     keep_pos.wait()
     for d in pos_copies + trig_over:
         d.wait_recv()
+    combined = poss[0]
+    for i in range(1, 8):
+        combined = combined + poss[i]
+    runs[...] = combined
     for d in wq_copies:
         d.wait_recv()
     wq_save = pltpu.make_async_copy(wq, wq_out, local.at[2])
@@ -575,12 +587,12 @@
 
     keeps = [
         pltpu.make_async_copy(kv, kvs.at[me.c, chip], local.at[0]),
-        pltpu.make_async_copy(poss, places.at[chip], local.at[1]),
+        pltpu.make_async_copy(runs, places.at[chip], local.at[1]),
         pltpu.make_async_copy(xs, xs_out, local.at[4]),
     ]
     for d in keeps:
         d.start()
-    pos_copies = [edges.copy(poss, places.at[chip], d) for d in far]
+    pos_copies = [edges.copy(runs, places.at[chip], d) for d in far]
     kv_copies = [edges.copy(kv, kvs.at[me.c, chip], d) for d in far]
     over = [edges.copy(kv, kvs.at[me.c, chip], core)]
     ring = RingGather(me, edges, cot, cots, local.at[pl.ds(6, 2)])
@@ -613,22 +625,24 @@
             shape((1024, Q_DEV)),
             shape((2, 512, 128), F32),
             shape((8, 64, 128), F32),
+            shape((8, TOK), jnp.int32),
             shape((8, TOK, D)),
             shape((320, D)),
+            shape((2, 8, 512, 128)),
             shape((8, 8, TOK), jnp.int32),
-            shape((2, 8, 512, 128)),
-            shape((8, 8, 8, TOK), jnp.int32),
             shape((8, TOK, D)),
             shape((8, 256, Q_DEV)),
             shape((QUARTER, D)),
         ),
         in_specs=[VMEM, VMEM, VMEM, VMEM] + [ANY] * 5,
-        out_specs=(VMEM, VMEM, VMEM) + (ANY,) * 8,
+        out_specs=(VMEM, VMEM, VMEM, VMEM) + (ANY,) * 7,
         scratch_shapes=[
             pltpu.VMEM((TOK, D), BF16),
             pltpu.VMEM((8, TOK, D), BF16),
             pltpu.VMEM((320, D), BF16),
             pltpu.VMEM((512, 128), BF16),
+            pltpu.VMEM((8, 8, TOK), jnp.int32),
+            pltpu.VMEM((8, TOK), jnp.int32),
         ]
         + sems(7 + 7 + 6 + 2 * GATHER_EDGES + 7 + 7 + 8)
         + sems(5)
@@ -661,22 +675,27 @@
 
 
 TILE = 256
-WIDE = 4
-
-
-def sort_keys(runs, seq, kv_ref, keys, values):
+WIDE = 8
+
+
+def run_rows(runs, seq, chip, core, u):
+    run = runs[16 * chip + 4 * seq + 2 * u + core]
+    return pl.ds(pl.multiple_of(run * 64, 64), 64)
+
+
+def sort_keys(runs, seq, kv_ref, sorted_kv):
     for j in range(32):
         chip, core, u = j // 4, (j // 2) % 2, j % 2
-        to = pl.ds(pl.multiple_of(runs[seq * 32 + j] * 64, 64), 64)
+        to = run_rows(runs, seq, chip, core, u)
         rows, lanes = slice(64 * u, 64 * u + 64), slice(HD * core, HD * core + HD)
-        keys[to, :] = kv_ref[0, chip, rows, lanes]
-        values[to, :] = kv_ref[1, chip, rows, lanes]
-
-
-def turn(rows, turned):
+        both = [kv_ref[0, chip, rows, lanes], kv_ref[1, chip, rows, lanes]]
+        sorted_kv[to, :] = jnp.concatenate(both, axis=1)
+
+
+def turn(rows, lanes, turned):
     for i in range(4):
         at = slice(512 * i, 512 * (i + 1))
-        turned[:, at] = rows[at, :].astype(F32).T.astype(BF16)
+        turned[:, at] = rows[at, lanes].astype(F32).T.astype(BF16)
 
 
 def allowed_tile(tile, run):
@@ -691,16 +710,18 @@
 
 def attend_kernel(
     key_runs, query_runs, q_ref, kv_ref, att_ref, ot_ref, lse_ref,
-    keys, values, values_t, high_ref, total_ref, acc_ref,
+    sorted_kv, values_t, high_ref, total_ref, acc_ref,
 ):
     seq = pl.program_id(0)
-    sort_keys(key_runs, seq, kv_ref, keys, values)
-    turn(values, values_t)
+    sort_keys(key_runs, seq, kv_ref, sorted_kv)
+    turn(sorted_kv, slice(HD, 2 * HD), values_t)
+    empty = jnp.zeros((HD, 256), BF16)
 
     def one_run(r, _):
         run = query_runs[seq * 4 + r]
         rows = pl.ds(pl.multiple_of(r * 64, 64), 64)
         query = split_heads(q_ref[rows, :]).astype(F32).T.astype(BF16)
+        query = jnp.concatenate([query, empty], axis=0)
         last = run // 4
         high_ref[...] = jnp.full((1, 256), FILLER, F32)
         total_ref[...] = jnp.zeros((1, 256), F32)
@@ -709,7 +730,7 @@
         def tiles(first, count, masked):
             scores = []
             for k in range(count):
-                score = dot(keys[tile_rows(first + k), :], query)
+                score = dot(sorted_kv[tile_rows(first + k), :], query)
                 if masked and k == count - 1:
                     score = jnp.where(allowed_tile(first + k, run), score, FILLER)
                 scores.append(score)
@@ -728,16 +749,11 @@
             total_ref[...] = total
             acc_ref[...] = acc
 
-        @pl.when(last >= WIDE)
-        def _():
-            tiles(0, WIDE, False)
-
-        start = (last // WIDE) * WIDE
         for n in range(WIDE):
 
-            @pl.when(last - start == n)
+            @pl.when(last == n)
             def _():
-                tiles(start, n + 1, True)
+                tiles(0, n + 1, True)
 
         total = total_ref[...]
         out = acc_ref[...] / total
@@ -766,8 +782,7 @@
                 pl.BlockSpec((4, 1, 256), lambda i, *_: (i, 0, 0)),
             ],
             scratch_shapes=[
-                pltpu.VMEM((2048, HD), BF16),
-                pltpu.VMEM((2048, HD), BF16),
+                pltpu.VMEM((2048, 2 * HD), BF16),
                 pltpu.VMEM((HD, 2048), BF16),
                 pltpu.VMEM((1, 256), F32),
                 pltpu.VMEM((1, 256), F32),
@@ -781,13 +796,14 @@
 
 def attend_back_kernel(
     key_runs, query_runs, q_ref, kv_ref, da_ref, ot_ref, lse_ref, trig_ref,
-    dq_ref, dkv_ref, keys, values, keys_t, dkeys, dvalues, dq_acc,
+    dq_ref, dkv_ref, sorted_kv, keys_t, grad_kv, dq_acc,
 ):
     seq = pl.program_id(0)
-    sort_keys(key_runs, seq, kv_ref, keys, values)
-    turn(keys, keys_t)
-    dkeys[...] = jnp.zeros_like(dkeys)
-    dvalues[...] = jnp.zeros_like(dvalues)
+    sort_keys(key_runs, seq, kv_ref, sorted_kv)
+    turn(sorted_kv, slice(0, HD), keys_t)
+    grad_kv[...] = jnp.zeros_like(grad_kv)
+    empty = jnp.zeros((HD, 256), BF16)
+    blank = jnp.zeros((256, HD), BF16)
 
     def one_run(r, _):
         run = query_runs[seq * 4 + r]
@@ -798,7 +814,15 @@
         query_t = query.astype(F32).T.astype(BF16)
         grad_t = grad.astype(F32).T
         delta = jnp.sum(grad_t * ot_ref[r], axis=0, keepdims=True)
-        grad_t = grad_t.astype(BF16)
+        query_t = jnp.concatenate([query_t, empty], axis=0)
+        grad_t = jnp.concatenate([empty, grad_t.astype(BF16)], axis=0)
+        right = jnp.concatenate(
+            [
+                jnp.concatenate([query, blank], axis=1),
+                jnp.concatenate([blank, grad], axis=1),
+            ],
+            axis=0,
+        )
         last = run // 4
         dq_acc[...] = jnp.zeros((HD, 256), F32)
 
@@ -806,27 +830,22 @@
             dq = dq_acc[...]
             for k in range(count):
                 at = tile_rows(first + k)
-                key = keys[at, :]
-                probs = jnp.exp(dot(key, query_t) - lse)
+                both = sorted_kv[at, :]
+                probs = jnp.exp(dot(both, query_t) - lse)
                 if masked and k == count - 1:
                     probs = jnp.where(allowed_tile(first + k, run), probs, 0.0)
-                grad_probs = dot(values[at, :], grad_t)
+                grad_probs = dot(both, grad_t)
                 grad_scores = (probs * (grad_probs - delta)).astype(BF16)
-                dvalues[at, :] += dot(probs.astype(BF16), grad)
-                dkeys[at, :] += dot(grad_scores, query)
+                left = jnp.concatenate([grad_scores, probs.astype(BF16)], axis=1)
+                grad_kv[at, :] += dot(left, right)
                 dq = dq + dot(keys_t[:, at], grad_scores)
             dq_acc[...] = dq
 
-        @pl.when(last >= WIDE)
-        def _():
-            tiles(0, WIDE, False)
-
-        start = (last // WIDE) * WIDE
         for n in range(WIDE):
 
-            @pl.when(last - start == n)
+            @pl.when(last == n)
             def _():
-                tiles(start, n + 1, True)
+                tiles(0, n + 1, True)
 
         pair_rows = trig_ref[lax.rem(r, 2)]
         table = jnp.where(r < 2, rotary_of(pair_rows, 0), rotary_of(pair_rows, 1))
@@ -838,10 +857,11 @@
     lax.fori_loop(0, 4, one_run, 0)
     for j in range(32):
         chip, core, u = j // 4, (j // 2) % 2, j % 2
-        at = pl.ds(pl.multiple_of(key_runs[seq * 32 + j] * 64, 64), 64)
+        at = run_rows(key_runs, seq, chip, core, u)
         rows, lanes = slice(64 * u, 64 * u + 64), slice(HD * core, HD * core + HD)
-        dkv_ref[0, chip, rows, lanes] = dkeys[at, :].astype(BF16)
-        dkv_ref[1, chip, rows, lanes] = dvalues[at, :].astype(BF16)
+        both = grad_kv[at, :].astype(BF16)
+        dkv_ref[0, chip, rows, lanes] = both[:, :HD]
+        dkv_ref[1, chip, rows, lanes] = both[:, HD:]
 
 
 def attend_back(key_runs, query_runs, q, kv, grad, ot, lse, trigs):
@@ -864,11 +884,9 @@
                 pl.BlockSpec((2, 8, 128, 128), lambda i, *_: (0, 0, i, 0)),
             ],
             scratch_shapes=[
-                pltpu.VMEM((2048, HD), BF16),
-                pltpu.VMEM((2048, HD), BF16),
+                pltpu.VMEM((2048, 2 * HD), BF16),
                 pltpu.VMEM((HD, 2048), BF16),
-                pltpu.VMEM((2048, HD), F32),
-                pltpu.VMEM((2048, HD), F32),
+                pltpu.VMEM((2048, 2 * HD), F32),
                 pltpu.VMEM((HD, 256), F32),
             ],
         ),
@@ -1260,7 +1278,7 @@
         + sems(2)
         + [pltpu.SemaphoreType.DMA((12,))],
         compiler_params=pltpu.CompilerParams(
-            collective_id=2, has_side_effects=True, vmem_limit_bytes=62 * 2**20
+            collective_id=2, has_side_effects=True, vmem_limit_bytes=61 * 2**20
         ),
         name="feed_forward",
     )(att, wo, tokens, cot, gain, cots, wgu, wdn, wswap, wnear_up, wnear_down)
@@ -1342,6 +1360,14 @@
     def x_columns(self, z):
         return pl.ds(pl.multiple_of(512 * self.held + 128 * z, 128), 128)
 
+    def side_block(self, dz):
+        held = self.held + 1 - 2 * lax.rem(self.held, 2)
+        z = lax.rem(self.me.z + dz + 4, 4)
+        return self.x_all.at[columns(128)(4 * held + z)]
+
+    def pass_core(self, ref):
+        self.over.append(self.edges.copy(ref, ref, self.core))
+
     def sideways(self):
         own = self.z_all.at[columns(128)(4 * self.me.z + self.held)]
         wait_got(own, self.recv.at[0])
@@ -1350,21 +1376,18 @@
         wait_got(own, self.recv.at[1])
         self.x_ring = RingBlocks(self.me, self.edges, self.x_all, self.x_columns)
         self.x_side = [self.edges.copy(own, own, self.side)]
+        self.over = []
+        self.pass_core(own)
 
     def along(self):
         self.z_side.wait_recv()
         self.z_ring = RingBlocks(self.me, self.edges, self.z_all, self.z_columns)
-        own = self.z_ring.block(0)
-        self.over = [self.edges.copy(own, own, self.core)]
+        self.pass_core(self.z_ring.block(0))
         self.x_ring.relay()
 
     def to_side(self, dz):
         ref = self.x_ring.block(dz)
         self.x_side.append(self.edges.copy(ref, ref, self.side))
-
-    def to_core(self, dz):
-        ref = self.z_ring.block(dz)
-        self.over.append(self.edges.copy(ref, ref, self.core))
 
     def near(self):
         self.x_ring.near()
@@ -1373,17 +1396,18 @@
         self.z_ring.relay()
         self.x_ring.far()
         self.to_side(2)
+        for dz in (1, -1, 2):
+            self.pass_core(self.x_ring.block(dz))
 
     def far(self):
         self.z_ring.near()
-        self.to_core(1)
-        self.to_core(-1)
+        self.pass_core(self.z_ring.block(1))
+        self.pass_core(self.z_ring.block(-1))
         self.z_ring.far()
-        self.to_core(2)
-        for d in self.x_side:
+        self.pass_core(self.z_ring.block(2))
+        for d, dz in zip(self.x_side, (0, 1, -1, 2)):
             d.wait_recv()
-        half = self.x_all.at[:, pl.ds(pl.multiple_of(1024 * self.me.c, 1024), 1024)]
-        self.over.append(self.edges.copy(half, half, self.core))
+            self.pass_core(self.side_block(dz))
 
     def finish(self):
         for d in self.over:
@@ -1392,7 +1416,7 @@
         wait_sent(self.x_piece, self.send.at[1], self.stays)
 
 
-PLANE_EDGES = 1 + 2 * SUM_EDGES + 4 + 5
+PLANE_EDGES = 1 + 2 * SUM_EDGES + 4 + 12
 
 
 class TwoSums:
@@ -1523,10 +1547,7 @@
     early_sum = TwoSums(me, edges, early, EARLY_ROWS, ((64, 64), (128, 128)), early_scratch)
     branch.far()
     branch.near()
-    plane.sideways()
     branch.add_core(0)
-    early_sum.second()
-    branch.second()
     for d in far_copies:
         d.wait_recv()
 
@@ -1546,8 +1567,8 @@
         grads[at, Q_DEV:] = rows.astype(BF16)
         grads_t[Q_DEV:, at] = rows.T.astype(BF16)
 
-    plane.along()
-
+    early_sum.second()
+    branch.second()
     def late_block(i, _):
         cols = pl.ds(pl.multiple_of(512 * i, 512), 512)
         rows = xs[:, :, cols].reshape(8 * TOK, 512)
@@ -1571,17 +1592,16 @@
     part(2)
     part(1)
     ring.far()
+    early_sum.cross()
     part(3)
-    early_sum.cross()
     ring.near()
-    lax.fori_loop(0, 4, late_block, 0)
-    late_sum = SumOfSixteen(me, late, columns(128), late_own, late_got, us, ur, local.at[4])
     part(0)
     ring.add_core(0)
     early_sum.fourth()
+    plane.sideways()
+    lax.fori_loop(0, 4, late_block, 0)
+    late_sum = SumOfSixteen(me, late, columns(128), late_own, late_got, us, ur, local.at[4])
     early_sum.total()
-    plane.near()
-    ring.second()
     wq_deliver = Deliver(me, ds, dr)
 
     def deliver_block(j, src, at):
@@ -1605,8 +1625,11 @@
         ]
         src = early_sum.out[i].at[pl.ds(128, 128)]
         wo_deliver.to_owner(src, dst, me.y // 2, at // 4, lax.rem(at // 2, 2))
+    plane.along()
     late_piece[...] = late_sum.total().astype(BF16)
     deliver_block(4, late_piece, place)
+    ring.second()
+    plane.near()
     branch.arrived()
 
     def out(at):
@@ -1729,7 +1752,7 @@
         + [many((40,)), many, many((16,)), many, many((2,)), many((2,))]
         + [many((7,)), many, many((16,)), many, many((15,)), many, many((5,))],
         compiler_params=pltpu.CompilerParams(
-            collective_id=3, has_side_effects=True, vmem_limit_bytes=60 * 2**20
+            collective_id=3, has_side_effects=True, vmem_limit_bytes=61 * 2**20
         ),
         name="ending",
     )(
@@ -1799,7 +1822,7 @@
     gain_two = gain_mlp.astype(F32).reshape(1, D)
     wgu = w_gate_up.reshape(2 * FF_DEV, D)
     wdn = w_down.T
-    query, kv_table, trigs, xs, wq, poss, kvs, places, cots, wo, wswap = begin(
+    query, kv_table, trigs, runs, xs, wq, kvs, places, cots, wo, wswap = begin(
         hidden[0],
         gain_one,
         jnp.broadcast_to(positions, (8, TOK)),
@@ -1811,10 +1834,8 @@
         w_out,
     )
     wo = wo.reshape(D, Q_DEV)
-    query_runs = poss[:, 0, ::64].reshape(4, 2, 2).transpose(0, 2, 1).reshape(16) // 64
-    key_runs = (
-        places[:, :, 0, ::64].reshape(8, 4, 2, 2).transpose(1, 0, 2, 3).reshape(128) // 64
-    )
+    query_runs = runs[0, :16]
+    key_runs = places[:, 0, :16].reshape(128)
     wnear_up = lax.ppermute(wswap, AXES, route(1))
     wnear_down = lax.ppermute(wswap, AXES, route(3))
     att, ot, lse = attend(key_runs, query_runs, query, kvs)

time: 390 us -> 381 us (0.977)
  Pallas kernels: 363 us -> 357 us
    unnamed x26 -> x10, local copies, waits for them, and re-layouts: 9.37 us -> 3.1 us
  transfers between devices with their start and end apart: 2 -> 2, of which waited for: 0 -> 0; matrix products, arithmetic and copies ran while one was open for 1% -> 1% of each run, Pallas kernels for 7% -> 6%
where the time goes in v7:
time: 381 us; the launch traced here: 375 us
  Pallas kernels  357 us (94%)
  local copies, waits for them, and re-layouts  9.02 us (2%)
  starting transfers between devices  5.5 us (1%)
    pallas_call x1, Pallas kernels, feed_forward(): pl.pallas_call(feed_forward_kernel, out_shape=(shape((TOK, D), F32), shap...  121 us
    pallas_call x1, Pallas kernels, ending(): pl.pallas_call(ending_kernel, out_shape=(shape((TOK, D)), shape((TOK, D),...  101 us
    pallas_call x1, Pallas kernels, begin(): pl.pallas_call(begin_kernel, out_shape=(shape((1024, Q_DEV)), shape((2, 5...  63.6 us
    pallas_call x1, Pallas kernels, attend_back(): pl.pallas_call(attend_back_kernel, out_shape=(shape((1024, 256)), shape((...  34.7 us
    pallas_call x1, Pallas kernels, attend(): pl.pallas_call(attend_kernel, out_shape=(shape((1024, 256)), shape((16, H...  23.8 us
    pallas_call x1, Pallas kernels, widen(): pl.pallas_call(widen_kernel, out_shape=(shape((2 * FF_DEV, D), F32), shap...  12.4 us
  transfers between devices with their start and end apart: 2, of which 0 were waited for; matrix products, arithmetic and copies ran while one was open for 1% of the time, Pallas kernels for 6%

profile of v7, /device:TPU:9, one launch (start us, length us, event | category | flops | bytes accessed | tf_op | source)
XLA Modules:
  0.0 375.1 jit_solution(15049847225377694778)
XLA Ops:
  0.6 0.7 convert_reduce_fusion
  1.3 0.1 convert_element_type.13
  1.4 1.3 reshape.80
  2.7 0.2 multiply_cosine_fusion
  2.9 0.7 copy.19.trig
  3.6 1.2 broadcast_in_dim.16.pos
  4.9 0.0 copy-start.3
  4.9 63.6 %begin.1 = (bf16[1024,256]{1,0:T(8,128)(2,1)}, f32[2,512,128]{2,1,0:T(8,128)}, f32[8,64,128]{2,1,0:T(8,128)}, s32[8,128]{1,0:T(8,128)}, bf16[8,128,2048]{2,1,0:T...) custom-call(bf16[128,2048]{1,0:T(8,128)(2,1)} %bitcast.23, ...), custom_call_target="tpu_custom_call" | custom-call | tf_op jit(solution)/shard_map/begin/pallas_call | solution.py:622
  68.5 2.3 collective-permute-start.1
  70.8 3.2 collective-permute-start
  74.0 0.0 copy-done.3
  74.0 0.6 reshape.82
  74.6 0.8 slice_reduce_fusion
  75.4 0.6 reshape_squeeze.3.key_runs
  75.9 1.2 slice_bitcast_fusion.query_runs
  77.1 23.8 %attend.1 = (bf16[1024,256]{1,0:T(8,128)(2,1)}, f32[16,64,256]{2,1,0:T(8,128)}, f32[16,1,256]{2,1,0:T(1,128)}) custom-call(s32[128]{0:T(128)} %reshape_squeeze.3.key_runs, s32[16]{0:T(128)} %slice_bitcast_fusion.query_runs, bf16[1024,256]{1,0:T(8,128)(2,1)} %get-tuple-element.45.q_ref, bf16[2,8,512,128]{3,2,1,0:T(8,128)(2,1)} %get-tuple-element.46.kv_ref), custom_call_target="tpu_custom_call" | custom-call | tf_op jit(solution)/shard_map/attend/pallas_call | solution.py:769
  101.0 0.0 collective-permute-done.1.wnear_down
  101.0 0.0 copy-start
  101.0 0.0 collective-permute-done.wnear_up
  101.0 1.3 copy-done
  102.3 121.4 %feed_forward.1 = (f32[128,2048]{1,0:T(8,128)}, f32[128,2048]{1,0:T(8,128)}, f32[1,2048]{1,0:T(1,128)}, bf16[1024,256]{1,0:T(8,128)(2,1)}, bf16[256,2048]{1,0:T(...) custom-call(bf16[1024,256]{1,0:T(8,128)(2,1)} %get-tuple-element.47.att, ...), custom_call_target="tpu_custom_call" | custom-call | tf_op jit(solution)/shard_map/feed_forward/pallas_call | solution.py:1253
  223.7 34.7 %attend_back.1 = (bf16[1024,256]{1,0:T(8,128)(2,1)}, bf16[2,8,512,128]{3,2,1,0:T(8,128)(2,1)}) custom-call(s32[128]{0:T(128)} %reshape_squeeze.3.key_runs, s32[16]{0:T(128)} %slice_bitcast_fusion.query_runs, bf16[1024,256]{1,0:T(8,128)(2,1)} %get-tuple-element.45.q_ref, bf16[2,8,512,128]{3,2,1,0:T(8,128)(2,1)} %get-tuple-element.46.kv_ref, ...), custom_call_target="tpu_custom_call" | custom-call | tf_op jit(solution)/shard_map/attend_back/pallas_call | solution.py:868
  258.4 101.0 %ending.1 = (bf16[128,2048]{1,0:T(8,128)(2,1)}, f32[128,2048]{1,0:T(8,128)}, f32[8,256]{1,0:T(8,128)}, bf16[320,2048]{1,0:T(8,128)(2,1)}, bf16[2048,256]{1,0:T(8...) custom-call(bf16[2,8,512,128]{3,2,1,0:T(8,128)(2,1)} %get-tuple-element.55.dkv, ...), custom_call_target="tpu_custom_call" | custom-call | tf_op jit(solution)/shard_map/ending/pallas_call | solution.py:1712
  359.4 1.3 fusion
  360.8 0.0 copy-start.2
  360.8 0.0 copy-start.1
  360.8 12.4 %widen.1 = (f32[1408,2048]{1,0:T(8,128)}, f32[704,2048]{1,0:T(8,128)}, f32[320,2048]{1,0:T(8,128)}, f32[256,2048]{1,0:T(8,128)}) custom-call(bf16[1056,2048]{1,0:T(8,128)(2,1)} %get-tuple-element.70.z_ref, bf16[1056,2048]{1,0:T(8,128)(2,1)} %get-tuple-element.71.x_ref, bf16[320,2048]{1,0:T(8,128)(2,1)} %get-tuple-element.72.wq_ref, ...), custom_call_target="tpu_custom_call" | custom-call | tf_op jit(solution)/shard_map/widen/pallas_call | solution.py:1785
  373.1 0.0 copy-done.2
  373.1 0.8 copy.22
  373.9 0.0 copy-done.1
  373.9 1.0 copy.23
  (2 shorter events, 0.0 us)
Async XLA Ops:
  4.9 69.1 %copy-start.3 = (bf16[2048]{0:T(1024)(128)(2,1)S(1)}, bf16[2048]{0:T(1024)(128)(2,1)}, u32[]{:S(2)}) copy-start(bf16[2048]{0:T(1024)(128)(2,1)} %param.14) | copy-start | bytes 12292
  68.5 32.5 %collective-permute-start.1 = (bf16[528,2048]{1,0:T(8,128)(2,1)}, bf16[528,2048]{1,0:T(8,128)(2,1)S(1)}, u32[]{:S(2)}, u32[]{:S(2)}) collective-permute-start(bf16[528,2048]{1,0:T(8,128)(2,1)} %get-tuple-element.50.wswap), channel_id=1, source_target_pairs={{1,97},{3,99},{5,101},{7,103},{8,104},{10,106},{12,108},{14,110},{... | collective-permute-start | bytes 6488072 | tf_op jit(solution)/shard_map/ppermute | solution.py:1840
  70.8 30.2 %collective-permute-start = (bf16[528,2048]{1,0:T(8,128)(2,1)}, bf16[528,2048]{1,0:T(8,128)(2,1)}, u32[]{:S(2)}, u32[]{:S(2)}) collective-permute-start(bf16[528,2048]{1,0:T(8,128)(2,1)} %get-tuple-element.50.wswap), channel_id=1, source_target_pairs={{1,33},{3,35},{5,37},{7,39},{8,40},{10,42},{12,44},{14,46},{17,49}... | collective-permute-start | bytes 6488072 | tf_op jit(solution)/shard_map/ppermute | solution.py:1839
  101.0 1.3 copy-start
  360.8 12.4 %copy-start.2 = (bf16[128,2048]{1,0:T(8,128)(2,1)S(1)}, bf16[128,2048]{1,0:T(8,128)(2,1)}, u32[]{:S(2)}) copy-start(bf16[128,2048]{1,0:T(8,128)(2,1)} %get-tuple-element.67) | copy-start | bytes 1572868
  360.8 13.2 %copy-start.1 = (f32[128,2048]{1,0:T(8,128)S(1)}, f32[128,2048]{1,0:T(8,128)}, u32[]{:S(2)}) copy-start(f32[128,2048]{1,0:T(8,128)} %get-tuple-element.68) | copy-start | bytes 3145732

commit v8 on v7

--- a/solution.py
+++ b/solution.py
@@ -397,15 +397,15 @@
     return jnp.concatenate([cosine, cosine, -sine, sine], axis=1)
 
 
-ROWS = 16
-
-
-def in_chunks(step, rows=TOK):
+ROWS = 32
+
+
+def in_chunks(step, rows=TOK, chunk=ROWS):
     def one(i, _):
-        step(pl.ds(pl.multiple_of(i * ROWS, ROWS), ROWS))
+        step(pl.ds(pl.multiple_of(i * chunk, chunk), chunk))
         return 0
 
-    lax.fori_loop(0, rows // ROWS, one, 0)
+    lax.fori_loop(0, rows // chunk, one, 0)
 
 
 def mean_last(rows):
@@ -1559,7 +1559,7 @@
             total * kv_table[0, at, :] - swapped_pairs(total) * kv_table[1, at, :]
         )
 
-    in_chunks(kv_total, 512)
+    in_chunks(kv_total, 512, 128)
     for i in range(8):
         rows = dkv_low[64 * i : 64 * (i + 1), :]
         rows = jnp.concatenate([rows[:, :HD], rows[:, HD:]], axis=0)

time: 381 us -> 378 us (level)
  Pallas kernels: 357 us -> 353 us
  transfers between devices with their start and end apart: 2 -> 2, of which waited for: 0 -> 1; matrix products, arithmetic and copies ran while one was open for 1% -> 1% of each run, Pallas kernels for 6% -> 6%
where the time goes in v8:
time: 378 us; the launch traced here: 372 us
  Pallas kernels  353 us (93%)
  local copies, waits for them, and re-layouts  8.44 us (2%)
  starting transfers between devices  5.81 us (2%)
    pallas_call x1, Pallas kernels, feed_forward(): pl.pallas_call(feed_forward_kernel, out_shape=(shape((TOK, D), F32), shap...  121 us
    pallas_call x1, Pallas kernels, ending(): pl.pallas_call(ending_kernel, out_shape=(shape((TOK, D)), shape((TOK, D),...  103 us
    pallas_call x1, Pallas kernels, begin(): pl.pallas_call(begin_kernel, out_shape=(shape((1024, Q_DEV)), shape((2, 5...  63.6 us
    pallas_call x1, Pallas kernels, attend_back(): pl.pallas_call(attend_back_kernel, out_shape=(shape((1024, 256)), shape((...  31.2 us
    pallas_call x1, Pallas kernels, attend(): pl.pallas_call(attend_kernel, out_shape=(shape((1024, 256)), shape((16, H...  21.8 us
    pallas_call x1, Pallas kernels, widen(): pl.pallas_call(widen_kernel, out_shape=(shape((2 * FF_DEV, D), F32), shap...  12.4 us
  transfers between devices with their start and end apart: 2, of which 1 were waited for; matrix products, arithmetic and copies ran while one was open for 1% of the time, Pallas kernels for 6%

profile of v8, /device:TPU:9, one launch (start us, length us, event | category | flops | bytes accessed | tf_op | source)
XLA Modules:
  0.0 371.5 jit_solution(5071313735735593356)
XLA Ops:
  0.6 0.7 convert_reduce_fusion
  1.3 0.1 convert_element_type.13
  1.4 1.3 reshape.80
  2.7 0.2 multiply_cosine_fusion
  2.9 0.7 copy.19.trig
  3.6 1.2 broadcast_in_dim.16.pos
  4.9 0.0 copy-start.3
  4.9 63.6 %begin.1 = (bf16[1024,256]{1,0:T(8,128)(2,1)}, f32[2,512,128]{2,1,0:T(8,128)}, f32[8,64,128]{2,1,0:T(8,128)}, s32[8,128]{1,0:T(8,128)}, bf16[8,128,2048]{2,1,0:T...) custom-call(bf16[128,2048]{1,0:T(8,128)(2,1)} %bitcast.23, ...), custom_call_target="tpu_custom_call" | custom-call | tf_op jit(solution)/shard_map/begin/pallas_call | solution.py:622
  68.5 2.3 collective-permute-start.1
  70.8 3.5 collective-permute-start
  74.3 0.0 copy-done.3
  74.3 0.6 reshape.82
  74.9 0.8 slice_reduce_fusion
  75.7 0.6 reshape_squeeze.3.key_runs
  76.3 1.2 slice_bitcast_fusion.query_runs
  77.4 21.8 %attend.1 = (bf16[1024,256]{1,0:T(8,128)(2,1)}, f32[16,64,256]{2,1,0:T(8,128)}, f32[16,1,256]{2,1,0:T(1,128)}) custom-call(s32[128]{0:T(128)} %reshape_squeeze.3.key_runs, s32[16]{0:T(128)} %slice_bitcast_fusion.query_runs, bf16[1024,256]{1,0:T(8,128)(2,1)} %get-tuple-element.45.q_ref, bf16[2,8,512,128]{3,2,1,0:T(8,128)(2,1)} %get-tuple-element.46.kv_ref), custom_call_target="tpu_custom_call" | custom-call | tf_op jit(solution)/shard_map/attend/pallas_call | solution.py:769
  99.2 0.0 collective-permute-done.1.wnear_down
  99.2 0.0 copy-start
  99.2 0.6 collective-permute-done.wnear_up
  99.8 0.7 copy-done
  100.6 121.0 %feed_forward.1 = (f32[128,2048]{1,0:T(8,128)}, f32[128,2048]{1,0:T(8,128)}, f32[1,2048]{1,0:T(1,128)}, bf16[1024,256]{1,0:T(8,128)(2,1)}, bf16[256,2048]{1,0:T(...) custom-call(bf16[1024,256]{1,0:T(8,128)(2,1)} %get-tuple-element.47.att, ...), custom_call_target="tpu_custom_call" | custom-call | tf_op jit(solution)/shard_map/feed_forward/pallas_call | solution.py:1253
  221.6 31.2 %attend_back.1 = (bf16[1024,256]{1,0:T(8,128)(2,1)}, bf16[2,8,512,128]{3,2,1,0:T(8,128)(2,1)}) custom-call(s32[128]{0:T(128)} %reshape_squeeze.3.key_runs, s32[16]{0:T(128)} %slice_bitcast_fusion.query_runs, bf16[1024,256]{1,0:T(8,128)(2,1)} %get-tuple-element.45.q_ref, bf16[2,8,512,128]{3,2,1,0:T(8,128)(2,1)} %get-tuple-element.46.kv_ref, ...), custom_call_target="tpu_custom_call" | custom-call | tf_op jit(solution)/shard_map/attend_back/pallas_call | solution.py:868
  252.7 102.8 %ending.1 = (bf16[128,2048]{1,0:T(8,128)(2,1)}, f32[128,2048]{1,0:T(8,128)}, f32[8,256]{1,0:T(8,128)}, bf16[320,2048]{1,0:T(8,128)(2,1)}, bf16[2048,256]{1,0:T(8...) custom-call(bf16[2,8,512,128]{3,2,1,0:T(8,128)(2,1)} %get-tuple-element.55.dkv, ...), custom_call_target="tpu_custom_call" | custom-call | tf_op jit(solution)/shard_map/ending/pallas_call | solution.py:1712
  355.6 1.3 fusion
  356.9 0.0 copy-start.2
  356.9 0.0 copy-start.1
  356.9 12.4 %widen.1 = (f32[1408,2048]{1,0:T(8,128)}, f32[704,2048]{1,0:T(8,128)}, f32[320,2048]{1,0:T(8,128)}, f32[256,2048]{1,0:T(8,128)}) custom-call(bf16[1056,2048]{1,0:T(8,128)(2,1)} %get-tuple-element.70.z_ref, bf16[1056,2048]{1,0:T(8,128)(2,1)} %get-tuple-element.71.x_ref, bf16[320,2048]{1,0:T(8,128)(2,1)} %get-tuple-element.72.wq_ref, ...), custom_call_target="tpu_custom_call" | custom-call | tf_op jit(solution)/shard_map/widen/pallas_call | solution.py:1785
  369.3 0.0 copy-done.2
  369.3 0.8 copy.22
  370.1 0.0 copy-done.1
  370.1 1.0 copy.23
  (2 shorter events, 0.0 us)
Async XLA Ops:
  4.9 69.4 %copy-start.3 = (bf16[2048]{0:T(1024)(128)(2,1)S(1)}, bf16[2048]{0:T(1024)(128)(2,1)}, u32[]{:S(2)}) copy-start(bf16[2048]{0:T(1024)(128)(2,1)} %param.14) | copy-start | bytes 12292
  68.5 30.8 %collective-permute-start.1 = (bf16[528,2048]{1,0:T(8,128)(2,1)}, bf16[528,2048]{1,0:T(8,128)(2,1)S(1)}, u32[]{:S(2)}, u32[]{:S(2)}) collective-permute-start(bf16[528,2048]{1,0:T(8,128)(2,1)} %get-tuple-element.50.wswap), channel_id=1, source_target_pairs={{1,97},{3,99},{5,101},{7,103},{8,104},{10,106},{12,108},{14,110},{... | collective-permute-start | bytes 6488072 | tf_op jit(solution)/shard_map/ppermute | solution.py:1840
  70.8 29.0 %collective-permute-start = (bf16[528,2048]{1,0:T(8,128)(2,1)}, bf16[528,2048]{1,0:T(8,128)(2,1)}, u32[]{:S(2)}, u32[]{:S(2)}) collective-permute-start(bf16[528,2048]{1,0:T(8,128)(2,1)} %get-tuple-element.50.wswap), channel_id=1, source_target_pairs={{1,33},{3,35},{5,37},{7,39},{8,40},{10,42},{12,44},{14,46},{17,49}... | collective-permute-start | bytes 6488072 | tf_op jit(solution)/shard_map/ppermute | solution.py:1839
  99.2 1.3 copy-start
  356.9 12.4 %copy-start.2 = (bf16[128,2048]{1,0:T(8,128)(2,1)S(1)}, bf16[128,2048]{1,0:T(8,128)(2,1)}, u32[]{:S(2)}) copy-start(bf16[128,2048]{1,0:T(8,128)(2,1)} %get-tuple-element.67) | copy-start | bytes 1572868
  356.9 13.2 %copy-start.1 = (f32[128,2048]{1,0:T(8,128)S(1)}, f32[128,2048]{1,0:T(8,128)}, u32[]{:S(2)}) copy-start(f32[128,2048]{1,0:T(8,128)} %get-tuple-element.68) | copy-start | bytes 3145732

commit v9 on v8

--- a/solution.py
+++ b/solution.py
@@ -1761,8 +1761,15 @@
     )
 
 
-def widen_kernel(z_ref, x_ref, wq_ref, wo_ref, gu_ref, dn_ref, gq_ref, go_ref):
+def widen_kernel(
+    z_ref, x_ref, wq_ref, wo_ref, out_ref, tokens_ref, gains_ref,
+    gu_ref, dn_ref, gq_ref, go_ref, output_ref, grad_ref, one_ref, two_ref,
+):
     i = pl.program_id(0)
+    output_ref[...] = out_ref[...]
+    grad_ref[...] = tokens_ref[...]
+    one_ref[...] = gains_ref[0:1, :]
+    two_ref[...] = gains_ref[1:2, :]
 
     @pl.when(i < 3)
     def _():
@@ -1780,7 +1787,7 @@
     go_ref[...] = wo_ref[...].astype(F32).T
 
 
-def widen(z_all, x_all, wq, wo):
+def widen(z_all, x_all, wq, wo, output, grad_tokens, gains):
     rows = PART // 3
     return pl.pallas_call(
         widen_kernel,
@@ -1789,6 +1796,10 @@
             shape((FF_DEV, D), F32),
             shape((320, D), F32),
             shape((256, D), F32),
+            shape((TOK, D)),
+            shape((TOK, D), F32),
+            shape((1, 256), F32),
+            shape((1, 256), F32),
         ),
         grid=(6,),
         in_specs=[
@@ -1796,16 +1807,23 @@
             pl.BlockSpec((rows, D), lambda i: (jnp.maximum(i - 3, 0), 0)),
             pl.BlockSpec((64, D), lambda i: (jnp.minimum(i, 4), 0)),
             pl.BlockSpec((512, 256), lambda i: (jnp.minimum(i, 3), 0)),
+            pl.BlockSpec((32, D), lambda i: (jnp.minimum(i, 3), 0)),
+            pl.BlockSpec((32, D), lambda i: (jnp.minimum(i, 3), 0)),
+            pl.BlockSpec((8, 256), lambda i: (0, 0)),
         ],
         out_specs=(
             pl.BlockSpec((rows, D), lambda i: (jnp.minimum(i, 3), 0)),
             pl.BlockSpec((rows, D), lambda i: (jnp.maximum(i - 4, 0), 0)),
             pl.BlockSpec((64, D), lambda i: (jnp.minimum(i, 4), 0)),
             pl.BlockSpec((256, 512), lambda i: (0, jnp.minimum(i, 3))),
+            pl.BlockSpec((32, D), lambda i: (jnp.minimum(i, 3), 0)),
+            pl.BlockSpec((32, D), lambda i: (jnp.minimum(i, 3), 0)),
+            pl.BlockSpec((1, 256), lambda i: (0, 0)),
+            pl.BlockSpec((1, 256), lambda i: (0, 0)),
         ),
         compiler_params=pltpu.CompilerParams(vmem_limit_bytes=61 * 2**20),
         name="widen",
-    )(z_all, x_all, wq, wo)
+    )(z_all, x_all, wq, wo, output, grad_tokens, gains)
 
 
 def route(dz):
@@ -1859,14 +1877,16 @@
         xs,
         branch,
     )
-    grad_gu, grad_dn, grad_w_qkv, grad_w_out = widen(z_all, x_all, grad_w_qkv, grad_w_out)
+    grad_gu, grad_dn, grad_w_qkv, grad_w_out, output, grad_tokens, gain_a, gain_b = widen(
+        z_all, x_all, grad_w_qkv, grad_w_out, output, grad_tokens, gains
+    )
     return (
         output[None],
         grad_tokens[None],
-        gains[0],
+        gain_a.reshape(256),
         grad_w_qkv,
         grad_w_out,
-        gains[1],
+        gain_b.reshape(256),
         grad_gu.reshape(2, FF_DEV, D),
         grad_dn.T,
     )

time: 378 us -> 375 us (level)
  no operation moved by 1% of the time
where the time goes in v9:
time: 375 us; the launch traced here: 368 us
  Pallas kernels  353 us (94%)
  starting transfers between devices  5.5 us (1%)
  local copies, waits for them, and re-layouts  5.32 us (1%)
    pallas_call x1, Pallas kernels, feed_forward(): pl.pallas_call(feed_forward_kernel, out_shape=(shape((TOK, D), F32), shap...  120 us
    pallas_call x1, Pallas kernels, ending(): pl.pallas_call(ending_kernel, out_shape=(shape((TOK, D)), shape((TOK, D),...  103 us
    pallas_call x1, Pallas kernels, begin(): pl.pallas_call(begin_kernel, out_shape=(shape((1024, Q_DEV)), shape((2, 5...  63.6 us
    pallas_call x1, Pallas kernels, attend_back(): pl.pallas_call(attend_back_kernel, out_shape=(shape((1024, 256)), shape((...  31.5 us
    pallas_call x1, Pallas kernels, attend(): pl.pallas_call(attend_kernel, out_shape=(shape((1024, 256)), shape((16, H...  22.1 us
    pallas_call x1, Pallas kernels, widen(): pl.pallas_call(widen_kernel, out_shape=(shape((2 * FF_DEV, D), F32), shap...  13 us
  transfers between devices with their start and end apart: 2, of which 1 were waited for; matrix products, arithmetic and copies ran while one was open for 1% of the time, Pallas kernels for 6%

profile of v9, /device:TPU:9, one launch (start us, length us, event | category | flops | bytes accessed | tf_op | source)
XLA Modules:
  0.0 368.4 jit_solution(14001449116107233188)
XLA Ops:
  0.6 0.7 convert_reduce_fusion
  1.3 0.1 convert_element_type.13
  1.4 1.3 reshape.88
  2.7 0.2 multiply_cosine_fusion
  2.9 0.7 copy.19.trig
  3.6 1.2 broadcast_in_dim.16.pos
  4.9 0.0 copy-start.1
  4.9 63.6 %begin.1 = (bf16[1024,256]{1,0:T(8,128)(2,1)}, f32[2,512,128]{2,1,0:T(8,128)}, f32[8,64,128]{2,1,0:T(8,128)}, s32[8,128]{1,0:T(8,128)}, bf16[8,128,2048]{2,1,0:T...) custom-call(bf16[128,2048]{1,0:T(8,128)(2,1)} %bitcast.23, ...), custom_call_target="tpu_custom_call" | custom-call | tf_op jit(solution)/shard_map/begin/pallas_call | solution.py:622
  68.4 2.3 collective-permute-start.1
  70.8 3.2 collective-permute-start
  74.0 0.0 copy-done.1
  74.0 0.6 reshape.90
  74.6 0.8 slice_reduce_fusion
  75.3 0.6 reshape_squeeze.3.key_runs
  75.9 1.2 slice_bitcast_fusion.query_runs
  77.1 22.1 %attend.1 = (bf16[1024,256]{1,0:T(8,128)(2,1)}, f32[16,64,256]{2,1,0:T(8,128)}, f32[16,1,256]{2,1,0:T(1,128)}) custom-call(s32[128]{0:T(128)} %reshape_squeeze.3.key_runs, s32[16]{0:T(128)} %slice_bitcast_fusion.query_runs, bf16[1024,256]{1,0:T(8,128)(2,1)} %get-tuple-element.49.q_ref, bf16[2,8,512,128]{3,2,1,0:T(8,128)(2,1)} %get-tuple-element.50.kv_ref), custom_call_target="tpu_custom_call" | custom-call | tf_op jit(solution)/shard_map/attend/pallas_call | solution.py:769
  99.2 0.0 collective-permute-done.1.wnear_down
  99.2 0.0 copy-start
  99.2 0.6 collective-permute-done.wnear_up
  99.8 0.7 copy-done
  100.5 120.2 %feed_forward.1 = (f32[128,2048]{1,0:T(8,128)}, f32[128,2048]{1,0:T(8,128)}, f32[1,2048]{1,0:T(1,128)}, bf16[1024,256]{1,0:T(8,128)(2,1)}, bf16[256,2048]{1,0:T(...) custom-call(bf16[1024,256]{1,0:T(8,128)(2,1)} %get-tuple-element.51.att, ...), custom_call_target="tpu_custom_call" | custom-call | tf_op jit(solution)/shard_map/feed_forward/pallas_call | solution.py:1253
  220.8 31.5 %attend_back.1 = (bf16[1024,256]{1,0:T(8,128)(2,1)}, bf16[2,8,512,128]{3,2,1,0:T(8,128)(2,1)}) custom-call(s32[128]{0:T(128)} %reshape_squeeze.3.key_runs, s32[16]{0:T(128)} %slice_bitcast_fusion.query_runs, bf16[1024,256]{1,0:T(8,128)(2,1)} %get-tuple-element.49.q_ref, bf16[2,8,512,128]{3,2,1,0:T(8,128)(2,1)} %get-tuple-element.50.kv_ref, ...), custom_call_target="tpu_custom_call" | custom-call | tf_op jit(solution)/shard_map/attend_back/pallas_call | solution.py:868
  252.3 102.8 %ending.1 = (bf16[128,2048]{1,0:T(8,128)(2,1)}, f32[128,2048]{1,0:T(8,128)}, f32[8,256]{1,0:T(8,128)}, bf16[320,2048]{1,0:T(8,128)(2,1)}, bf16[2048,256]{1,0:T(8...) custom-call(bf16[2,8,512,128]{3,2,1,0:T(8,128)(2,1)} %get-tuple-element.59.dkv, ...), custom_call_target="tpu_custom_call" | custom-call | tf_op jit(solution)/shard_map/ending/pallas_call | solution.py:1712
  355.1 13.0 %widen.1 = (f32[1408,2048]{1,0:T(8,128)}, f32[704,2048]{1,0:T(8,128)}, f32[320,2048]{1,0:T(8,128)}, f32[256,2048]{1,0:T(8,128)}, bf16[128,2048]{1,0:T(8,128)(2,1...) custom-call(bf16[1056,2048]{1,0:T(8,128)(2,1)} %get-tuple-element.71.z_ref, ...), custom_call_target="tpu_custom_call" | custom-call | tf_op jit(solution)/shard_map/widen/pallas_call | solution.py:1792
  (2 shorter events, 0.0 us)
Async XLA Ops:
  4.9 69.1 %copy-start.1 = (bf16[2048]{0:T(1024)(128)(2,1)S(1)}, bf16[2048]{0:T(1024)(128)(2,1)}, u32[]{:S(2)}) copy-start(bf16[2048]{0:T(1024)(128)(2,1)} %param.14) | copy-start | bytes 12292
  68.4 30.7 %collective-permute-start.1 = (bf16[528,2048]{1,0:T(8,128)(2,1)}, bf16[528,2048]{1,0:T(8,128)(2,1)S(1)}, u32[]{:S(2)}, u32[]{:S(2)}) collective-permute-start(bf16[528,2048]{1,0:T(8,128)(2,1)} %get-tuple-element.54.wswap), channel_id=1, source_target_pairs={{1,97},{3,99},{5,101},{7,103},{8,104},{10,106},{12,108},{14,110},{... | collective-permute-start | bytes 6488072 | tf_op jit(solution)/shard_map/ppermute | solution.py:1858
  70.8 29.0 %collective-permute-start = (bf16[528,2048]{1,0:T(8,128)(2,1)}, bf16[528,2048]{1,0:T(8,128)(2,1)}, u32[]{:S(2)}, u32[]{:S(2)}) collective-permute-start(bf16[528,2048]{1,0:T(8,128)(2,1)} %get-tuple-element.54.wswap), channel_id=1, source_target_pairs={{1,33},{3,35},{5,37},{7,39},{8,40},{10,42},{12,44},{14,46},{17,49}... | collective-permute-start | bytes 6488072 | tf_op jit(solution)/shard_map/ppermute | solution.py:1857
  99.2 1.3 copy-start
